TPU v7x, 32 devices: a whole 2x2x4 slice. The times are simulated.
32 devices in a mesh: site: 8 (over z, x), phonon: 4 (over y, core).
Axes of the slice: x: 2, y: 2, z: 4, core: 2. Of those that a mesh axis runs over, the one named last changes fastest.
Arguments:
- state: float32 [8192, 512], P('site', 'phonon'), may hold values from -4.5 to 6.5
- operators: bfloat16 [3, 1024, 1024], replicated, may hold values from -0.1875 to 0.1875
- op_mask: int32 [3, 8, 8], replicated, may hold values 0 or 1
- site_bits: int32 [3], replicated, may hold values from 0 to 2, each once
- field: float32 [3], replicated, may hold values from 0.25 to 1
- site_coupling: float32 [13], replicated, may hold values from 0.1 to 0.6
- mode_coupling: float32 [64], replicated, may hold values from 0.2 to 1
Outputs:
- chebyshev_last: float32 [8192, 512], P('site', 'phonon')
- chebyshev_prev: float32 [8192, 512], P('site', 'phonon')
- moments: float32 [3], replicated
Inputs may be any that keep to these rules, and one draw needn't show every extreme that they name: `site_bits`: each of 0 to 2 exactly once.
All inputs are finite; a program needn't handle non-finite values.
Results may differ from a plain program's by a relative error of at most 0.0011.
The roundings to bfloat16 on the way count: a program that leaves them out, or rounds other values in their place, can miss the bound.
Values sent between devices are 32-bit elements; how exact they have to be, the bound alone decides.
No kernel may reach another device: no remote copies, remote signals or barrier semaphores. Data moves between devices by JAX's collectives and lax.ppermute only.
A program may use at most 64 MiB of HBM per device.

v0:
```python
import jax
import jax.numpy as jnp
from jax import lax
from jax.sharding import PartitionSpec as P

LBITS = 10
MODES = 64
LEV_DEV = 2
STEPS = 3


epsilon = 1e-06


def extended_2(block, sides, width):
    for axis, dim in sides:
        count = lax.axis_size(axis)
        forward = [(i, i + 1) for i in range(count - 1)]
        backward = [(target, source) for source, target in forward]
        low = lax.ppermute(
            lax.slice_in_dim(block, block.shape[dim] - width, None, axis=dim), axis, forward
        )
        high = lax.ppermute(lax.slice_in_dim(block, 0, width, axis=dim), axis, backward)
        block = jnp.concatenate([low, block, high], axis=dim)
    return block


def partner(value, axis, bit):
    mask = 2**bit
    pairs = [(source, source ^ mask) for source in range(lax.axis_size(axis))]
    return lax.ppermute(value, axis, pairs)


def shards(state, operators, op_mask, site_bits, field, site_coupling, mode_coupling):
    site_count = lax.axis_size("site")
    phonon_count = lax.axis_size("phonon")
    bit_count = site_count.bit_length() - 1
    rows_here = state.shape[0]
    columns_here = state.shape[1]
    block_edge = rows_here // op_mask.shape[1]
    expanded = jnp.repeat(jnp.repeat(op_mask, block_edge, axis=1), block_edge, axis=2)
    masked = jnp.where(expanded > 0, operators, jnp.zeros((), jnp.bfloat16))
    entries = jnp.float32(rows_here * columns_here * site_count * phonon_count)
    level_total = jnp.sqrt(jnp.float32(LEV_DEV * phonon_count))
    device = lax.axis_index("site")
    inside = lax.iota(jnp.int32, rows_here)
    weight_rows = jnp.zeros((rows_here,), jnp.float32)
    for position in range(bit_count):
        weight_rows = weight_rows + site_coupling[site_bits[position]] * (
            device >> position & 1
        ).astype(jnp.float32)
    for local_bit in range(LBITS):
        weight_rows = weight_rows + site_coupling[bit_count + local_bit] * (
            inside >> local_bit & 1
        ).astype(jnp.float32)
    levels = (
        lax.axis_index("phonon") * LEV_DEV + lax.iota(jnp.int32, columns_here) // MODES
    ).astype(jnp.float32)
    lower_weight = jnp.sqrt(levels)
    upper_weight = jnp.sqrt(levels + 1.0)
    mode_weight = jnp.tile(mode_coupling, columns_here // MODES) / level_total
    start_squares = lax.psum(jnp.sum(state * state), ("site", "phonon"))
    initial = state / jnp.sqrt(start_squares / entries + epsilon)
    previous = initial
    current = initial
    scale_prev = jnp.float32(1.0)
    moments = []
    for iteration in range(STEPS):
        extended = extended_2(current, (("phonon", 1),), MODES)
        lower_part = extended[:, :columns_here]
        upper_part = extended[:, 2 * MODES :]
        summed = weight_rows[:, None] * (
            mode_weight * (lower_weight * lower_part + upper_weight * upper_part)
        )
        for operate_position in range(bit_count):
            chosen = site_bits[operate_position]
            flipped = partner(current, "site", operate_position)
            product = jnp.dot(
                masked[chosen], flipped.astype(jnp.bfloat16), preferred_element_type=jnp.float32
            )
            summed = summed + (field[chosen] * flipped + product)
        if iteration == 0:
            vector_new = summed
        else:
            vector_new = 2.0 * summed - previous / scale_prev
        squares, intersection = lax.psum(
            (jnp.sum(vector_new * vector_new), jnp.sum(initial * vector_new)), ("site", "phonon")
        )
        scale_now = jnp.sqrt(squares / entries + epsilon)
        updated = vector_new / scale_now
        moment = intersection / (entries * scale_now)
        moments.append(moment)
        previous = current
        current = updated
        scale_prev = scale_now
    return (current, previous, jnp.stack(moments))


def solution(mesh):
    in_specs = (P("site", "phonon"), P(), P(), P(), P(), P(), P())
    out_specs = (P("site", "phonon"), P("site", "phonon"), P())
    return jax.shard_map(shards, mesh=mesh, in_specs=in_specs, out_specs=out_specs, check_vma=False)
```

profile of v0, /device:TPU:0, one launch (start us, length us, event | category | flops | bytes accessed | tf_op | source)
XLA Modules:
  0.0 298.6 jit_solution(18351212490473741110)
XLA Ops:
  0.6 1.8 multiply_reduce_fusion.6
  2.4 1.2 copy.10
  3.7 0.0 copy-start
  3.7 42.3 %psum.49 = f32[]{:T(128)} all-reduce(f32[]{:T(128)} %multiply_reduce_fusion.6), channel_id=1, replica_groups=mesh['site'=8,'phonon'=4] {'site','phonon'}, use_global_device_ids=true, to_apply=%region_1.2 | all-reduce | flops 1 | bytes 8 | tf_op jit(solution)/shard_map/psum | solution.py:62
  46.6 0.9 broadcast_divide_fusion.3
  47.5 1.5 collective-permute-start.3
  49.0 2.3 collective-permute-start.2
  51.3 1.3 collective-permute-start.4
  52.5 1.9 fusion.90
  54.4 1.3 collective-permute-start
  55.7 1.3 collective-permute-start.1
  57.0 1.4 fusion.93
  62.2 0.7 broadcast_compare_fusion
  62.9 0.1 broadcast_in_dim.8
  63.0 4.6 %broadcast_in_dim.9 = pred[3,1024,8,128]{3,2,1,0:T(8,128)(4,1)S(1)} broadcast(pred[3,1024,8]{2,1,0:T(8,128)(4,1)S(1)} %bitcast.58), dimensions={0,1,2} | broadcast | bytes 3170304 | tf_op jit(solution)/shard_map/broadcast_in_dim | solution.py:41
  67.6 6.2 %gt.17 = pred[3,1024,1024]{2,1,0:T(8,128)(4,1)} reshape(pred[3,1024,8,128]{3,2,1,0:T(8,128)(4,1)S(1)} %broadcast_in_dim.9) | data formatting | bytes 6291456 | tf_op jit(solution)/shard_map/gt | solution.py:42
  75.7 0.0 copy-start.4
  75.8 0.0 copy-start.2
  75.8 0.0 copy-start.3
  75.8 7.0 %broadcast_select_fusion = bf16[3,1024,1024]{2,1,0:T(8,128)(2,1)} fusion(pred[3,1024,1024]{2,1,0:T(8,128)(4,1)} %gt.17, bf16[3,1024,1024]{2,1,0:T(8,128)(2,1)} %param.8), kind=kLoop, calls=%fused_computation | loop fusion | flops 3145728 | bytes 15728640 | tf_op jit(solution)/shard_map/jit(_where)/select_n | solution.py:42
  82.8 0.7 fusion.91
  85.4 6.2 %multiply_add_fusion = f32[1024]{0:T(1024)S(1)} fusion(f32[]{:T(128)} %bitcast.15, f32[]{:T(128)} %bitcast.14, f32[]{:T(128)} %bitcast.13, f32[]{:T(128)} %bitcast.12, f32[]{:T(128)} %bitcast.11, f32[]{:T(128)} %bitcast.10, f32[]{:T(128)} %bitcast.9, f32[]{:T(128)} %bitcast.8, f32[]{:T(128)} %bitcast.7, f32[]{:T(128)} %bitcast.6, f32[]{:T(128)S(6)} %add.240), kind=kLoop, calls=%fused_computation.83 | loop fusion | flops 51200 | bytes 4140 | tf_op jit(solution)/shard_map/add | solution.py:53
  95.4 0.1 div.75
  95.5 0.6 fusion.92
  96.2 2.5 fusion.10
  98.7 0.0 collective-permute-done.2
  98.7 2.5 fusion.16
  101.2 0.0 collective-permute-done
  101.2 0.0 collective-permute-done.1
  101.2 0.0 copy-start.1
  101.2 6.1 %multiply_reduce_fusion.2 = (f32[]{:T(128)}, f32[]{:T(128)}, f32[1024,128]{0,1:T(8,128)S(1)}) fusion(f32[1024,128]{0,1:T(8,128)} %broadcast_divide_fusion.3, f32[1024,128]{0,1:T(8,128)} %collective-permute-done.4, bf16[3,1024,1024]{2,1,0:T(8,128)(2,1)} %broadcast_select_fusion, s32[]{:T(128)S(6)} %select_n.56, f32[]{:T(128)} %bitcast.21, ...), kind=kOutput, calls=%fused_computation.64 | convolution fusion | flops 271187968 | bytes 6822924 | tf_op jit(solution)/shard_map/dot_general | solution.py:78
  107.4 42.7 %psum.50 = f32[]{:T(128)} all-reduce(f32[]{:T(128)} %get-tuple-element.7), channel_id=1, replica_groups=mesh['site'=8,'phonon'=4] {'site','phonon'}, use_global_device_ids=true, to_apply=%region_3.4 | all-reduce | flops 1 | bytes 8 | tf_op jit(solution)/shard_map/psum | solution.py:86
  150.8 0.1 broadcast_divide_fusion.2
  150.8 2.3 collective-permute-start.7
  153.2 0.3 collective-permute-start.8
  153.5 1.7 collective-permute-start.9
  155.3 1.3 collective-permute-start.5
  156.6 1.3 collective-permute-start.6
  157.9 6.0 %collective-permute-done.7 = f32[1024,128]{0,1:T(8,128)S(1)} collective-permute-done((f32[1024,128]{0,1:T(8,128)S(1)}, f32[1024,128]{0,1:T(8,128)S(1)}, u32[]{:S(2)}, u32[]{:S(2)}) %collective-permute-start.7) | collective-permute-done | bytes 524320 | tf_op jit(solution)/shard_map/ppermute | solution.py:31
  163.9 2.4 fusion.14
  166.3 9.0 %collective-permute-done.8 = f32[1024,128]{0,1:T(8,128)S(1)} collective-permute-done((f32[1024,128]{0,1:T(8,128)S(1)}, f32[1024,128]{0,1:T(8,128)S(1)}, u32[]{:S(2)}, u32[]{:S(2)}) %collective-permute-start.8) | collective-permute-done | bytes 524320 | tf_op jit(solution)/shard_map/ppermute | solution.py:31
  175.3 2.4 fusion.8
  177.8 0.0 collective-permute-done.5
  177.8 0.0 collective-permute-done.9
  177.8 5.3 %multiply_reduce_fusion.1 = (f32[]{:T(128)}, f32[]{:T(128)}, f32[1024,128]{0,1:T(8,128)S(1)}) fusion(f32[1024,128]{0,1:T(8,128)S(1)} %copy-done.1, f32[]{:T(128)S(6)} %multiply.19, f32[1024,128]{0,1:T(8,128)} %collective-permute-done.9, bf16[3,1024,1024]{2,1,0:T(8,128)(2,1)} %broadcast_select_fusion, s32[]{:T(128)S(6)} %select_n.56, f32[]{:T(128)} %bitcast.21, ...), kind=kOutput, calls=%fused_computation.63 | convolution fusion | flops 271712256 | bytes 7347220 | tf_op jit(solution)/shard_map/dot_general | solution.py:78
  183.2 37.5 %psum.51 = f32[]{:T(128)} all-reduce(f32[]{:T(128)} %get-tuple-element.9), channel_id=1, replica_groups=mesh['site'=8,'phonon'=4] {'site','phonon'}, use_global_device_ids=true, to_apply=%region_5.6 | all-reduce | flops 1 | bytes 8 | tf_op jit(solution)/shard_map/psum | solution.py:86
  221.4 0.1 broadcast_divide_fusion.1
  221.4 2.3 collective-permute-start.12
  223.8 2.4 collective-permute-start.13
  226.2 0.6 collective-permute-start.14
  226.8 1.0 copy.16
  227.8 1.3 collective-permute-start.10
  229.1 1.3 collective-permute-start.11
  230.4 4.7 %collective-permute-done.12 = f32[1024,128]{0,1:T(8,128)S(1)} collective-permute-done((f32[1024,128]{0,1:T(8,128)S(1)}, f32[1024,128]{0,1:T(8,128)S(1)}, u32[]{:S(2)}, u32[]{:S(2)}) %collective-permute-start.12) | collective-permute-done | bytes 524320 | tf_op jit(solution)/shard_map/ppermute | solution.py:31
  235.1 2.4 fusion.12
  237.5 10.3 %collective-permute-done.13 = f32[1024,128]{0,1:T(8,128)S(1)} collective-permute-done((f32[1024,128]{0,1:T(8,128)S(1)}, f32[1024,128]{0,1:T(8,128)S(1)}, u32[]{:S(2)}, u32[]{:S(2)}) %collective-permute-start.13) | collective-permute-done | bytes 524320 | tf_op jit(solution)/shard_map/ppermute | solution.py:31
  247.8 2.4 fusion.6
  250.3 0.0 collective-permute-done.10
  250.3 0.7 collective-permute-done.14
  251.0 5.3 %multiply_reduce_fusion = (f32[]{:T(128)}, f32[]{:T(128)}, f32[1024,128]{0,1:T(8,128)S(1)}) fusion(f32[1024,128]{0,1:T(8,128)S(1)} %get-tuple-element.41, f32[]{:T(128)S(6)} %multiply.20, f32[1024,128]{0,1:T(8,128)} %collective-permute-done.14, bf16[3,1024,1024]{2,1,0:T(8,128)(2,1)} %broadcast_select_fusion, s32[]{:T(128)S(6)} %select_n.56, f32[]{:T(128)} %bitcast.21, ...), kind=kOutput, calls=%fused_computation.62 | convolution fusion | flops 271712256 | bytes 7871508 | tf_op jit(solution)/shard_map/dot_general | solution.py:78
  256.3 38.1 %all-reduce = (f32[]{:T(128)}, f32[]{:T(128)}, f32[]{:T(128)}, f32[]{:T(128)}) all-reduce(f32[]{:T(128)} %get-tuple-element.11, f32[]{:T(128)} %get-tuple-element.10, f32[]{:T(128)} %get-tuple-element.8, f32[]{:T(128)} %get-tuple-element.6), channel_id=1, replica_groups=mesh['site'=8,'phonon'=4] {'site','phonon'}, use_global_device_ids=true, to_apply=%region_7.8 | all-reduce | flops 4 | bytes 32 | tf_op jit(solution)/shard_map/psum | solution.py:86
  295.0 0.1 broadcast_divide_fusion
  295.1 1.0 copy.15
  298.0 0.6 pad_maximum_fusion.6
  (14 shorter events, 0.1 us)
Async XLA Ops:
  3.7 59.3 %copy-start = (f32[1024,128]{0,1:T(8,128)}, f32[1024,128]{0,1:T(8,128)S(1)}, u32[]{:S(2)}) copy-start(f32[1024,128]{0,1:T(8,128)S(1)} %copy.10) | copy-start | bytes 1572868
  47.5 48.7 %collective-permute-start.3 = (f32[1024,128]{0,1:T(8,128)}, f32[1024,128]{0,1:T(8,128)}, u32[]{:S(2)}, u32[]{:S(2)}) collective-permute-start(f32[1024,128]{0,1:T(8,128)} %broadcast_divide_fusion.3), channel_id=1, source_target_pairs={{0,8},{4,12},{8,0},{12,4},{16,24},{20,28},{24,16},{28,20},{1,9},{5... | collective-permute-start | bytes 1572872 | tf_op jit(solution)/shard_map/ppermute | solution.py:31
  49.0 49.7 %collective-permute-start.2 = (f32[1024,128]{0,1:T(8,128)}, f32[1024,128]{0,1:T(8,128)}, u32[]{:S(2)}, u32[]{:S(2)}) collective-permute-start(f32[1024,128]{0,1:T(8,128)} %broadcast_divide_fusion.3), channel_id=1, source_target_pairs={{0,4},{4,0},{8,12},{12,8},{16,20},{20,16},{24,28},{28,24},{1,5},{5... | collective-permute-start | bytes 1572872 | tf_op jit(solution)/shard_map/ppermute | solution.py:31
  51.3 50.0 %collective-permute-start.4 = (f32[1024,128]{0,1:T(8,128)}, f32[1024,128]{0,1:T(8,128)}, u32[]{:S(2)}, u32[]{:S(2)}) collective-permute-start(f32[1024,128]{0,1:T(8,128)} %broadcast_divide_fusion.3), channel_id=1, source_target_pairs={{0,16},{4,20},{8,24},{12,28},{16,0},{20,4},{24,8},{28,12},{1,17},{... | collective-permute-start | bytes 1572872 | tf_op jit(solution)/shard_map/ppermute | solution.py:31
  54.4 46.8 %collective-permute-start = (f32[1024,64]{0,1:T(8,128)}, f32[1024,64]{0,1:T(8,128)S(1)}, u32[]{:S(2)}, u32[]{:S(2)}) collective-permute-start(f32[1024,64]{0,1:T(8,128)} %get-tuple-element.20), channel_id=1, source_target_pairs={{0,1},{1,2},{2,3},{4,5},{5,6},{6,7},{8,9},{9,10},{10,11},{12,13},{... | collective-permute-start | bytes 786440 | tf_op jit(solution)/shard_map/ppermute | solution.py:20
  55.7 45.5 %collective-permute-start.1 = (f32[1024,64]{0,1:T(8,128)}, f32[1024,64]{0,1:T(8,128)}, u32[]{:S(2)}, u32[]{:S(2)}) collective-permute-start(f32[1024,64]{0,1:T(8,128)} %get-tuple-element.21), channel_id=1, source_target_pairs={{1,0},{2,1},{3,2},{5,4},{6,5},{7,6},{9,8},{10,9},{11,10},{13,12},{... | collective-permute-start | bytes 786440 | tf_op jit(solution)/shard_map/ppermute | solution.py:23
  75.7 7.1 %copy-start.4 = (f32[64]{0:T(128)S(1)}, f32[64]{0:T(128)}, u32[]{:S(2)}) copy-start(f32[64]{0:T(128)} %param.13) | copy-start | bytes 772
  75.8 7.1 %copy-start.2 = (f32[13]{0:T(128)S(1)}, f32[13]{0:T(128)}, u32[]{:S(2)}) copy-start(f32[13]{0:T(128)} %param.12) | copy-start | bytes 160
  75.8 19.7 %copy-start.3 = (f32[3]{0:T(128)S(1)}, f32[3]{0:T(128)}, u32[]{:S(2)}) copy-start(f32[3]{0:T(128)} %param.11) | copy-start | bytes 40
  101.2 76.6 %copy-start.1 = (f32[1024,128]{0,1:T(8,128)S(1)}, f32[1024,128]{0,1:T(8,128)}, u32[]{:S(2)}) copy-start(f32[1024,128]{0,1:T(8,128)} %copy-done) | copy-start | bytes 1572868
  150.8 13.1 %collective-permute-start.7 = (f32[1024,128]{0,1:T(8,128)S(1)}, f32[1024,128]{0,1:T(8,128)S(1)}, u32[]{:S(2)}, u32[]{:S(2)}) collective-permute-start(f32[1024,128]{0,1:T(8,128)S(1)} %broadcast_divide_fusion.2), channel_id=1, source_target_pairs={{0,4},{4,0},{8,12},{12,8},{16,20},{20,16},{24,28},{28,24},{1,5},{5... | collective-permute-start | bytes 1572872 | tf_op jit(solution)/shard_map/ppermute | solution.py:31
  153.2 22.2 %collective-permute-start.8 = (f32[1024,128]{0,1:T(8,128)S(1)}, f32[1024,128]{0,1:T(8,128)S(1)}, u32[]{:S(2)}, u32[]{:S(2)}) collective-permute-start(f32[1024,128]{0,1:T(8,128)S(1)} %broadcast_divide_fusion.2), channel_id=1, source_target_pairs={{0,8},{4,12},{8,0},{12,4},{16,24},{20,28},{24,16},{28,20},{1,9},{5... | collective-permute-start | bytes 1572872 | tf_op jit(solution)/shard_map/ppermute | solution.py:31
  153.5 24.3 %collective-permute-start.9 = (f32[1024,128]{0,1:T(8,128)S(1)}, f32[1024,128]{0,1:T(8,128)}, u32[]{:S(2)}, u32[]{:S(2)}) collective-permute-start(f32[1024,128]{0,1:T(8,128)S(1)} %broadcast_divide_fusion.2), channel_id=1, source_target_pairs={{0,16},{4,20},{8,24},{12,28},{16,0},{20,4},{24,8},{28,12},{1,17},{... | collective-permute-start | bytes 1572872 | tf_op jit(solution)/shard_map/ppermute | solution.py:31
  155.3 22.5 %collective-permute-start.5 = (f32[1024,64]{0,1:T(8,128)S(1)}, f32[1024,64]{0,1:T(8,128)S(1)}, u32[]{:S(2)}, u32[]{:S(2)}) collective-permute-start(f32[1024,64]{0,1:T(8,128)S(1)} %get-tuple-element.18), channel_id=1, source_target_pairs={{0,1},{1,2},{2,3},{4,5},{5,6},{6,7},{8,9},{9,10},{10,11},{12,13},{... | collective-permute-start | bytes 786440 | tf_op jit(solution)/shard_map/ppermute | solution.py:20
  156.6 21.2 %collective-permute-start.6 = (f32[1024,64]{0,1:T(8,128)S(1)}, f32[1024,64]{0,1:T(8,128)S(1)}, u32[]{:S(2)}, u32[]{:S(2)}) collective-permute-start(f32[1024,64]{0,1:T(8,128)S(1)} %get-tuple-element.19), channel_id=1, source_target_pairs={{1,0},{2,1},{3,2},{5,4},{6,5},{7,6},{9,8},{10,9},{11,10},{13,12},{... | collective-permute-start | bytes 786440 | tf_op jit(solution)/shard_map/ppermute | solution.py:23
  221.4 13.6 %collective-permute-start.12 = (f32[1024,128]{0,1:T(8,128)S(1)}, f32[1024,128]{0,1:T(8,128)S(1)}, u32[]{:S(2)}, u32[]{:S(2)}) collective-permute-start(f32[1024,128]{0,1:T(8,128)S(1)} %broadcast_divide_fusion.1), channel_id=1, source_target_pairs={{0,4},{4,0},{8,12},{12,8},{16,20},{20,16},{24,28},{28,24},{1,5},{5... | collective-permute-start | bytes 1572872 | tf_op jit(solution)/shard_map/ppermute | solution.py:31
  223.8 24.0 %collective-permute-start.13 = (f32[1024,128]{0,1:T(8,128)S(1)}, f32[1024,128]{0,1:T(8,128)S(1)}, u32[]{:S(2)}, u32[]{:S(2)}) collective-permute-start(f32[1024,128]{0,1:T(8,128)S(1)} %broadcast_divide_fusion.1), channel_id=1, source_target_pairs={{0,8},{4,12},{8,0},{12,4},{16,24},{20,28},{24,16},{28,20},{1,9},{5... | collective-permute-start | bytes 1572872 | tf_op jit(solution)/shard_map/ppermute | solution.py:31
  226.2 24.8 %collective-permute-start.14 = (f32[1024,128]{0,1:T(8,128)S(1)}, f32[1024,128]{0,1:T(8,128)}, u32[]{:S(2)}, u32[]{:S(2)}) collective-permute-start(f32[1024,128]{0,1:T(8,128)S(1)} %broadcast_divide_fusion.1), channel_id=1, source_target_pairs={{0,16},{4,20},{8,24},{12,28},{16,0},{20,4},{24,8},{28,12},{1,17},{... | collective-permute-start | bytes 1572872 | tf_op jit(solution)/shard_map/ppermute | solution.py:31
  227.8 22.5 %collective-permute-start.10 = (f32[1024,64]{0,1:T(8,128)S(1)}, f32[1024,64]{0,1:T(8,128)S(1)}, u32[]{:S(2)}, u32[]{:S(2)}) collective-permute-start(f32[1024,64]{0,1:T(8,128)S(1)} %get-tuple-element.16), channel_id=1, source_target_pairs={{0,1},{1,2},{2,3},{4,5},{5,6},{6,7},{8,9},{9,10},{10,11},{12,13},{... | collective-permute-start | bytes 786440 | tf_op jit(solution)/shard_map/ppermute | solution.py:20
  229.1 21.2 %collective-permute-start.11 = (f32[1024,64]{0,1:T(8,128)S(1)}, f32[1024,64]{0,1:T(8,128)S(1)}, u32[]{:S(2)}, u32[]{:S(2)}) collective-permute-start(f32[1024,64]{0,1:T(8,128)S(1)} %get-tuple-element.17), channel_id=1, source_target_pairs={{1,0},{2,1},{3,2},{5,4},{6,5},{7,6},{9,8},{10,9},{11,10},{13,12},{... | collective-permute-start | bytes 786440 | tf_op jit(solution)/shard_map/ppermute | solution.py:23
where the time goes:
time: 300 us; the launch traced here: 299 us
  blocking collectives  161 us (54%)
  matrix products  31.5 us (10%)
  waiting for transfers between devices  30.8 us (10%)
  starting transfers between devices  22.5 us (8%)
  local copies, waits for them, and re-layouts  19 us (6%)
  other arithmetic  17.4 us (6%)
  between operations  17 us (6%)
    psum x3, blocking collectives, shards(): lax.psum((jnp.sum(vector_new * vector_new), jnp.sum(initial * vector_new)...  118 us
    psum x1, blocking collectives, shards(): start_squares = lax.psum(jnp.sum(state * state), ('site', 'phonon'))  42.3 us
    dot_general x9, matrix products, shards(): jnp.dot(masked[chosen], flipped.astype(jnp.bfloat16), preferred_element_t...  31.5 us
    ppermute x9, waiting for transfers between devices, partner(): return lax.ppermute(value, axis, pairs)  30.7 us
    ppermute x9, starting transfers between devices, partner(): return lax.ppermute(value, axis, pairs)  14.7 us
    select_n x1, other arithmetic, shards(): masked = jnp.where(expanded > 0, operators, jnp.zeros((), jnp.bfloat16))  7.02 us
    gt x1, local copies, waits for them, and re-layouts, shards(): masked = jnp.where(expanded > 0, operators, jnp.zeros((), jnp.bfloat16))  6.23 us
    add x1, other arithmetic, shards(): weight_rows + site_coupling[bit_count + local_bit] * (inside >> local_bit...  6.23 us
  transfers between devices with their start and end apart: 15, of which 5 were waited for; matrix products, arithmetic and copies ran while one was open for 15% of the time, Pallas kernels for 0%

commit v1 on v0

--- a/solution.py
+++ b/solution.py
@@ -5,11 +5,105 @@
 
 LBITS = 10
 MODES = 64
-LEV_DEV = 2
 STEPS = 3
+LANES = 128
+AXES = ("site", "phonon")
+
+epsilon = 1e-06
 
 
-epsilon = 1e-06
+def exchange(block):
+    return lax.all_to_all(block, AXES, 0, 0, tiled=True)
+
+
+def shards(state, operators, op_mask, site_bits, field, site_coupling, mode_coupling):
+    site_count = lax.axis_size("site")
+    phonon_count = lax.axis_size("phonon")
+    groups = site_count * phonon_count
+    bit_count = site_count.bit_length() - 1
+    rows, columns = state.shape
+    levels_here = columns // MODES
+    level_count = levels_here * phonon_count
+    share = MODES // groups
+    entries = jnp.float32(rows * columns * groups)
+    block_edge = rows // op_mask.shape[1]
+    me = lax.axis_index("site") * phonon_count + lax.axis_index("phonon")
+
+    expanded = jnp.repeat(jnp.repeat(op_mask, block_edge, axis=1), block_edge, axis=2)
+    masked = jnp.where(expanded > 0, operators, jnp.zeros((), jnp.bfloat16))
+
+    outgoing = state.reshape(rows, levels_here, groups, share).transpose(2, 1, 3, 0)
+    outgoing = outgoing.reshape(groups, levels_here * share, rows)
+    tail = jnp.full((groups, levels_here * share, LANES), jnp.sum(state * state))
+    arrived = exchange(jnp.concatenate([outgoing, tail], axis=2))
+    start_squares = jnp.sum(arrived[:, 0, rows])
+    scale = jnp.sqrt(start_squares / entries + epsilon)
+    shape = (site_count, level_count, share, rows)
+    initial = (arrived[:, :, :rows] / scale).reshape(shape)
+
+    bits = lax.iota(jnp.int32, rows)
+    device = lax.iota(jnp.int32, site_count)
+    weight = jnp.zeros((site_count, rows), jnp.float32)
+    for position in range(bit_count):
+        weight = weight + site_coupling[site_bits[position]] * (device >> position & 1).astype(jnp.float32)[:, None]
+    for local_bit in range(LBITS):
+        weight = weight + site_coupling[bit_count + local_bit] * (bits >> local_bit & 1).astype(jnp.float32)
+    modes = lax.dynamic_slice(mode_coupling, (me * share,), (share,)) / jnp.sqrt(jnp.float32(level_count))
+    levels = lax.iota(jnp.float32, level_count)
+    lower_weight = (jnp.sqrt(levels)[:, None] * modes)[None, :, :, None]
+    upper_weight = (jnp.sqrt(levels + 1.0)[:, None] * modes)[None, :, :, None]
+    weight = weight[:, None, None, :]
+
+    def operate(vector, exact):
+        lower = jnp.pad(vector, ((0, 0), (1, 0), (0, 0), (0, 0)))[:, :level_count]
+        upper = jnp.pad(vector, ((0, 0), (0, 1), (0, 0), (0, 0)))[:, 1:]
+        total = weight * (lower_weight * lower + upper_weight * upper)
+        high = vector.astype(jnp.bfloat16)
+        parts = [high]
+        if exact:
+            parts.append((vector - high.astype(jnp.float32)).astype(jnp.bfloat16))
+        for position in range(bit_count):
+            chosen = site_bits[position]
+            part_total = field[chosen] * vector
+            for part in parts:
+                part_total = part_total + lax.dot_general(
+                    part, masked[chosen], (((3,), (1,)), ((), ())), preferred_element_type=jnp.float32
+                )
+            total = total + jnp.stack([part_total[index ^ (1 << position)] for index in range(site_count)])
+        return total
+
+    first = operate(initial, False)
+    second = 2.0 * operate(first, True) - initial
+    third = 2.0 * operate(second, True) - first
+    sums = []
+    for vector in (first, second, third):
+        sums += [jnp.sum(vector * vector), jnp.sum(initial * vector)]
+    tail = jnp.pad(jnp.stack(sums), (0, LANES - 2 * STEPS))
+    packed = jnp.concatenate(
+        [
+            second.reshape(groups, levels_here * share, rows),
+            third.reshape(groups, levels_here * share, rows),
+            jnp.broadcast_to(tail, (groups, levels_here * share, LANES)),
+        ],
+        axis=2,
+    )
+    back = exchange(packed)
+    sums = jnp.sum(back[:, 0, 2 * rows :], axis=0)
+    running = jnp.float32(1.0)
+    scales = []
+    moments = []
+    for step in range(STEPS):
+        running = running * jnp.sqrt(sums[2 * step] / entries / (running * running) + epsilon)
+        scales.append(running)
+        moments.append(sums[2 * step + 1] / (entries * running))
+
+    def placed(block, factor):
+        block = (block / factor).reshape(groups, levels_here, share, rows)
+        return block.transpose(3, 1, 0, 2).reshape(rows, columns)
+
+    last = placed(back[:, :, rows : 2 * rows], scales[2])
+    before = placed(back[:, :, :rows], scales[1])
+    return last, before, jnp.stack(moments)
 
 
 def extended_2(block, sides, width):
@@ -31,17 +125,18 @@
     return lax.ppermute(value, axis, pairs)
 
 
-def shards(state, operators, op_mask, site_bits, field, site_coupling, mode_coupling):
+def halo_shards(state, operators, op_mask, site_bits, field, site_coupling, mode_coupling):
     site_count = lax.axis_size("site")
     phonon_count = lax.axis_size("phonon")
     bit_count = site_count.bit_length() - 1
     rows_here = state.shape[0]
     columns_here = state.shape[1]
+    levels_here = columns_here // MODES
     block_edge = rows_here // op_mask.shape[1]
     expanded = jnp.repeat(jnp.repeat(op_mask, block_edge, axis=1), block_edge, axis=2)
     masked = jnp.where(expanded > 0, operators, jnp.zeros((), jnp.bfloat16))
     entries = jnp.float32(rows_here * columns_here * site_count * phonon_count)
-    level_total = jnp.sqrt(jnp.float32(LEV_DEV * phonon_count))
+    level_total = jnp.sqrt(jnp.float32(levels_here * phonon_count))
     device = lax.axis_index("site")
     inside = lax.iota(jnp.int32, rows_here)
     weight_rows = jnp.zeros((rows_here,), jnp.float32)
@@ -54,7 +149,7 @@
             inside >> local_bit & 1
         ).astype(jnp.float32)
     levels = (
-        lax.axis_index("phonon") * LEV_DEV + lax.iota(jnp.int32, columns_here) // MODES
+        lax.axis_index("phonon") * levels_here + lax.iota(jnp.int32, columns_here) // MODES
     ).astype(jnp.float32)
     lower_weight = jnp.sqrt(levels)
     upper_weight = jnp.sqrt(levels + 1.0)
@@ -99,4 +194,6 @@
 def solution(mesh):
     in_specs = (P("site", "phonon"), P(), P(), P(), P(), P(), P())
     out_specs = (P("site", "phonon"), P("site", "phonon"), P())
-    return jax.shard_map(shards, mesh=mesh, in_specs=in_specs, out_specs=out_specs, check_vma=False)
+    groups = mesh.shape["site"] * mesh.shape["phonon"]
+    body = shards if MODES % groups == 0 else halo_shards
+    return jax.shard_map(body, mesh=mesh, in_specs=in_specs, out_specs=out_specs, check_vma=False)

time: 300 us -> 132 us (0.44)
  blocking collectives: 161 us -> 34.9 us
  waiting for transfers between devices: 30.8 us -> 0.01 us
  starting transfers between devices: 22.5 us -> 7.41 us
  matrix products: 31.5 us -> 21.5 us
  local copies, waits for them, and re-layouts: 19 us -> 27.6 us
  other arithmetic: 17.4 us -> 23.6 us
    psum x4 -> x0, blocking collectives: 161 us -> none  [the longest x3 118 us: shards(): lax.psum((jnp.sum(vector_new * vector_new), jnp.sum(initial * vector_new)...]
    all_to_all x0 -> x1, blocking collectives: none -> 34.9 us  [exchange(): return lax.all_to_all(block, AXES, 0, 0, tiled=True)]
    ppermute x15 -> x0, waiting for transfers between devices: 30.8 us -> none  [the longest x9 30.7 us: partner(): return lax.ppermute(value, axis, pairs)]
    ppermute x15 -> x0, starting transfers between devices: 22.5 us -> none  [the longest x9 14.7 us: partner(): return lax.ppermute(value, axis, pairs)]
    dot_general x9 -> x15, matrix products: 31.5 us -> 21.5 us  [operate(): lax.dot_general(part, masked[chosen], (((3,), (1,)), ((), ())), preferred...]
    all_to_all x0 -> x1, starting transfers between devices: none -> 7.41 us  [exchange(): return lax.all_to_all(block, AXES, 0, 0, tiled=True)]
    mul x0 -> x6, other arithmetic: none -> 6.41 us  [the longest x5 6.34 us: shards(): site_coupling[bit_count + local_bit]]
    add x1 -> x2, other arithmetic: 6.23 us -> 1.9 us  [the longest x1 1.81 us: shards(): weight + site_coupling[site_bits[position]] * (device >> position & 1).as...]
  transfers between devices with their start and end apart: 15 -> 1, of which waited for: 5 -> 0; matrix products, arithmetic and copies ran while one was open for 15% -> 22% of each run, Pallas kernels for 0% -> 0%
where the time goes in v1:
time: 132 us; the launch traced here: 131 us
  blocking collectives  34.9 us (26%)
  local copies, waits for them, and re-layouts  27.6 us (21%)
  other arithmetic  23.6 us (18%)
  matrix products  21.5 us (16%)
  between operations  15.8 us (12%)
  starting transfers between devices  7.41 us (6%)
    all_to_all x1, blocking collectives, exchange(): return lax.all_to_all(block, AXES, 0, 0, tiled=True)  34.9 us
    dot_general x15, matrix products, operate(): lax.dot_general(part, masked[chosen], (((3,), (1,)), ((), ())), preferred...  21.5 us
    all_to_all x1, starting transfers between devices, exchange(): return lax.all_to_all(block, AXES, 0, 0, tiled=True)  7.41 us
    select_n x1, other arithmetic, shards(): masked = jnp.where(expanded > 0, operators, jnp.zeros((), jnp.bfloat16))  7.01 us
    mul x5, other arithmetic, shards(): site_coupling[bit_count + local_bit]  6.34 us
    gt x1, local copies, waits for them, and re-layouts, shards(): masked = jnp.where(expanded > 0, operators, jnp.zeros((), jnp.bfloat16))  6.24 us
    broadcast_in_dim x1, local copies, waits for them, and re-layouts, shards(): jnp.repeat(jnp.repeat(op_mask, block_edge, axis=1), block_edge, axis=2)  4.58 us
    another operation x1, local copies, waits for them, and re-layouts, shards(): tail = jnp.pad(jnp.stack(sums), (0, LANES - 2 * STEPS))  3.88 us
  transfers between devices with their start and end apart: 1, of which 0 were waited for; matrix products, arithmetic and copies ran while one was open for 22% of the time, Pallas kernels for 0%

profile of v1, /device:TPU:0, one launch (start us, length us, event | category | flops | bytes accessed | tf_op | source)
XLA Modules:
  0.0 130.8 jit_solution(15931074695105712357)
XLA Ops:
  0.6 1.2 copy.80
  1.9 1.8 %multiply_reduce_fusion.6 = f32[]{:T(128)} fusion(f32[1024,128]{1,0:T(8,128)} %param.7), kind=kLoop, calls=%fused_computation.104 | loop fusion | flops 262143 | bytes 524292 | tf_op jit(solution)/shard_map/reduce_sum | solution.py:37
  3.7 0.3 reshape.341
  4.0 0.2 copy.81
  4.2 0.3 copy.108
  4.5 1.6 %concatenate.6.clone = f32[32,4,1152]{2,1,0:T(4,128)} pad(f32[32,4,1024]{2,1,0:T(4,128)S(1)} %copy.108, f32[]{:T(128)} %multiply_reduce_fusion.6), padding=0_0x0_0x0_128 | pad | bytes 1114116 | tf_op jit(solution)/shard_map/concatenate | solution.py:38
  6.1 7.4 %all-to-all-start = ((f32[32,4,1152]{2,1,0:T(4,128)}), f32[32,4,1152]{2,1,0:T(4,128)}, u32[]{:S(2)}, u32[]{:S(2)}) async-start(f32[32,4,1152]{2,1,0:T(4,128)} %concatenate.6.clone), calls=%async_computation | async-start | bytes 1179648 | tf_op jit(solution)/shard_map/all_to_all | solution.py:16
  13.5 0.6 fusion.147
  20.0 0.7 fusion.145
  20.7 1.4 %convert_multiply_fusion = (f32[1024]{0:T(1024)S(1)}, f32[1024]{0:T(1024)S(1)}) fusion(f32[]{:T(128)} %bitcast.15, f32[]{:T(128)} %bitcast.14), kind=kLoop, calls=%fused_computation.138 | loop fusion | flops 8192 | bytes 8200 | tf_op jit(solution)/shard_map/mul | solution.py:50
  22.1 1.3 convert_multiply_fusion.2
  23.4 1.2 convert_multiply_fusion.4
  24.6 1.3 convert_multiply_fusion.6
  25.9 0.1 dynamic-slice_multiply_fusion
  25.9 0.1 broadcast_multiply_fusion.1
  26.0 1.8 %multiply_add_fusion = f32[8]{0:T(128)S(1)} fusion(f32[]{:T(128)} %bitcast.5, f32[]{:T(128)} %bitcast.3, f32[]{:T(128)} %bitcast.1), kind=kLoop, calls=%fused_computation.169 | loop fusion | flops 112 | bytes 44 | tf_op jit(solution)/shard_map/add | solution.py:48
  31.7 0.1 broadcast_in_dim.10
  31.8 4.6 %broadcast_in_dim.11 = pred[3,1024,8,128]{3,2,1,0:T(8,128)(4,1)S(1)} broadcast(pred[3,1024,8]{2,1,0:T(8,128)(4,1)S(1)} %bitcast.144), dimensions={0,1,2} | broadcast | bytes 3170304 | tf_op jit(solution)/shard_map/broadcast_in_dim | solution.py:32
  36.4 6.2 %gt.17 = pred[3,1024,1024]{2,1,0:T(8,128)(4,1)} reshape(pred[3,1024,8,128]{3,2,1,0:T(8,128)(4,1)S(1)} %broadcast_in_dim.11) | data formatting | bytes 6291456 | tf_op jit(solution)/shard_map/gt | solution.py:33
  42.7 0.7 fusion.146
  43.3 1.2 convert_multiply_fusion.8
  44.6 0.1 add_add_fusion
  44.7 7.0 %broadcast_select_fusion = bf16[3,1024,1024]{2,1,0:T(8,128)(2,1)} fusion(pred[3,1024,1024]{2,1,0:T(8,128)(4,1)} %gt.17, bf16[3,1024,1024]{2,1,0:T(8,128)(2,1)} %param.8), kind=kLoop, calls=%fused_computation | loop fusion | flops 3145728 | bytes 15728640 | tf_op jit(solution)/shard_map/jit(_where)/select_n | solution.py:33
  51.7 1.5 %slice_reduce_fusion.1 = f32[]{:T(128)} fusion(f32[32,4,1152]{2,1,0:T(4,128)} %all-to-all-done), kind=kLoop, calls=%fused_computation.134 | loop fusion | flops 31 | bytes 132 | tf_op jit(solution)/shard_map/reduce_sum | solution.py:39
  53.9 1.2 fusion.136
  55.1 0.4 reshape.343
  55.5 0.1 convert_element_type.141
  55.6 0.2 copy.83
  55.8 3.4 %fusion.30 = f32[8,8,2,1024]{3,1,2,0:T(8,128)S(1)} fusion(bf16[3,1024,1024]{2,1,0:T(8,128)(2,1)} %broadcast_select_fusion, s32[]{:T(128)S(6)} %select_n.22, f32[]{:T(128)} %bitcast.18, bf16[8,8,2,1024]{3,2,1,0:T(2,128)(2,1)S(1)} %convert_element_type.141, f32[8,8,2,1024]{3,2,1,0:T(2,128)S(1)} %reshape.343), kind=kOutput, calls=%fused_computation.31 | convolution fusion | flops 268697600 | bytes 3408388 | tf_op jit(solution)/shard_map/dot_general | solution.py:69
  59.4 1.6 %fusion.45 = f32[8,8,2,1024]{3,1,2,0:T(8,128)S(1)} fusion(bf16[3,1024,1024]{2,1,0:T(8,128)(2,1)S(1)} %bitcast.139, s32[]{:T(128)S(6)} %select_n.24, f32[]{:T(128)} %bitcast.23, bf16[8,8,2,1024]{3,2,1,0:T(2,128)(2,1)S(1)} %convert_element_type.141, f32[8,8,2,1024]{3,2,1,0:T(2,128)S(1)} %reshape.343), kind=kOutput, calls=%fused_computation.36 | convolution fusion | flops 268697600 | bytes 3407880 | tf_op jit(solution)/shard_map/dot_general | solution.py:69
  61.0 2.4 %fusion.60 = f32[8,8,2,1024]{3,1,2,0:T(8,128)S(1)} fusion(bf16[3,1024,1024]{2,1,0:T(8,128)(2,1)S(1)} %bitcast.139, s32[]{:T(128)S(6)} %select_n.25, f32[]{:T(128)} %bitcast.27, bf16[8,8,2,1024]{3,2,1,0:T(2,128)(2,1)} %copy-done, f32[8,8,2,1024]{3,2,1,0:T(2,128)S(1)} %reshape.343), kind=kOutput, calls=%fused_computation.41 | convolution fusion | flops 268697600 | bytes 3407880 | tf_op jit(solution)/shard_map/dot_general | solution.py:69
  63.5 0.3 subtract_convert_fusion.1
  63.8 0.8 fusion.24
  64.6 0.8 fusion.14
  65.5 0.8 fusion.4
  66.3 1.5 %fusion.36 = f32[8,8,2,1024]{3,1,2,0:T(8,128)S(1)} fusion(f32[8,8,2,1024]{3,1,2,0:T(8,128)S(1)} %fusion.24, bf16[8,8,2,1024]{3,1,2,0:T(8,128)(2,1)S(1)} %get-tuple-element.26, bf16[3,1024,1024]{2,1,0:T(8,128)(2,1)S(1)} %bitcast.139, s32[]{:T(128)S(6)} %select_n.22, f32[8,8,2,1024]{3,1,2,0:T(8,128)S(1)} %get-tuple-element.27, f32[]{:T(128)} %bitcast.18), kind=kOutput, calls=%fused_computation.33 | convolution fusion | flops 268828672 | bytes 3932168 | tf_op jit(solution)/shard_map/dot_general | solution.py:69
  67.9 1.5 %fusion.51 = f32[8,8,2,1024]{3,1,2,0:T(8,128)S(1)} fusion(f32[8,8,2,1024]{3,1,2,0:T(8,128)S(1)} %fusion.14, bf16[8,8,2,1024]{3,1,2,0:T(8,128)(2,1)S(1)} %get-tuple-element.26, bf16[3,1024,1024]{2,1,0:T(8,128)(2,1)S(1)} %bitcast.139, s32[]{:T(128)S(6)} %select_n.24, f32[8,8,2,1024]{3,1,2,0:T(8,128)S(1)} %get-tuple-element.27, f32[]{:T(128)} %bitcast.23), kind=kOutput, calls=%fused_computation.38 | convolution fusion | flops 268828672 | bytes 3932168 | tf_op jit(solution)/shard_map/dot_general | solution.py:69
  69.5 1.5 %fusion.66 = f32[8,8,2,1024]{3,1,2,0:T(8,128)S(1)} fusion(f32[8,8,2,1024]{3,1,2,0:T(8,128)S(1)} %fusion.4, bf16[8,8,2,1024]{3,1,2,0:T(8,128)(2,1)S(1)} %get-tuple-element.26, bf16[3,1024,1024]{2,1,0:T(8,128)(2,1)S(1)} %bitcast.139, s32[]{:T(128)S(6)} %select_n.25, f32[8,8,2,1024]{3,1,2,0:T(8,128)S(1)} %get-tuple-element.27, f32[]{:T(128)} %bitcast.27), kind=kOutput, calls=%fused_computation.43 | convolution fusion | flops 268828672 | bytes 3932168 | tf_op jit(solution)/shard_map/dot_general | solution.py:69
  71.0 0.4 subtract_convert_fusion
  71.4 0.8 fusion.20
  72.3 0.8 fusion.10
  73.1 0.8 fusion
  73.9 0.4 copy.92
  74.4 1.5 %fusion.42 = f32[8,8,2,1024]{3,1,2,0:T(8,128)S(1)} fusion(f32[8,8,2,1024]{3,1,2,0:T(8,128)S(1)} %fusion.20, bf16[8,8,2,1024]{3,1,2,0:T(8,128)(2,1)S(1)} %get-tuple-element.23, bf16[3,1024,1024]{2,1,0:T(8,128)(2,1)S(1)} %bitcast.139, s32[]{:T(128)S(6)} %select_n.22, f32[8,8,2,1024]{3,1,2,0:T(8,128)S(1)} %get-tuple-element.24, f32[]{:T(128)} %bitcast.18), kind=kOutput, calls=%fused_computation.35 | convolution fusion | flops 268828672 | bytes 3932168 | tf_op jit(solution)/shard_map/dot_general | solution.py:69
  76.0 1.5 %fusion.57 = f32[8,8,2,1024]{3,1,2,0:T(8,128)S(1)} fusion(f32[8,8,2,1024]{3,1,2,0:T(8,128)S(1)} %fusion.10, bf16[8,8,2,1024]{3,1,2,0:T(8,128)(2,1)S(1)} %get-tuple-element.23, bf16[3,1024,1024]{2,1,0:T(8,128)(2,1)S(1)} %bitcast.139, s32[]{:T(128)S(6)} %select_n.24, f32[8,8,2,1024]{3,1,2,0:T(8,128)S(1)} %get-tuple-element.24, f32[]{:T(128)} %bitcast.23), kind=kOutput, calls=%fused_computation.40 | convolution fusion | flops 268828672 | bytes 3932168 | tf_op jit(solution)/shard_map/dot_general | solution.py:69
  77.5 1.7 %fusion.72 = f32[8,8,2,1024]{3,1,2,0:T(8,128)S(1)} fusion(f32[8,8,2,1024]{3,1,2,0:T(8,128)S(1)} %fusion, bf16[8,8,2,1024]{3,1,2,0:T(8,128)(2,1)S(1)} %get-tuple-element.23, bf16[3,1024,1024]{2,1,0:T(8,128)(2,1)S(1)} %bitcast.139, s32[]{:T(128)S(6)} %select_n.25, f32[8,8,2,1024]{3,1,2,0:T(8,128)S(1)} %get-tuple-element.24, f32[]{:T(128)} %bitcast.27), kind=kOutput, calls=%fused_computation.45 | convolution fusion | flops 268828672 | bytes 3932168 | tf_op jit(solution)/shard_map/dot_general | solution.py:69
  79.3 1.4 %multiply_reduce_fusion = (f32[]{:T(128)}, f32[]{:T(128)}, f32[]{:T(128)}, f32[]{:T(128)}, f32[]{:T(128)}, /*index=5*/f32[]{:T(128)}, f32[8,8,2,1024]{3,1,2,0:T(8,128)S(1)}) fusion(f32[8,8,2,1024]{3,2,1,0:T(2,128)S(1)} %reshape.343, f32[8,8,2,1024]{3,1,2,0:T(8,128)S(1)} %get-tuple-element.27, f32[8,8,2,1024]{3,1,2,0:T(8,128)S(1)} %get-tuple-element.24, ...), kind=kLoop, calls=%fused_computation.96 | loop fusion | flops 3276794 | bytes 3702936 | tf_op jit(solution)/shard_map/reduce_sum | solution.py:80
  80.7 3.9 %stack.81 = f32[6]{0:T(128)S(1)} concatenate(f32[1]{0:T(128)} %bitcast.37, f32[1]{0:T(128)} %bitcast.38, f32[1]{0:T(128)} %bitcast.39, f32[1]{0:T(128)} %bitcast.40, f32[1]{0:T(128)} %bitcast.41, f32[1]{0:T(128)} %bitcast.42), dimensions={0} | concatenate | bytes 48 | tf_op jit(solution)/shard_map/stack | solution.py:81
  84.6 0.4 copy.93
  85.0 0.5 reshape.345
  85.4 0.5 reshape.344
  85.9 0.3 maximum_maximum_fusion
  86.2 34.9 %all_to_all.10 = f32[32,4,2176]{2,1,0:T(4,128)S(1)} all-to-all(f32[32,4,2176]{2,1,0:T(4,128)S(1)} %maximum_maximum_fusion), channel_id=1, replica_groups=mesh['site'=8,'phonon'=4] {'site','phonon'}, dimensions={0} | all-to-all | bytes 2228224 | tf_op jit(solution)/shard_map/all_to_all | solution.py:16
  121.2 0.7 fusion.144
  124.0 0.1 fusion.137
  124.1 0.3 copy_divide_fusion
  124.4 0.4 copy.100
  124.9 0.4 reshape.349
  125.2 1.0 copy.102
  126.2 0.3 copy_divide_fusion.1
  126.5 0.4 copy.98
  126.9 0.4 reshape.347
  127.3 1.0 copy.101
  130.2 0.6 pad_maximum_fusion
  (52 shorter events, 0.5 us)
Async XLA Ops:
  4.0 9.6 %copy-start.3 = (s32[3]{0:T(128)S(1)}, s32[3]{0:T(128)}, u32[]{:S(2)}) copy-start(s32[3]{0:T(128)} %param.10) | copy-start | bytes 40
  4.0 14.1 %copy-start.2 = (s32[3,8,8]{2,1,0:T(8,128)S(1)}, s32[3,8,8]{2,1,0:T(8,128)}, u32[]{:S(2)}) copy-start(s32[3,8,8]{2,1,0:T(8,128)} %param.9) | copy-start | bytes 2308
  4.0 16.0 %copy-start.1 = (f32[13]{0:T(128)S(1)}, f32[13]{0:T(128)}, u32[]{:S(2)}) copy-start(f32[13]{0:T(128)} %param.12) | copy-start | bytes 160
  4.0 21.8 %copy-start.5 = (f32[64]{0:T(128)S(1)}, f32[64]{0:T(128)}, u32[]{:S(2)}) copy-start(f32[64]{0:T(128)} %param.13) | copy-start | bytes 772
  6.1 45.6 %all-to-all-start = ((f32[32,4,1152]{2,1,0:T(4,128)}), f32[32,4,1152]{2,1,0:T(4,128)}, u32[]{:S(2)}, u32[]{:S(2)}) async-start(f32[32,4,1152]{2,1,0:T(4,128)} %concatenate.6.clone), calls=%async_computation | async-start | bytes 1179648 | tf_op jit(solution)/shard_map/all_to_all | solution.py:16
  36.4 6.3 %copy-start.4 = (f32[3]{0:T(128)S(1)}, f32[3]{0:T(128)}, u32[]{:S(2)}) copy-start(f32[3]{0:T(128)} %param.11) | copy-start | bytes 40
  55.1 4.3 %slice-start = ((s8[6291456]{0:T(1024)(128)(4,1)}), s8[2097152]{0:T(1024)(128)(4,1)S(1)}, s32[]{:S(2)}) async-start(s8[6291456]{0:T(1024)(128)(4,1)} %bitcast.138), calls=%async_computation.2 | async-start | bytes 4194304
  55.6 5.3 %copy-start = (bf16[8,8,2,1024]{3,2,1,0:T(2,128)(2,1)}, bf16[8,8,2,1024]{3,2,1,0:T(2,128)(2,1)S(1)}, u32[]{:S(2)}) copy-start(bf16[8,8,2,1024]{3,2,1,0:T(2,128)(2,1)S(1)} %convert_element_type.141) | copy-start | bytes 786436
  55.8 3.5 %slice-start.1 = ((s8[6291456]{0:T(1024)(128)(4,1)}), s8[4194304]{0:T(1024)(128)(4,1)S(1)}, s32[]{:S(2)}) async-start(s8[6291456]{0:T(1024)(128)(4,1)} %bitcast.138), calls=%async_computation.3 | async-start | bytes 8388608

commit v2 on v0

--- a/solution.py
+++ b/solution.py
@@ -1,15 +1,353 @@
+import functools
+
 import jax
 import jax.numpy as jnp
 from jax import lax
+from jax.experimental import pallas as pl
+from jax.experimental.pallas import tpu as pltpu
 from jax.sharding import PartitionSpec as P
 
 LBITS = 10
 MODES = 64
-LEV_DEV = 2
 STEPS = 3
-
+LANES = 128
+SUBLANES = 8
+EXTRA = 2
+AXES = ("site", "phonon")
 
 epsilon = 1e-06
+
+
+VMEM = pl.BlockSpec(memory_space=pltpu.VMEM)
+SMEM = pl.BlockSpec(memory_space=pltpu.SMEM)
+
+
+class Plan:
+    def __init__(self, mesh, rows, columns, blocks):
+        self.sites = mesh.shape["site"]
+        self.phonons = mesh.shape["phonon"]
+        self.groups = self.sites * self.phonons
+        self.bits = self.sites.bit_length() - 1
+        self.rows = rows
+        self.columns = columns
+        self.blocks = blocks
+        self.edge = rows // blocks
+        self.levels_here = columns // MODES
+        self.level_count = self.levels_here * self.phonons
+        self.share = MODES // self.groups
+        self.pieces = self.levels_here * self.share
+        self.lane_blocks = rows // LANES
+        self.body = self.pieces * self.lane_blocks
+        self.message = self.body + EXTRA
+        self.places = self.pieces * self.groups
+        self.entries = float(rows * columns * self.groups)
+
+    def fits(self):
+        return (
+            MODES % self.groups == 0
+            and self.columns == LANES
+            and self.rows % LANES == 0
+            and self.edge % LANES == 0
+            and self.groups % SUBLANES == 0
+        )
+
+
+def params(mib):
+    return pltpu.CompilerParams(vmem_limit_bytes=mib * 2**20)
+
+
+def lane_sums(values):
+    return jnp.sum(values, axis=0, keepdims=True)
+
+
+def put_extra(plan, out_ref, sums):
+    for index, value in enumerate(sums):
+        out_ref[pl.ds(plan.body + index, plan.groups, stride=plan.message), :] = jnp.broadcast_to(
+            value, (plan.groups, LANES)
+        )
+
+
+def total_of(plan, ref, start, stride):
+    lanes = lane_sums(ref[pl.ds(start, plan.groups, stride=stride), :])
+    return jnp.sum(lanes, axis=1, keepdims=True)
+
+
+def scale_of(plan, squares):
+    return jnp.sqrt(squares / plan.entries + epsilon)
+
+
+def depart_kernel(plan, state_ref, out_ref):
+    sums = jnp.zeros((1, LANES), jnp.float32)
+    for block in range(plan.lane_blocks):
+        tile = state_ref[pl.ds(block * LANES, LANES), :]
+        sums = sums + lane_sums(tile * tile)
+        turned = tile.T
+        for piece in range(plan.pieces):
+            out_ref[pl.ds(piece * plan.lane_blocks + block, plan.groups, stride=plan.message), :] = turned[
+                piece * plan.groups : (piece + 1) * plan.groups
+            ]
+    put_extra(plan, out_ref, (sums, jnp.zeros_like(sums)))
+
+
+def prepare_kernel(
+    plan, bits_ref, mask_ref, field_ref, coupling_ref, mode_ref, operators_ref, masked_ref, place_ref, inside_ref
+):
+    me = lax.axis_index("site") * plan.phonons + lax.axis_index("phonon")
+    for position in range(plan.bits):
+        chosen = bits_ref[position]
+        for across in range(plan.blocks):
+            rows = pl.ds(across * plan.edge, plan.edge)
+            for along in range(plan.blocks):
+                columns = pl.ds(along * plan.edge, plan.edge)
+                keep = (mask_ref[chosen, across, along] > 0).astype(jnp.float32).astype(jnp.bfloat16)
+                masked_ref[position, rows, columns] = operators_ref[chosen, rows, columns] * keep
+    place = lax.broadcasted_iota(jnp.int32, (plan.places, LANES), 0)
+    phonon = place % plan.phonons
+    site = place // plan.phonons % plan.sites
+    mode = place // plan.groups % plan.share
+    level = phonon * plan.levels_here + place // (plan.groups * plan.share)
+    occupied = jnp.zeros((plan.places, LANES), jnp.float32)
+    for position in range(plan.bits):
+        held = (site >> position & 1).astype(jnp.float32)
+        occupied = occupied + coupling_ref[bits_ref[position]] * held
+    strength = jnp.zeros((plan.places, LANES), jnp.float32)
+    for index in range(plan.share):
+        strength = jnp.where(mode == index, mode_ref[index * plan.groups + me], strength)
+    strength = strength / jnp.sqrt(jnp.full((1, LANES), plan.level_count, jnp.float32))
+    height = level.astype(jnp.float32)
+    place_ref[0] = occupied
+    place_ref[1] = strength * jnp.sqrt(height)
+    place_ref[2] = jnp.where(level == plan.level_count - 1, 0.0, strength * jnp.sqrt(height + 1.0))
+    for position in range(plan.bits):
+        place_ref[3 + position] = jnp.full((plan.places, LANES), field_ref[bits_ref[position]])
+    inside = lax.broadcasted_iota(jnp.int32, (SUBLANES, plan.rows), 1)
+    weight = jnp.zeros((SUBLANES, plan.rows), jnp.float32)
+    for local_bit in range(LBITS):
+        weight = weight + coupling_ref[plan.bits + local_bit] * (inside >> local_bit & 1).astype(jnp.float32)
+    inside_ref[...] = weight
+
+
+def flipped(values, stride):
+    places, width = values.shape
+    if stride % SUBLANES == 0:
+        shaped = values.reshape(places // (2 * stride), 2, stride, width)
+        return jnp.concatenate([shaped[:, 1:], shaped[:, :1]], axis=1).reshape(places, width)
+    tiles = values.reshape(places // SUBLANES, SUBLANES, width)
+    if 2 * stride == SUBLANES:
+        return pltpu.roll(tiles, stride, 1).reshape(places, width)
+    spot = lax.broadcasted_iota(jnp.int32, tiles.shape, 1)
+    down = pltpu.roll(tiles, stride, 1)
+    up = pltpu.roll(tiles, SUBLANES - stride, 1)
+    return jnp.where(spot & stride > 0, down, up).reshape(places, width)
+
+
+def shifted(values, by):
+    places, width = values.shape
+    tiles = values.reshape(places // SUBLANES, SUBLANES, width)
+    return pltpu.roll(tiles, by % SUBLANES, 1).reshape(places, width)
+
+
+def operate(plan, vector_ref, masked_ref, place_ref, inside_ref, rounded_ref, total_ref):
+    span = plan.places // plan.levels_here
+    for block in range(plan.lane_blocks):
+        lanes = pl.ds(block * LANES, LANES)
+        vector = vector_ref[:, lanes]
+        levels = [vector[index * span : (index + 1) * span] for index in range(plan.levels_here)]
+        lower = jnp.concatenate([shifted(levels[-1], 1)] + levels[:-1], axis=0)
+        upper = jnp.concatenate(levels[1:] + [shifted(levels[0], -1)], axis=0)
+        weight = place_ref[0] + inside_ref[:1, lanes]
+        total = weight * (place_ref[1] * lower + place_ref[2] * upper)
+        for position in range(plan.bits):
+            turned = flipped(vector, plan.phonons << position)
+            total = total + place_ref[3 + position] * turned
+            rounded_ref[:, pl.ds(position * plan.rows + block * LANES, LANES)] = turned.astype(jnp.bfloat16)
+        total_ref[:, lanes] = total
+    width = 2 * LANES
+    for column in range(plan.rows // width):
+        lanes = pl.ds(column * width, width)
+        total = total_ref[:, lanes]
+        for position in range(plan.bits):
+            total = total + lax.dot_general(
+                rounded_ref[:, pl.ds(position * plan.rows, plan.rows)],
+                masked_ref[position, lanes, :],
+                (((1,), (1,)), ((), ())),
+                preferred_element_type=jnp.float32,
+            )
+        total_ref[:, lanes] = total
+
+
+def first_kernel(
+    plan, arrived_ref, masked_ref, place_ref, inside_ref, initial_ref, new_ref, sums_ref, rounded_ref
+):
+    scale = scale_of(plan, total_of(plan, arrived_ref, plan.body, plan.message))
+    for piece in range(plan.pieces):
+        for block in range(plan.lane_blocks):
+            part = arrived_ref[pl.ds(piece * plan.lane_blocks + block, plan.groups, stride=plan.message), :]
+            initial_ref[pl.ds(piece * plan.groups, plan.groups), pl.ds(block * LANES, LANES)] = part / scale
+    operate(plan, initial_ref, masked_ref, place_ref, inside_ref, rounded_ref, new_ref)
+    squares = jnp.zeros((1, LANES), jnp.float32)
+    overlap = jnp.zeros((1, LANES), jnp.float32)
+    for block in range(plan.lane_blocks):
+        lanes = pl.ds(block * LANES, LANES)
+        new = new_ref[:, lanes]
+        squares = squares + lane_sums(new * new)
+        overlap = overlap + lane_sums(new * initial_ref[:, lanes])
+    for index, value in enumerate((squares, overlap)):
+        sums_ref[pl.ds(index, plan.groups, stride=EXTRA), :] = jnp.broadcast_to(value, (plan.groups, LANES))
+
+
+def later_kernel(
+    plan,
+    body,
+    keep,
+    arrived_ref,
+    raw_ref,
+    previous_ref,
+    initial_ref,
+    masked_ref,
+    place_ref,
+    inside_ref,
+    *refs,
+):
+    if keep:
+        current_ref, new_ref, out_ref, moment_ref, rounded_ref = refs
+    else:
+        out_ref, moment_ref, rounded_ref, current_ref, new_ref = refs
+    stride = body + EXTRA
+    scale = scale_of(plan, total_of(plan, arrived_ref, body, stride))
+    moment = total_of(plan, arrived_ref, body + 1, stride) / (plan.entries * scale)
+    moment_ref[...] = jnp.broadcast_to(moment, moment_ref.shape)
+    for block in range(plan.lane_blocks):
+        lanes = pl.ds(block * LANES, LANES)
+        current_ref[:, lanes] = raw_ref[:, lanes] / scale
+    operate(plan, current_ref, masked_ref, place_ref, inside_ref, rounded_ref, new_ref)
+    squares = jnp.zeros((1, LANES), jnp.float32)
+    overlap = jnp.zeros((1, LANES), jnp.float32)
+    for block in range(plan.lane_blocks):
+        lanes = pl.ds(block * LANES, LANES)
+        new = 2.0 * new_ref[:, lanes] - previous_ref[:, lanes] / scale
+        squares = squares + lane_sums(new * new)
+        overlap = overlap + lane_sums(new * initial_ref[:, lanes])
+        if keep:
+            new_ref[:, lanes] = new
+        for piece in range(plan.pieces):
+            out_ref[pl.ds(piece * plan.lane_blocks + block, plan.groups, stride=plan.message), :] = new[
+                piece * plan.groups : (piece + 1) * plan.groups
+            ]
+    put_extra(plan, out_ref, (squares, overlap))
+
+
+def arrive_kernel(plan, arrived_ref, *refs):
+    scale = scale_of(plan, total_of(plan, arrived_ref, plan.body, plan.message))
+    if len(refs) > 1:
+        first_ref, second_ref, out_ref, moments_ref = refs
+        moment = total_of(plan, arrived_ref, plan.body + 1, plan.message) / (plan.entries * scale)
+        moments_ref[0] = first_ref[0, 0]
+        moments_ref[1] = second_ref[0, 0]
+        moments_ref[2] = moment[0, 0]
+    else:
+        (out_ref,) = refs
+    for block in range(plan.lane_blocks):
+        parts = [
+            arrived_ref[pl.ds(piece * plan.lane_blocks + block, plan.groups, stride=plan.message), :]
+            for piece in range(plan.pieces)
+        ]
+        out_ref[pl.ds(block * LANES, LANES), :] = (jnp.concatenate(parts, axis=0) / scale).T
+
+
+def exchange(plan, values):
+    rows = values.shape[0] // plan.groups
+    shaped = values.reshape(plan.groups, rows // EXTRA, EXTRA, LANES)
+    return lax.all_to_all(shaped, AXES, 0, 0, tiled=True).reshape(values.shape)
+
+
+def shards(plan, state, operators, op_mask, site_bits, field, site_coupling, mode_coupling):
+    f32 = jnp.float32
+    message = jax.ShapeDtypeStruct((plan.groups * plan.message, LANES), f32)
+    vector = jax.ShapeDtypeStruct((plan.places, plan.rows), f32)
+    moment = jax.ShapeDtypeStruct((SUBLANES, LANES), f32)
+    held = jax.ShapeDtypeStruct((plan.rows, plan.columns), f32)
+    rounded = pltpu.VMEM((plan.places, plan.bits * plan.rows), jnp.bfloat16)
+    kept = pltpu.VMEM((plan.places, plan.rows), f32)
+    work = 2 * plan.bits * plan.places * plan.rows * plan.rows
+
+    def cost(flops, moved):
+        return pl.CostEstimate(flops=flops, bytes_accessed=moved, transcendentals=0)
+
+    departing = pl.pallas_call(
+        functools.partial(depart_kernel, plan),
+        out_shape=message,
+        in_specs=[VMEM],
+        out_specs=VMEM,
+        compiler_params=params(16),
+        name="depart",
+    )(state)
+    arrived = exchange(plan, departing)
+    masked, place, inside = pl.pallas_call(
+        functools.partial(prepare_kernel, plan),
+        out_shape=[
+            jax.ShapeDtypeStruct((plan.bits, plan.rows, plan.rows), jnp.bfloat16),
+            jax.ShapeDtypeStruct((3 + plan.bits, plan.places, LANES), f32),
+            jax.ShapeDtypeStruct((SUBLANES, plan.rows), f32),
+        ],
+        in_specs=[SMEM] * 5 + [VMEM],
+        out_specs=[VMEM] * 3,
+        compiler_params=params(32),
+        cost_estimate=cost(plan.bits * plan.rows * plan.rows, 4 * plan.bits * plan.rows * plan.rows),
+        name="prepare",
+    )(site_bits, op_mask, field, site_coupling, mode_coupling, operators)
+    tables = (masked, place, inside)
+    initial, raw, sums = pl.pallas_call(
+        functools.partial(first_kernel, plan),
+        out_shape=[vector, vector, jax.ShapeDtypeStruct((plan.groups * EXTRA, LANES), f32)],
+        in_specs=[VMEM] * 4,
+        out_specs=[VMEM] * 3,
+        scratch_shapes=[rounded],
+        compiler_params=params(32),
+        cost_estimate=cost(work, 4 * plan.places * plan.rows),
+        name="first",
+    )(arrived, *tables)
+    sums = exchange(plan, sums)
+    current, raw, departing, moment_one = pl.pallas_call(
+        functools.partial(later_kernel, plan, 0, True),
+        out_shape=[vector, vector, message, moment],
+        in_specs=[VMEM] * 7,
+        out_specs=[VMEM] * 4,
+        scratch_shapes=[rounded],
+        compiler_params=params(32),
+        cost_estimate=cost(work, 4 * plan.places * plan.rows),
+        name="second",
+    )(sums, raw, initial, initial, *tables)
+    before = exchange(plan, departing)
+    departing, moment_two = pl.pallas_call(
+        functools.partial(later_kernel, plan, plan.body, False),
+        out_shape=[message, moment],
+        in_specs=[VMEM] * 7,
+        out_specs=[VMEM] * 2,
+        scratch_shapes=[rounded, kept, kept],
+        compiler_params=params(32),
+        cost_estimate=cost(work, 4 * plan.places * plan.rows),
+        name="third",
+    )(before, raw, current, initial, *tables)
+    last = exchange(plan, departing)
+    before = pl.pallas_call(
+        functools.partial(arrive_kernel, plan),
+        out_shape=held,
+        in_specs=[VMEM],
+        out_specs=VMEM,
+        compiler_params=params(16),
+        cost_estimate=cost(plan.places * plan.rows, 8 * plan.places * plan.rows),
+        name="arrive_before",
+    )(before)
+    last, moments = pl.pallas_call(
+        functools.partial(arrive_kernel, plan),
+        out_shape=[held, jax.ShapeDtypeStruct((STEPS,), f32)],
+        in_specs=[VMEM] * 3,
+        out_specs=[VMEM, SMEM],
+        compiler_params=params(16),
+        name="arrive_last",
+    )(last, moment_one, moment_two)
+    return last, before, moments
 
 
 def extended_2(block, sides, width):
@@ -31,17 +369,18 @@
     return lax.ppermute(value, axis, pairs)
 
 
-def shards(state, operators, op_mask, site_bits, field, site_coupling, mode_coupling):
+def halo_shards(state, operators, op_mask, site_bits, field, site_coupling, mode_coupling):
     site_count = lax.axis_size("site")
     phonon_count = lax.axis_size("phonon")
     bit_count = site_count.bit_length() - 1
     rows_here = state.shape[0]
     columns_here = state.shape[1]
+    levels_here = columns_here // MODES
     block_edge = rows_here // op_mask.shape[1]
     expanded = jnp.repeat(jnp.repeat(op_mask, block_edge, axis=1), block_edge, axis=2)
     masked = jnp.where(expanded > 0, operators, jnp.zeros((), jnp.bfloat16))
     entries = jnp.float32(rows_here * columns_here * site_count * phonon_count)
-    level_total = jnp.sqrt(jnp.float32(LEV_DEV * phonon_count))
+    level_total = jnp.sqrt(jnp.float32(levels_here * phonon_count))
     device = lax.axis_index("site")
     inside = lax.iota(jnp.int32, rows_here)
     weight_rows = jnp.zeros((rows_here,), jnp.float32)
@@ -54,7 +393,7 @@
             inside >> local_bit & 1
         ).astype(jnp.float32)
     levels = (
-        lax.axis_index("phonon") * LEV_DEV + lax.iota(jnp.int32, columns_here) // MODES
+        lax.axis_index("phonon") * levels_here + lax.iota(jnp.int32, columns_here) // MODES
     ).astype(jnp.float32)
     lower_weight = jnp.sqrt(levels)
     upper_weight = jnp.sqrt(levels + 1.0)
@@ -99,4 +438,13 @@
 def solution(mesh):
     in_specs = (P("site", "phonon"), P(), P(), P(), P(), P(), P())
     out_specs = (P("site", "phonon"), P("site", "phonon"), P())
-    return jax.shard_map(shards, mesh=mesh, in_specs=in_specs, out_specs=out_specs, check_vma=False)
+
+    def whole(state, operators, op_mask, *rest):
+        rows = state.shape[0] // mesh.shape["site"]
+        columns = state.shape[1] // mesh.shape["phonon"]
+        plan = Plan(mesh, rows, columns, op_mask.shape[1])
+        body = functools.partial(shards, plan) if plan.fits() else halo_shards
+        run = jax.shard_map(body, mesh=mesh, in_specs=in_specs, out_specs=out_specs, check_vma=False)
+        return run(state, operators, op_mask, *rest)
+
+    return whole

time: 300 us -> 85.9 us (0.29)
  blocking collectives: 161 us -> 28.1 us
  matrix products: 31.5 us -> 0 us
  other arithmetic: 17.4 us -> 0 us
  between operations: 17 us -> 0.7 us
  Pallas kernels: 0 us -> 14 us
  starting transfers between devices: 22.5 us -> 10.4 us
  waiting for transfers between devices: 30.8 us -> 19.6 us
  local copies, waits for them, and re-layouts: 19 us -> 12.6 us
    psum x4 -> x0, blocking collectives: 161 us -> none  [the longest x3 118 us: shards(): lax.psum((jnp.sum(vector_new * vector_new), jnp.sum(initial * vector_new)...]
    dot_general x9 -> x0, matrix products: 31.5 us -> none  [shards(): jnp.dot(masked[chosen], flipped.astype(jnp.bfloat16), preferred_element_t...]
    ppermute x15 -> x0, waiting for transfers between devices: 30.8 us -> none  [the longest x9 30.7 us: partner(): return lax.ppermute(value, axis, pairs)]
    all_to_all x0 -> x2, blocking collectives: none -> 28.1 us  [exchange(): return lax.all_to_all(shaped, AXES, 0, 0, tiled=True).reshape(values.shape)]
    ppermute x15 -> x0, starting transfers between devices: 22.5 us -> none  [the longest x9 14.7 us: partner(): return lax.ppermute(value, axis, pairs)]
    all_to_all x0 -> x2, waiting for transfers between devices: none -> 19.6 us  [exchange(): return lax.all_to_all(shaped, AXES, 0, 0, tiled=True).reshape(values.shape)]
    pallas_call x0 -> x7, Pallas kernels: none -> 14 us  [the longest x1 3.2 us: shards(): pl.pallas_call(functools.partial(later_kernel, plan, plan.body, False), o...]
    all_to_all x0 -> x2, starting transfers between devices: none -> 10.4 us  [exchange(): return lax.all_to_all(shaped, AXES, 0, 0, tiled=True).reshape(values.shape)]
  transfers between devices with their start and end apart: 15 -> 2, of which waited for: 5 -> 2; matrix products, arithmetic and copies ran while one was open for 15% -> 0% of each run, Pallas kernels for 0% -> 5%
where the time goes in v2:
time: 85.9 us; the launch traced here: 85.4 us
  blocking collectives  28.1 us (33%)
  waiting for transfers between devices  19.6 us (23%)
  Pallas kernels  14 us (16%)
  local copies, waits for them, and re-layouts  12.6 us (15%)
  starting transfers between devices  10.4 us (12%)
    all_to_all x2, blocking collectives, exchange(): return lax.all_to_all(shaped, AXES, 0, 0, tiled=True).reshape(values.shape)  28.1 us
    all_to_all x2, waiting for transfers between devices, exchange(): return lax.all_to_all(shaped, AXES, 0, 0, tiled=True).reshape(values.shape)  19.6 us
    unnamed x18, local copies, waits for them, and re-layouts  12.6 us
    all_to_all x2, starting transfers between devices, exchange(): return lax.all_to_all(shaped, AXES, 0, 0, tiled=True).reshape(values.shape)  10.4 us
    pallas_call x1, Pallas kernels, shards(): pl.pallas_call(functools.partial(later_kernel, plan, plan.body, False), o...  3.2 us
    pallas_call x1, Pallas kernels, shards(): pl.pallas_call(functools.partial(prepare_kernel, plan), out_shape=[jax.Sh...  2.77 us
    pallas_call x1, Pallas kernels, shards(): pl.pallas_call(functools.partial(later_kernel, plan, 0, True), out_shape=...  2.43 us
    pallas_call x1, Pallas kernels, shards(): pl.pallas_call(functools.partial(first_kernel, plan), out_shape=[vector,...  2.4 us
  transfers between devices with their start and end apart: 2, of which 2 were waited for; matrix products, arithmetic and copies ran while one was open for 0% of the time, Pallas kernels for 5%

profile of v2, /device:TPU:0, one launch (start us, length us, event | category | flops | bytes accessed | tf_op | source)
XLA Modules:
  0.0 85.4 jit_solution(3298590731352418691)
XLA Ops:
  0.6 0.0 copy-start.3
  0.6 1.0 %copy-done.3 = f32[1024,128]{1,0:T(8,128)S(1)} copy-done((f32[1024,128]{1,0:T(8,128)S(1)}, f32[1024,128]{1,0:T(8,128)}, u32[]{:S(2)}) %copy-start.3) | copy-done | bytes 524312
  1.7 1.0 %depart.1 = f32[1088,128]{1,0:T(8,128)} custom-call(f32[1024,128]{1,0:T(8,128)S(1)} %copy-done.3), custom_call_target="tpu_custom_call" | custom-call | tf_op jit(solution)/shard_map/depart/pallas_call | solution.py:277
  2.7 7.3 %all-to-all-start = ((f32[32,17,2,128]{3,2,1,0:T(2,128)}), f32[32,17,2,128]{3,2,1,0:T(2,128)S(1)}, u32[]{:S(2)}, u32[]{:S(2)}) async-start(f32[32,17,2,128]{3,2,1,0:T(2,128)} %bitcast), calls=%async_computation | async-start | bytes 1114112 | tf_op jit(solution)/shard_map/all_to_all | solution.py:261
  10.0 0.0 copy-start.2
  10.0 2.8 %copy-done.2 = bf16[3,1024,1024]{2,1,0:T(8,128)(2,1)S(1)} copy-done((bf16[3,1024,1024]{2,1,0:T(8,128)(2,1)S(1)}, bf16[3,1024,1024]{2,1,0:T(8,128)(2,1)}, u32[]{:S(2)}) %copy-start.2) | copy-done | bytes 6291480
  12.8 0.0 copy-start.4
  12.8 0.7 copy-done.4
  13.5 0.0 copy-start.5
  13.5 0.7 copy-done.5
  14.1 0.0 copy-start.6
  14.1 0.7 copy-done.6
  14.8 0.0 copy-start.7
  14.8 0.7 copy-done.7
  15.4 0.0 copy-start.8
  15.4 0.7 copy-done.8
  16.1 2.8 %prepare.1 = (bf16[3,1024,1024]{2,1,0:T(8,128)(2,1)S(1)}, f32[6,128,128]{2,1,0:T(8,128)S(1)}, f32[8,1024]{1,0:T(8,128)S(1)}) custom-call(s32[3]{0:T(128)S(1)} %copy-done.5, s32[3,8,8]{2,1,0:T(8,128)S(1)} %copy-done.4, f32[3]{0:T(128)S(1)} %copy-done.6, f32[13]{0:T(128)S(1)} %copy-done.7, f32[64]{0:T(128)S(1)} %copy-done.8, bf16[3,1024,1024]{2,1,0:T(8,128)(2,1)S(1)} %copy-done.2), custom_call_target="tpu_custom_call" | custom-call | flops 3145728 | bytes 12582912 | tf_op jit(solution)/shard_map/prepare/pallas_call | solution.py:286
  18.9 0.0 copy-start
  18.9 2.7 %copy-done = bf16[3,1024,1024]{2,1,0:T(8,128)(2,1)} copy-done((bf16[3,1024,1024]{2,1,0:T(8,128)(2,1)}, bf16[3,1024,1024]{2,1,0:T(8,128)(2,1)S(1)}, u32[]{:S(2)}) %copy-start) | copy-done | bytes 6291480
  21.5 4.6 %all-to-all-done = f32[32,17,2,128]{3,2,1,0:T(2,128)S(1)} async-done(((f32[32,17,2,128]{3,2,1,0:T(2,128)}), f32[32,17,2,128]{3,2,1,0:T(2,128)S(1)}, u32[]{:S(2)}, u32[]{:S(2)}) %all-to-all-start) | async-done | bytes 557088 | tf_op jit(solution)/shard_map/all_to_all | solution.py:261
  26.1 0.0 copy-start.1
  26.1 2.8 %copy-done.1 = bf16[3,1024,1024]{2,1,0:T(8,128)(2,1)S(1)} copy-done((bf16[3,1024,1024]{2,1,0:T(8,128)(2,1)S(1)}, bf16[3,1024,1024]{2,1,0:T(8,128)(2,1)}, u32[]{:S(2)}) %copy-start.1) | copy-done | bytes 6291480
  28.9 2.4 %first.1 = (f32[128,1024]{1,0:T(8,128)S(1)}, f32[128,1024]{1,0:T(8,128)S(1)}, f32[64,128]{1,0:T(8,128)S(1)}) custom-call(f32[1088,128]{1,0:T(8,128)S(1)} %bitcast.12, bf16[3,1024,1024]{2,1,0:T(8,128)(2,1)S(1)} %copy-done.1, f32[6,128,128]{2,1,0:T(8,128)S(1)} %get-tuple-element.18.place_ref, f32[8,1024]{1,0:T(8,128)S(1)} %get-tuple-element.19.inside_ref), custom_call_target="tpu_custom_call" | custom-call | flops 805306368 | bytes 524288 | tf_op jit(solution)/shard_map/first/pallas_call | solution.py:300
  31.3 10.2 %all_to_all.20 = f32[32,1,2,128]{3,2,1,0:T(2,128)S(1)} all-to-all(f32[32,1,2,128]{3,2,1,0:T(2,128)S(1)} %bitcast.16), channel_id=1, replica_groups=mesh['site'=8,'phonon'=4] {'site','phonon'}, dimensions={0} | all-to-all | bytes 65536 | tf_op jit(solution)/shard_map/all_to_all | solution.py:261
  41.6 2.4 %second.1 = (f32[128,1024]{1,0:T(8,128)S(1)}, f32[128,1024]{1,0:T(8,128)S(1)}, f32[1088,128]{1,0:T(8,128)S(1)}, f32[8,128]{1,0:T(8,128)S(1)}) custom-call(f32[64,128]{1,0:T(8,128)S(1)} %bitcast.15, f32[128,1024]{1,0:T(8,128)S(1)} %get-tuple-element.21.raw_ref, f32[128,1024]{1,0:T(8,128)S(1)} %get-tuple-element.22.previous_ref.initial_ref, ...), custom_call_target="tpu_custom_call" | custom-call | flops 805306368 | bytes 524288 | tf_op jit(solution)/shard_map/second/pallas_call | solution.py:311
  44.0 17.9 %all_to_all.21 = f32[32,17,2,128]{3,2,1,0:T(2,128)S(1)} all-to-all(f32[32,17,2,128]{3,2,1,0:T(2,128)S(1)} %bitcast.14), channel_id=1, replica_groups=mesh['site'=8,'phonon'=4] {'site','phonon'}, dimensions={0} | all-to-all | bytes 1114112 | tf_op jit(solution)/shard_map/all_to_all | solution.py:261
  61.9 3.2 %third.1 = (f32[1088,128]{1,0:T(8,128)}, f32[8,128]{1,0:T(8,128)S(1)}) custom-call(f32[1088,128]{1,0:T(8,128)S(1)} %bitcast.10, f32[128,1024]{1,0:T(8,128)S(1)} %get-tuple-element.24.raw_ref, f32[128,1024]{1,0:T(8,128)S(1)} %get-tuple-element.25.previous_ref, f32[128,1024]{1,0:T(8,128)S(1)} %get-tuple-element.22.previous_ref.initial_ref, ...), custom_call_target="tpu_custom_call" | custom-call | flops 805306368 | bytes 524288 | tf_op jit(solution)/shard_map/third/pallas_call | solution.py:322
  65.1 3.1 %all-to-all-start.3 = ((f32[32,17,2,128]{3,2,1,0:T(2,128)}), f32[32,17,2,128]{3,2,1,0:T(2,128)S(1)}, u32[]{:S(2)}, u32[]{:S(2)}) async-start(f32[32,17,2,128]{3,2,1,0:T(2,128)} %bitcast.7), calls=%async_computation.3 | async-start | bytes 1114112 | tf_op jit(solution)/shard_map/all_to_all | solution.py:261
  68.2 1.1 %arrive_before.1 = f32[1024,128]{1,0:T(8,128)} custom-call(f32[1088,128]{1,0:T(8,128)S(1)} %bitcast.11), custom_call_target="tpu_custom_call" | custom-call | flops 131072 | bytes 1048576 | tf_op jit(solution)/shard_map/arrive_before/pallas_call | solution.py:333
  69.2 15.0 %all-to-all-done.3 = f32[32,17,2,128]{3,2,1,0:T(2,128)S(1)} async-done(((f32[32,17,2,128]{3,2,1,0:T(2,128)}), f32[32,17,2,128]{3,2,1,0:T(2,128)S(1)}, u32[]{:S(2)}, u32[]{:S(2)}) %all-to-all-start.3) | async-done | bytes 557088 | tf_op jit(solution)/shard_map/all_to_all | solution.py:261
  84.3 1.1 %arrive_last.1 = (f32[1024,128]{1,0:T(8,128)}, f32[3]{0:T(128)}) custom-call(f32[1088,128]{1,0:T(8,128)S(1)} %bitcast.13, f32[8,128]{1,0:T(8,128)S(1)} %get-tuple-element.27.refs_0_, f32[8,128]{1,0:T(8,128)S(1)} %get-tuple-element.28.refs_1_), custom_call_target="tpu_custom_call" | custom-call | tf_op jit(solution)/shard_map/arrive_last/pallas_call | solution.py:342
Async XLA Ops:
  0.6 1.0 %copy-start.3 = (f32[1024,128]{1,0:T(8,128)S(1)}, f32[1024,128]{1,0:T(8,128)}, u32[]{:S(2)}) copy-start(f32[1024,128]{1,0:T(8,128)} %state_ref.1) | copy-start | bytes 1572868
  2.7 23.4 %all-to-all-start = ((f32[32,17,2,128]{3,2,1,0:T(2,128)}), f32[32,17,2,128]{3,2,1,0:T(2,128)S(1)}, u32[]{:S(2)}, u32[]{:S(2)}) async-start(f32[32,17,2,128]{3,2,1,0:T(2,128)} %bitcast), calls=%async_computation | async-start | bytes 1114112 | tf_op jit(solution)/shard_map/all_to_all | solution.py:261
  10.0 2.8 %copy-start.2 = (bf16[3,1024,1024]{2,1,0:T(8,128)(2,1)S(1)}, bf16[3,1024,1024]{2,1,0:T(8,128)(2,1)}, u32[]{:S(2)}) copy-start(bf16[3,1024,1024]{2,1,0:T(8,128)(2,1)} %operators_ref.1) | copy-start | bytes 18874372
  12.8 0.7 copy-start.4
  13.5 0.7 copy-start.5
  14.1 0.7 copy-start.6
  14.8 0.7 copy-start.7
  15.4 0.7 copy-start.8
  18.9 2.7 %copy-start = (bf16[3,1024,1024]{2,1,0:T(8,128)(2,1)}, bf16[3,1024,1024]{2,1,0:T(8,128)(2,1)S(1)}, u32[]{:S(2)}) copy-start(bf16[3,1024,1024]{2,1,0:T(8,128)(2,1)S(1)} %get-tuple-element.17.masked_ref) | copy-start | bytes 18874372
  26.1 2.8 %copy-start.1 = (bf16[3,1024,1024]{2,1,0:T(8,128)(2,1)S(1)}, bf16[3,1024,1024]{2,1,0:T(8,128)(2,1)}, u32[]{:S(2)}) copy-start(bf16[3,1024,1024]{2,1,0:T(8,128)(2,1)} %copy-done) | copy-start | bytes 18874372
  65.1 19.2 %all-to-all-start.3 = ((f32[32,17,2,128]{3,2,1,0:T(2,128)}), f32[32,17,2,128]{3,2,1,0:T(2,128)S(1)}, u32[]{:S(2)}, u32[]{:S(2)}) async-start(f32[32,17,2,128]{3,2,1,0:T(2,128)} %bitcast.7), calls=%async_computation.3 | async-start | bytes 1114112 | tf_op jit(solution)/shard_map/all_to_all | solution.py:261

commit v3 on v2

--- a/solution.py
+++ b/solution.py
@@ -60,11 +60,9 @@
     return jnp.sum(values, axis=0, keepdims=True)
 
 
-def put_extra(plan, out_ref, sums):
+def put_extra(plan, out_ref, sums, start, stride):
     for index, value in enumerate(sums):
-        out_ref[pl.ds(plan.body + index, plan.groups, stride=plan.message), :] = jnp.broadcast_to(
-            value, (plan.groups, LANES)
-        )
+        out_ref[pl.ds(start + index, plan.groups, stride=stride), :] = jnp.broadcast_to(value, (plan.groups, LANES))
 
 
 def total_of(plan, ref, start, stride):
@@ -86,7 +84,7 @@
             out_ref[pl.ds(piece * plan.lane_blocks + block, plan.groups, stride=plan.message), :] = turned[
                 piece * plan.groups : (piece + 1) * plan.groups
             ]
-    put_extra(plan, out_ref, (sums, jnp.zeros_like(sums)))
+    put_extra(plan, out_ref, (sums, jnp.zeros_like(sums)), plan.body, plan.message)
 
 
 def prepare_kernel(
@@ -192,13 +190,11 @@
         new = new_ref[:, lanes]
         squares = squares + lane_sums(new * new)
         overlap = overlap + lane_sums(new * initial_ref[:, lanes])
-    for index, value in enumerate((squares, overlap)):
-        sums_ref[pl.ds(index, plan.groups, stride=EXTRA), :] = jnp.broadcast_to(value, (plan.groups, LANES))
+    put_extra(plan, sums_ref, (squares, overlap), 0, EXTRA)
 
 
 def later_kernel(
     plan,
-    body,
     keep,
     arrived_ref,
     raw_ref,
@@ -210,12 +206,11 @@
     *refs,
 ):
     if keep:
-        current_ref, new_ref, out_ref, moment_ref, rounded_ref = refs
+        current_ref, new_ref, out_ref, moment_ref, sums_ref, rounded_ref = refs
     else:
         out_ref, moment_ref, rounded_ref, current_ref, new_ref = refs
-    stride = body + EXTRA
-    scale = scale_of(plan, total_of(plan, arrived_ref, body, stride))
-    moment = total_of(plan, arrived_ref, body + 1, stride) / (plan.entries * scale)
+    scale = scale_of(plan, total_of(plan, arrived_ref, 0, EXTRA))
+    moment = total_of(plan, arrived_ref, 1, EXTRA) / (plan.entries * scale)
     moment_ref[...] = jnp.broadcast_to(moment, moment_ref.shape)
     for block in range(plan.lane_blocks):
         lanes = pl.ds(block * LANES, LANES)
@@ -234,7 +229,9 @@
             out_ref[pl.ds(piece * plan.lane_blocks + block, plan.groups, stride=plan.message), :] = new[
                 piece * plan.groups : (piece + 1) * plan.groups
             ]
-    put_extra(plan, out_ref, (squares, overlap))
+    put_extra(plan, out_ref, (squares, overlap), plan.body, plan.message)
+    if keep:
+        put_extra(plan, sums_ref, (squares, overlap), 0, EXTRA)
 
 
 def arrive_kernel(plan, arrived_ref, *refs):
@@ -297,9 +294,10 @@
         name="prepare",
     )(site_bits, op_mask, field, site_coupling, mode_coupling, operators)
     tables = (masked, place, inside)
+    small = jax.ShapeDtypeStruct((plan.groups * EXTRA, LANES), f32)
     initial, raw, sums = pl.pallas_call(
         functools.partial(first_kernel, plan),
-        out_shape=[vector, vector, jax.ShapeDtypeStruct((plan.groups * EXTRA, LANES), f32)],
+        out_shape=[vector, vector, small],
         in_specs=[VMEM] * 4,
         out_specs=[VMEM] * 3,
         scratch_shapes=[rounded],
@@ -308,19 +306,20 @@
         name="first",
     )(arrived, *tables)
     sums = exchange(plan, sums)
-    current, raw, departing, moment_one = pl.pallas_call(
-        functools.partial(later_kernel, plan, 0, True),
-        out_shape=[vector, vector, message, moment],
+    current, raw, departing, moment_one, sums = pl.pallas_call(
+        functools.partial(later_kernel, plan, True),
+        out_shape=[vector, vector, message, moment, small],
         in_specs=[VMEM] * 7,
-        out_specs=[VMEM] * 4,
+        out_specs=[VMEM] * 5,
         scratch_shapes=[rounded],
         compiler_params=params(32),
         cost_estimate=cost(work, 4 * plan.places * plan.rows),
         name="second",
     )(sums, raw, initial, initial, *tables)
     before = exchange(plan, departing)
+    sums = exchange(plan, sums)
     departing, moment_two = pl.pallas_call(
-        functools.partial(later_kernel, plan, plan.body, False),
+        functools.partial(later_kernel, plan, False),
         out_shape=[message, moment],
         in_specs=[VMEM] * 7,
         out_specs=[VMEM] * 2,
@@ -328,7 +327,7 @@
         compiler_params=params(32),
         cost_estimate=cost(work, 4 * plan.places * plan.rows),
         name="third",
-    )(before, raw, current, initial, *tables)
+    )(sums, raw, current, initial, *tables)
     last = exchange(plan, departing)
     before = pl.pallas_call(
         functools.partial(arrive_kernel, plan),

time: 85.9 us -> 93.4 us (1.087)
  waiting for transfers between devices: 19.6 us -> 29.8 us
  blocking collectives: 28.1 us -> 19.2 us
  local copies, waits for them, and re-layouts: 12.6 us -> 15.4 us
  starting transfers between devices: 10.4 us -> 13 us
    all_to_all x2 -> x3, waiting for transfers between devices: 19.6 us -> 29.8 us  [exchange(): return lax.all_to_all(shaped, AXES, 0, 0, tiled=True).reshape(values.shape)]
    all_to_all x2, blocking collectives: 28.1 us -> 19.2 us  [exchange(): return lax.all_to_all(shaped, AXES, 0, 0, tiled=True).reshape(values.shape)]
    unnamed x18 -> x20, local copies, waits for them, and re-layouts: 12.6 us -> 15.4 us
    all_to_all x2 -> x3, starting transfers between devices: 10.4 us -> 13 us  [exchange(): return lax.all_to_all(shaped, AXES, 0, 0, tiled=True).reshape(values.shape)]
  transfers between devices with their start and end apart: 2 -> 3, of which waited for: 2 -> 3; matrix products, arithmetic and copies ran while one was open for 0% -> 0% of each run, Pallas kernels for 5% -> 8%
where the time goes in v3:
time: 93.4 us; the launch traced here: 92.7 us
  waiting for transfers between devices  29.8 us (32%)
  blocking collectives  19.2 us (21%)
  local copies, waits for them, and re-layouts  15.4 us (16%)
  Pallas kernels  14.8 us (16%)
  starting transfers between devices  13 us (14%)
    all_to_all x3, waiting for transfers between devices, exchange(): return lax.all_to_all(shaped, AXES, 0, 0, tiled=True).reshape(values.shape)  29.8 us
    all_to_all x2, blocking collectives, exchange(): return lax.all_to_all(shaped, AXES, 0, 0, tiled=True).reshape(values.shape)  19.2 us
    unnamed x20, local copies, waits for them, and re-layouts  15.4 us
    all_to_all x3, starting transfers between devices, exchange(): return lax.all_to_all(shaped, AXES, 0, 0, tiled=True).reshape(values.shape)  13 us
    pallas_call x1, Pallas kernels, shards(): pl.pallas_call(functools.partial(later_kernel, plan, False), out_shape=[m...  3.21 us
    pallas_call x1, Pallas kernels, shards(): pl.pallas_call(functools.partial(later_kernel, plan, True), out_shape=[ve...  3.2 us
    pallas_call x1, Pallas kernels, shards(): pl.pallas_call(functools.partial(prepare_kernel, plan), out_shape=[jax.Sh...  2.77 us
    pallas_call x1, Pallas kernels, shards(): pl.pallas_call(functools.partial(first_kernel, plan), out_shape=[vector,...  2.36 us
  transfers between devices with their start and end apart: 3, of which 3 were waited for; matrix products, arithmetic and copies ran while one was open for 0% of the time, Pallas kernels for 8%

profile of v3, /device:TPU:0, one launch (start us, length us, event | category | flops | bytes accessed | tf_op | source)
XLA Modules:
  0.0 92.7 jit_solution(4990946684324460051)
XLA Ops:
  0.6 0.0 copy-start.4
  0.6 1.0 %copy-done.4 = f32[1024,128]{1,0:T(8,128)S(1)} copy-done((f32[1024,128]{1,0:T(8,128)S(1)}, f32[1024,128]{1,0:T(8,128)}, u32[]{:S(2)}) %copy-start.4) | copy-done | bytes 524312
  1.7 1.0 %depart.1 = f32[1088,128]{1,0:T(8,128)} custom-call(f32[1024,128]{1,0:T(8,128)S(1)} %copy-done.4), custom_call_target="tpu_custom_call" | custom-call | tf_op jit(solution)/shard_map/depart/pallas_call | solution.py:274
  2.7 7.3 %all-to-all-start = ((f32[32,17,2,128]{3,2,1,0:T(2,128)}), f32[32,17,2,128]{3,2,1,0:T(2,128)S(1)}, u32[]{:S(2)}, u32[]{:S(2)}) async-start(f32[32,17,2,128]{3,2,1,0:T(2,128)} %bitcast), calls=%async_computation | async-start | bytes 1114112 | tf_op jit(solution)/shard_map/all_to_all | solution.py:258
  10.0 0.0 copy-start.3
  10.0 2.8 %copy-done.3 = bf16[3,1024,1024]{2,1,0:T(8,128)(2,1)S(1)} copy-done((bf16[3,1024,1024]{2,1,0:T(8,128)(2,1)S(1)}, bf16[3,1024,1024]{2,1,0:T(8,128)(2,1)}, u32[]{:S(2)}) %copy-start.3) | copy-done | bytes 6291480
  12.8 0.0 copy-start.5
  12.8 0.7 copy-done.5
  13.5 0.0 copy-start.6
  13.5 0.7 copy-done.6
  14.1 0.0 copy-start.7
  14.1 0.7 copy-done.7
  14.8 0.0 copy-start.8
  14.8 0.7 copy-done.8
  15.5 0.0 copy-start.9
  15.5 0.7 copy-done.9
  16.1 2.8 %prepare.1 = (bf16[3,1024,1024]{2,1,0:T(8,128)(2,1)S(1)}, f32[6,128,128]{2,1,0:T(8,128)S(1)}, f32[8,1024]{1,0:T(8,128)S(1)}) custom-call(s32[3]{0:T(128)S(1)} %copy-done.6, s32[3,8,8]{2,1,0:T(8,128)S(1)} %copy-done.5, f32[3]{0:T(128)S(1)} %copy-done.7, f32[13]{0:T(128)S(1)} %copy-done.8, f32[64]{0:T(128)S(1)} %copy-done.9, bf16[3,1024,1024]{2,1,0:T(8,128)(2,1)S(1)} %copy-done.3), custom_call_target="tpu_custom_call" | custom-call | flops 3145728 | bytes 12582912 | tf_op jit(solution)/shard_map/prepare/pallas_call | solution.py:283
  18.9 0.0 copy-start
  18.9 2.7 %copy-done = bf16[3,1024,1024]{2,1,0:T(8,128)(2,1)} copy-done((bf16[3,1024,1024]{2,1,0:T(8,128)(2,1)}, bf16[3,1024,1024]{2,1,0:T(8,128)(2,1)S(1)}, u32[]{:S(2)}) %copy-start) | copy-done | bytes 6291480
  21.5 4.6 %all-to-all-done = f32[32,17,2,128]{3,2,1,0:T(2,128)S(1)} async-done(((f32[32,17,2,128]{3,2,1,0:T(2,128)}), f32[32,17,2,128]{3,2,1,0:T(2,128)S(1)}, u32[]{:S(2)}, u32[]{:S(2)}) %all-to-all-start) | async-done | bytes 557088 | tf_op jit(solution)/shard_map/all_to_all | solution.py:258
  26.1 0.0 copy-start.1
  26.1 2.8 %copy-done.1 = bf16[3,1024,1024]{2,1,0:T(8,128)(2,1)S(1)} copy-done((bf16[3,1024,1024]{2,1,0:T(8,128)(2,1)S(1)}, bf16[3,1024,1024]{2,1,0:T(8,128)(2,1)}, u32[]{:S(2)}) %copy-start.1) | copy-done | bytes 6291480
  28.9 2.4 %first.1 = (f32[128,1024]{1,0:T(8,128)S(1)}, f32[128,1024]{1,0:T(8,128)S(1)}, f32[64,128]{1,0:T(8,128)S(1)}) custom-call(f32[1088,128]{1,0:T(8,128)S(1)} %bitcast.14, bf16[3,1024,1024]{2,1,0:T(8,128)(2,1)S(1)} %copy-done.1, f32[6,128,128]{2,1,0:T(8,128)S(1)} %get-tuple-element.19.place_ref, f32[8,1024]{1,0:T(8,128)S(1)} %get-tuple-element.20.inside_ref), custom_call_target="tpu_custom_call" | custom-call | flops 805306368 | bytes 524288 | tf_op jit(solution)/shard_map/first/pallas_call | solution.py:298
  31.3 10.2 %all_to_all.25 = f32[32,1,2,128]{3,2,1,0:T(2,128)S(1)} all-to-all(f32[32,1,2,128]{3,2,1,0:T(2,128)S(1)} %bitcast.20), channel_id=1, replica_groups=mesh['site'=8,'phonon'=4] {'site','phonon'}, dimensions={0} | all-to-all | bytes 65536 | tf_op jit(solution)/shard_map/all_to_all | solution.py:258
  41.5 3.2 %second.1 = (f32[128,1024]{1,0:T(8,128)S(1)}, f32[128,1024]{1,0:T(8,128)S(1)}, f32[1088,128]{1,0:T(8,128)}, f32[8,128]{1,0:T(8,128)S(1)}, f32[64,128]{1,0:T(8,128)S(1)}) custom-call(f32[64,128]{1,0:T(8,128)S(1)} %bitcast.18, f32[128,1024]{1,0:T(8,128)S(1)} %get-tuple-element.22.raw_ref, f32[128,1024]{1,0:T(8,128)S(1)} %get-tuple-element.23.previous_ref.initial_ref, ...), custom_call_target="tpu_custom_call" | custom-call | flops 805306368 | bytes 524288 | tf_op jit(solution)/shard_map/second/pallas_call | solution.py:309
  44.7 8.9 %all_to_all.26 = f32[32,1,2,128]{3,2,1,0:T(2,128)S(1)} all-to-all(f32[32,1,2,128]{3,2,1,0:T(2,128)S(1)} %bitcast.19), channel_id=1, replica_groups=mesh['site'=8,'phonon'=4] {'site','phonon'}, dimensions={0} | all-to-all | bytes 65536 | tf_op jit(solution)/shard_map/all_to_all | solution.py:258
  53.7 2.6 %all-to-all-start.4 = ((f32[32,17,2,128]{3,2,1,0:T(2,128)}), f32[32,17,2,128]{3,2,1,0:T(2,128)S(1)}, u32[]{:S(2)}, u32[]{:S(2)}) async-start(f32[32,17,2,128]{3,2,1,0:T(2,128)} %bitcast.10), calls=%async_computation.4 | async-start | bytes 1114112 | tf_op jit(solution)/shard_map/all_to_all | solution.py:258
  56.3 0.0 copy-start.2
  56.3 2.8 %copy-done.2 = bf16[3,1024,1024]{2,1,0:T(8,128)(2,1)S(1)} copy-done((bf16[3,1024,1024]{2,1,0:T(8,128)(2,1)S(1)}, bf16[3,1024,1024]{2,1,0:T(8,128)(2,1)}, u32[]{:S(2)}) %copy-start.2) | copy-done | bytes 6291480
  59.1 3.2 %third.1 = (f32[1088,128]{1,0:T(8,128)}, f32[8,128]{1,0:T(8,128)S(1)}) custom-call(f32[64,128]{1,0:T(8,128)S(1)} %bitcast.17, f32[128,1024]{1,0:T(8,128)S(1)} %get-tuple-element.25.raw_ref, f32[128,1024]{1,0:T(8,128)S(1)} %get-tuple-element.26.previous_ref, f32[128,1024]{1,0:T(8,128)S(1)} %get-tuple-element.23.previous_ref.initial_ref, ...), custom_call_target="tpu_custom_call" | custom-call | flops 805306368 | bytes 524288 | tf_op jit(solution)/shard_map/third/pallas_call | solution.py:321
  62.3 10.1 %all-to-all-done.4 = f32[32,17,2,128]{3,2,1,0:T(2,128)S(1)} async-done(((f32[32,17,2,128]{3,2,1,0:T(2,128)}), f32[32,17,2,128]{3,2,1,0:T(2,128)S(1)}, u32[]{:S(2)}, u32[]{:S(2)}) %all-to-all-start.4) | async-done | bytes 557088 | tf_op jit(solution)/shard_map/all_to_all | solution.py:258
  72.4 3.1 %all-to-all-start.3 = ((f32[32,17,2,128]{3,2,1,0:T(2,128)}), f32[32,17,2,128]{3,2,1,0:T(2,128)S(1)}, u32[]{:S(2)}, u32[]{:S(2)}) async-start(f32[32,17,2,128]{3,2,1,0:T(2,128)} %bitcast.8), calls=%async_computation.3 | async-start | bytes 1114112 | tf_op jit(solution)/shard_map/all_to_all | solution.py:258
  75.5 1.1 %arrive_before.1 = f32[1024,128]{1,0:T(8,128)} custom-call(f32[1088,128]{1,0:T(8,128)S(1)} %bitcast.15), custom_call_target="tpu_custom_call" | custom-call | flops 131072 | bytes 1048576 | tf_op jit(solution)/shard_map/arrive_before/pallas_call | solution.py:332
  76.6 15.0 %all-to-all-done.3 = f32[32,17,2,128]{3,2,1,0:T(2,128)S(1)} async-done(((f32[32,17,2,128]{3,2,1,0:T(2,128)}), f32[32,17,2,128]{3,2,1,0:T(2,128)S(1)}, u32[]{:S(2)}, u32[]{:S(2)}) %all-to-all-start.3) | async-done | bytes 557088 | tf_op jit(solution)/shard_map/all_to_all | solution.py:258
  91.6 1.1 %arrive_last.1 = (f32[1024,128]{1,0:T(8,128)}, f32[3]{0:T(128)}) custom-call(f32[1088,128]{1,0:T(8,128)S(1)} %bitcast.16, f32[8,128]{1,0:T(8,128)S(1)} %get-tuple-element.28.refs_0_, f32[8,128]{1,0:T(8,128)S(1)} %get-tuple-element.29.refs_1_), custom_call_target="tpu_custom_call" | custom-call | tf_op jit(solution)/shard_map/arrive_last/pallas_call | solution.py:341
Async XLA Ops:
  0.6 1.0 %copy-start.4 = (f32[1024,128]{1,0:T(8,128)S(1)}, f32[1024,128]{1,0:T(8,128)}, u32[]{:S(2)}) copy-start(f32[1024,128]{1,0:T(8,128)} %state_ref.1) | copy-start | bytes 1572868
  2.7 23.4 %all-to-all-start = ((f32[32,17,2,128]{3,2,1,0:T(2,128)}), f32[32,17,2,128]{3,2,1,0:T(2,128)S(1)}, u32[]{:S(2)}, u32[]{:S(2)}) async-start(f32[32,17,2,128]{3,2,1,0:T(2,128)} %bitcast), calls=%async_computation | async-start | bytes 1114112 | tf_op jit(solution)/shard_map/all_to_all | solution.py:258
  10.0 2.8 %copy-start.3 = (bf16[3,1024,1024]{2,1,0:T(8,128)(2,1)S(1)}, bf16[3,1024,1024]{2,1,0:T(8,128)(2,1)}, u32[]{:S(2)}) copy-start(bf16[3,1024,1024]{2,1,0:T(8,128)(2,1)} %operators_ref.1) | copy-start | bytes 18874372
  12.8 0.7 copy-start.5
  13.5 0.7 copy-start.6
  14.1 0.7 copy-start.7
  14.8 0.7 copy-start.8
  15.5 0.7 copy-start.9
  18.9 2.7 %copy-start = (bf16[3,1024,1024]{2,1,0:T(8,128)(2,1)}, bf16[3,1024,1024]{2,1,0:T(8,128)(2,1)S(1)}, u32[]{:S(2)}) copy-start(bf16[3,1024,1024]{2,1,0:T(8,128)(2,1)S(1)} %get-tuple-element.18.masked_ref) | copy-start | bytes 18874372
  26.1 2.8 %copy-start.1 = (bf16[3,1024,1024]{2,1,0:T(8,128)(2,1)S(1)}, bf16[3,1024,1024]{2,1,0:T(8,128)(2,1)}, u32[]{:S(2)}) copy-start(bf16[3,1024,1024]{2,1,0:T(8,128)(2,1)} %copy-done) | copy-start | bytes 18874372
  53.7 18.8 %all-to-all-start.4 = ((f32[32,17,2,128]{3,2,1,0:T(2,128)}), f32[32,17,2,128]{3,2,1,0:T(2,128)S(1)}, u32[]{:S(2)}, u32[]{:S(2)}) async-start(f32[32,17,2,128]{3,2,1,0:T(2,128)} %bitcast.10), calls=%async_computation.4 | async-start | bytes 1114112 | tf_op jit(solution)/shard_map/all_to_all | solution.py:258
  56.3 2.8 %copy-start.2 = (bf16[3,1024,1024]{2,1,0:T(8,128)(2,1)S(1)}, bf16[3,1024,1024]{2,1,0:T(8,128)(2,1)}, u32[]{:S(2)}) copy-start(bf16[3,1024,1024]{2,1,0:T(8,128)(2,1)} %copy-done) | copy-start | bytes 18874372
  72.4 19.2 %all-to-all-start.3 = ((f32[32,17,2,128]{3,2,1,0:T(2,128)}), f32[32,17,2,128]{3,2,1,0:T(2,128)S(1)}, u32[]{:S(2)}, u32[]{:S(2)}) async-start(f32[32,17,2,128]{3,2,1,0:T(2,128)} %bitcast.8), calls=%async_computation.3 | async-start | bytes 1114112 | tf_op jit(solution)/shard_map/all_to_all | solution.py:258

commit v4 on v2

--- a/solution.py
+++ b/solution.py
@@ -13,13 +13,14 @@
 LANES = 128
 SUBLANES = 8
 EXTRA = 2
-AXES = ("site", "phonon")
+AXES = ("phonon", "site")
 
 epsilon = 1e-06
 
 
 VMEM = pl.BlockSpec(memory_space=pltpu.VMEM)
 SMEM = pl.BlockSpec(memory_space=pltpu.SMEM)
+HBM = pl.BlockSpec(memory_space=pltpu.HBM)
 
 
 class Plan:
@@ -76,10 +77,17 @@
     return jnp.sqrt(squares / plan.entries + epsilon)
 
 
-def depart_kernel(plan, state_ref, out_ref):
+def depart_kernel(plan, state_ref, out_ref, tiles_ref, semaphores):
+    copies = [
+        pltpu.make_async_copy(state_ref.at[pl.ds(block * LANES, LANES), :], tiles_ref.at[block], semaphores.at[block])
+        for block in range(plan.lane_blocks)
+    ]
+    for copy in copies:
+        copy.start()
     sums = jnp.zeros((1, LANES), jnp.float32)
     for block in range(plan.lane_blocks):
-        tile = state_ref[pl.ds(block * LANES, LANES), :]
+        copies[block].wait()
+        tile = tiles_ref[block]
         sums = sums + lane_sums(tile * tile)
         turned = tile.T
         for piece in range(plan.pieces):
@@ -90,20 +98,44 @@
 
 
 def prepare_kernel(
-    plan, bits_ref, mask_ref, field_ref, coupling_ref, mode_ref, operators_ref, masked_ref, place_ref, inside_ref
+    plan,
+    bits_ref,
+    mask_ref,
+    field_ref,
+    coupling_ref,
+    mode_ref,
+    operators_ref,
+    masked_ref,
+    place_ref,
+    inside_ref,
+    held_ref,
+    in_semaphores,
+    out_semaphores,
 ):
-    me = lax.axis_index("site") * plan.phonons + lax.axis_index("phonon")
+    me = lax.axis_index("phonon") * plan.sites + lax.axis_index("site")
+    fetches = []
     for position in range(plan.bits):
+        fetch = pltpu.make_async_copy(
+            operators_ref.at[bits_ref[position]], held_ref.at[position], in_semaphores.at[position]
+        )
+        fetch.start()
+        fetches.append(fetch)
+    stores = []
+    for position in range(plan.bits):
+        fetches[position].wait()
         chosen = bits_ref[position]
         for across in range(plan.blocks):
             rows = pl.ds(across * plan.edge, plan.edge)
             for along in range(plan.blocks):
                 columns = pl.ds(along * plan.edge, plan.edge)
                 keep = (mask_ref[chosen, across, along] > 0).astype(jnp.float32).astype(jnp.bfloat16)
-                masked_ref[position, rows, columns] = operators_ref[chosen, rows, columns] * keep
+                held_ref[position, rows, columns] = held_ref[position, rows, columns] * keep
+        store = pltpu.make_async_copy(held_ref.at[position], masked_ref.at[position], out_semaphores.at[position])
+        store.start()
+        stores.append(store)
     place = lax.broadcasted_iota(jnp.int32, (plan.places, LANES), 0)
-    phonon = place % plan.phonons
-    site = place // plan.phonons % plan.sites
+    site = place % plan.sites
+    phonon = place // plan.sites % plan.phonons
     mode = place // plan.groups % plan.share
     level = phonon * plan.levels_here + place // (plan.groups * plan.share)
     occupied = jnp.zeros((plan.places, LANES), jnp.float32)
@@ -125,6 +157,8 @@
     for local_bit in range(LBITS):
         weight = weight + coupling_ref[plan.bits + local_bit] * (inside >> local_bit & 1).astype(jnp.float32)
     inside_ref[...] = weight
+    for store in stores:
+        store.wait()
 
 
 def flipped(values, stride):
@@ -143,48 +177,69 @@
 
 def shifted(values, by):
     places, width = values.shape
+    if by % SUBLANES == 0:
+        return jnp.concatenate([values[-by:], values[:-by]], axis=0)
     tiles = values.reshape(places // SUBLANES, SUBLANES, width)
     return pltpu.roll(tiles, by % SUBLANES, 1).reshape(places, width)
 
 
-def operate(plan, vector_ref, masked_ref, place_ref, inside_ref, rounded_ref, total_ref):
+def operate(plan, vector_ref, masked_ref, place_ref, inside_ref, rounded_ref, total_ref, fetches=None):
     span = plan.places // plan.levels_here
     for block in range(plan.lane_blocks):
         lanes = pl.ds(block * LANES, LANES)
         vector = vector_ref[:, lanes]
         levels = [vector[index * span : (index + 1) * span] for index in range(plan.levels_here)]
-        lower = jnp.concatenate([shifted(levels[-1], 1)] + levels[:-1], axis=0)
-        upper = jnp.concatenate(levels[1:] + [shifted(levels[0], -1)], axis=0)
+        lower = jnp.concatenate([shifted(levels[-1], plan.sites)] + levels[:-1], axis=0)
+        upper = jnp.concatenate(levels[1:] + [shifted(levels[0], -plan.sites)], axis=0)
         weight = place_ref[0] + inside_ref[:1, lanes]
         total = weight * (place_ref[1] * lower + place_ref[2] * upper)
         for position in range(plan.bits):
-            turned = flipped(vector, plan.phonons << position)
+            turned = flipped(vector, 1 << position)
             total = total + place_ref[3 + position] * turned
             rounded_ref[:, pl.ds(position * plan.rows + block * LANES, LANES)] = turned.astype(jnp.bfloat16)
         total_ref[:, lanes] = total
     width = 2 * LANES
-    for column in range(plan.rows // width):
-        lanes = pl.ds(column * width, width)
-        total = total_ref[:, lanes]
-        for position in range(plan.bits):
-            total = total + lax.dot_general(
-                rounded_ref[:, pl.ds(position * plan.rows, plan.rows)],
-                masked_ref[position, lanes, :],
-                (((1,), (1,)), ((), ())),
-                preferred_element_type=jnp.float32,
-            )
-        total_ref[:, lanes] = total
+    rounds = [[position] for position in range(plan.bits)] if fetches else [range(plan.bits)]
+    for positions in rounds:
+        if fetches:
+            fetches[positions[0]].wait()
+        for column in range(plan.rows // width):
+            lanes = pl.ds(column * width, width)
+            total = total_ref[:, lanes]
+            for position in positions:
+                total = total + lax.dot_general(
+                    rounded_ref[:, pl.ds(position * plan.rows, plan.rows)],
+                    masked_ref[position, lanes, :],
+                    (((1,), (1,)), ((), ())),
+                    preferred_element_type=jnp.float32,
+                )
+            total_ref[:, lanes] = total
 
 
 def first_kernel(
-    plan, arrived_ref, masked_ref, place_ref, inside_ref, initial_ref, new_ref, sums_ref, rounded_ref
+    plan,
+    arrived_ref,
+    stored_ref,
+    place_ref,
+    inside_ref,
+    initial_ref,
+    new_ref,
+    sums_ref,
+    masked_ref,
+    rounded_ref,
+    semaphores,
 ):
+    fetches = []
+    for position in range(plan.bits):
+        fetch = pltpu.make_async_copy(stored_ref.at[position], masked_ref.at[position], semaphores.at[position])
+        fetch.start()
+        fetches.append(fetch)
     scale = scale_of(plan, total_of(plan, arrived_ref, plan.body, plan.message))
     for piece in range(plan.pieces):
         for block in range(plan.lane_blocks):
             part = arrived_ref[pl.ds(piece * plan.lane_blocks + block, plan.groups, stride=plan.message), :]
             initial_ref[pl.ds(piece * plan.groups, plan.groups), pl.ds(block * LANES, LANES)] = part / scale
-    operate(plan, initial_ref, masked_ref, place_ref, inside_ref, rounded_ref, new_ref)
+    operate(plan, initial_ref, masked_ref, place_ref, inside_ref, rounded_ref, new_ref, fetches)
     squares = jnp.zeros((1, LANES), jnp.float32)
     overlap = jnp.zeros((1, LANES), jnp.float32)
     for block in range(plan.lane_blocks):
@@ -277,36 +332,46 @@
     departing = pl.pallas_call(
         functools.partial(depart_kernel, plan),
         out_shape=message,
-        in_specs=[VMEM],
+        in_specs=[HBM],
         out_specs=VMEM,
-        compiler_params=params(16),
+        scratch_shapes=[
+            pltpu.VMEM((plan.lane_blocks, LANES, plan.columns), f32),
+            pltpu.SemaphoreType.DMA((plan.lane_blocks,)),
+        ],
+        compiler_params=params(60),
         name="depart",
     )(state)
     arrived = exchange(plan, departing)
-    masked, place, inside = pl.pallas_call(
+    operators_shape = jax.ShapeDtypeStruct((plan.bits, plan.rows, plan.rows), jnp.bfloat16)
+    stored, place, inside = pl.pallas_call(
         functools.partial(prepare_kernel, plan),
         out_shape=[
-            jax.ShapeDtypeStruct((plan.bits, plan.rows, plan.rows), jnp.bfloat16),
+            operators_shape,
             jax.ShapeDtypeStruct((3 + plan.bits, plan.places, LANES), f32),
             jax.ShapeDtypeStruct((SUBLANES, plan.rows), f32),
         ],
-        in_specs=[SMEM] * 5 + [VMEM],
-        out_specs=[VMEM] * 3,
-        compiler_params=params(32),
+        in_specs=[SMEM] * 5 + [HBM],
+        out_specs=[HBM, VMEM, VMEM],
+        scratch_shapes=[
+            pltpu.VMEM((plan.bits, plan.rows, plan.rows), jnp.bfloat16),
+            pltpu.SemaphoreType.DMA((plan.bits,)),
+            pltpu.SemaphoreType.DMA((plan.bits,)),
+        ],
+        compiler_params=params(58),
         cost_estimate=cost(plan.bits * plan.rows * plan.rows, 4 * plan.bits * plan.rows * plan.rows),
         name="prepare",
     )(site_bits, op_mask, field, site_coupling, mode_coupling, operators)
-    tables = (masked, place, inside)
-    initial, raw, sums = pl.pallas_call(
+    initial, raw, sums, masked = pl.pallas_call(
         functools.partial(first_kernel, plan),
-        out_shape=[vector, vector, jax.ShapeDtypeStruct((plan.groups * EXTRA, LANES), f32)],
-        in_specs=[VMEM] * 4,
-        out_specs=[VMEM] * 3,
-        scratch_shapes=[rounded],
-        compiler_params=params(32),
+        out_shape=[vector, vector, jax.ShapeDtypeStruct((plan.groups * EXTRA, LANES), f32), operators_shape],
+        in_specs=[VMEM, HBM, VMEM, VMEM],
+        out_specs=[VMEM] * 4,
+        scratch_shapes=[rounded, pltpu.SemaphoreType.DMA((plan.bits,))],
+        compiler_params=params(40),
         cost_estimate=cost(work, 4 * plan.places * plan.rows),
         name="first",
-    )(arrived, *tables)
+    )(arrived, stored, place, inside)
+    tables = (masked, place, inside)
     sums = exchange(plan, sums)
     current, raw, departing, moment_one = pl.pallas_call(
         functools.partial(later_kernel, plan, 0, True),

time: 85.9 us -> 88.1 us (1.026)
  local copies, waits for them, and re-layouts: 12.6 us -> 1.76 us
  Pallas kernels: 14 us -> 20.8 us
  waiting for transfers between devices: 19.6 us -> 26.4 us
    unnamed x18 -> x8, local copies, waits for them, and re-layouts: 12.6 us -> 1.76 us
    all_to_all x2, waiting for transfers between devices: 19.6 us -> 26.4 us  [exchange(): return lax.all_to_all(shaped, AXES, 0, 0, tiled=True).reshape(values.shape)]
    pallas_call x1, Pallas kernels: 2.77 us -> 6.58 us  [shards(): pl.pallas_call(functools.partial(prepare_kernel, plan), out_shape=[operat...]
    pallas_call x1, Pallas kernels: 2.4 us -> 3.97 us  [shards(): pl.pallas_call(functools.partial(first_kernel, plan), out_shape=[vector,...]
    pallas_call x1, Pallas kernels: 1.01 us -> 2.53 us  [shards(): pl.pallas_call(functools.partial(depart_kernel, plan), out_shape=message,...]
  transfers between devices with their start and end apart: 2 -> 2, of which waited for: 2 -> 2; matrix products, arithmetic and copies ran while one was open for 0% -> 0% of each run, Pallas kernels for 5% -> 9%
where the time goes in v4:
time: 88.1 us; the launch traced here: 87.6 us
  blocking collectives  28 us (32%)
  waiting for transfers between devices  26.4 us (30%)
  Pallas kernels  20.8 us (24%)
  starting transfers between devices  9.91 us (11%)
  local copies, waits for them, and re-layouts  1.76 us (2%)
    all_to_all x2, blocking collectives, exchange(): return lax.all_to_all(shaped, AXES, 0, 0, tiled=True).reshape(values.shape)  28 us
    all_to_all x2, waiting for transfers between devices, exchange(): return lax.all_to_all(shaped, AXES, 0, 0, tiled=True).reshape(values.shape)  26.4 us
    all_to_all x2, starting transfers between devices, exchange(): return lax.all_to_all(shaped, AXES, 0, 0, tiled=True).reshape(values.shape)  9.91 us
    pallas_call x1, Pallas kernels, shards(): pl.pallas_call(functools.partial(prepare_kernel, plan), out_shape=[operat...  6.58 us
    pallas_call x1, Pallas kernels, shards(): pl.pallas_call(functools.partial(first_kernel, plan), out_shape=[vector,...  3.97 us
    pallas_call x1, Pallas kernels, shards(): pl.pallas_call(functools.partial(later_kernel, plan, plan.body, False), o...  3.15 us
    pallas_call x1, Pallas kernels, shards(): pl.pallas_call(functools.partial(depart_kernel, plan), out_shape=message,...  2.53 us
    pallas_call x1, Pallas kernels, shards(): pl.pallas_call(functools.partial(later_kernel, plan, 0, True), out_shape=...  2.35 us
  transfers between devices with their start and end apart: 2, of which 2 were waited for; matrix products, arithmetic and copies ran while one was open for 0% of the time, Pallas kernels for 9%

profile of v4, /device:TPU:0, one launch (start us, length us, event | category | flops | bytes accessed | tf_op | source)
XLA Modules:
  0.0 87.6 jit_solution(16214675820139421183)
XLA Ops:
  0.6 2.5 %depart.1 = f32[1088,128]{1,0:T(8,128)} custom-call(f32[1024,128]{1,0:T(8,128)} %state_ref.1), custom_call_target="tpu_custom_call" | custom-call | tf_op jit(solution)/shard_map/depart/pallas_call | solution.py:332
  3.2 7.3 %all-to-all-start = ((f32[32,17,2,128]{3,2,1,0:T(2,128)}), f32[32,17,2,128]{3,2,1,0:T(2,128)S(1)}, u32[]{:S(2)}, u32[]{:S(2)}) async-start(f32[32,17,2,128]{3,2,1,0:T(2,128)} %bitcast.17), calls=%async_computation | async-start | bytes 1114112 | tf_op jit(solution)/shard_map/all_to_all | solution.py:316
  10.5 6.6 %prepare.1 = (bf16[3,1024,1024]{2,1,0:T(8,128)(2,1)}, f32[6,128,128]{2,1,0:T(8,128)}, f32[8,1024]{1,0:T(8,128)}) custom-call(s32[3]{0:T(128)} %bits_ref.1, s32[3,8,8]{2,1,0:T(8,128)} %mask_ref.1, f32[3]{0:T(128)} %field_ref.1, f32[13]{0:T(128)} %coupling_ref.1, f32[64]{0:T(128)} %mode_ref.1, bf16[3,1024,1024]{2,1,0:T(8,128)(2,1)} %operators_ref.1), custom_call_target="tpu_custom_call" | custom-call | flops 3145728 | bytes 12582912 | tf_op jit(solution)/shard_map/prepare/pallas_call | solution.py:346
  17.1 10.5 %all-to-all-done = f32[32,17,2,128]{3,2,1,0:T(2,128)S(1)} async-done(((f32[32,17,2,128]{3,2,1,0:T(2,128)}), f32[32,17,2,128]{3,2,1,0:T(2,128)S(1)}, u32[]{:S(2)}, u32[]{:S(2)}) %all-to-all-start) | async-done | bytes 557088 | tf_op jit(solution)/shard_map/all_to_all | solution.py:316
  27.5 0.0 copy-start
  27.5 1.0 %copy-done = f32[6,128,128]{2,1,0:T(8,128)S(1)} copy-done((f32[6,128,128]{2,1,0:T(8,128)S(1)}, f32[6,128,128]{2,1,0:T(8,128)}, u32[]{:S(2)}) %copy-start) | copy-done | bytes 393240
  28.5 0.0 copy-start.2
  28.5 0.8 copy-done.2
  29.3 0.0 copy-start.1
  29.3 0.0 copy-start.3
  29.3 4.0 %first.1 = (f32[128,1024]{1,0:T(8,128)S(1)}, f32[128,1024]{1,0:T(8,128)S(1)}, f32[64,128]{1,0:T(8,128)S(1)}, bf16[3,1024,1024]{2,1,0:T(8,128)(2,1)S(1)}) custom-call(f32[1088,128]{1,0:T(8,128)S(1)} %bitcast.12, bf16[3,1024,1024]{2,1,0:T(8,128)(2,1)} %get-tuple-element.18.stored_ref, f32[6,128,128]{2,1,0:T(8,128)S(1)} %copy-done, f32[8,1024]{1,0:T(8,128)S(1)} %copy-done.2), custom_call_target="tpu_custom_call" | custom-call | flops 805306368 | bytes 524288 | tf_op jit(solution)/shard_map/first/pallas_call | solution.py:364
  33.3 9.3 %all_to_all.20 = f32[32,1,2,128]{3,2,1,0:T(2,128)S(1)} all-to-all(f32[32,1,2,128]{3,2,1,0:T(2,128)S(1)} %bitcast.16), channel_id=1, replica_groups=mesh['site'=8,'phonon'=4] {'phonon','site'}, dimensions={0} | all-to-all | bytes 65536 | tf_op jit(solution)/shard_map/all_to_all | solution.py:316
  42.5 0.0 copy-done.1
  42.5 0.0 copy-done.3
  42.5 2.3 %second.1 = (f32[128,1024]{1,0:T(8,128)S(1)}, f32[128,1024]{1,0:T(8,128)S(1)}, f32[1088,128]{1,0:T(8,128)S(1)}, f32[8,128]{1,0:T(8,128)S(1)}) custom-call(f32[64,128]{1,0:T(8,128)S(1)} %bitcast.15, f32[128,1024]{1,0:T(8,128)S(1)} %get-tuple-element.22.raw_ref, f32[128,1024]{1,0:T(8,128)S(1)} %get-tuple-element.23.previous_ref.initial_ref, ...), custom_call_target="tpu_custom_call" | custom-call | flops 805306368 | bytes 524288 | tf_op jit(solution)/shard_map/second/pallas_call | solution.py:376
  44.9 18.8 %all_to_all.21 = f32[32,17,2,128]{3,2,1,0:T(2,128)S(1)} all-to-all(f32[32,17,2,128]{3,2,1,0:T(2,128)S(1)} %bitcast.14), channel_id=1, replica_groups=mesh['site'=8,'phonon'=4] {'phonon','site'}, dimensions={0} | all-to-all | bytes 1114112 | tf_op jit(solution)/shard_map/all_to_all | solution.py:316
  63.7 3.2 %third.1 = (f32[1088,128]{1,0:T(8,128)}, f32[8,128]{1,0:T(8,128)S(1)}) custom-call(f32[1088,128]{1,0:T(8,128)S(1)} %bitcast.10, f32[128,1024]{1,0:T(8,128)S(1)} %get-tuple-element.26.raw_ref, f32[128,1024]{1,0:T(8,128)S(1)} %get-tuple-element.27.previous_ref, f32[128,1024]{1,0:T(8,128)S(1)} %get-tuple-element.23.previous_ref.initial_ref, ...), custom_call_target="tpu_custom_call" | custom-call | flops 805306368 | bytes 524288 | tf_op jit(solution)/shard_map/third/pallas_call | solution.py:387
  66.8 2.6 %all-to-all-start.3 = ((f32[32,17,2,128]{3,2,1,0:T(2,128)}), f32[32,17,2,128]{3,2,1,0:T(2,128)S(1)}, u32[]{:S(2)}, u32[]{:S(2)}) async-start(f32[32,17,2,128]{3,2,1,0:T(2,128)} %bitcast.7), calls=%async_computation.3 | async-start | bytes 1114112 | tf_op jit(solution)/shard_map/all_to_all | solution.py:316
  69.4 1.1 %arrive_before.1 = f32[1024,128]{1,0:T(8,128)} custom-call(f32[1088,128]{1,0:T(8,128)S(1)} %bitcast.11), custom_call_target="tpu_custom_call" | custom-call | flops 131072 | bytes 1048576 | tf_op jit(solution)/shard_map/arrive_before/pallas_call | solution.py:398
  70.5 16.0 %all-to-all-done.3 = f32[32,17,2,128]{3,2,1,0:T(2,128)S(1)} async-done(((f32[32,17,2,128]{3,2,1,0:T(2,128)}), f32[32,17,2,128]{3,2,1,0:T(2,128)S(1)}, u32[]{:S(2)}, u32[]{:S(2)}) %all-to-all-start.3) | async-done | bytes 557088 | tf_op jit(solution)/shard_map/all_to_all | solution.py:316
  86.5 1.1 %arrive_last.1 = (f32[1024,128]{1,0:T(8,128)}, f32[3]{0:T(128)}) custom-call(f32[1088,128]{1,0:T(8,128)S(1)} %bitcast.13, f32[8,128]{1,0:T(8,128)S(1)} %get-tuple-element.29.refs_0_, f32[8,128]{1,0:T(8,128)S(1)} %get-tuple-element.30.refs_1_), custom_call_target="tpu_custom_call" | custom-call | tf_op jit(solution)/shard_map/arrive_last/pallas_call | solution.py:407
Async XLA Ops:
  3.2 24.4 %all-to-all-start = ((f32[32,17,2,128]{3,2,1,0:T(2,128)}), f32[32,17,2,128]{3,2,1,0:T(2,128)S(1)}, u32[]{:S(2)}, u32[]{:S(2)}) async-start(f32[32,17,2,128]{3,2,1,0:T(2,128)} %bitcast.17), calls=%async_computation | async-start | bytes 1114112 | tf_op jit(solution)/shard_map/all_to_all | solution.py:316
  27.5 1.0 %copy-start = (f32[6,128,128]{2,1,0:T(8,128)S(1)}, f32[6,128,128]{2,1,0:T(8,128)}, u32[]{:S(2)}) copy-start(f32[6,128,128]{2,1,0:T(8,128)} %get-tuple-element.19.place_ref) | copy-start | bytes 1179652
  28.5 0.8 copy-start.2
  29.3 13.3 %copy-start.1 = (f32[6,128,128]{2,1,0:T(8,128)S(1)}, f32[6,128,128]{2,1,0:T(8,128)}, u32[]{:S(2)}) copy-start(f32[6,128,128]{2,1,0:T(8,128)} %get-tuple-element.19.place_ref) | copy-start | bytes 1179652
  29.3 13.3 %copy-start.3 = (f32[8,1024]{1,0:T(8,128)S(1)}, f32[8,1024]{1,0:T(8,128)}, u32[]{:S(2)}) copy-start(f32[8,1024]{1,0:T(8,128)} %get-tuple-element.20.inside_ref) | copy-start | bytes 98308
  66.8 19.7 %all-to-all-start.3 = ((f32[32,17,2,128]{3,2,1,0:T(2,128)}), f32[32,17,2,128]{3,2,1,0:T(2,128)S(1)}, u32[]{:S(2)}, u32[]{:S(2)}) async-start(f32[32,17,2,128]{3,2,1,0:T(2,128)} %bitcast.7), calls=%async_computation.3 | async-start | bytes 1114112 | tf_op jit(solution)/shard_map/all_to_all | solution.py:316

commit v5 on v3

--- a/solution.py
+++ b/solution.py
@@ -63,6 +63,12 @@
 def put_extra(plan, out_ref, sums, start, stride):
     for index, value in enumerate(sums):
         out_ref[pl.ds(start + index, plan.groups, stride=stride), :] = jnp.broadcast_to(value, (plan.groups, LANES))
+
+
+def put_sums(sums_ref, sums):
+    for index, value in enumerate(sums):
+        sums_ref[pl.ds(index, 1), :] = value
+    sums_ref[pl.ds(len(sums), SUBLANES - len(sums)), :] = jnp.zeros((SUBLANES - len(sums), LANES), jnp.float32)
 
 
 def total_of(plan, ref, start, stride):
@@ -190,7 +196,7 @@
         new = new_ref[:, lanes]
         squares = squares + lane_sums(new * new)
         overlap = overlap + lane_sums(new * initial_ref[:, lanes])
-    put_extra(plan, sums_ref, (squares, overlap), 0, EXTRA)
+    put_sums(sums_ref, (squares, overlap))
 
 
 def later_kernel(
@@ -209,8 +215,8 @@
         current_ref, new_ref, out_ref, moment_ref, sums_ref, rounded_ref = refs
     else:
         out_ref, moment_ref, rounded_ref, current_ref, new_ref = refs
-    scale = scale_of(plan, total_of(plan, arrived_ref, 0, EXTRA))
-    moment = total_of(plan, arrived_ref, 1, EXTRA) / (plan.entries * scale)
+    scale = scale_of(plan, total_of(plan, arrived_ref, 0, SUBLANES))
+    moment = total_of(plan, arrived_ref, 1, SUBLANES) / (plan.entries * scale)
     moment_ref[...] = jnp.broadcast_to(moment, moment_ref.shape)
     for block in range(plan.lane_blocks):
         lanes = pl.ds(block * LANES, LANES)
@@ -231,7 +237,7 @@
             ]
     put_extra(plan, out_ref, (squares, overlap), plan.body, plan.message)
     if keep:
-        put_extra(plan, sums_ref, (squares, overlap), 0, EXTRA)
+        put_sums(sums_ref, (squares, overlap))
 
 
 def arrive_kernel(plan, arrived_ref, *refs):
@@ -256,6 +262,10 @@
     rows = values.shape[0] // plan.groups
     shaped = values.reshape(plan.groups, rows // EXTRA, EXTRA, LANES)
     return lax.all_to_all(shaped, AXES, 0, 0, tiled=True).reshape(values.shape)
+
+
+def gathered(plan, sums):
+    return lax.all_gather(sums, AXES, axis=0, tiled=True)
 
 
 def shards(plan, state, operators, op_mask, site_bits, field, site_coupling, mode_coupling):
@@ -294,7 +304,7 @@
         name="prepare",
     )(site_bits, op_mask, field, site_coupling, mode_coupling, operators)
     tables = (masked, place, inside)
-    small = jax.ShapeDtypeStruct((plan.groups * EXTRA, LANES), f32)
+    small = jax.ShapeDtypeStruct((SUBLANES, LANES), f32)
     initial, raw, sums = pl.pallas_call(
         functools.partial(first_kernel, plan),
         out_shape=[vector, vector, small],
@@ -305,7 +315,7 @@
         cost_estimate=cost(work, 4 * plan.places * plan.rows),
         name="first",
     )(arrived, *tables)
-    sums = exchange(plan, sums)
+    sums = gathered(plan, sums)
     current, raw, departing, moment_one, sums = pl.pallas_call(
         functools.partial(later_kernel, plan, True),
         out_shape=[vector, vector, message, moment, small],
@@ -317,7 +327,7 @@
         name="second",
     )(sums, raw, initial, initial, *tables)
     before = exchange(plan, departing)
-    sums = exchange(plan, sums)
+    sums = gathered(plan, sums)
     departing, moment_two = pl.pallas_call(
         functools.partial(later_kernel, plan, False),
         out_shape=[message, moment],

time: 93.4 us -> 148 us (1.58)
  blocking collectives: 19.2 us -> 84.1 us
  waiting for transfers between devices: 29.8 us -> 19.6 us
    all_gather x0 -> x2, blocking collectives: none -> 84.1 us  [gathered(): return lax.all_gather(sums, AXES, axis=0, tiled=True)]
    all_to_all x2 -> x0, blocking collectives: 19.2 us -> none  [exchange(): return lax.all_to_all(shaped, AXES, 0, 0, tiled=True).reshape(values.shape)]
    all_to_all x3, waiting for transfers between devices: 29.8 us -> 19.6 us  [exchange(): return lax.all_to_all(shaped, AXES, 0, 0, tiled=True).reshape(values.shape)]
  transfers between devices with their start and end apart: 3 -> 3, of which waited for: 3 -> 2; matrix products, arithmetic and copies ran while one was open for 0% -> 0% of each run, Pallas kernels for 8% -> 5%
where the time goes in v5:
time: 148 us; the launch traced here: 147 us
  blocking collectives  84.1 us (57%)
  waiting for transfers between devices  19.6 us (13%)
  local copies, waits for them, and re-layouts  15.4 us (10%)
  Pallas kernels  14.8 us (10%)
  starting transfers between devices  12.5 us (8%)
    all_gather x2, blocking collectives, gathered(): return lax.all_gather(sums, AXES, axis=0, tiled=True)  84.1 us
    all_to_all x3, waiting for transfers between devices, exchange(): return lax.all_to_all(shaped, AXES, 0, 0, tiled=True).reshape(values.shape)  19.6 us
    unnamed x20, local copies, waits for them, and re-layouts  15.4 us
    all_to_all x3, starting transfers between devices, exchange(): return lax.all_to_all(shaped, AXES, 0, 0, tiled=True).reshape(values.shape)  12.5 us
    pallas_call x1, Pallas kernels, shards(): pl.pallas_call(functools.partial(later_kernel, plan, False), out_shape=[m...  3.21 us
    pallas_call x1, Pallas kernels, shards(): pl.pallas_call(functools.partial(later_kernel, plan, True), out_shape=[ve...  3.2 us
  transfers between devices with their start and end apart: 3, of which 2 were waited for; matrix products, arithmetic and copies ran while one was open for 0% of the time, Pallas kernels for 5%

profile of v5, /device:TPU:0, one launch (start us, length us, event | category | flops | bytes accessed | tf_op | source)
XLA Modules:
  0.0 147.0 jit_solution(9619855111153491753)
XLA Ops:
  0.6 0.0 copy-start.4
  0.6 1.0 copy-done.4
  1.7 1.0 depart.1
  2.7 7.3 %all-to-all-start = ((f32[32,17,2,128]{3,2,1,0:T(2,128)}), f32[32,17,2,128]{3,2,1,0:T(2,128)S(1)}, u32[]{:S(2)}, u32[]{:S(2)}) async-start(f32[32,17,2,128]{3,2,1,0:T(2,128)} %bitcast), calls=%async_computation | async-start | bytes 1114112 | tf_op jit(solution)/shard_map/all_to_all | solution.py:264
  10.0 0.0 copy-start.3
  10.0 2.8 %copy-done.3 = bf16[3,1024,1024]{2,1,0:T(8,128)(2,1)S(1)} copy-done((bf16[3,1024,1024]{2,1,0:T(8,128)(2,1)S(1)}, bf16[3,1024,1024]{2,1,0:T(8,128)(2,1)}, u32[]{:S(2)}) %copy-start.3) | copy-done | bytes 6291480
  12.8 0.0 copy-start.5
  12.8 0.7 copy-done.5
  13.5 0.0 copy-start.6
  13.5 0.7 copy-done.6
  14.1 0.0 copy-start.7
  14.1 0.7 copy-done.7
  14.8 0.0 copy-start.8
  14.8 0.7 copy-done.8
  15.5 0.0 copy-start.9
  15.5 0.7 copy-done.9
  16.1 2.8 %prepare.1 = (bf16[3,1024,1024]{2,1,0:T(8,128)(2,1)S(1)}, f32[6,128,128]{2,1,0:T(8,128)S(1)}, f32[8,1024]{1,0:T(8,128)S(1)}) custom-call(s32[3]{0:T(128)S(1)} %copy-done.6, s32[3,8,8]{2,1,0:T(8,128)S(1)} %copy-done.5, f32[3]{0:T(128)S(1)} %copy-done.7, f32[13]{0:T(128)S(1)} %copy-done.8, f32[64]{0:T(128)S(1)} %copy-done.9, bf16[3,1024,1024]{2,1,0:T(8,128)(2,1)S(1)} %copy-done.3), custom_call_target="tpu_custom_call" | custom-call | flops 3145728 | bytes 12582912 | tf_op jit(solution)/shard_map/prepare/pallas_call | solution.py:293
  18.9 0.0 copy-start
  18.9 2.7 %copy-done = bf16[3,1024,1024]{2,1,0:T(8,128)(2,1)} copy-done((bf16[3,1024,1024]{2,1,0:T(8,128)(2,1)}, bf16[3,1024,1024]{2,1,0:T(8,128)(2,1)S(1)}, u32[]{:S(2)}) %copy-start) | copy-done | bytes 6291480
  21.5 4.6 %all-to-all-done = f32[32,17,2,128]{3,2,1,0:T(2,128)S(1)} async-done(((f32[32,17,2,128]{3,2,1,0:T(2,128)}), f32[32,17,2,128]{3,2,1,0:T(2,128)S(1)}, u32[]{:S(2)}, u32[]{:S(2)}) %all-to-all-start) | async-done | bytes 557088 | tf_op jit(solution)/shard_map/all_to_all | solution.py:264
  26.1 0.0 copy-start.1
  26.1 2.8 %copy-done.1 = bf16[3,1024,1024]{2,1,0:T(8,128)(2,1)S(1)} copy-done((bf16[3,1024,1024]{2,1,0:T(8,128)(2,1)S(1)}, bf16[3,1024,1024]{2,1,0:T(8,128)(2,1)}, u32[]{:S(2)}) %copy-start.1) | copy-done | bytes 6291480
  28.9 2.4 %first.1 = (f32[128,1024]{1,0:T(8,128)S(1)}, f32[128,1024]{1,0:T(8,128)S(1)}, f32[8,128]{1,0:T(8,128)S(1)}) custom-call(f32[1088,128]{1,0:T(8,128)S(1)} %bitcast.6, bf16[3,1024,1024]{2,1,0:T(8,128)(2,1)S(1)} %copy-done.1, f32[6,128,128]{2,1,0:T(8,128)S(1)} %get-tuple-element.19.place_ref, f32[8,1024]{1,0:T(8,128)S(1)} %get-tuple-element.20.inside_ref), custom_call_target="tpu_custom_call" | custom-call | flops 805306368 | bytes 524288 | tf_op jit(solution)/shard_map/first/pallas_call | solution.py:308
  31.3 39.5 %all_gather.6.arrived_ref = f32[256,128]{1,0:T(8,128)S(1)} all-gather(f32[8,128]{1,0:T(8,128)S(1)} %get-tuple-element.21), channel_id=1, replica_groups=mesh['site'=8,'phonon'=4] {'site','phonon'}, dimensions={0}, use_global_device_ids=true | all-gather | bytes 135168 | tf_op jit(solution)/shard_map/all_gather | solution.py:268
  70.7 3.2 %second.1 = (f32[128,1024]{1,0:T(8,128)S(1)}, f32[128,1024]{1,0:T(8,128)S(1)}, f32[1088,128]{1,0:T(8,128)}, f32[8,128]{1,0:T(8,128)S(1)}, f32[8,128]{1,0:T(8,128)S(1)}) custom-call(f32[256,128]{1,0:T(8,128)S(1)} %all_gather.6.arrived_ref, f32[128,1024]{1,0:T(8,128)S(1)} %get-tuple-element.22.raw_ref, ...), custom_call_target="tpu_custom_call" | custom-call | flops 805306368 | bytes 524288 | tf_op jit(solution)/shard_map/second/pallas_call | solution.py:319
  74.0 2.6 %all-to-all-start.2 = ((f32[32,17,2,128]{3,2,1,0:T(2,128)}), f32[32,17,2,128]{3,2,1,0:T(2,128)S(1)}, u32[]{:S(2)}, u32[]{:S(2)}) async-start(f32[32,17,2,128]{3,2,1,0:T(2,128)} %bitcast.4), calls=%async_computation.2 | async-start | bytes 1114112 | tf_op jit(solution)/shard_map/all_to_all | solution.py:264
  76.6 44.6 %all_gather.7.arrived_ref = f32[256,128]{1,0:T(8,128)S(1)} all-gather(f32[8,128]{1,0:T(8,128)S(1)} %get-tuple-element.24), channel_id=1, replica_groups=mesh['site'=8,'phonon'=4] {'site','phonon'}, dimensions={0}, use_global_device_ids=true | all-gather | bytes 135168 | tf_op jit(solution)/shard_map/all_gather | solution.py:268
  121.2 0.0 copy-start.2
  121.2 2.8 %copy-done.2 = bf16[3,1024,1024]{2,1,0:T(8,128)(2,1)S(1)} copy-done((bf16[3,1024,1024]{2,1,0:T(8,128)(2,1)S(1)}, bf16[3,1024,1024]{2,1,0:T(8,128)(2,1)}, u32[]{:S(2)}) %copy-start.2) | copy-done | bytes 6291480
  124.0 3.2 %third.1 = (f32[1088,128]{1,0:T(8,128)}, f32[8,128]{1,0:T(8,128)S(1)}) custom-call(f32[256,128]{1,0:T(8,128)S(1)} %all_gather.7.arrived_ref, f32[128,1024]{1,0:T(8,128)S(1)} %get-tuple-element.25.raw_ref, f32[128,1024]{1,0:T(8,128)S(1)} %get-tuple-element.26.previous_ref, f32[128,1024]{1,0:T(8,128)S(1)} %get-tuple-element.23.previous_ref.initial_ref, ...), custom_call_target="tpu_custom_call" | custom-call | flops 805306368 | bytes 524288 | tf_op jit(solution)/shard_map/third/pallas_call | solution.py:331
  127.2 0.0 all-to-all-done.2
  127.2 2.6 %all-to-all-start.1 = ((f32[32,17,2,128]{3,2,1,0:T(2,128)}), f32[32,17,2,128]{3,2,1,0:T(2,128)S(1)}, u32[]{:S(2)}, u32[]{:S(2)}) async-start(f32[32,17,2,128]{3,2,1,0:T(2,128)} %bitcast.2), calls=%async_computation.1 | async-start | bytes 1114112 | tf_op jit(solution)/shard_map/all_to_all | solution.py:264
  129.8 1.1 arrive_before.1
  130.9 15.0 %all-to-all-done.1 = f32[32,17,2,128]{3,2,1,0:T(2,128)S(1)} async-done(((f32[32,17,2,128]{3,2,1,0:T(2,128)}), f32[32,17,2,128]{3,2,1,0:T(2,128)S(1)}, u32[]{:S(2)}, u32[]{:S(2)}) %all-to-all-start.1) | async-done | bytes 557088 | tf_op jit(solution)/shard_map/all_to_all | solution.py:264
  145.9 1.1 arrive_last.1
Async XLA Ops:
  0.6 1.0 copy-start.4
  2.7 23.4 %all-to-all-start = ((f32[32,17,2,128]{3,2,1,0:T(2,128)}), f32[32,17,2,128]{3,2,1,0:T(2,128)S(1)}, u32[]{:S(2)}, u32[]{:S(2)}) async-start(f32[32,17,2,128]{3,2,1,0:T(2,128)} %bitcast), calls=%async_computation | async-start | bytes 1114112 | tf_op jit(solution)/shard_map/all_to_all | solution.py:264
  10.0 2.8 %copy-start.3 = (bf16[3,1024,1024]{2,1,0:T(8,128)(2,1)S(1)}, bf16[3,1024,1024]{2,1,0:T(8,128)(2,1)}, u32[]{:S(2)}) copy-start(bf16[3,1024,1024]{2,1,0:T(8,128)(2,1)} %operators_ref.1) | copy-start | bytes 18874372
  12.8 0.7 copy-start.5
  13.5 0.7 copy-start.6
  14.1 0.7 copy-start.7
  14.8 0.7 copy-start.8
  15.5 0.7 copy-start.9
  18.9 2.7 %copy-start = (bf16[3,1024,1024]{2,1,0:T(8,128)(2,1)}, bf16[3,1024,1024]{2,1,0:T(8,128)(2,1)S(1)}, u32[]{:S(2)}) copy-start(bf16[3,1024,1024]{2,1,0:T(8,128)(2,1)S(1)} %get-tuple-element.18.masked_ref) | copy-start | bytes 18874372
  26.1 2.8 %copy-start.1 = (bf16[3,1024,1024]{2,1,0:T(8,128)(2,1)S(1)}, bf16[3,1024,1024]{2,1,0:T(8,128)(2,1)}, u32[]{:S(2)}) copy-start(bf16[3,1024,1024]{2,1,0:T(8,128)(2,1)} %copy-done) | copy-start | bytes 18874372
  74.0 53.2 %all-to-all-start.2 = ((f32[32,17,2,128]{3,2,1,0:T(2,128)}), f32[32,17,2,128]{3,2,1,0:T(2,128)S(1)}, u32[]{:S(2)}, u32[]{:S(2)}) async-start(f32[32,17,2,128]{3,2,1,0:T(2,128)} %bitcast.4), calls=%async_computation.2 | async-start | bytes 1114112 | tf_op jit(solution)/shard_map/all_to_all | solution.py:264
  121.2 2.8 %copy-start.2 = (bf16[3,1024,1024]{2,1,0:T(8,128)(2,1)S(1)}, bf16[3,1024,1024]{2,1,0:T(8,128)(2,1)}, u32[]{:S(2)}) copy-start(bf16[3,1024,1024]{2,1,0:T(8,128)(2,1)} %copy-done) | copy-start | bytes 18874372
  127.2 18.8 %all-to-all-start.1 = ((f32[32,17,2,128]{3,2,1,0:T(2,128)}), f32[32,17,2,128]{3,2,1,0:T(2,128)S(1)}, u32[]{:S(2)}, u32[]{:S(2)}) async-start(f32[32,17,2,128]{3,2,1,0:T(2,128)} %bitcast.2), calls=%async_computation.1 | async-start | bytes 1114112 | tf_op jit(solution)/shard_map/all_to_all | solution.py:264

commit v6 on v2

--- a/solution.py
+++ b/solution.py
@@ -12,7 +12,7 @@
 STEPS = 3
 LANES = 128
 SUBLANES = 8
-EXTRA = 2
+EXTRA = 1
 AXES = ("site", "phonon")
 
 epsilon = 1e-06
@@ -20,6 +20,7 @@
 
 VMEM = pl.BlockSpec(memory_space=pltpu.VMEM)
 SMEM = pl.BlockSpec(memory_space=pltpu.SMEM)
+HBM = pl.BlockSpec(memory_space=pltpu.HBM)
 
 
 class Plan:
@@ -60,16 +61,22 @@
     return jnp.sum(values, axis=0, keepdims=True)
 
 
-def put_extra(plan, out_ref, sums):
-    for index, value in enumerate(sums):
-        out_ref[pl.ds(plan.body + index, plan.groups, stride=plan.message), :] = jnp.broadcast_to(
-            value, (plan.groups, LANES)
-        )
-
-
-def total_of(plan, ref, start, stride):
+def folded(value):
+    return value + pltpu.roll(value, LANES // 2, 1)
+
+
+def put_sums(plan, out_ref, squares, overlap, start, stride):
+    lane = lax.broadcasted_iota(jnp.int32, (1, LANES), 1)
+    row = jnp.where(lane < LANES // 2, folded(squares), folded(overlap))
+    out_ref[pl.ds(start, plan.groups, stride=stride), :] = jnp.broadcast_to(row, (plan.groups, LANES))
+
+
+def totals_of(plan, ref, start, stride):
     lanes = lane_sums(ref[pl.ds(start, plan.groups, stride=stride), :])
-    return jnp.sum(lanes, axis=1, keepdims=True)
+    lane = lax.broadcasted_iota(jnp.int32, (1, LANES), 1)
+    squares = jnp.sum(jnp.where(lane < LANES // 2, lanes, 0.0), axis=1, keepdims=True)
+    overlap = jnp.sum(jnp.where(lane < LANES // 2, 0.0, lanes), axis=1, keepdims=True)
+    return squares, overlap
 
 
 def scale_of(plan, squares):
@@ -86,11 +93,11 @@
             out_ref[pl.ds(piece * plan.lane_blocks + block, plan.groups, stride=plan.message), :] = turned[
                 piece * plan.groups : (piece + 1) * plan.groups
             ]
-    put_extra(plan, out_ref, (sums, jnp.zeros_like(sums)))
+    put_sums(plan, out_ref, sums, jnp.zeros_like(sums), plan.body, plan.message)
 
 
 def prepare_kernel(
-    plan, bits_ref, mask_ref, field_ref, coupling_ref, mode_ref, operators_ref, masked_ref, place_ref, inside_ref
+    plan, bits_ref, mask_ref, field_ref, coupling_ref, mode_ref, operators_ref, place_ref, inside_ref, *masked_refs
 ):
     me = lax.axis_index("site") * plan.phonons + lax.axis_index("phonon")
     for position in range(plan.bits):
@@ -100,7 +107,7 @@
             for along in range(plan.blocks):
                 columns = pl.ds(along * plan.edge, plan.edge)
                 keep = (mask_ref[chosen, across, along] > 0).astype(jnp.float32).astype(jnp.bfloat16)
-                masked_ref[position, rows, columns] = operators_ref[chosen, rows, columns] * keep
+                masked_refs[position][rows, columns] = operators_ref[chosen, rows, columns] * keep
     place = lax.broadcasted_iota(jnp.int32, (plan.places, LANES), 0)
     phonon = place % plan.phonons
     site = place // plan.phonons % plan.sites
@@ -147,10 +154,17 @@
     return pltpu.roll(tiles, by % SUBLANES, 1).reshape(places, width)
 
 
-def operate(plan, vector_ref, masked_ref, place_ref, inside_ref, rounded_ref, total_ref):
+def step(plan, vector_ref, masked_refs, place_ref, inside_ref, rounded_ref, finish, fetches=()):
     span = plan.places // plan.levels_here
     for block in range(plan.lane_blocks):
-        lanes = pl.ds(block * LANES, LANES)
+        vector = vector_ref[:, pl.ds(block * LANES, LANES)]
+        for position in range(plan.bits):
+            rounded_ref[:, pl.ds(position * plan.rows + block * LANES, LANES)] = flipped(
+                vector, plan.phonons << position
+            ).astype(jnp.bfloat16)
+
+    def local(start):
+        lanes = pl.ds(start, LANES)
         vector = vector_ref[:, lanes]
         levels = [vector[index * span : (index + 1) * span] for index in range(plan.levels_here)]
         lower = jnp.concatenate([shifted(levels[-1], 1)] + levels[:-1], axis=0)
@@ -158,90 +172,119 @@
         weight = place_ref[0] + inside_ref[:1, lanes]
         total = weight * (place_ref[1] * lower + place_ref[2] * upper)
         for position in range(plan.bits):
-            turned = flipped(vector, plan.phonons << position)
-            total = total + place_ref[3 + position] * turned
-            rounded_ref[:, pl.ds(position * plan.rows + block * LANES, LANES)] = turned.astype(jnp.bfloat16)
-        total_ref[:, lanes] = total
+            total = total + place_ref[3 + position, :1] * flipped(vector, plan.phonons << position)
+        return total
+
+    def product(lanes, position):
+        return lax.dot_general(
+            rounded_ref[:, pl.ds(position * plan.rows, plan.rows)],
+            masked_refs[position][lanes, :],
+            (((1,), (1,)), ((), ())),
+            preferred_element_type=jnp.float32,
+        )
+
+    early = range(plan.bits - len(fetches))
+    late = range(plan.bits - len(fetches), plan.bits)
     width = 2 * LANES
-    for column in range(plan.rows // width):
-        lanes = pl.ds(column * width, width)
-        total = total_ref[:, lanes]
-        for position in range(plan.bits):
-            total = total + lax.dot_general(
-                rounded_ref[:, pl.ds(position * plan.rows, plan.rows)],
-                masked_ref[position, lanes, :],
-                (((1,), (1,)), ((), ())),
-                preferred_element_type=jnp.float32,
-            )
-        total_ref[:, lanes] = total
-
-
-def first_kernel(
-    plan, arrived_ref, masked_ref, place_ref, inside_ref, initial_ref, new_ref, sums_ref, rounded_ref
-):
-    scale = scale_of(plan, total_of(plan, arrived_ref, plan.body, plan.message))
+    parts = [pl.ds(start, width) for start in range(0, plan.rows, width)]
+
+    def begun(lanes):
+        total = jnp.concatenate([local(start) for start in range(lanes.start, lanes.start + width, LANES)], axis=1)
+        for position in early:
+            total = total + product(lanes, position)
+        return total
+
+    if not fetches:
+        for lanes in parts:
+            finish(lanes, begun(lanes))
+        return
+    held_ref = fetches[0][0]
+    for lanes in parts:
+        held_ref[:, lanes] = begun(lanes)
+    for _, fetch in fetches:
+        fetch.wait()
+    for lanes in parts:
+        total = held_ref[:, lanes]
+        for position in late:
+            total = total + product(lanes, position)
+        finish(lanes, total)
+
+
+def first_kernel(plan, arrived_ref, place_ref, inside_ref, *refs):
+    kept = 1
+    masked_refs = refs[:kept]
+    stored_refs = refs[kept : plan.bits]
+    initial_ref, new_ref, sums_ref = refs[plan.bits : plan.bits + 3]
+    fetched_refs = refs[plan.bits + 3 : -2]
+    rounded_ref, semaphores = refs[-2:]
+    fetches = []
+    for index, (stored_ref, fetched_ref) in enumerate(zip(stored_refs, fetched_refs)):
+        fetch = pltpu.make_async_copy(stored_ref, fetched_ref, semaphores.at[index])
+        fetch.start()
+        fetches.append((new_ref, fetch))
+    squares, _ = totals_of(plan, arrived_ref, plan.body, plan.message)
+    inverse = 1.0 / scale_of(plan, squares)
     for piece in range(plan.pieces):
         for block in range(plan.lane_blocks):
             part = arrived_ref[pl.ds(piece * plan.lane_blocks + block, plan.groups, stride=plan.message), :]
-            initial_ref[pl.ds(piece * plan.groups, plan.groups), pl.ds(block * LANES, LANES)] = part / scale
-    operate(plan, initial_ref, masked_ref, place_ref, inside_ref, rounded_ref, new_ref)
-    squares = jnp.zeros((1, LANES), jnp.float32)
-    overlap = jnp.zeros((1, LANES), jnp.float32)
+            initial_ref[pl.ds(piece * plan.groups, plan.groups), pl.ds(block * LANES, LANES)] = part * inverse
+    squares = []
+    overlap = []
+
+    def finish(lanes, new):
+        new_ref[:, lanes] = new
+        squares.append(lane_sums(new * new))
+        overlap.append(lane_sums(new * initial_ref[:, lanes]))
+
+    step(
+        plan, initial_ref, (*masked_refs, *fetched_refs), place_ref, inside_ref, rounded_ref, finish, fetches
+    )
+    put_sums(plan, sums_ref, one_row(squares), one_row(overlap), 0, EXTRA)
+
+
+def one_row(rows):
+    total = sum(rows[1:], rows[0])
+    return sum(total[:, start : start + LANES] for start in range(0, total.shape[1], LANES))
+
+
+def later_kernel(plan, body, keep, arrived_ref, raw_ref, previous_ref, initial_ref, place_ref, inside_ref, *refs):
+    masked_refs = refs[: plan.bits]
+    if keep:
+        current_ref, new_ref, out_ref, moment_ref, rounded_ref = refs[plan.bits :]
+    else:
+        out_ref, moment_ref, rounded_ref, current_ref = refs[plan.bits :]
+    squares, overlap = totals_of(plan, arrived_ref, body, body + EXTRA)
+    inverse = 1.0 / scale_of(plan, squares)
+    moment_ref[...] = jnp.broadcast_to(overlap * inverse / plan.entries, moment_ref.shape)
     for block in range(plan.lane_blocks):
         lanes = pl.ds(block * LANES, LANES)
-        new = new_ref[:, lanes]
-        squares = squares + lane_sums(new * new)
-        overlap = overlap + lane_sums(new * initial_ref[:, lanes])
-    for index, value in enumerate((squares, overlap)):
-        sums_ref[pl.ds(index, plan.groups, stride=EXTRA), :] = jnp.broadcast_to(value, (plan.groups, LANES))
-
-
-def later_kernel(
-    plan,
-    body,
-    keep,
-    arrived_ref,
-    raw_ref,
-    previous_ref,
-    initial_ref,
-    masked_ref,
-    place_ref,
-    inside_ref,
-    *refs,
-):
-    if keep:
-        current_ref, new_ref, out_ref, moment_ref, rounded_ref = refs
-    else:
-        out_ref, moment_ref, rounded_ref, current_ref, new_ref = refs
-    stride = body + EXTRA
-    scale = scale_of(plan, total_of(plan, arrived_ref, body, stride))
-    moment = total_of(plan, arrived_ref, body + 1, stride) / (plan.entries * scale)
-    moment_ref[...] = jnp.broadcast_to(moment, moment_ref.shape)
-    for block in range(plan.lane_blocks):
-        lanes = pl.ds(block * LANES, LANES)
-        current_ref[:, lanes] = raw_ref[:, lanes] / scale
-    operate(plan, current_ref, masked_ref, place_ref, inside_ref, rounded_ref, new_ref)
-    squares = jnp.zeros((1, LANES), jnp.float32)
-    overlap = jnp.zeros((1, LANES), jnp.float32)
-    for block in range(plan.lane_blocks):
-        lanes = pl.ds(block * LANES, LANES)
-        new = 2.0 * new_ref[:, lanes] - previous_ref[:, lanes] / scale
-        squares = squares + lane_sums(new * new)
-        overlap = overlap + lane_sums(new * initial_ref[:, lanes])
+        current_ref[:, lanes] = raw_ref[:, lanes] * inverse
+    squares = []
+    overlap = []
+
+    def finish(lanes, total):
+        new = 2.0 * total - previous_ref[:, lanes] * inverse
         if keep:
             new_ref[:, lanes] = new
-        for piece in range(plan.pieces):
-            out_ref[pl.ds(piece * plan.lane_blocks + block, plan.groups, stride=plan.message), :] = new[
-                piece * plan.groups : (piece + 1) * plan.groups
-            ]
-    put_extra(plan, out_ref, (squares, overlap))
+        squares.append(lane_sums(new * new))
+        overlap.append(lane_sums(new * initial_ref[:, lanes]))
+        for start in range(0, lanes.size, LANES):
+            block = (lanes.start + start) // LANES
+            for piece in range(plan.pieces):
+                out_ref[pl.ds(piece * plan.lane_blocks + block, plan.groups, stride=plan.message), :] = new[
+                    piece * plan.groups : (piece + 1) * plan.groups, start : start + LANES
+                ]
+
+    step(plan, current_ref, masked_refs, place_ref, inside_ref, rounded_ref, finish)
+    put_sums(plan, out_ref, one_row(squares), one_row(overlap), plan.body, plan.message)
 
 
 def arrive_kernel(plan, arrived_ref, *refs):
-    scale = scale_of(plan, total_of(plan, arrived_ref, plan.body, plan.message))
+    squares, overlap = totals_of(plan, arrived_ref, plan.body, plan.message)
+    inverse = 1.0 / scale_of(plan, squares)
     if len(refs) > 1:
         first_ref, second_ref, out_ref, moments_ref = refs
-        moment = total_of(plan, arrived_ref, plan.body + 1, plan.message) / (plan.entries * scale)
+        moment = overlap * inverse / plan.entries
         moments_ref[0] = first_ref[0, 0]
         moments_ref[1] = second_ref[0, 0]
         moments_ref[2] = moment[0, 0]
@@ -252,7 +295,7 @@
             arrived_ref[pl.ds(piece * plan.lane_blocks + block, plan.groups, stride=plan.message), :]
             for piece in range(plan.pieces)
         ]
-        out_ref[pl.ds(block * LANES, LANES), :] = (jnp.concatenate(parts, axis=0) / scale).T
+        out_ref[pl.ds(block * LANES, LANES), :] = (jnp.concatenate(parts, axis=0) * inverse).T
 
 
 def exchange(plan, values):
@@ -283,35 +326,37 @@
         name="depart",
     )(state)
     arrived = exchange(plan, departing)
-    masked, place, inside = pl.pallas_call(
+    operator = jax.ShapeDtypeStruct((plan.rows, plan.rows), jnp.bfloat16)
+    place, inside, *masked = pl.pallas_call(
         functools.partial(prepare_kernel, plan),
         out_shape=[
-            jax.ShapeDtypeStruct((plan.bits, plan.rows, plan.rows), jnp.bfloat16),
             jax.ShapeDtypeStruct((3 + plan.bits, plan.places, LANES), f32),
             jax.ShapeDtypeStruct((SUBLANES, plan.rows), f32),
-        ],
+        ]
+        + [operator] * plan.bits,
         in_specs=[SMEM] * 5 + [VMEM],
-        out_specs=[VMEM] * 3,
+        out_specs=[VMEM] * (2 + plan.bits),
         compiler_params=params(32),
         cost_estimate=cost(plan.bits * plan.rows * plan.rows, 4 * plan.bits * plan.rows * plan.rows),
         name="prepare",
     )(site_bits, op_mask, field, site_coupling, mode_coupling, operators)
-    tables = (masked, place, inside)
-    initial, raw, sums = pl.pallas_call(
+    fetched = plan.bits - 1
+    initial, raw, sums, *fetched_masked = pl.pallas_call(
         functools.partial(first_kernel, plan),
-        out_shape=[vector, vector, jax.ShapeDtypeStruct((plan.groups * EXTRA, LANES), f32)],
-        in_specs=[VMEM] * 4,
-        out_specs=[VMEM] * 3,
-        scratch_shapes=[rounded],
+        out_shape=[vector, vector, jax.ShapeDtypeStruct((plan.groups * EXTRA, LANES), f32)] + [operator] * fetched,
+        in_specs=[VMEM] * 4 + [HBM] * fetched,
+        out_specs=[VMEM] * (3 + fetched),
+        scratch_shapes=[rounded, pltpu.SemaphoreType.DMA((fetched,))],
         compiler_params=params(32),
         cost_estimate=cost(work, 4 * plan.places * plan.rows),
         name="first",
-    )(arrived, *tables)
+    )(arrived, place, inside, *masked)
+    tables = (place, inside, masked[0], *fetched_masked)
     sums = exchange(plan, sums)
     current, raw, departing, moment_one = pl.pallas_call(
         functools.partial(later_kernel, plan, 0, True),
         out_shape=[vector, vector, message, moment],
-        in_specs=[VMEM] * 7,
+        in_specs=[VMEM] * (6 + plan.bits),
         out_specs=[VMEM] * 4,
         scratch_shapes=[rounded],
         compiler_params=params(32),
@@ -322,9 +367,9 @@
     departing, moment_two = pl.pallas_call(
         functools.partial(later_kernel, plan, plan.body, False),
         out_shape=[message, moment],
-        in_specs=[VMEM] * 7,
+        in_specs=[VMEM] * (6 + plan.bits),
         out_specs=[VMEM] * 2,
-        scratch_shapes=[rounded, kept, kept],
+        scratch_shapes=[rounded, kept],
         compiler_params=params(32),
         cost_estimate=cost(work, 4 * plan.places * plan.rows),
         name="third",

time: 85.9 us -> 85.8 us (level)
  waiting for transfers between devices: 19.6 us -> 22.3 us
  local copies, waits for them, and re-layouts: 12.6 us -> 10.5 us
    all_to_all x2, waiting for transfers between devices: 19.6 us -> 22.3 us  [exchange(): return lax.all_to_all(shaped, AXES, 0, 0, tiled=True).reshape(values.shape)]
    unnamed x18 -> x24, local copies, waits for them, and re-layouts: 12.6 us -> 10.5 us
where the time goes in v6:
time: 85.8 us; the launch traced here: 85.4 us
  blocking collectives  27.6 us (32%)
  waiting for transfers between devices  22.3 us (26%)
  Pallas kernels  13.9 us (16%)
  local copies, waits for them, and re-layouts  10.5 us (12%)
  starting transfers between devices  10.3 us (12%)
    all_to_all x2, blocking collectives, exchange(): return lax.all_to_all(shaped, AXES, 0, 0, tiled=True).reshape(values.shape)  27.6 us
    all_to_all x2, waiting for transfers between devices, exchange(): return lax.all_to_all(shaped, AXES, 0, 0, tiled=True).reshape(values.shape)  22.3 us
    unnamed x24, local copies, waits for them, and re-layouts  10.5 us
    all_to_all x2, starting transfers between devices, exchange(): return lax.all_to_all(shaped, AXES, 0, 0, tiled=True).reshape(values.shape)  10.3 us
    pallas_call x1, Pallas kernels, shards(): pl.pallas_call(functools.partial(first_kernel, plan), out_shape=[vector,...  2.83 us
    pallas_call x1, Pallas kernels, shards(): pl.pallas_call(functools.partial(prepare_kernel, plan), out_shape=[jax.Sh...  2.77 us
    pallas_call x1, Pallas kernels, shards(): pl.pallas_call(functools.partial(later_kernel, plan, plan.body, False), o...  2.5 us
    pallas_call x1, Pallas kernels, shards(): pl.pallas_call(functools.partial(later_kernel, plan, 0, True), out_shape=...  2.46 us
  transfers between devices with their start and end apart: 2, of which 2 were waited for; matrix products, arithmetic and copies ran while one was open for 0% of the time, Pallas kernels for 5%

profile of v6, /device:TPU:0, one launch (start us, length us, event | category | flops | bytes accessed | tf_op | source)
XLA Modules:
  0.0 85.4 jit_solution(8955368920580942828)
XLA Ops:
  0.6 0.0 copy-start.6
  0.6 1.0 %copy-done.6 = f32[1024,128]{1,0:T(8,128)S(1)} copy-done((f32[1024,128]{1,0:T(8,128)S(1)}, f32[1024,128]{1,0:T(8,128)}, u32[]{:S(2)}) %copy-start.6) | copy-done | bytes 524312
  1.7 0.0 copy-start.7
  1.7 0.0 copy-start.8
  1.7 0.0 copy-start.9
  1.7 0.0 copy-start.10
  1.7 0.0 copy-start.11
  1.7 1.1 %depart.1 = f32[1056,128]{1,0:T(8,128)} custom-call(f32[1024,128]{1,0:T(8,128)S(1)} %copy-done.6), custom_call_target="tpu_custom_call" | custom-call | tf_op jit(solution)/shard_map/depart/pallas_call | solution.py:320
  2.8 7.3 %all-to-all-start = ((f32[32,33,1,128]{3,2,1,0:T(1,128)}), f32[32,33,1,128]{3,2,1,0:T(1,128)S(1)}, u32[]{:S(2)}, u32[]{:S(2)}) async-start(f32[32,33,1,128]{3,2,1,0:T(1,128)} %bitcast), calls=%async_computation | async-start | bytes 1081344 | tf_op jit(solution)/shard_map/all_to_all | solution.py:304
  10.1 0.0 copy-done.7
  10.1 0.0 copy-done.8
  10.1 0.0 copy-done.9
  10.1 0.0 copy-done.10
  10.1 0.0 copy-done.11
  10.1 0.0 copy-start
  10.1 2.8 %copy-done = bf16[3,1024,1024]{2,1,0:T(8,128)(2,1)S(1)} copy-done((bf16[3,1024,1024]{2,1,0:T(8,128)(2,1)S(1)}, bf16[3,1024,1024]{2,1,0:T(8,128)(2,1)}, u32[]{:S(2)}) %copy-start) | copy-done | bytes 6291480
  12.9 2.8 %prepare.1 = (f32[6,128,128]{2,1,0:T(8,128)S(1)}, f32[8,1024]{1,0:T(8,128)S(1)}, bf16[1024,1024]{1,0:T(8,128)(2,1)S(1)}, bf16[1024,1024]{1,0:T(8,128)(2,1)S(1)}, bf16[1024,1024]{1,0:T(8,128)(2,1)S(1)}) custom-call(s32[3]{0:T(128)S(1)} %copy-done.8, s32[3,8,8]{2,1,0:T(8,128)S(1)} %copy-done.7, f32[3]{0:T(128)S(1)} %copy-done.9, f32[13]{0:T(128)S(1)} %copy-done.10, ...), custom_call_target="tpu_custom_call" | custom-call | flops 3145728 | bytes 12582912 | tf_op jit(solution)/shard_map/prepare/pallas_call | solution.py:330
  15.7 0.0 copy-start.1
  15.7 1.3 %copy-done.1 = bf16[1024,1024]{1,0:T(8,128)(2,1)} copy-done((bf16[1024,1024]{1,0:T(8,128)(2,1)}, bf16[1024,1024]{1,0:T(8,128)(2,1)S(1)}, u32[]{:S(2)}) %copy-start.1) | copy-done | bytes 2097176
  17.0 0.0 copy-start.3
  17.0 1.3 %copy-done.3 = bf16[1024,1024]{1,0:T(8,128)(2,1)} copy-done((bf16[1024,1024]{1,0:T(8,128)(2,1)}, bf16[1024,1024]{1,0:T(8,128)(2,1)S(1)}, u32[]{:S(2)}) %copy-start.3) | copy-done | bytes 2097176
  18.3 7.6 %all-to-all-done = f32[32,33,1,128]{3,2,1,0:T(1,128)S(1)} async-done(((f32[32,33,1,128]{3,2,1,0:T(1,128)}), f32[32,33,1,128]{3,2,1,0:T(1,128)S(1)}, u32[]{:S(2)}, u32[]{:S(2)}) %all-to-all-start) | async-done | bytes 540704 | tf_op jit(solution)/shard_map/all_to_all | solution.py:304
  25.9 0.0 copy-start.2
  25.9 1.6 %copy-done.2 = bf16[1024,1024]{1,0:T(8,128)(2,1)S(1)} copy-done((bf16[1024,1024]{1,0:T(8,128)(2,1)S(1)}, bf16[1024,1024]{1,0:T(8,128)(2,1)}, u32[]{:S(2)}) %copy-start.2) | copy-done | bytes 2097176
  27.5 0.0 copy-start.4
  27.5 1.6 %copy-done.4 = bf16[1024,1024]{1,0:T(8,128)(2,1)S(1)} copy-done((bf16[1024,1024]{1,0:T(8,128)(2,1)S(1)}, bf16[1024,1024]{1,0:T(8,128)(2,1)}, u32[]{:S(2)}) %copy-start.4) | copy-done | bytes 2097176
  29.1 2.8 %first.1 = (f32[128,1024]{1,0:T(8,128)S(1)}, f32[128,1024]{1,0:T(8,128)S(1)}, f32[32,128]{1,0:T(8,128)S(1)}, bf16[1024,1024]{1,0:T(8,128)(2,1)S(1)}, bf16[1024,1024]{1,0:T(8,128)(2,1)S(1)}) custom-call(f32[1056,128]{1,0:T(8,128)S(1)} %bitcast.12, f32[6,128,128]{2,1,0:T(8,128)S(1)} %get-tuple-element.21.place_ref, ...), custom_call_target="tpu_custom_call" | custom-call | flops 805306368 | bytes 524288 | tf_op jit(solution)/shard_map/first/pallas_call | solution.py:344
  31.9 10.1 %all_to_all.20 = f32[32,1,1,128]{3,2,1,0:T(1,128)S(1)} all-to-all(f32[32,1,1,128]{3,2,1,0:T(1,128)S(1)} %bitcast.17), channel_id=1, replica_groups=mesh['site'=8,'phonon'=4] {'site','phonon'}, dimensions={0} | all-to-all | bytes 32768 | tf_op jit(solution)/shard_map/all_to_all | solution.py:304
  42.0 2.5 %second.1 = (f32[128,1024]{1,0:T(8,128)S(1)}, f32[128,1024]{1,0:T(8,128)S(1)}, f32[1056,128]{1,0:T(8,128)S(1)}, f32[8,128]{1,0:T(8,128)S(1)}) custom-call(f32[32,128]{1,0:T(8,128)S(1)} %bitcast.16, f32[128,1024]{1,0:T(8,128)S(1)} %get-tuple-element.27.raw_ref, f32[128,1024]{1,0:T(8,128)S(1)} %get-tuple-element.28.previous_ref.initial_ref, ...), custom_call_target="tpu_custom_call" | custom-call | flops 805306368 | bytes 524288 | tf_op jit(solution)/shard_map/second/pallas_call | solution.py:356
  44.5 17.6 %all_to_all.21 = f32[32,33,1,128]{3,2,1,0:T(1,128)S(1)} all-to-all(f32[32,33,1,128]{3,2,1,0:T(1,128)S(1)} %bitcast.15), channel_id=1, replica_groups=mesh['site'=8,'phonon'=4] {'site','phonon'}, dimensions={0} | all-to-all | bytes 1081344 | tf_op jit(solution)/shard_map/all_to_all | solution.py:304
  62.1 2.5 %third.1 = (f32[1056,128]{1,0:T(8,128)S(1)}, f32[8,128]{1,0:T(8,128)S(1)}) custom-call(f32[1056,128]{1,0:T(8,128)S(1)} %bitcast.10, f32[128,1024]{1,0:T(8,128)S(1)} %get-tuple-element.32.raw_ref, f32[128,1024]{1,0:T(8,128)S(1)} %get-tuple-element.33.previous_ref, f32[128,1024]{1,0:T(8,128)S(1)} %get-tuple-element.28.previous_ref.initial_ref, ...), custom_call_target="tpu_custom_call" | custom-call | flops 805306368 | bytes 524288 | tf_op jit(solution)/shard_map/third/pallas_call | solution.py:367
  64.6 0.0 copy-start.5
  64.6 0.8 copy-done.5
  65.4 3.0 %all-to-all-start.3 = ((f32[32,33,1,128]{3,2,1,0:T(1,128)}), f32[32,33,1,128]{3,2,1,0:T(1,128)S(1)}, u32[]{:S(2)}, u32[]{:S(2)}) async-start(f32[32,33,1,128]{3,2,1,0:T(1,128)} %bitcast.14), calls=%async_computation.3 | async-start | bytes 1081344 | tf_op jit(solution)/shard_map/all_to_all | solution.py:304
  68.4 1.1 %arrive_before.1 = f32[1024,128]{1,0:T(8,128)} custom-call(f32[1056,128]{1,0:T(8,128)S(1)} %bitcast.11), custom_call_target="tpu_custom_call" | custom-call | flops 131072 | bytes 1048576 | tf_op jit(solution)/shard_map/arrive_before/pallas_call | solution.py:378
  69.5 14.7 %all-to-all-done.3 = f32[32,33,1,128]{3,2,1,0:T(1,128)S(1)} async-done(((f32[32,33,1,128]{3,2,1,0:T(1,128)}), f32[32,33,1,128]{3,2,1,0:T(1,128)S(1)}, u32[]{:S(2)}, u32[]{:S(2)}) %all-to-all-start.3) | async-done | bytes 540704 | tf_op jit(solution)/shard_map/all_to_all | solution.py:304
  84.2 1.1 %arrive_last.1 = (f32[1024,128]{1,0:T(8,128)}, f32[3]{0:T(128)}) custom-call(f32[1056,128]{1,0:T(8,128)S(1)} %bitcast.13, f32[8,128]{1,0:T(8,128)S(1)} %get-tuple-element.35.refs_0_, f32[8,128]{1,0:T(8,128)S(1)} %get-tuple-element.36.refs_1_), custom_call_target="tpu_custom_call" | custom-call | tf_op jit(solution)/shard_map/arrive_last/pallas_call | solution.py:387
Async XLA Ops:
  0.6 1.0 %copy-start.6 = (f32[1024,128]{1,0:T(8,128)S(1)}, f32[1024,128]{1,0:T(8,128)}, u32[]{:S(2)}) copy-start(f32[1024,128]{1,0:T(8,128)} %state_ref.1) | copy-start | bytes 1572868
  1.7 8.4 %copy-start.7 = (s32[3,8,8]{2,1,0:T(8,128)S(1)}, s32[3,8,8]{2,1,0:T(8,128)}, u32[]{:S(2)}) copy-start(s32[3,8,8]{2,1,0:T(8,128)} %mask_ref.1) | copy-start | bytes 2308
  1.7 8.4 %copy-start.8 = (s32[3]{0:T(128)S(1)}, s32[3]{0:T(128)}, u32[]{:S(2)}) copy-start(s32[3]{0:T(128)} %bits_ref.1) | copy-start | bytes 40
  1.7 8.4 %copy-start.9 = (f32[3]{0:T(128)S(1)}, f32[3]{0:T(128)}, u32[]{:S(2)}) copy-start(f32[3]{0:T(128)} %field_ref.1) | copy-start | bytes 40
  1.7 8.4 %copy-start.10 = (f32[13]{0:T(128)S(1)}, f32[13]{0:T(128)}, u32[]{:S(2)}) copy-start(f32[13]{0:T(128)} %coupling_ref.1) | copy-start | bytes 160
  1.7 8.4 %copy-start.11 = (f32[64]{0:T(128)S(1)}, f32[64]{0:T(128)}, u32[]{:S(2)}) copy-start(f32[64]{0:T(128)} %mode_ref.1) | copy-start | bytes 772
  2.8 23.1 %all-to-all-start = ((f32[32,33,1,128]{3,2,1,0:T(1,128)}), f32[32,33,1,128]{3,2,1,0:T(1,128)S(1)}, u32[]{:S(2)}, u32[]{:S(2)}) async-start(f32[32,33,1,128]{3,2,1,0:T(1,128)} %bitcast), calls=%async_computation | async-start | bytes 1081344 | tf_op jit(solution)/shard_map/all_to_all | solution.py:304
  10.1 2.8 %copy-start = (bf16[3,1024,1024]{2,1,0:T(8,128)(2,1)S(1)}, bf16[3,1024,1024]{2,1,0:T(8,128)(2,1)}, u32[]{:S(2)}) copy-start(bf16[3,1024,1024]{2,1,0:T(8,128)(2,1)} %operators_ref.1) | copy-start | bytes 18874372
  15.7 1.3 %copy-start.1 = (bf16[1024,1024]{1,0:T(8,128)(2,1)}, bf16[1024,1024]{1,0:T(8,128)(2,1)S(1)}, u32[]{:S(2)}) copy-start(bf16[1024,1024]{1,0:T(8,128)(2,1)S(1)} %get-tuple-element.24.refs_1_) | copy-start | bytes 6291460
  17.0 1.3 %copy-start.3 = (bf16[1024,1024]{1,0:T(8,128)(2,1)}, bf16[1024,1024]{1,0:T(8,128)(2,1)S(1)}, u32[]{:S(2)}) copy-start(bf16[1024,1024]{1,0:T(8,128)(2,1)S(1)} %get-tuple-element.25.refs_2_) | copy-start | bytes 6291460
  25.9 1.6 %copy-start.2 = (bf16[1024,1024]{1,0:T(8,128)(2,1)S(1)}, bf16[1024,1024]{1,0:T(8,128)(2,1)}, u32[]{:S(2)}) copy-start(bf16[1024,1024]{1,0:T(8,128)(2,1)} %copy-done.1) | copy-start | bytes 6291460
  27.5 1.6 %copy-start.4 = (bf16[1024,1024]{1,0:T(8,128)(2,1)S(1)}, bf16[1024,1024]{1,0:T(8,128)(2,1)}, u32[]{:S(2)}) copy-start(bf16[1024,1024]{1,0:T(8,128)(2,1)} %copy-done.3) | copy-start | bytes 6291460
  64.6 0.8 copy-start.5
  65.4 18.9 %all-to-all-start.3 = ((f32[32,33,1,128]{3,2,1,0:T(1,128)}), f32[32,33,1,128]{3,2,1,0:T(1,128)S(1)}, u32[]{:S(2)}, u32[]{:S(2)}) async-start(f32[32,33,1,128]{3,2,1,0:T(1,128)} %bitcast.14), calls=%async_computation.3 | async-start | bytes 1081344 | tf_op jit(solution)/shard_map/all_to_all | solution.py:304

commit v7 on v6

--- a/solution.py
+++ b/solution.py
@@ -96,18 +96,56 @@
     put_sums(plan, out_ref, sums, jnp.zeros_like(sums), plan.body, plan.message)
 
 
+def mask_operator(plan, chosen, mask_ref, held_ref, out_ref):
+    for across in range(plan.blocks):
+        rows = pl.ds(across * plan.edge, plan.edge)
+        for along in range(plan.blocks):
+            columns = pl.ds(along * plan.edge, plan.edge)
+            keep = (mask_ref[chosen, across, along] > 0).astype(jnp.float32).astype(jnp.bfloat16)
+            out_ref[columns, rows] = (held_ref[rows, columns] * keep).T
+
+
+def store_kernel(plan, kept, bits_ref, mask_ref, operators_ref, *refs):
+    count = plan.bits - kept
+    stored_refs, (held_ref, masked_ref, in_semaphores, out_semaphores) = refs[:count], refs[count:]
+    fetches = [
+        pltpu.make_async_copy(operators_ref.at[bits_ref[kept + index]], held_ref.at[index], in_semaphores.at[index])
+        for index in range(count)
+    ]
+    for fetch in fetches:
+        fetch.start()
+    stores = []
+    for index in range(count):
+        fetches[index].wait()
+        mask_operator(plan, bits_ref[kept + index], mask_ref, held_ref.at[index], masked_ref.at[index])
+        store = pltpu.make_async_copy(masked_ref.at[index], stored_refs[index], out_semaphores.at[index])
+        store.start()
+        stores.append(store)
+    for store in stores:
+        store.wait()
+
+
 def prepare_kernel(
-    plan, bits_ref, mask_ref, field_ref, coupling_ref, mode_ref, operators_ref, place_ref, inside_ref, *masked_refs
+    plan,
+    kept,
+    bits_ref,
+    mask_ref,
+    field_ref,
+    coupling_ref,
+    mode_ref,
+    operators_ref,
+    place_ref,
+    inside_ref,
+    *refs,
 ):
+    masked_refs, (held_ref, semaphores) = refs[:kept], refs[kept:]
+    fetches = [
+        pltpu.make_async_copy(operators_ref.at[bits_ref[index]], held_ref.at[index], semaphores.at[index])
+        for index in range(kept)
+    ]
+    for fetch in fetches:
+        fetch.start()
     me = lax.axis_index("site") * plan.phonons + lax.axis_index("phonon")
-    for position in range(plan.bits):
-        chosen = bits_ref[position]
-        for across in range(plan.blocks):
-            rows = pl.ds(across * plan.edge, plan.edge)
-            for along in range(plan.blocks):
-                columns = pl.ds(along * plan.edge, plan.edge)
-                keep = (mask_ref[chosen, across, along] > 0).astype(jnp.float32).astype(jnp.bfloat16)
-                masked_refs[position][rows, columns] = operators_ref[chosen, rows, columns] * keep
     place = lax.broadcasted_iota(jnp.int32, (plan.places, LANES), 0)
     phonon = place % plan.phonons
     site = place // plan.phonons % plan.sites
@@ -132,6 +170,9 @@
     for local_bit in range(LBITS):
         weight = weight + coupling_ref[plan.bits + local_bit] * (inside >> local_bit & 1).astype(jnp.float32)
     inside_ref[...] = weight
+    for index in range(kept):
+        fetches[index].wait()
+        mask_operator(plan, bits_ref[index], mask_ref, held_ref.at[index], masked_refs[index])
 
 
 def flipped(values, stride):
@@ -176,10 +217,9 @@
         return total
 
     def product(lanes, position):
-        return lax.dot_general(
+        return jnp.dot(
             rounded_ref[:, pl.ds(position * plan.rows, plan.rows)],
-            masked_refs[position][lanes, :],
-            (((1,), (1,)), ((), ())),
+            masked_refs[position][:, lanes],
             preferred_element_type=jnp.float32,
         )
 
@@ -210,8 +250,7 @@
         finish(lanes, total)
 
 
-def first_kernel(plan, arrived_ref, place_ref, inside_ref, *refs):
-    kept = 1
+def first_kernel(plan, kept, arrived_ref, place_ref, inside_ref, *refs):
     masked_refs = refs[:kept]
     stored_refs = refs[kept : plan.bits]
     initial_ref, new_ref, sums_ref = refs[plan.bits : plan.bits + 3]
@@ -311,7 +350,7 @@
     moment = jax.ShapeDtypeStruct((SUBLANES, LANES), f32)
     held = jax.ShapeDtypeStruct((plan.rows, plan.columns), f32)
     rounded = pltpu.VMEM((plan.places, plan.bits * plan.rows), jnp.bfloat16)
-    kept = pltpu.VMEM((plan.places, plan.rows), f32)
+    working = pltpu.VMEM((plan.places, plan.rows), f32)
     work = 2 * plan.bits * plan.places * plan.rows * plan.rows
 
     def cost(flops, moved):
@@ -327,31 +366,51 @@
     )(state)
     arrived = exchange(plan, departing)
     operator = jax.ShapeDtypeStruct((plan.rows, plan.rows), jnp.bfloat16)
+    kept = 1
+    fetched = plan.bits - kept
     place, inside, *masked = pl.pallas_call(
-        functools.partial(prepare_kernel, plan),
+        functools.partial(prepare_kernel, plan, kept),
         out_shape=[
             jax.ShapeDtypeStruct((3 + plan.bits, plan.places, LANES), f32),
             jax.ShapeDtypeStruct((SUBLANES, plan.rows), f32),
         ]
-        + [operator] * plan.bits,
-        in_specs=[SMEM] * 5 + [VMEM],
-        out_specs=[VMEM] * (2 + plan.bits),
-        compiler_params=params(32),
-        cost_estimate=cost(plan.bits * plan.rows * plan.rows, 4 * plan.bits * plan.rows * plan.rows),
+        + [operator] * kept,
+        in_specs=[SMEM] * 5 + [HBM],
+        out_specs=[VMEM] * (2 + kept),
+        scratch_shapes=[
+            pltpu.VMEM((kept, plan.rows, plan.rows), jnp.bfloat16),
+            pltpu.SemaphoreType.DMA((kept,)),
+        ],
+        compiler_params=params(50),
+        cost_estimate=cost(plan.rows * plan.rows, 4 * kept * plan.rows * plan.rows),
         name="prepare",
     )(site_bits, op_mask, field, site_coupling, mode_coupling, operators)
-    fetched = plan.bits - 1
+    stored = pl.pallas_call(
+        functools.partial(store_kernel, plan, kept),
+        out_shape=[operator] * fetched,
+        in_specs=[SMEM] * 2 + [HBM],
+        out_specs=[HBM] * fetched,
+        scratch_shapes=[
+            pltpu.VMEM((fetched, plan.rows, plan.rows), jnp.bfloat16),
+            pltpu.VMEM((fetched, plan.rows, plan.rows), jnp.bfloat16),
+            pltpu.SemaphoreType.DMA((fetched,)),
+            pltpu.SemaphoreType.DMA((fetched,)),
+        ],
+        compiler_params=params(60),
+        cost_estimate=cost(plan.rows * plan.rows, 4 * fetched * plan.rows * plan.rows),
+        name="store",
+    )(site_bits, op_mask, operators)
     initial, raw, sums, *fetched_masked = pl.pallas_call(
-        functools.partial(first_kernel, plan),
+        functools.partial(first_kernel, plan, kept),
         out_shape=[vector, vector, jax.ShapeDtypeStruct((plan.groups * EXTRA, LANES), f32)] + [operator] * fetched,
         in_specs=[VMEM] * 4 + [HBM] * fetched,
         out_specs=[VMEM] * (3 + fetched),
         scratch_shapes=[rounded, pltpu.SemaphoreType.DMA((fetched,))],
-        compiler_params=params(32),
+        compiler_params=params(46),
         cost_estimate=cost(work, 4 * plan.places * plan.rows),
         name="first",
-    )(arrived, place, inside, *masked)
-    tables = (place, inside, masked[0], *fetched_masked)
+    )(arrived, place, inside, *masked, *stored)
+    tables = (place, inside, *masked, *fetched_masked)
     sums = exchange(plan, sums)
     current, raw, departing, moment_one = pl.pallas_call(
         functools.partial(later_kernel, plan, 0, True),
@@ -369,7 +428,7 @@
         out_shape=[message, moment],
         in_specs=[VMEM] * (6 + plan.bits),
         out_specs=[VMEM] * 2,
-        scratch_shapes=[rounded, kept],
+        scratch_shapes=[rounded, working],
         compiler_params=params(32),
         cost_estimate=cost(work, 4 * plan.places * plan.rows),
         name="third",

time: 85.8 us -> 81.1 us (0.945)
  local copies, waits for them, and re-layouts: 10.5 us -> 1.87 us
  Pallas kernels: 13.9 us -> 18 us
    unnamed x24 -> x14, local copies, waits for them, and re-layouts: 10.5 us -> 1.87 us
    pallas_call x2 -> x3, Pallas kernels: 5.6 us -> 12 us  [the longest x1 5.35 us: shards(): pl.pallas_call(functools.partial(store_kernel, plan, kept), out_shape=[op...]
    pallas_call x1, Pallas kernels: 2.5 us -> 1.33 us  [shards(): pl.pallas_call(functools.partial(later_kernel, plan, plan.body, False), o...]
    pallas_call x1, Pallas kernels: 2.46 us -> 1.36 us  [shards(): pl.pallas_call(functools.partial(later_kernel, plan, 0, True), out_shape=...]
  transfers between devices with their start and end apart: 2 -> 2, of which waited for: 2 -> 2; matrix products, arithmetic and copies ran while one was open for 0% -> 0% of each run, Pallas kernels for 5% -> 12%
where the time goes in v7:
time: 81.1 us; the launch traced here: 80.7 us
  blocking collectives  27.6 us (34%)
  waiting for transfers between devices  22 us (27%)
  Pallas kernels  18 us (22%)
  starting transfers between devices  10.3 us (13%)
  local copies, waits for them, and re-layouts  1.87 us (2%)
    all_to_all x2, blocking collectives, exchange(): return lax.all_to_all(shaped, AXES, 0, 0, tiled=True).reshape(values.shape)  27.6 us
    all_to_all x2, waiting for transfers between devices, exchange(): return lax.all_to_all(shaped, AXES, 0, 0, tiled=True).reshape(values.shape)  22 us
    all_to_all x2, starting transfers between devices, exchange(): return lax.all_to_all(shaped, AXES, 0, 0, tiled=True).reshape(values.shape)  10.3 us
    pallas_call x1, Pallas kernels, shards(): pl.pallas_call(functools.partial(store_kernel, plan, kept), out_shape=[op...  5.35 us
    pallas_call x1, Pallas kernels, shards(): pl.pallas_call(functools.partial(first_kernel, plan, kept), out_shape=[ve...  3.62 us
    pallas_call x1, Pallas kernels, shards(): pl.pallas_call(functools.partial(prepare_kernel, plan, kept), out_shape=[...  3.07 us
    unnamed x14, local copies, waits for them, and re-layouts  1.87 us
  transfers between devices with their start and end apart: 2, of which 2 were waited for; matrix products, arithmetic and copies ran while one was open for 0% of the time, Pallas kernels for 12%

profile of v7, /device:TPU:0, one launch (start us, length us, event | category | flops | bytes accessed | tf_op | source)
XLA Modules:
  0.0 80.7 jit_solution(13406715081041670496)
XLA Ops:
  0.6 0.0 copy-start.1
  0.6 1.0 %copy-done.1 = f32[1024,128]{1,0:T(8,128)S(1)} copy-done((f32[1024,128]{1,0:T(8,128)S(1)}, f32[1024,128]{1,0:T(8,128)}, u32[]{:S(2)}) %copy-start.1) | copy-done | bytes 524312
  1.7 1.1 %depart.1 = f32[1056,128]{1,0:T(8,128)} custom-call(f32[1024,128]{1,0:T(8,128)S(1)} %copy-done.1), custom_call_target="tpu_custom_call" | custom-call | tf_op jit(solution)/shard_map/depart/pallas_call | solution.py:359
  2.8 7.3 %all-to-all-start = ((f32[32,33,1,128]{3,2,1,0:T(1,128)}), f32[32,33,1,128]{3,2,1,0:T(1,128)S(1)}, u32[]{:S(2)}, u32[]{:S(2)}) async-start(f32[32,33,1,128]{3,2,1,0:T(1,128)} %bitcast), calls=%async_computation | async-start | bytes 1081344 | tf_op jit(solution)/shard_map/all_to_all | solution.py:343
  10.1 0.0 copy-start.2
  10.1 0.0 copy-start.3
  10.1 0.0 copy-start.4
  10.1 0.0 copy-start.5
  10.1 0.0 copy-start.6
  10.1 5.4 %store.1 = (bf16[1024,1024]{1,0:T(8,128)(2,1)}, bf16[1024,1024]{1,0:T(8,128)(2,1)}) custom-call(s32[3]{0:T(128)} %bits_ref.3, s32[3,8,8]{2,1,0:T(8,128)} %mask_ref.3, bf16[3,1024,1024]{2,1,0:T(8,128)(2,1)} %operators_ref.3), custom_call_target="tpu_custom_call" | custom-call | flops 1048576 | bytes 8388608 | tf_op jit(solution)/shard_map/store/pallas_call | solution.py:388
  15.5 0.0 copy-done.2
  15.5 0.0 copy-done.3
  15.5 0.0 copy-done.4
  15.5 0.0 copy-done.5
  15.5 0.0 copy-done.6
  15.5 3.1 %prepare.1 = (f32[6,128,128]{2,1,0:T(8,128)S(1)}, f32[8,1024]{1,0:T(8,128)S(1)}, bf16[1024,1024]{1,0:T(8,128)(2,1)S(1)}) custom-call(s32[3]{0:T(128)S(1)} %copy-done.3, s32[3,8,8]{2,1,0:T(8,128)S(1)} %copy-done.2, f32[3]{0:T(128)S(1)} %copy-done.4, f32[13]{0:T(128)S(1)} %copy-done.5, f32[64]{0:T(128)S(1)} %copy-done.6, bf16[3,1024,1024]{2,1,0:T(8,128)(2,1)} %operators_ref.3), custom_call_target="tpu_custom_call" | custom-call | flops 1048576 | bytes 4194304 | tf_op jit(solution)/shard_map/prepare/pallas_call | solution.py:371
  18.6 7.3 %all-to-all-done = f32[32,33,1,128]{3,2,1,0:T(1,128)S(1)} async-done(((f32[32,33,1,128]{3,2,1,0:T(1,128)}), f32[32,33,1,128]{3,2,1,0:T(1,128)S(1)}, u32[]{:S(2)}, u32[]{:S(2)}) %all-to-all-start) | async-done | bytes 540704 | tf_op jit(solution)/shard_map/all_to_all | solution.py:343
  25.9 3.6 %first.1 = (f32[128,1024]{1,0:T(8,128)S(1)}, f32[128,1024]{1,0:T(8,128)S(1)}, f32[32,128]{1,0:T(8,128)S(1)}, bf16[1024,1024]{1,0:T(8,128)(2,1)S(1)}, bf16[1024,1024]{1,0:T(8,128)(2,1)S(1)}) custom-call(f32[1056,128]{1,0:T(8,128)S(1)} %bitcast.12, f32[6,128,128]{2,1,0:T(8,128)S(1)} %get-tuple-element.21.place_ref, ...), custom_call_target="tpu_custom_call" | custom-call | flops 805306368 | bytes 524288 | tf_op jit(solution)/shard_map/first/pallas_call | solution.py:403
  29.5 10.1 %all_to_all.20 = f32[32,1,1,128]{3,2,1,0:T(1,128)S(1)} all-to-all(f32[32,1,1,128]{3,2,1,0:T(1,128)S(1)} %bitcast.17), channel_id=1, replica_groups=mesh['site'=8,'phonon'=4] {'site','phonon'}, dimensions={0} | all-to-all | bytes 32768 | tf_op jit(solution)/shard_map/all_to_all | solution.py:343
  39.6 1.4 %second.1 = (f32[128,1024]{1,0:T(8,128)S(1)}, f32[128,1024]{1,0:T(8,128)S(1)}, f32[1056,128]{1,0:T(8,128)S(1)}, f32[8,128]{1,0:T(8,128)S(1)}) custom-call(f32[32,128]{1,0:T(8,128)S(1)} %bitcast.16, f32[128,1024]{1,0:T(8,128)S(1)} %get-tuple-element.27.raw_ref, f32[128,1024]{1,0:T(8,128)S(1)} %get-tuple-element.28.previous_ref.initial_ref, ...), custom_call_target="tpu_custom_call" | custom-call | flops 805306368 | bytes 524288 | tf_op jit(solution)/shard_map/second/pallas_call | solution.py:415
  41.0 17.6 %all_to_all.21 = f32[32,33,1,128]{3,2,1,0:T(1,128)S(1)} all-to-all(f32[32,33,1,128]{3,2,1,0:T(1,128)S(1)} %bitcast.15), channel_id=1, replica_groups=mesh['site'=8,'phonon'=4] {'site','phonon'}, dimensions={0} | all-to-all | bytes 1081344 | tf_op jit(solution)/shard_map/all_to_all | solution.py:343
  58.5 1.3 %third.1 = (f32[1056,128]{1,0:T(8,128)S(1)}, f32[8,128]{1,0:T(8,128)S(1)}) custom-call(f32[1056,128]{1,0:T(8,128)S(1)} %bitcast.10, f32[128,1024]{1,0:T(8,128)S(1)} %get-tuple-element.32.raw_ref, f32[128,1024]{1,0:T(8,128)S(1)} %get-tuple-element.33.previous_ref, f32[128,1024]{1,0:T(8,128)S(1)} %get-tuple-element.28.previous_ref.initial_ref, ...), custom_call_target="tpu_custom_call" | custom-call | flops 805306368 | bytes 524288 | tf_op jit(solution)/shard_map/third/pallas_call | solution.py:426
  59.9 0.0 copy-start
  59.9 0.8 copy-done
  60.7 3.0 %all-to-all-start.3 = ((f32[32,33,1,128]{3,2,1,0:T(1,128)}), f32[32,33,1,128]{3,2,1,0:T(1,128)S(1)}, u32[]{:S(2)}, u32[]{:S(2)}) async-start(f32[32,33,1,128]{3,2,1,0:T(1,128)} %bitcast.14), calls=%async_computation.3 | async-start | bytes 1081344 | tf_op jit(solution)/shard_map/all_to_all | solution.py:343
  63.7 1.1 %arrive_before.1 = f32[1024,128]{1,0:T(8,128)} custom-call(f32[1056,128]{1,0:T(8,128)S(1)} %bitcast.11), custom_call_target="tpu_custom_call" | custom-call | flops 131072 | bytes 1048576 | tf_op jit(solution)/shard_map/arrive_before/pallas_call | solution.py:437
  64.8 14.7 %all-to-all-done.3 = f32[32,33,1,128]{3,2,1,0:T(1,128)S(1)} async-done(((f32[32,33,1,128]{3,2,1,0:T(1,128)}), f32[32,33,1,128]{3,2,1,0:T(1,128)S(1)}, u32[]{:S(2)}, u32[]{:S(2)}) %all-to-all-start.3) | async-done | bytes 540704 | tf_op jit(solution)/shard_map/all_to_all | solution.py:343
  79.6 1.1 %arrive_last.1 = (f32[1024,128]{1,0:T(8,128)}, f32[3]{0:T(128)}) custom-call(f32[1056,128]{1,0:T(8,128)S(1)} %bitcast.13, f32[8,128]{1,0:T(8,128)S(1)} %get-tuple-element.35.refs_0_, f32[8,128]{1,0:T(8,128)S(1)} %get-tuple-element.36.refs_1_), custom_call_target="tpu_custom_call" | custom-call | tf_op jit(solution)/shard_map/arrive_last/pallas_call | solution.py:446
Async XLA Ops:
  0.6 1.0 %copy-start.1 = (f32[1024,128]{1,0:T(8,128)S(1)}, f32[1024,128]{1,0:T(8,128)}, u32[]{:S(2)}) copy-start(f32[1024,128]{1,0:T(8,128)} %state_ref.1) | copy-start | bytes 1572868
  2.8 23.1 %all-to-all-start = ((f32[32,33,1,128]{3,2,1,0:T(1,128)}), f32[32,33,1,128]{3,2,1,0:T(1,128)S(1)}, u32[]{:S(2)}, u32[]{:S(2)}) async-start(f32[32,33,1,128]{3,2,1,0:T(1,128)} %bitcast), calls=%async_computation | async-start | bytes 1081344 | tf_op jit(solution)/shard_map/all_to_all | solution.py:343
  10.1 5.4 %copy-start.2 = (s32[3,8,8]{2,1,0:T(8,128)S(1)}, s32[3,8,8]{2,1,0:T(8,128)}, u32[]{:S(2)}) copy-start(s32[3,8,8]{2,1,0:T(8,128)} %mask_ref.3) | copy-start | bytes 2308
  10.1 5.4 %copy-start.3 = (s32[3]{0:T(128)S(1)}, s32[3]{0:T(128)}, u32[]{:S(2)}) copy-start(s32[3]{0:T(128)} %bits_ref.3) | copy-start | bytes 40
  10.1 5.4 %copy-start.4 = (f32[3]{0:T(128)S(1)}, f32[3]{0:T(128)}, u32[]{:S(2)}) copy-start(f32[3]{0:T(128)} %field_ref.1) | copy-start | bytes 40
  10.1 5.4 %copy-start.5 = (f32[13]{0:T(128)S(1)}, f32[13]{0:T(128)}, u32[]{:S(2)}) copy-start(f32[13]{0:T(128)} %coupling_ref.1) | copy-start | bytes 160
  10.1 5.4 %copy-start.6 = (f32[64]{0:T(128)S(1)}, f32[64]{0:T(128)}, u32[]{:S(2)}) copy-start(f32[64]{0:T(128)} %mode_ref.1) | copy-start | bytes 772
  59.9 0.8 copy-start
  60.7 18.9 %all-to-all-start.3 = ((f32[32,33,1,128]{3,2,1,0:T(1,128)}), f32[32,33,1,128]{3,2,1,0:T(1,128)S(1)}, u32[]{:S(2)}, u32[]{:S(2)}) async-start(f32[32,33,1,128]{3,2,1,0:T(1,128)} %bitcast.14), calls=%async_computation.3 | async-start | bytes 1081344 | tf_op jit(solution)/shard_map/all_to_all | solution.py:343

commit v8 on v7

--- a/solution.py
+++ b/solution.py
@@ -65,14 +65,14 @@
     return value + pltpu.roll(value, LANES // 2, 1)
 
 
-def put_sums(plan, out_ref, squares, overlap, start, stride):
+def put_sums(out_ref, squares, overlap, start, stride, count):
     lane = lax.broadcasted_iota(jnp.int32, (1, LANES), 1)
     row = jnp.where(lane < LANES // 2, folded(squares), folded(overlap))
-    out_ref[pl.ds(start, plan.groups, stride=stride), :] = jnp.broadcast_to(row, (plan.groups, LANES))
-
-
-def totals_of(plan, ref, start, stride):
-    lanes = lane_sums(ref[pl.ds(start, plan.groups, stride=stride), :])
+    out_ref[pl.ds(start, count, stride=stride), :] = jnp.broadcast_to(row, (count, LANES))
+
+
+def totals_of(ref, start, stride, count):
+    lanes = lane_sums(ref[pl.ds(start, count, stride=stride), :])
     lane = lax.broadcasted_iota(jnp.int32, (1, LANES), 1)
     squares = jnp.sum(jnp.where(lane < LANES // 2, lanes, 0.0), axis=1, keepdims=True)
     overlap = jnp.sum(jnp.where(lane < LANES // 2, 0.0, lanes), axis=1, keepdims=True)
@@ -93,7 +93,7 @@
             out_ref[pl.ds(piece * plan.lane_blocks + block, plan.groups, stride=plan.message), :] = turned[
                 piece * plan.groups : (piece + 1) * plan.groups
             ]
-    put_sums(plan, out_ref, sums, jnp.zeros_like(sums), plan.body, plan.message)
+    put_sums(out_ref, sums, jnp.zeros_like(sums), plan.body, plan.message, plan.groups)
 
 
 def mask_operator(plan, chosen, mask_ref, held_ref, out_ref):
@@ -195,7 +195,7 @@
     return pltpu.roll(tiles, by % SUBLANES, 1).reshape(places, width)
 
 
-def step(plan, vector_ref, masked_refs, place_ref, inside_ref, rounded_ref, finish, fetches=()):
+def step(plan, vector_ref, masked_refs, place_ref, inside_ref, rounded_ref, finish, fetches={}):
     span = plan.places // plan.levels_here
     for block in range(plan.lane_blocks):
         vector = vector_ref[:, pl.ds(block * LANES, LANES)]
@@ -223,31 +223,19 @@
             preferred_element_type=jnp.float32,
         )
 
-    early = range(plan.bits - len(fetches))
-    late = range(plan.bits - len(fetches), plan.bits)
-    width = 2 * LANES
-    parts = [pl.ds(start, width) for start in range(0, plan.rows, width)]
-
-    def begun(lanes):
-        total = jnp.concatenate([local(start) for start in range(lanes.start, lanes.start + width, LANES)], axis=1)
-        for position in early:
-            total = total + product(lanes, position)
-        return total
-
-    if not fetches:
-        for lanes in parts:
-            finish(lanes, begun(lanes))
-        return
-    held_ref = fetches[0][0]
-    for lanes in parts:
-        held_ref[:, lanes] = begun(lanes)
-    for _, fetch in fetches:
-        fetch.wait()
-    for lanes in parts:
-        total = held_ref[:, lanes]
-        for position in late:
+    for index, lanes in enumerate(parts_of(plan)):
+        total = jnp.concatenate(
+            [local(start) for start in range(lanes.start, lanes.start + lanes.size, LANES)], axis=1
+        )
+        for position in range(plan.bits):
+            if (position, index) in fetches:
+                fetches[position, index].wait()
             total = total + product(lanes, position)
         finish(lanes, total)
+
+
+def parts_of(plan):
+    return [pl.ds(start, 2 * LANES) for start in range(0, plan.rows, 2 * LANES)]
 
 
 def first_kernel(plan, kept, arrived_ref, place_ref, inside_ref, *refs):
@@ -256,12 +244,15 @@
     initial_ref, new_ref, sums_ref = refs[plan.bits : plan.bits + 3]
     fetched_refs = refs[plan.bits + 3 : -2]
     rounded_ref, semaphores = refs[-2:]
-    fetches = []
-    for index, (stored_ref, fetched_ref) in enumerate(zip(stored_refs, fetched_refs)):
-        fetch = pltpu.make_async_copy(stored_ref, fetched_ref, semaphores.at[index])
-        fetch.start()
-        fetches.append((new_ref, fetch))
-    squares, _ = totals_of(plan, arrived_ref, plan.body, plan.message)
+    fetches = {}
+    for part, lanes in enumerate(parts_of(plan)):
+        for index, (stored_ref, fetched_ref) in enumerate(zip(stored_refs, fetched_refs)):
+            fetch = pltpu.make_async_copy(
+                stored_ref.at[:, lanes], fetched_ref.at[:, lanes], semaphores.at[index, part]
+            )
+            fetch.start()
+            fetches[kept + index, part] = fetch
+    squares, _ = totals_of(arrived_ref, plan.body, plan.message, plan.groups)
     inverse = 1.0 / scale_of(plan, squares)
     for piece in range(plan.pieces):
         for block in range(plan.lane_blocks):
@@ -278,7 +269,7 @@
     step(
         plan, initial_ref, (*masked_refs, *fetched_refs), place_ref, inside_ref, rounded_ref, finish, fetches
     )
-    put_sums(plan, sums_ref, one_row(squares), one_row(overlap), 0, EXTRA)
+    put_sums(sums_ref, one_row(squares), one_row(overlap), 0, 1, plan.sites)
 
 
 def one_row(rows):
@@ -286,13 +277,26 @@
     return sum(total[:, start : start + LANES] for start in range(0, total.shape[1], LANES))
 
 
-def later_kernel(plan, body, keep, arrived_ref, raw_ref, previous_ref, initial_ref, place_ref, inside_ref, *refs):
+def place_block(plan, arrived_ref, out_ref, inverse, block):
+    parts = [
+        arrived_ref[pl.ds(piece * plan.lane_blocks + block, plan.groups, stride=plan.message), :]
+        for piece in range(plan.pieces)
+    ]
+    out_ref[pl.ds(block * LANES, LANES), :] = (jnp.concatenate(parts, axis=0) * inverse).T
+
+
+def relay_kernel(plan, arrived_ref, out_ref):
+    out_ref[...] = jnp.broadcast_to(lane_sums(arrived_ref[...]), out_ref.shape)
+
+
+def later_kernel(plan, keep, arrived_ref, raw_ref, previous_ref, initial_ref, place_ref, inside_ref, *refs):
     masked_refs = refs[: plan.bits]
     if keep:
         current_ref, new_ref, out_ref, moment_ref, rounded_ref = refs[plan.bits :]
+        squares, overlap = totals_of(arrived_ref, 0, 1, plan.phonons)
     else:
-        out_ref, moment_ref, rounded_ref, current_ref = refs[plan.bits :]
-    squares, overlap = totals_of(plan, arrived_ref, body, body + EXTRA)
+        out_ref, moment_ref, placed_ref, rounded_ref, current_ref = refs[plan.bits :]
+        squares, overlap = totals_of(arrived_ref, plan.body, plan.message, plan.groups)
     inverse = 1.0 / scale_of(plan, squares)
     moment_ref[...] = jnp.broadcast_to(overlap * inverse / plan.entries, moment_ref.shape)
     for block in range(plan.lane_blocks):
@@ -309,38 +313,31 @@
         overlap.append(lane_sums(new * initial_ref[:, lanes]))
         for start in range(0, lanes.size, LANES):
             block = (lanes.start + start) // LANES
+            if not keep:
+                place_block(plan, arrived_ref, placed_ref, inverse, block)
             for piece in range(plan.pieces):
                 out_ref[pl.ds(piece * plan.lane_blocks + block, plan.groups, stride=plan.message), :] = new[
                     piece * plan.groups : (piece + 1) * plan.groups, start : start + LANES
                 ]
 
     step(plan, current_ref, masked_refs, place_ref, inside_ref, rounded_ref, finish)
-    put_sums(plan, out_ref, one_row(squares), one_row(overlap), plan.body, plan.message)
-
-
-def arrive_kernel(plan, arrived_ref, *refs):
-    squares, overlap = totals_of(plan, arrived_ref, plan.body, plan.message)
+    put_sums(out_ref, one_row(squares), one_row(overlap), plan.body, plan.message, plan.groups)
+
+
+def arrive_kernel(plan, arrived_ref, first_ref, second_ref, out_ref, moments_ref):
+    squares, overlap = totals_of(arrived_ref, plan.body, plan.message, plan.groups)
     inverse = 1.0 / scale_of(plan, squares)
-    if len(refs) > 1:
-        first_ref, second_ref, out_ref, moments_ref = refs
-        moment = overlap * inverse / plan.entries
-        moments_ref[0] = first_ref[0, 0]
-        moments_ref[1] = second_ref[0, 0]
-        moments_ref[2] = moment[0, 0]
-    else:
-        (out_ref,) = refs
+    moment = overlap * inverse / plan.entries
+    moments_ref[0] = first_ref[0, 0]
+    moments_ref[1] = second_ref[0, 0]
+    moments_ref[2] = moment[0, 0]
     for block in range(plan.lane_blocks):
-        parts = [
-            arrived_ref[pl.ds(piece * plan.lane_blocks + block, plan.groups, stride=plan.message), :]
-            for piece in range(plan.pieces)
-        ]
-        out_ref[pl.ds(block * LANES, LANES), :] = (jnp.concatenate(parts, axis=0) * inverse).T
-
-
-def exchange(plan, values):
-    rows = values.shape[0] // plan.groups
-    shaped = values.reshape(plan.groups, rows // EXTRA, EXTRA, LANES)
-    return lax.all_to_all(shaped, AXES, 0, 0, tiled=True).reshape(values.shape)
+        place_block(plan, arrived_ref, out_ref, inverse, block)
+
+
+def exchange(values, count, axes):
+    shaped = values.reshape(count, values.shape[0] // count, 1, LANES)
+    return lax.all_to_all(shaped, axes, 0, 0, tiled=True).reshape(values.shape)
 
 
 def shards(plan, state, operators, op_mask, site_bits, field, site_coupling, mode_coupling):
@@ -364,7 +361,7 @@
         compiler_params=params(16),
         name="depart",
     )(state)
-    arrived = exchange(plan, departing)
+    arrived = exchange(departing, plan.groups, AXES)
     operator = jax.ShapeDtypeStruct((plan.rows, plan.rows), jnp.bfloat16)
     kept = 1
     fetched = plan.bits - kept
@@ -402,18 +399,27 @@
     )(site_bits, op_mask, operators)
     initial, raw, sums, *fetched_masked = pl.pallas_call(
         functools.partial(first_kernel, plan, kept),
-        out_shape=[vector, vector, jax.ShapeDtypeStruct((plan.groups * EXTRA, LANES), f32)] + [operator] * fetched,
+        out_shape=[vector, vector, jax.ShapeDtypeStruct((plan.sites, LANES), f32)] + [operator] * fetched,
         in_specs=[VMEM] * 4 + [HBM] * fetched,
         out_specs=[VMEM] * (3 + fetched),
-        scratch_shapes=[rounded, pltpu.SemaphoreType.DMA((fetched,))],
+        scratch_shapes=[rounded, pltpu.SemaphoreType.DMA((fetched, len(parts_of(plan))))],
         compiler_params=params(46),
         cost_estimate=cost(work, 4 * plan.places * plan.rows),
         name="first",
     )(arrived, place, inside, *masked, *stored)
     tables = (place, inside, *masked, *fetched_masked)
-    sums = exchange(plan, sums)
+    sums = exchange(sums, plan.sites, "site")
+    sums = pl.pallas_call(
+        functools.partial(relay_kernel, plan),
+        out_shape=jax.ShapeDtypeStruct((plan.phonons, LANES), f32),
+        in_specs=[VMEM],
+        out_specs=VMEM,
+        compiler_params=params(4),
+        name="relay",
+    )(sums)
+    sums = exchange(sums, plan.phonons, "phonon")
     current, raw, departing, moment_one = pl.pallas_call(
-        functools.partial(later_kernel, plan, 0, True),
+        functools.partial(later_kernel, plan, True),
         out_shape=[vector, vector, message, moment],
         in_specs=[VMEM] * (6 + plan.bits),
         out_specs=[VMEM] * 4,
@@ -422,27 +428,18 @@
         cost_estimate=cost(work, 4 * plan.places * plan.rows),
         name="second",
     )(sums, raw, initial, initial, *tables)
-    before = exchange(plan, departing)
-    departing, moment_two = pl.pallas_call(
-        functools.partial(later_kernel, plan, plan.body, False),
-        out_shape=[message, moment],
+    before = exchange(departing, plan.groups, AXES)
+    departing, moment_two, before = pl.pallas_call(
+        functools.partial(later_kernel, plan, False),
+        out_shape=[message, moment, held],
         in_specs=[VMEM] * (6 + plan.bits),
-        out_specs=[VMEM] * 2,
+        out_specs=[VMEM] * 3,
         scratch_shapes=[rounded, working],
         compiler_params=params(32),
         cost_estimate=cost(work, 4 * plan.places * plan.rows),
         name="third",
     )(before, raw, current, initial, *tables)
-    last = exchange(plan, departing)
-    before = pl.pallas_call(
-        functools.partial(arrive_kernel, plan),
-        out_shape=held,
-        in_specs=[VMEM],
-        out_specs=VMEM,
-        compiler_params=params(16),
-        cost_estimate=cost(plan.places * plan.rows, 8 * plan.places * plan.rows),
-        name="arrive_before",
-    )(before)
+    last = exchange(departing, plan.groups, AXES)
     last, moments = pl.pallas_call(
         functools.partial(arrive_kernel, plan),
         out_shape=[held, jax.ShapeDtypeStruct((STEPS,), f32)],

time: 81.1 us -> 86.3 us (1.064)
  blocking collectives: 27.6 us -> 51.9 us
  waiting for transfers between devices: 22 us -> 7.32 us
  starting transfers between devices: 10.3 us -> 7.3 us
    all_to_all x2 -> x4, blocking collectives: 27.6 us -> 51.9 us  [exchange(): return lax.all_to_all(shaped, axes, 0, 0, tiled=True).reshape(values.shape)]
    all_to_all x2 -> x1, waiting for transfers between devices: 22 us -> 7.32 us  [exchange(): return lax.all_to_all(shaped, axes, 0, 0, tiled=True).reshape(values.shape)]
    all_to_all x2 -> x1, starting transfers between devices: 10.3 us -> 7.3 us  [exchange(): return lax.all_to_all(shaped, axes, 0, 0, tiled=True).reshape(values.shape)]
    unnamed x14 -> x12, local copies, waits for them, and re-layouts: 1.87 us -> 1.07 us
  transfers between devices with their start and end apart: 2 -> 1, of which waited for: 2 -> 1; matrix products, arithmetic and copies ran while one was open for 0% -> 0% of each run, Pallas kernels for 12% -> 10%
where the time goes in v8:
time: 86.3 us; the launch traced here: 85.9 us
  blocking collectives  51.9 us (60%)
  Pallas kernels  17.6 us (20%)
  waiting for transfers between devices  7.32 us (8%)
  starting transfers between devices  7.3 us (8%)
  local copies, waits for them, and re-layouts  1.07 us (1%)
    all_to_all x4, blocking collectives, exchange(): return lax.all_to_all(shaped, axes, 0, 0, tiled=True).reshape(values.shape)  51.9 us
    all_to_all x1, waiting for transfers between devices, exchange(): return lax.all_to_all(shaped, axes, 0, 0, tiled=True).reshape(values.shape)  7.32 us
    all_to_all x1, starting transfers between devices, exchange(): return lax.all_to_all(shaped, axes, 0, 0, tiled=True).reshape(values.shape)  7.3 us
    pallas_call x1, Pallas kernels, shards(): pl.pallas_call(functools.partial(store_kernel, plan, kept), out_shape=[op...  5.33 us
    pallas_call x1, Pallas kernels, shards(): pl.pallas_call(functools.partial(first_kernel, plan, kept), out_shape=[ve...  3.35 us
    pallas_call x1, Pallas kernels, shards(): pl.pallas_call(functools.partial(prepare_kernel, plan, kept), out_shape=[...  3.07 us
    pallas_call x1, Pallas kernels, shards(): pl.pallas_call(functools.partial(later_kernel, plan, False), out_shape=[m...  2.22 us
  transfers between devices with their start and end apart: 1, of which 1 were waited for; matrix products, arithmetic and copies ran while one was open for 0% of the time, Pallas kernels for 10%

profile of v8, /device:TPU:0, one launch (start us, length us, event | category | flops | bytes accessed | tf_op | source)
XLA Modules:
  0.0 85.9 jit_solution(2304163147296315649)
XLA Ops:
  0.6 0.0 copy-start
  0.6 1.0 %copy-done = f32[1024,128]{1,0:T(8,128)S(1)} copy-done((f32[1024,128]{1,0:T(8,128)S(1)}, f32[1024,128]{1,0:T(8,128)}, u32[]{:S(2)}) %copy-start) | copy-done | bytes 524312
  1.7 1.1 %depart.1 = f32[1056,128]{1,0:T(8,128)} custom-call(f32[1024,128]{1,0:T(8,128)S(1)} %copy-done), custom_call_target="tpu_custom_call" | custom-call | tf_op jit(solution)/shard_map/depart/pallas_call | solution.py:356
  2.8 7.3 %all-to-all-start = ((f32[32,33,1,128]{3,2,1,0:T(1,128)}), f32[32,33,1,128]{3,2,1,0:T(1,128)S(1)}, u32[]{:S(2)}, u32[]{:S(2)}) async-start(f32[32,33,1,128]{3,2,1,0:T(1,128)} %bitcast), calls=%async_computation | async-start | bytes 1081344 | tf_op jit(solution)/shard_map/all_to_all | solution.py:340
  10.1 0.0 copy-start.1
  10.1 0.0 copy-start.2
  10.1 0.0 copy-start.3
  10.1 0.0 copy-start.4
  10.1 0.0 copy-start.5
  10.1 5.3 %store.1 = (bf16[1024,1024]{1,0:T(8,128)(2,1)}, bf16[1024,1024]{1,0:T(8,128)(2,1)}) custom-call(s32[3]{0:T(128)} %bits_ref.3, s32[3,8,8]{2,1,0:T(8,128)} %mask_ref.3, bf16[3,1024,1024]{2,1,0:T(8,128)(2,1)} %operators_ref.3), custom_call_target="tpu_custom_call" | custom-call | flops 1048576 | bytes 8388608 | tf_op jit(solution)/shard_map/store/pallas_call | solution.py:385
  15.5 0.0 copy-done.1
  15.5 0.0 copy-done.2
  15.5 0.0 copy-done.3
  15.5 0.0 copy-done.4
  15.5 0.0 copy-done.5
  15.5 3.1 %prepare.1 = (f32[6,128,128]{2,1,0:T(8,128)S(1)}, f32[8,1024]{1,0:T(8,128)S(1)}, bf16[1024,1024]{1,0:T(8,128)(2,1)S(1)}) custom-call(s32[3]{0:T(128)S(1)} %copy-done.2, s32[3,8,8]{2,1,0:T(8,128)S(1)} %copy-done.1, f32[3]{0:T(128)S(1)} %copy-done.3, f32[13]{0:T(128)S(1)} %copy-done.4, f32[64]{0:T(128)S(1)} %copy-done.5, bf16[3,1024,1024]{2,1,0:T(8,128)(2,1)} %operators_ref.3), custom_call_target="tpu_custom_call" | custom-call | flops 1048576 | bytes 4194304 | tf_op jit(solution)/shard_map/prepare/pallas_call | solution.py:368
  18.6 7.3 %all-to-all-done = f32[32,33,1,128]{3,2,1,0:T(1,128)S(1)} async-done(((f32[32,33,1,128]{3,2,1,0:T(1,128)}), f32[32,33,1,128]{3,2,1,0:T(1,128)S(1)}, u32[]{:S(2)}, u32[]{:S(2)}) %all-to-all-start) | async-done | bytes 540704 | tf_op jit(solution)/shard_map/all_to_all | solution.py:340
  25.9 3.4 %first.1 = (f32[128,1024]{1,0:T(8,128)S(1)}, f32[128,1024]{1,0:T(8,128)S(1)}, f32[8,128]{1,0:T(8,128)S(1)}, bf16[1024,1024]{1,0:T(8,128)(2,1)S(1)}, bf16[1024,1024]{1,0:T(8,128)(2,1)S(1)}) custom-call(f32[1056,128]{1,0:T(8,128)S(1)} %bitcast.14, f32[6,128,128]{2,1,0:T(8,128)S(1)} %get-tuple-element.22.place_ref, f32[8,1024]{1,0:T(8,128)S(1)} %get-tuple-element.23.inside_ref, ...), custom_call_target="tpu_custom_call" | custom-call | flops 805306368 | bytes 524288 | tf_op jit(solution)/shard_map/first/pallas_call | solution.py:400
  29.3 9.4 %all_to_all.25 = f32[8,1,1,128]{3,2,1,0:T(1,128)S(1)} all-to-all(f32[8,1,1,128]{3,2,1,0:T(1,128)S(1)} %bitcast.22), channel_id=1, replica_groups=mesh['site'=8,'phonon'=4] {'site'}, dimensions={0} | all-to-all | bytes 8192 | tf_op jit(solution)/shard_map/all_to_all | solution.py:340
  38.7 6.3 %all_to_all.26 = f32[4,1,1,128]{3,2,1,0:T(1,128)S(1)} all-to-all(f32[4,1,1,128]{3,2,1,0:T(1,128)S(1)} %bitcast.21), channel_id=1, replica_groups=mesh['site'=8,'phonon'=4] {'phonon'}, dimensions={0} | all-to-all | bytes 4096 | tf_op jit(solution)/shard_map/all_to_all | solution.py:340
  45.0 1.4 %second.1 = (f32[128,1024]{1,0:T(8,128)S(1)}, f32[128,1024]{1,0:T(8,128)S(1)}, f32[1056,128]{1,0:T(8,128)S(1)}, f32[8,128]{1,0:T(8,128)S(1)}) custom-call(f32[4,128]{1,0:T(4,128)S(1)} %bitcast.20, f32[128,1024]{1,0:T(8,128)S(1)} %get-tuple-element.28.raw_ref, f32[128,1024]{1,0:T(8,128)S(1)} %get-tuple-element.29.previous_ref.initial_ref, ...), custom_call_target="tpu_custom_call" | custom-call | flops 805306368 | bytes 524288 | tf_op jit(solution)/shard_map/second/pallas_call | solution.py:421
  46.3 17.6 %all_to_all.27 = f32[32,33,1,128]{3,2,1,0:T(1,128)S(1)} all-to-all(f32[32,33,1,128]{3,2,1,0:T(1,128)S(1)} %bitcast.18), channel_id=1, replica_groups=mesh['site'=8,'phonon'=4] {'site','phonon'}, dimensions={0} | all-to-all | bytes 1081344 | tf_op jit(solution)/shard_map/all_to_all | solution.py:340
  63.9 2.2 %third.1 = (f32[1056,128]{1,0:T(8,128)S(1)}, f32[8,128]{1,0:T(8,128)S(1)}, f32[1024,128]{1,0:T(8,128)}) custom-call(f32[1056,128]{1,0:T(8,128)S(1)} %bitcast.15, f32[128,1024]{1,0:T(8,128)S(1)} %get-tuple-element.33.raw_ref, f32[128,1024]{1,0:T(8,128)S(1)} %get-tuple-element.34.previous_ref, f32[128,1024]{1,0:T(8,128)S(1)} %get-tuple-element.29.previous_ref.initial_ref, ...), custom_call_target="tpu_custom_call" | custom-call | flops 805306368 | bytes 524288 | tf_op jit(solution)/shard_map/third/pallas_call | solution.py:432
  66.1 18.7 %all_to_all.28 = f32[32,33,1,128]{3,2,1,0:T(1,128)S(1)} all-to-all(f32[32,33,1,128]{3,2,1,0:T(1,128)S(1)} %bitcast.17), channel_id=1, replica_groups=mesh['site'=8,'phonon'=4] {'site','phonon'}, dimensions={0} | all-to-all | bytes 1081344 | tf_op jit(solution)/shard_map/all_to_all | solution.py:340
  84.8 1.1 %arrive_last.1 = (f32[1024,128]{1,0:T(8,128)}, f32[3]{0:T(128)}) custom-call(f32[1056,128]{1,0:T(8,128)S(1)} %bitcast.16, f32[8,128]{1,0:T(8,128)S(1)} %get-tuple-element.36.first_ref, f32[8,128]{1,0:T(8,128)S(1)} %get-tuple-element.37.second_ref), custom_call_target="tpu_custom_call" | custom-call | tf_op jit(solution)/shard_map/arrive_last/pallas_call | solution.py:443
  (1 shorter events, 0.0 us)
Async XLA Ops:
  0.6 1.0 %copy-start = (f32[1024,128]{1,0:T(8,128)S(1)}, f32[1024,128]{1,0:T(8,128)}, u32[]{:S(2)}) copy-start(f32[1024,128]{1,0:T(8,128)} %state_ref.1) | copy-start | bytes 1572868
  2.8 23.1 %all-to-all-start = ((f32[32,33,1,128]{3,2,1,0:T(1,128)}), f32[32,33,1,128]{3,2,1,0:T(1,128)S(1)}, u32[]{:S(2)}, u32[]{:S(2)}) async-start(f32[32,33,1,128]{3,2,1,0:T(1,128)} %bitcast), calls=%async_computation | async-start | bytes 1081344 | tf_op jit(solution)/shard_map/all_to_all | solution.py:340
  10.1 5.4 %copy-start.1 = (s32[3,8,8]{2,1,0:T(8,128)S(1)}, s32[3,8,8]{2,1,0:T(8,128)}, u32[]{:S(2)}) copy-start(s32[3,8,8]{2,1,0:T(8,128)} %mask_ref.3) | copy-start | bytes 2308
  10.1 5.4 %copy-start.2 = (s32[3]{0:T(128)S(1)}, s32[3]{0:T(128)}, u32[]{:S(2)}) copy-start(s32[3]{0:T(128)} %bits_ref.3) | copy-start | bytes 40
  10.1 5.4 %copy-start.3 = (f32[3]{0:T(128)S(1)}, f32[3]{0:T(128)}, u32[]{:S(2)}) copy-start(f32[3]{0:T(128)} %field_ref.1) | copy-start | bytes 40
  10.1 5.4 %copy-start.4 = (f32[13]{0:T(128)S(1)}, f32[13]{0:T(128)}, u32[]{:S(2)}) copy-start(f32[13]{0:T(128)} %coupling_ref.1) | copy-start | bytes 160
  10.1 5.4 %copy-start.5 = (f32[64]{0:T(128)S(1)}, f32[64]{0:T(128)}, u32[]{:S(2)}) copy-start(f32[64]{0:T(128)} %mode_ref.1) | copy-start | bytes 772

commit v9 on v8

--- a/solution.py
+++ b/solution.py
@@ -47,7 +47,7 @@
         return (
             MODES % self.groups == 0
             and self.columns == LANES
-            and self.rows % LANES == 0
+            and self.rows % (2 * LANES) == 0
             and self.edge % LANES == 0
             and self.groups % SUBLANES == 0
         )
@@ -83,10 +83,21 @@
     return jnp.sqrt(squares / plan.entries + epsilon)
 
 
-def depart_kernel(plan, state_ref, out_ref):
+def depart_kernel(plan, state_ref, out_ref, held_ref, semaphores):
+    half = plan.rows // 2
+    fetches = [
+        pltpu.make_async_copy(
+            state_ref.at[pl.ds(index * half, half), :], held_ref.at[pl.ds(index * half, half), :], semaphores.at[index]
+        )
+        for index in range(2)
+    ]
+    for fetch in fetches:
+        fetch.start()
     sums = jnp.zeros((1, LANES), jnp.float32)
     for block in range(plan.lane_blocks):
-        tile = state_ref[pl.ds(block * LANES, LANES), :]
+        if block * LANES % half == 0:
+            fetches[block * LANES // half].wait()
+        tile = held_ref[pl.ds(block * LANES, LANES), :]
         sums = sums + lane_sums(tile * tile)
         turned = tile.T
         for piece in range(plan.pieces):
@@ -195,7 +206,7 @@
     return pltpu.roll(tiles, by % SUBLANES, 1).reshape(places, width)
 
 
-def step(plan, vector_ref, masked_refs, place_ref, inside_ref, rounded_ref, finish, fetches={}):
+def step(plan, vector_ref, masked_refs, place_ref, inside_ref, rounded_ref, finish, kept, ready=None):
     span = plan.places // plan.levels_here
     for block in range(plan.lane_blocks):
         vector = vector_ref[:, pl.ds(block * LANES, LANES)]
@@ -227,9 +238,11 @@
         total = jnp.concatenate(
             [local(start) for start in range(lanes.start, lanes.start + lanes.size, LANES)], axis=1
         )
-        for position in range(plan.bits):
-            if (position, index) in fetches:
-                fetches[position, index].wait()
+        for position in range(kept):
+            total = total + product(lanes, position)
+        if ready:
+            ready(index)
+        for position in range(kept, plan.bits):
             total = total + product(lanes, position)
         finish(lanes, total)
 
@@ -244,14 +257,28 @@
     initial_ref, new_ref, sums_ref = refs[plan.bits : plan.bits + 3]
     fetched_refs = refs[plan.bits + 3 : -2]
     rounded_ref, semaphores = refs[-2:]
-    fetches = {}
-    for part, lanes in enumerate(parts_of(plan)):
-        for index, (stored_ref, fetched_ref) in enumerate(zip(stored_refs, fetched_refs)):
-            fetch = pltpu.make_async_copy(
-                stored_ref.at[:, lanes], fetched_ref.at[:, lanes], semaphores.at[index, part]
-            )
-            fetch.start()
-            fetches[kept + index, part] = fetch
+    parts = parts_of(plan)
+    fetches = [
+        [
+            pltpu.make_async_copy(stored_ref.at[:, lanes], fetched_ref.at[:, lanes], semaphores.at[index, part])
+            for index, (stored_ref, fetched_ref) in enumerate(zip(stored_refs, fetched_refs))
+        ]
+        for part, lanes in enumerate(parts)
+    ]
+    flying = 2
+
+    def fetch(part):
+        if part < len(parts):
+            for copy in fetches[part]:
+                copy.start()
+
+    def ready(part):
+        for copy in fetches[part]:
+            copy.wait()
+        fetch(part + flying)
+
+    for part in range(flying):
+        fetch(part)
     squares, _ = totals_of(arrived_ref, plan.body, plan.message, plan.groups)
     inverse = 1.0 / scale_of(plan, squares)
     for piece in range(plan.pieces):
@@ -266,10 +293,9 @@
         squares.append(lane_sums(new * new))
         overlap.append(lane_sums(new * initial_ref[:, lanes]))
 
-    step(
-        plan, initial_ref, (*masked_refs, *fetched_refs), place_ref, inside_ref, rounded_ref, finish, fetches
-    )
-    put_sums(sums_ref, one_row(squares), one_row(overlap), 0, 1, plan.sites)
+    tables = (place_ref, inside_ref)
+    step(plan, initial_ref, (*masked_refs, *fetched_refs), *tables, rounded_ref, finish, kept, ready)
+    put_sums(sums_ref, one_row(squares), one_row(overlap), 0, 1, plan.groups)
 
 
 def one_row(rows):
@@ -277,28 +303,35 @@
     return sum(total[:, start : start + LANES] for start in range(0, total.shape[1], LANES))
 
 
-def place_block(plan, arrived_ref, out_ref, inverse, block):
-    parts = [
-        arrived_ref[pl.ds(piece * plan.lane_blocks + block, plan.groups, stride=plan.message), :]
-        for piece in range(plan.pieces)
-    ]
-    out_ref[pl.ds(block * LANES, LANES), :] = (jnp.concatenate(parts, axis=0) * inverse).T
-
-
-def relay_kernel(plan, arrived_ref, out_ref):
-    out_ref[...] = jnp.broadcast_to(lane_sums(arrived_ref[...]), out_ref.shape)
+def place(plan, arrived_ref, out_ref, turned_ref, semaphores, inverse):
+    copies = []
+    for block in range(plan.lane_blocks):
+        rows = pl.ds(block * LANES, LANES)
+        parts = [
+            arrived_ref[pl.ds(piece * plan.lane_blocks + block, plan.groups, stride=plan.message), :]
+            for piece in range(plan.pieces)
+        ]
+        turned_ref[rows, :] = (jnp.concatenate(parts, axis=0) * inverse).T
+        if block % 2:
+            half = block // 2
+            rows = pl.ds((block - 1) * LANES, 2 * LANES)
+            copy = pltpu.make_async_copy(turned_ref.at[rows, :], out_ref.at[rows, :], semaphores.at[half])
+            copy.start()
+            copies.append(copy)
+    return copies
 
 
 def later_kernel(plan, keep, arrived_ref, raw_ref, previous_ref, initial_ref, place_ref, inside_ref, *refs):
     masked_refs = refs[: plan.bits]
     if keep:
         current_ref, new_ref, out_ref, moment_ref, rounded_ref = refs[plan.bits :]
-        squares, overlap = totals_of(arrived_ref, 0, 1, plan.phonons)
+        squares, overlap = totals_of(arrived_ref, 0, 1, plan.groups)
     else:
-        out_ref, moment_ref, placed_ref, rounded_ref, current_ref = refs[plan.bits :]
+        out_ref, moment_ref, placed_ref, rounded_ref, current_ref, turned_ref, semaphores = refs[plan.bits :]
         squares, overlap = totals_of(arrived_ref, plan.body, plan.message, plan.groups)
     inverse = 1.0 / scale_of(plan, squares)
     moment_ref[...] = jnp.broadcast_to(overlap * inverse / plan.entries, moment_ref.shape)
+    copies = [] if keep else place(plan, arrived_ref, placed_ref, turned_ref, semaphores, inverse)
     for block in range(plan.lane_blocks):
         lanes = pl.ds(block * LANES, LANES)
         current_ref[:, lanes] = raw_ref[:, lanes] * inverse
@@ -313,31 +346,32 @@
         overlap.append(lane_sums(new * initial_ref[:, lanes]))
         for start in range(0, lanes.size, LANES):
             block = (lanes.start + start) // LANES
-            if not keep:
-                place_block(plan, arrived_ref, placed_ref, inverse, block)
             for piece in range(plan.pieces):
                 out_ref[pl.ds(piece * plan.lane_blocks + block, plan.groups, stride=plan.message), :] = new[
                     piece * plan.groups : (piece + 1) * plan.groups, start : start + LANES
                 ]
 
-    step(plan, current_ref, masked_refs, place_ref, inside_ref, rounded_ref, finish)
+    step(plan, current_ref, masked_refs, place_ref, inside_ref, rounded_ref, finish, plan.bits)
     put_sums(out_ref, one_row(squares), one_row(overlap), plan.body, plan.message, plan.groups)
-
-
-def arrive_kernel(plan, arrived_ref, first_ref, second_ref, out_ref, moments_ref):
+    for copy in copies:
+        copy.wait()
+
+
+def arrive_kernel(plan, arrived_ref, first_ref, second_ref, out_ref, moments_ref, turned_ref, semaphores):
     squares, overlap = totals_of(arrived_ref, plan.body, plan.message, plan.groups)
     inverse = 1.0 / scale_of(plan, squares)
+    copies = place(plan, arrived_ref, out_ref, turned_ref, semaphores, inverse)
     moment = overlap * inverse / plan.entries
     moments_ref[0] = first_ref[0, 0]
     moments_ref[1] = second_ref[0, 0]
     moments_ref[2] = moment[0, 0]
-    for block in range(plan.lane_blocks):
-        place_block(plan, arrived_ref, out_ref, inverse, block)
-
-
-def exchange(values, count, axes):
+    for copy in copies:
+        copy.wait()
+
+
+def exchange(values, count):
     shaped = values.reshape(count, values.shape[0] // count, 1, LANES)
-    return lax.all_to_all(shaped, axes, 0, 0, tiled=True).reshape(values.shape)
+    return lax.all_to_all(shaped, AXES, 0, 0, tiled=True).reshape(values.shape)
 
 
 def shards(plan, state, operators, op_mask, site_bits, field, site_coupling, mode_coupling):
@@ -347,6 +381,7 @@
     moment = jax.ShapeDtypeStruct((SUBLANES, LANES), f32)
     held = jax.ShapeDtypeStruct((plan.rows, plan.columns), f32)
     rounded = pltpu.VMEM((plan.places, plan.bits * plan.rows), jnp.bfloat16)
+    turned = [pltpu.VMEM((plan.rows, plan.columns), f32), pltpu.SemaphoreType.DMA((plan.lane_blocks // 2,))]
     working = pltpu.VMEM((plan.places, plan.rows), f32)
     work = 2 * plan.bits * plan.places * plan.rows * plan.rows
 
@@ -356,12 +391,13 @@
     departing = pl.pallas_call(
         functools.partial(depart_kernel, plan),
         out_shape=message,
-        in_specs=[VMEM],
+        in_specs=[HBM],
         out_specs=VMEM,
-        compiler_params=params(16),
+        scratch_shapes=[pltpu.VMEM((plan.rows, plan.columns), f32), pltpu.SemaphoreType.DMA((2,))],
+        compiler_params=params(60),
         name="depart",
     )(state)
-    arrived = exchange(departing, plan.groups, AXES)
+    arrived = exchange(departing, plan.groups)
     operator = jax.ShapeDtypeStruct((plan.rows, plan.rows), jnp.bfloat16)
     kept = 1
     fetched = plan.bits - kept
@@ -399,7 +435,7 @@
     )(site_bits, op_mask, operators)
     initial, raw, sums, *fetched_masked = pl.pallas_call(
         functools.partial(first_kernel, plan, kept),
-        out_shape=[vector, vector, jax.ShapeDtypeStruct((plan.sites, LANES), f32)] + [operator] * fetched,
+        out_shape=[vector, vector, jax.ShapeDtypeStruct((plan.groups, LANES), f32)] + [operator] * fetched,
         in_specs=[VMEM] * 4 + [HBM] * fetched,
         out_specs=[VMEM] * (3 + fetched),
         scratch_shapes=[rounded, pltpu.SemaphoreType.DMA((fetched, len(parts_of(plan))))],
@@ -408,16 +444,7 @@
         name="first",
     )(arrived, place, inside, *masked, *stored)
     tables = (place, inside, *masked, *fetched_masked)
-    sums = exchange(sums, plan.sites, "site")
-    sums = pl.pallas_call(
-        functools.partial(relay_kernel, plan),
-        out_shape=jax.ShapeDtypeStruct((plan.phonons, LANES), f32),
-        in_specs=[VMEM],
-        out_specs=VMEM,
-        compiler_params=params(4),
-        name="relay",
-    )(sums)
-    sums = exchange(sums, plan.phonons, "phonon")
+    sums = exchange(sums, plan.groups)
     current, raw, departing, moment_one = pl.pallas_call(
         functools.partial(later_kernel, plan, True),
         out_shape=[vector, vector, message, moment],
@@ -428,23 +455,24 @@
         cost_estimate=cost(work, 4 * plan.places * plan.rows),
         name="second",
     )(sums, raw, initial, initial, *tables)
-    before = exchange(departing, plan.groups, AXES)
+    before = exchange(departing, plan.groups)
     departing, moment_two, before = pl.pallas_call(
         functools.partial(later_kernel, plan, False),
         out_shape=[message, moment, held],
         in_specs=[VMEM] * (6 + plan.bits),
-        out_specs=[VMEM] * 3,
-        scratch_shapes=[rounded, working],
+        out_specs=[VMEM, VMEM, HBM],
+        scratch_shapes=[rounded, working, *turned],
         compiler_params=params(32),
         cost_estimate=cost(work, 4 * plan.places * plan.rows),
         name="third",
     )(before, raw, current, initial, *tables)
-    last = exchange(departing, plan.groups, AXES)
+    last = exchange(departing, plan.groups)
     last, moments = pl.pallas_call(
         functools.partial(arrive_kernel, plan),
         out_shape=[held, jax.ShapeDtypeStruct((STEPS,), f32)],
         in_specs=[VMEM] * 3,
-        out_specs=[VMEM, SMEM],
+        out_specs=[HBM, SMEM],
+        scratch_shapes=turned,
         compiler_params=params(16),
         name="arrive_last",
     )(last, moment_one, moment_two)

time: 86.3 us -> 81.3 us (0.942)
  blocking collectives: 51.9 us -> 46.3 us
  Pallas kernels: 17.6 us -> 19.1 us
  local copies, waits for them, and re-layouts: 1.07 us -> 0.03 us
    all_to_all x4 -> x3, blocking collectives: 51.9 us -> 46.3 us  [exchange(): return lax.all_to_all(shaped, AXES, 0, 0, tiled=True).reshape(values.shape)]
    unnamed x12 -> x10, local copies, waits for them, and re-layouts: 1.07 us -> 0.03 us
    pallas_call x1, Pallas kernels: 1.09 us -> 2.09 us  [shards(): pl.pallas_call(functools.partial(depart_kernel, plan), out_shape=message,...]
where the time goes in v9:
time: 81.3 us; the launch traced here: 80.8 us
  blocking collectives  46.3 us (57%)
  Pallas kernels  19.1 us (23%)
  waiting for transfers between devices  7.31 us (9%)
  starting transfers between devices  7.3 us (9%)
    all_to_all x3, blocking collectives, exchange(): return lax.all_to_all(shaped, AXES, 0, 0, tiled=True).reshape(values.shape)  46.3 us
    all_to_all x1, waiting for transfers between devices, exchange(): return lax.all_to_all(shaped, AXES, 0, 0, tiled=True).reshape(values.shape)  7.31 us
    all_to_all x1, starting transfers between devices, exchange(): return lax.all_to_all(shaped, AXES, 0, 0, tiled=True).reshape(values.shape)  7.3 us
    pallas_call x1, Pallas kernels, shards(): pl.pallas_call(functools.partial(store_kernel, plan, kept), out_shape=[op...  5.34 us
    pallas_call x1, Pallas kernels, shards(): pl.pallas_call(functools.partial(first_kernel, plan, kept), out_shape=[ve...  3.6 us
    pallas_call x1, Pallas kernels, shards(): pl.pallas_call(functools.partial(prepare_kernel, plan, kept), out_shape=[...  3.07 us
    pallas_call x1, Pallas kernels, shards(): pl.pallas_call(functools.partial(later_kernel, plan, False), out_shape=[m...  2.1 us
    pallas_call x1, Pallas kernels, shards(): pl.pallas_call(functools.partial(depart_kernel, plan), out_shape=message,...  2.09 us
  transfers between devices with their start and end apart: 1, of which 1 were waited for; matrix products, arithmetic and copies ran while one was open for 0% of the time, Pallas kernels for 10%

profile of v9, /device:TPU:0, one launch (start us, length us, event | category | flops | bytes accessed | tf_op | source)
XLA Modules:
  0.0 80.8 jit_solution(9261012775846102912)
XLA Ops:
  0.6 2.1 %depart.1 = f32[1056,128]{1,0:T(8,128)} custom-call(f32[1024,128]{1,0:T(8,128)} %state_ref.1), custom_call_target="tpu_custom_call" | custom-call | tf_op jit(solution)/shard_map/depart/pallas_call | solution.py:391
  2.7 7.3 %all-to-all-start = ((f32[32,33,1,128]{3,2,1,0:T(1,128)}), f32[32,33,1,128]{3,2,1,0:T(1,128)S(1)}, u32[]{:S(2)}, u32[]{:S(2)}) async-start(f32[32,33,1,128]{3,2,1,0:T(1,128)} %bitcast.17), calls=%async_computation | async-start | bytes 1081344 | tf_op jit(solution)/shard_map/all_to_all | solution.py:374
  10.0 0.0 copy-start
  10.1 0.0 copy-start.1
  10.1 0.0 copy-start.2
  10.1 0.0 copy-start.3
  10.1 0.0 copy-start.4
  10.1 5.3 %store.1 = (bf16[1024,1024]{1,0:T(8,128)(2,1)}, bf16[1024,1024]{1,0:T(8,128)(2,1)}) custom-call(s32[3]{0:T(128)} %bits_ref.3, s32[3,8,8]{2,1,0:T(8,128)} %mask_ref.3, bf16[3,1024,1024]{2,1,0:T(8,128)(2,1)} %operators_ref.3), custom_call_target="tpu_custom_call" | custom-call | flops 1048576 | bytes 8388608 | tf_op jit(solution)/shard_map/store/pallas_call | solution.py:421
  15.4 0.0 copy-done
  15.5 0.0 copy-done.1
  15.5 0.0 copy-done.2
  15.5 0.0 copy-done.3
  15.5 0.0 copy-done.4
  15.5 3.1 %prepare.1 = (f32[6,128,128]{2,1,0:T(8,128)S(1)}, f32[8,1024]{1,0:T(8,128)S(1)}, bf16[1024,1024]{1,0:T(8,128)(2,1)S(1)}) custom-call(s32[3]{0:T(128)S(1)} %copy-done.1, s32[3,8,8]{2,1,0:T(8,128)S(1)} %copy-done, f32[3]{0:T(128)S(1)} %copy-done.2, f32[13]{0:T(128)S(1)} %copy-done.3, f32[64]{0:T(128)S(1)} %copy-done.4, bf16[3,1024,1024]{2,1,0:T(8,128)(2,1)} %operators_ref.3), custom_call_target="tpu_custom_call" | custom-call | flops 1048576 | bytes 4194304 | tf_op jit(solution)/shard_map/prepare/pallas_call | solution.py:404
  18.6 7.3 %all-to-all-done = f32[32,33,1,128]{3,2,1,0:T(1,128)S(1)} async-done(((f32[32,33,1,128]{3,2,1,0:T(1,128)}), f32[32,33,1,128]{3,2,1,0:T(1,128)S(1)}, u32[]{:S(2)}, u32[]{:S(2)}) %all-to-all-start) | async-done | bytes 540704 | tf_op jit(solution)/shard_map/all_to_all | solution.py:374
  25.9 3.6 %first.1 = (f32[128,1024]{1,0:T(8,128)S(1)}, f32[128,1024]{1,0:T(8,128)S(1)}, f32[32,128]{1,0:T(8,128)S(1)}, bf16[1024,1024]{1,0:T(8,128)(2,1)S(1)}, bf16[1024,1024]{1,0:T(8,128)(2,1)S(1)}) custom-call(f32[1056,128]{1,0:T(8,128)S(1)} %bitcast.10, f32[6,128,128]{2,1,0:T(8,128)S(1)} %get-tuple-element.22.place_ref, ...), custom_call_target="tpu_custom_call" | custom-call | flops 805306368 | bytes 524288 | tf_op jit(solution)/shard_map/first/pallas_call | solution.py:436
  29.5 10.1 %all_to_all.20 = f32[32,1,1,128]{3,2,1,0:T(1,128)S(1)} all-to-all(f32[32,1,1,128]{3,2,1,0:T(1,128)S(1)} %bitcast.16), channel_id=1, replica_groups=mesh['site'=8,'phonon'=4] {'site','phonon'}, dimensions={0} | all-to-all | bytes 32768 | tf_op jit(solution)/shard_map/all_to_all | solution.py:374
  39.6 1.4 %second.1 = (f32[128,1024]{1,0:T(8,128)S(1)}, f32[128,1024]{1,0:T(8,128)S(1)}, f32[1056,128]{1,0:T(8,128)S(1)}, f32[8,128]{1,0:T(8,128)S(1)}) custom-call(f32[32,128]{1,0:T(8,128)S(1)} %bitcast.15, f32[128,1024]{1,0:T(8,128)S(1)} %get-tuple-element.28.raw_ref, f32[128,1024]{1,0:T(8,128)S(1)} %get-tuple-element.29.previous_ref.initial_ref, ...), custom_call_target="tpu_custom_call" | custom-call | flops 805306368 | bytes 524288 | tf_op jit(solution)/shard_map/second/pallas_call | solution.py:448
  40.9 17.6 %all_to_all.21 = f32[32,33,1,128]{3,2,1,0:T(1,128)S(1)} all-to-all(f32[32,33,1,128]{3,2,1,0:T(1,128)S(1)} %bitcast.14), channel_id=1, replica_groups=mesh['site'=8,'phonon'=4] {'site','phonon'}, dimensions={0} | all-to-all | bytes 1081344 | tf_op jit(solution)/shard_map/all_to_all | solution.py:374
  58.5 2.1 %third.1 = (f32[1056,128]{1,0:T(8,128)S(1)}, f32[8,128]{1,0:T(8,128)S(1)}, f32[1024,128]{1,0:T(8,128)}) custom-call(f32[1056,128]{1,0:T(8,128)S(1)} %bitcast.11, f32[128,1024]{1,0:T(8,128)S(1)} %get-tuple-element.33.raw_ref, f32[128,1024]{1,0:T(8,128)S(1)} %get-tuple-element.34.previous_ref, f32[128,1024]{1,0:T(8,128)S(1)} %get-tuple-element.29.previous_ref.initial_ref, ...), custom_call_target="tpu_custom_call" | custom-call | flops 805306368 | bytes 524288 | tf_op jit(solution)/shard_map/third/pallas_call | solution.py:459
  60.6 18.7 %all_to_all.22 = f32[32,33,1,128]{3,2,1,0:T(1,128)S(1)} all-to-all(f32[32,33,1,128]{3,2,1,0:T(1,128)S(1)} %bitcast.13), channel_id=1, replica_groups=mesh['site'=8,'phonon'=4] {'site','phonon'}, dimensions={0} | all-to-all | bytes 1081344 | tf_op jit(solution)/shard_map/all_to_all | solution.py:374
  79.3 1.5 %arrive_last.1 = (f32[1024,128]{1,0:T(8,128)}, f32[3]{0:T(128)}) custom-call(f32[1056,128]{1,0:T(8,128)S(1)} %bitcast.12, f32[8,128]{1,0:T(8,128)S(1)} %get-tuple-element.36.first_ref, f32[8,128]{1,0:T(8,128)S(1)} %get-tuple-element.37.second_ref), custom_call_target="tpu_custom_call" | custom-call | tf_op jit(solution)/shard_map/arrive_last/pallas_call | solution.py:470
Async XLA Ops:
  2.7 23.2 %all-to-all-start = ((f32[32,33,1,128]{3,2,1,0:T(1,128)}), f32[32,33,1,128]{3,2,1,0:T(1,128)S(1)}, u32[]{:S(2)}, u32[]{:S(2)}) async-start(f32[32,33,1,128]{3,2,1,0:T(1,128)} %bitcast.17), calls=%async_computation | async-start | bytes 1081344 | tf_op jit(solution)/shard_map/all_to_all | solution.py:374
  10.0 5.4 %copy-start = (s32[3,8,8]{2,1,0:T(8,128)S(1)}, s32[3,8,8]{2,1,0:T(8,128)}, u32[]{:S(2)}) copy-start(s32[3,8,8]{2,1,0:T(8,128)} %mask_ref.3) | copy-start | bytes 2308
  10.1 5.4 %copy-start.1 = (s32[3]{0:T(128)S(1)}, s32[3]{0:T(128)}, u32[]{:S(2)}) copy-start(s32[3]{0:T(128)} %bits_ref.3) | copy-start | bytes 40
  10.1 5.4 %copy-start.2 = (f32[3]{0:T(128)S(1)}, f32[3]{0:T(128)}, u32[]{:S(2)}) copy-start(f32[3]{0:T(128)} %field_ref.1) | copy-start | bytes 40
  10.1 5.4 %copy-start.3 = (f32[13]{0:T(128)S(1)}, f32[13]{0:T(128)}, u32[]{:S(2)}) copy-start(f32[13]{0:T(128)} %coupling_ref.1) | copy-start | bytes 160
  10.1 5.4 %copy-start.4 = (f32[64]{0:T(128)S(1)}, f32[64]{0:T(128)}, u32[]{:S(2)}) copy-start(f32[64]{0:T(128)} %mode_ref.1) | copy-start | bytes 772

commit v10 on v9

--- a/solution.py
+++ b/solution.py
@@ -41,14 +41,17 @@
         self.body = self.pieces * self.lane_blocks
         self.message = self.body + EXTRA
         self.places = self.pieces * self.groups
+        self.width = 2 * LANES
+        self.parts = rows // self.width
         self.entries = float(rows * columns * self.groups)
 
     def fits(self):
         return (
             MODES % self.groups == 0
             and self.columns == LANES
-            and self.rows % (2 * LANES) == 0
+            and self.rows % self.width == 0
             and self.edge % LANES == 0
+            and self.width % self.edge == 0
             and self.groups % SUBLANES == 0
         )
 
@@ -113,7 +116,8 @@
         for along in range(plan.blocks):
             columns = pl.ds(along * plan.edge, plan.edge)
             keep = (mask_ref[chosen, across, along] > 0).astype(jnp.float32).astype(jnp.bfloat16)
-            out_ref[columns, rows] = (held_ref[rows, columns] * keep).T
+            part, start = divmod(across * plan.edge, plan.width)
+            out_ref[part, columns, pl.ds(start, plan.edge)] = (held_ref[rows, columns] * keep).T
 
 
 def store_kernel(plan, kept, bits_ref, mask_ref, operators_ref, *refs):
@@ -206,7 +210,7 @@
     return pltpu.roll(tiles, by % SUBLANES, 1).reshape(places, width)
 
 
-def step(plan, vector_ref, masked_refs, place_ref, inside_ref, rounded_ref, finish, kept, ready=None):
+def step(plan, vector_ref, masked_refs, place_ref, inside_ref, rounded_ref, finish, kept, ready=None, begun_ref=None):
     span = plan.places // plan.levels_here
     for block in range(plan.lane_blocks):
         vector = vector_ref[:, pl.ds(block * LANES, LANES)]
@@ -227,28 +231,32 @@
             total = total + place_ref[3 + position, :1] * flipped(vector, plan.phonons << position)
         return total
 
-    def product(lanes, position):
+    def product(part, position):
         return jnp.dot(
             rounded_ref[:, pl.ds(position * plan.rows, plan.rows)],
-            masked_refs[position][:, lanes],
+            masked_refs[position][part],
             preferred_element_type=jnp.float32,
         )
 
-    for index, lanes in enumerate(parts_of(plan)):
-        total = jnp.concatenate(
-            [local(start) for start in range(lanes.start, lanes.start + lanes.size, LANES)], axis=1
-        )
+    def begun(lanes, part):
+        total = jnp.concatenate([local(start) for start in range(lanes.start, lanes.start + plan.width, LANES)], axis=1)
         for position in range(kept):
-            total = total + product(lanes, position)
-        if ready:
-            ready(index)
+            total = total + product(part, position)
+        return total
+
+    parts = [pl.ds(part * plan.width, plan.width) for part in range(plan.parts)]
+    if ready is None:
+        for part, lanes in enumerate(parts):
+            finish(lanes, begun(lanes, part))
+        return
+    for part, lanes in enumerate(parts):
+        begun_ref[:, lanes] = begun(lanes, part)
+    for part, lanes in enumerate(parts):
+        total = begun_ref[:, lanes]
         for position in range(kept, plan.bits):
-            total = total + product(lanes, position)
+            ready(part, position)
+            total = total + product(part, position)
         finish(lanes, total)
-
-
-def parts_of(plan):
-    return [pl.ds(start, 2 * LANES) for start in range(0, plan.rows, 2 * LANES)]
 
 
 def first_kernel(plan, kept, arrived_ref, place_ref, inside_ref, *refs):
@@ -257,28 +265,16 @@
     initial_ref, new_ref, sums_ref = refs[plan.bits : plan.bits + 3]
     fetched_refs = refs[plan.bits + 3 : -2]
     rounded_ref, semaphores = refs[-2:]
-    parts = parts_of(plan)
-    fetches = [
-        [
-            pltpu.make_async_copy(stored_ref.at[:, lanes], fetched_ref.at[:, lanes], semaphores.at[index, part])
-            for index, (stored_ref, fetched_ref) in enumerate(zip(stored_refs, fetched_refs))
-        ]
-        for part, lanes in enumerate(parts)
-    ]
-    flying = 2
-
-    def fetch(part):
-        if part < len(parts):
-            for copy in fetches[part]:
-                copy.start()
-
-    def ready(part):
-        for copy in fetches[part]:
-            copy.wait()
-        fetch(part + flying)
-
-    for part in range(flying):
-        fetch(part)
+    fetches = {}
+    for part in range(plan.parts):
+        for index, (stored_ref, fetched_ref) in enumerate(zip(stored_refs, fetched_refs)):
+            fetch = pltpu.make_async_copy(stored_ref.at[part], fetched_ref.at[part], semaphores.at[index, part])
+            fetch.start()
+            fetches[part, kept + index] = fetch
+
+    def ready(part, position):
+        fetches[part, position].wait()
+
     squares, _ = totals_of(arrived_ref, plan.body, plan.message, plan.groups)
     inverse = 1.0 / scale_of(plan, squares)
     for piece in range(plan.pieces):
@@ -294,7 +290,7 @@
         overlap.append(lane_sums(new * initial_ref[:, lanes]))
 
     tables = (place_ref, inside_ref)
-    step(plan, initial_ref, (*masked_refs, *fetched_refs), *tables, rounded_ref, finish, kept, ready)
+    step(plan, initial_ref, (*masked_refs, *fetched_refs), *tables, rounded_ref, finish, kept, ready, new_ref)
     put_sums(sums_ref, one_row(squares), one_row(overlap), 0, 1, plan.groups)
 
 
@@ -303,22 +299,16 @@
     return sum(total[:, start : start + LANES] for start in range(0, total.shape[1], LANES))
 
 
-def place(plan, arrived_ref, out_ref, turned_ref, semaphores, inverse):
-    copies = []
+def place(plan, arrived_ref, out_ref):
+    squares, overlap = totals_of(arrived_ref, plan.body, plan.message, plan.groups)
+    inverse = 1.0 / scale_of(plan, squares)
     for block in range(plan.lane_blocks):
-        rows = pl.ds(block * LANES, LANES)
         parts = [
             arrived_ref[pl.ds(piece * plan.lane_blocks + block, plan.groups, stride=plan.message), :]
             for piece in range(plan.pieces)
         ]
-        turned_ref[rows, :] = (jnp.concatenate(parts, axis=0) * inverse).T
-        if block % 2:
-            half = block // 2
-            rows = pl.ds((block - 1) * LANES, 2 * LANES)
-            copy = pltpu.make_async_copy(turned_ref.at[rows, :], out_ref.at[rows, :], semaphores.at[half])
-            copy.start()
-            copies.append(copy)
-    return copies
+        out_ref[pl.ds(block * LANES, LANES), :] = (jnp.concatenate(parts, axis=0) * inverse).T
+    return overlap * inverse / plan.entries
 
 
 def later_kernel(plan, keep, arrived_ref, raw_ref, previous_ref, initial_ref, place_ref, inside_ref, *refs):
@@ -327,11 +317,11 @@
         current_ref, new_ref, out_ref, moment_ref, rounded_ref = refs[plan.bits :]
         squares, overlap = totals_of(arrived_ref, 0, 1, plan.groups)
     else:
-        out_ref, moment_ref, placed_ref, rounded_ref, current_ref, turned_ref, semaphores = refs[plan.bits :]
+        out_ref, rounded_ref, current_ref = refs[plan.bits :]
         squares, overlap = totals_of(arrived_ref, plan.body, plan.message, plan.groups)
     inverse = 1.0 / scale_of(plan, squares)
-    moment_ref[...] = jnp.broadcast_to(overlap * inverse / plan.entries, moment_ref.shape)
-    copies = [] if keep else place(plan, arrived_ref, placed_ref, turned_ref, semaphores, inverse)
+    if keep:
+        moment_ref[...] = jnp.broadcast_to(overlap * inverse / plan.entries, moment_ref.shape)
     for block in range(plan.lane_blocks):
         lanes = pl.ds(block * LANES, LANES)
         current_ref[:, lanes] = raw_ref[:, lanes] * inverse
@@ -353,20 +343,14 @@
 
     step(plan, current_ref, masked_refs, place_ref, inside_ref, rounded_ref, finish, plan.bits)
     put_sums(out_ref, one_row(squares), one_row(overlap), plan.body, plan.message, plan.groups)
-    for copy in copies:
-        copy.wait()
-
-
-def arrive_kernel(plan, arrived_ref, first_ref, second_ref, out_ref, moments_ref, turned_ref, semaphores):
-    squares, overlap = totals_of(arrived_ref, plan.body, plan.message, plan.groups)
-    inverse = 1.0 / scale_of(plan, squares)
-    copies = place(plan, arrived_ref, out_ref, turned_ref, semaphores, inverse)
-    moment = overlap * inverse / plan.entries
-    moments_ref[0] = first_ref[0, 0]
-    moments_ref[1] = second_ref[0, 0]
-    moments_ref[2] = moment[0, 0]
-    for copy in copies:
-        copy.wait()
+
+
+def arrive_kernel(plan, before_ref, last_ref, moment_ref, before_out_ref, last_out_ref, moments_ref):
+    second = place(plan, before_ref, before_out_ref)
+    third = place(plan, last_ref, last_out_ref)
+    moments_ref[0] = moment_ref[0, 0]
+    moments_ref[1] = second[0, 0]
+    moments_ref[2] = third[0, 0]
 
 
 def exchange(values, count):
@@ -381,7 +365,6 @@
     moment = jax.ShapeDtypeStruct((SUBLANES, LANES), f32)
     held = jax.ShapeDtypeStruct((plan.rows, plan.columns), f32)
     rounded = pltpu.VMEM((plan.places, plan.bits * plan.rows), jnp.bfloat16)
-    turned = [pltpu.VMEM((plan.rows, plan.columns), f32), pltpu.SemaphoreType.DMA((plan.lane_blocks // 2,))]
     working = pltpu.VMEM((plan.places, plan.rows), f32)
     work = 2 * plan.bits * plan.places * plan.rows * plan.rows
 
@@ -398,7 +381,7 @@
         name="depart",
     )(state)
     arrived = exchange(departing, plan.groups)
-    operator = jax.ShapeDtypeStruct((plan.rows, plan.rows), jnp.bfloat16)
+    operator = jax.ShapeDtypeStruct((plan.parts, plan.rows, plan.width), jnp.bfloat16)
     kept = 1
     fetched = plan.bits - kept
     place, inside, *masked = pl.pallas_call(
@@ -425,7 +408,7 @@
         out_specs=[HBM] * fetched,
         scratch_shapes=[
             pltpu.VMEM((fetched, plan.rows, plan.rows), jnp.bfloat16),
-            pltpu.VMEM((fetched, plan.rows, plan.rows), jnp.bfloat16),
+            pltpu.VMEM((fetched, *operator.shape), jnp.bfloat16),
             pltpu.SemaphoreType.DMA((fetched,)),
             pltpu.SemaphoreType.DMA((fetched,)),
         ],
@@ -438,7 +421,7 @@
         out_shape=[vector, vector, jax.ShapeDtypeStruct((plan.groups, LANES), f32)] + [operator] * fetched,
         in_specs=[VMEM] * 4 + [HBM] * fetched,
         out_specs=[VMEM] * (3 + fetched),
-        scratch_shapes=[rounded, pltpu.SemaphoreType.DMA((fetched, len(parts_of(plan))))],
+        scratch_shapes=[rounded, pltpu.SemaphoreType.DMA((fetched, plan.parts))],
         compiler_params=params(46),
         cost_estimate=cost(work, 4 * plan.places * plan.rows),
         name="first",
@@ -456,26 +439,25 @@
         name="second",
     )(sums, raw, initial, initial, *tables)
     before = exchange(departing, plan.groups)
-    departing, moment_two, before = pl.pallas_call(
+    departing = pl.pallas_call(
         functools.partial(later_kernel, plan, False),
-        out_shape=[message, moment, held],
+        out_shape=message,
         in_specs=[VMEM] * (6 + plan.bits),
-        out_specs=[VMEM, VMEM, HBM],
-        scratch_shapes=[rounded, working, *turned],
+        out_specs=VMEM,
+        scratch_shapes=[rounded, working],
         compiler_params=params(32),
         cost_estimate=cost(work, 4 * plan.places * plan.rows),
         name="third",
     )(before, raw, current, initial, *tables)
     last = exchange(departing, plan.groups)
-    last, moments = pl.pallas_call(
+    before, last, moments = pl.pallas_call(
         functools.partial(arrive_kernel, plan),
-        out_shape=[held, jax.ShapeDtypeStruct((STEPS,), f32)],
+        out_shape=[held, held, jax.ShapeDtypeStruct((STEPS,), f32)],
         in_specs=[VMEM] * 3,
-        out_specs=[HBM, SMEM],
-        scratch_shapes=turned,
+        out_specs=[VMEM, VMEM, SMEM],
         compiler_params=params(16),
-        name="arrive_last",
-    )(last, moment_one, moment_two)
+        name="arrive",
+    )(before, last, moment_one)
     return last, before, moments
 
 

time: 81.3 us -> 79.6 us (0.979)
  Pallas kernels: 19.1 us -> 17.3 us
    pallas_call x2, Pallas kernels: 3.65 us -> 2.67 us  [the longest x1 1.35 us: shards(): pl.pallas_call(functools.partial(later_kernel, plan, False), out_shape=me...]
where the time goes in v10:
time: 79.6 us; the launch traced here: 79.3 us
  blocking collectives  46.3 us (58%)
  Pallas kernels  17.3 us (22%)
  waiting for transfers between devices  7.56 us (9%)
  starting transfers between devices  7.3 us (9%)
    all_to_all x3, blocking collectives, exchange(): return lax.all_to_all(shaped, AXES, 0, 0, tiled=True).reshape(values.shape)  46.3 us
    all_to_all x1, waiting for transfers between devices, exchange(): return lax.all_to_all(shaped, AXES, 0, 0, tiled=True).reshape(values.shape)  7.56 us
    all_to_all x1, starting transfers between devices, exchange(): return lax.all_to_all(shaped, AXES, 0, 0, tiled=True).reshape(values.shape)  7.3 us
    pallas_call x1, Pallas kernels, shards(): pl.pallas_call(functools.partial(store_kernel, plan, kept), out_shape=[op...  5.18 us
    pallas_call x1, Pallas kernels, shards(): pl.pallas_call(functools.partial(first_kernel, plan, kept), out_shape=[ve...  3.05 us
    pallas_call x1, Pallas kernels, shards(): pl.pallas_call(functools.partial(prepare_kernel, plan, kept), out_shape=[...  2.97 us
    pallas_call x1, Pallas kernels, shards(): pl.pallas_call(functools.partial(depart_kernel, plan), out_shape=message,...  2.09 us
  transfers between devices with their start and end apart: 1, of which 1 were waited for; matrix products, arithmetic and copies ran while one was open for 0% of the time, Pallas kernels for 10%

profile of v10, /device:TPU:0, one launch (start us, length us, event | category | flops | bytes accessed | tf_op | source)
XLA Modules:
  0.0 79.3 jit_solution(18249791041839904136)
XLA Ops:
  0.6 2.1 %depart.1 = f32[1056,128]{1,0:T(8,128)} custom-call(f32[1024,128]{1,0:T(8,128)} %state_ref.1), custom_call_target="tpu_custom_call" | custom-call | tf_op jit(solution)/shard_map/depart/pallas_call | solution.py:374
  2.7 7.3 %all-to-all-start = ((f32[32,33,1,128]{3,2,1,0:T(1,128)}), f32[32,33,1,128]{3,2,1,0:T(1,128)S(1)}, u32[]{:S(2)}, u32[]{:S(2)}) async-start(f32[32,33,1,128]{3,2,1,0:T(1,128)} %bitcast.18), calls=%async_computation | async-start | bytes 1081344 | tf_op jit(solution)/shard_map/all_to_all | solution.py:358
  10.0 0.0 copy-start
  10.1 0.0 copy-start.1
  10.1 0.0 copy-start.2
  10.1 0.0 copy-start.3
  10.1 0.0 copy-start.4
  10.1 5.2 %store.1 = (bf16[4,1024,256]{2,1,0:T(8,128)(2,1)}, bf16[4,1024,256]{2,1,0:T(8,128)(2,1)}) custom-call(s32[3]{0:T(128)} %bits_ref.3, s32[3,8,8]{2,1,0:T(8,128)} %mask_ref.3, bf16[3,1024,1024]{2,1,0:T(8,128)(2,1)} %operators_ref.3), custom_call_target="tpu_custom_call" | custom-call | flops 1048576 | bytes 8388608 | tf_op jit(solution)/shard_map/store/pallas_call | solution.py:404
  15.3 0.0 copy-done
  15.3 0.0 copy-done.1
  15.3 0.0 copy-done.2
  15.3 0.0 copy-done.3
  15.3 0.0 copy-done.4
  15.3 3.0 %prepare.1 = (f32[6,128,128]{2,1,0:T(8,128)S(1)}, f32[8,1024]{1,0:T(8,128)S(1)}, bf16[4,1024,256]{2,1,0:T(8,128)(2,1)S(1)}) custom-call(s32[3]{0:T(128)S(1)} %copy-done.1, s32[3,8,8]{2,1,0:T(8,128)S(1)} %copy-done, f32[3]{0:T(128)S(1)} %copy-done.2, f32[13]{0:T(128)S(1)} %copy-done.3, f32[64]{0:T(128)S(1)} %copy-done.4, bf16[3,1024,1024]{2,1,0:T(8,128)(2,1)} %operators_ref.3), custom_call_target="tpu_custom_call" | custom-call | flops 1048576 | bytes 4194304 | tf_op jit(solution)/shard_map/prepare/pallas_call | solution.py:387
  18.3 7.6 %all-to-all-done = f32[32,33,1,128]{3,2,1,0:T(1,128)S(1)} async-done(((f32[32,33,1,128]{3,2,1,0:T(1,128)}), f32[32,33,1,128]{3,2,1,0:T(1,128)S(1)}, u32[]{:S(2)}, u32[]{:S(2)}) %all-to-all-start) | async-done | bytes 540704 | tf_op jit(solution)/shard_map/all_to_all | solution.py:358
  25.9 3.0 %first.1 = (f32[128,1024]{1,0:T(8,128)S(1)}, f32[128,1024]{1,0:T(8,128)S(1)}, f32[32,128]{1,0:T(8,128)S(1)}, bf16[4,1024,256]{2,1,0:T(8,128)(2,1)S(1)}, bf16[4,1024,256]{2,1,0:T(8,128)(2,1)S(1)}) custom-call(f32[1056,128]{1,0:T(8,128)S(1)} %bitcast.12, f32[6,128,128]{2,1,0:T(8,128)S(1)} %get-tuple-element.20.place_ref, ...), custom_call_target="tpu_custom_call" | custom-call | flops 805306368 | bytes 524288 | tf_op jit(solution)/shard_map/first/pallas_call | solution.py:419
  28.9 10.1 %all_to_all.20 = f32[32,1,1,128]{3,2,1,0:T(1,128)S(1)} all-to-all(f32[32,1,1,128]{3,2,1,0:T(1,128)S(1)} %bitcast.17), channel_id=1, replica_groups=mesh['site'=8,'phonon'=4] {'site','phonon'}, dimensions={0} | all-to-all | bytes 32768 | tf_op jit(solution)/shard_map/all_to_all | solution.py:358
  39.0 1.3 %second.1 = (f32[128,1024]{1,0:T(8,128)S(1)}, f32[128,1024]{1,0:T(8,128)S(1)}, f32[1056,128]{1,0:T(8,128)S(1)}, f32[8,128]{1,0:T(8,128)S(1)}) custom-call(f32[32,128]{1,0:T(8,128)S(1)} %bitcast.16, f32[128,1024]{1,0:T(8,128)S(1)} %get-tuple-element.26.raw_ref, f32[128,1024]{1,0:T(8,128)S(1)} %get-tuple-element.27.previous_ref.initial_ref, ...), custom_call_target="tpu_custom_call" | custom-call | flops 805306368 | bytes 524288 | tf_op jit(solution)/shard_map/second/pallas_call | solution.py:431
  40.4 17.6 %all_to_all.21 = f32[32,33,1,128]{3,2,1,0:T(1,128)S(1)} all-to-all(f32[32,33,1,128]{3,2,1,0:T(1,128)S(1)} %bitcast.15), channel_id=1, replica_groups=mesh['site'=8,'phonon'=4] {'site','phonon'}, dimensions={0} | all-to-all | bytes 1081344 | tf_op jit(solution)/shard_map/all_to_all | solution.py:358
  57.9 1.3 %third.1 = f32[1056,128]{1,0:T(8,128)S(1)} custom-call(f32[1056,128]{1,0:T(8,128)S(1)} %bitcast.10, f32[128,1024]{1,0:T(8,128)S(1)} %get-tuple-element.31.raw_ref, f32[128,1024]{1,0:T(8,128)S(1)} %get-tuple-element.32.previous_ref, f32[128,1024]{1,0:T(8,128)S(1)} %get-tuple-element.27.previous_ref.initial_ref, ...), custom_call_target="tpu_custom_call" | custom-call | flops 805306368 | bytes 524288 | tf_op jit(solution)/shard_map/third/pallas_call | solution.py:442
  59.3 18.7 %all_to_all.22 = f32[32,33,1,128]{3,2,1,0:T(1,128)S(1)} all-to-all(f32[32,33,1,128]{3,2,1,0:T(1,128)S(1)} %bitcast.13), channel_id=1, replica_groups=mesh['site'=8,'phonon'=4] {'site','phonon'}, dimensions={0} | all-to-all | bytes 1081344 | tf_op jit(solution)/shard_map/all_to_all | solution.py:358
  77.9 1.3 %arrive.1 = (f32[1024,128]{1,0:T(8,128)}, f32[1024,128]{1,0:T(8,128)}, f32[3]{0:T(128)}) custom-call(f32[1056,128]{1,0:T(8,128)S(1)} %bitcast.11, f32[1056,128]{1,0:T(8,128)S(1)} %bitcast.14, f32[8,128]{1,0:T(8,128)S(1)} %get-tuple-element.33.moment_ref), custom_call_target="tpu_custom_call" | custom-call | tf_op jit(solution)/shard_map/arrive/pallas_call | solution.py:453
Async XLA Ops:
  2.7 23.2 %all-to-all-start = ((f32[32,33,1,128]{3,2,1,0:T(1,128)}), f32[32,33,1,128]{3,2,1,0:T(1,128)S(1)}, u32[]{:S(2)}, u32[]{:S(2)}) async-start(f32[32,33,1,128]{3,2,1,0:T(1,128)} %bitcast.18), calls=%async_computation | async-start | bytes 1081344 | tf_op jit(solution)/shard_map/all_to_all | solution.py:358
  10.0 5.3 %copy-start = (s32[3,8,8]{2,1,0:T(8,128)S(1)}, s32[3,8,8]{2,1,0:T(8,128)}, u32[]{:S(2)}) copy-start(s32[3,8,8]{2,1,0:T(8,128)} %mask_ref.3) | copy-start | bytes 2308
  10.1 5.3 %copy-start.1 = (s32[3]{0:T(128)S(1)}, s32[3]{0:T(128)}, u32[]{:S(2)}) copy-start(s32[3]{0:T(128)} %bits_ref.3) | copy-start | bytes 40
  10.1 5.3 %copy-start.2 = (f32[3]{0:T(128)S(1)}, f32[3]{0:T(128)}, u32[]{:S(2)}) copy-start(f32[3]{0:T(128)} %field_ref.1) | copy-start | bytes 40
  10.1 5.2 %copy-start.3 = (f32[13]{0:T(128)S(1)}, f32[13]{0:T(128)}, u32[]{:S(2)}) copy-start(f32[13]{0:T(128)} %coupling_ref.1) | copy-start | bytes 160
  10.1 5.2 %copy-start.4 = (f32[64]{0:T(128)S(1)}, f32[64]{0:T(128)}, u32[]{:S(2)}) copy-start(f32[64]{0:T(128)} %mode_ref.1) | copy-start | bytes 772

commit v11 on v10

--- a/solution.py
+++ b/solution.py
@@ -291,7 +291,7 @@
 
     tables = (place_ref, inside_ref)
     step(plan, initial_ref, (*masked_refs, *fetched_refs), *tables, rounded_ref, finish, kept, ready, new_ref)
-    put_sums(sums_ref, one_row(squares), one_row(overlap), 0, 1, plan.groups)
+    put_sums(sums_ref, one_row(squares), one_row(overlap), 0, 1, 1)
 
 
 def one_row(rows):
@@ -315,7 +315,7 @@
     masked_refs = refs[: plan.bits]
     if keep:
         current_ref, new_ref, out_ref, moment_ref, rounded_ref = refs[plan.bits :]
-        squares, overlap = totals_of(arrived_ref, 0, 1, plan.groups)
+        squares, overlap = totals_of(arrived_ref, 0, 1, 1)
     else:
         out_ref, rounded_ref, current_ref = refs[plan.bits :]
         squares, overlap = totals_of(arrived_ref, plan.body, plan.message, plan.groups)
@@ -356,6 +356,24 @@
 def exchange(values, count):
     shaped = values.reshape(count, values.shape[0] // count, 1, LANES)
     return lax.all_to_all(shaped, AXES, 0, 0, tiled=True).reshape(values.shape)
+
+
+def summed(plan, values):
+    for axis, size in (("phonon", plan.phonons), ("site", plan.sites)):
+        bits = [1 << bit for bit in range(size.bit_length() - 1)]
+        while bits:
+            near, bits = bits[-2:], bits[:-2]
+            first = values + swapped(values, axis, size, near[0])
+            if len(near) == 2:
+                first = first + (
+                    swapped(values, axis, size, near[1]) + swapped(values, axis, size, near[0] ^ near[1])
+                )
+            values = first
+    return values
+
+
+def swapped(values, axis, size, mask):
+    return lax.ppermute(values, axis, [(source, source ^ mask) for source in range(size)])
 
 
 def shards(plan, state, operators, op_mask, site_bits, field, site_coupling, mode_coupling):
@@ -418,7 +436,7 @@
     )(site_bits, op_mask, operators)
     initial, raw, sums, *fetched_masked = pl.pallas_call(
         functools.partial(first_kernel, plan, kept),
-        out_shape=[vector, vector, jax.ShapeDtypeStruct((plan.groups, LANES), f32)] + [operator] * fetched,
+        out_shape=[vector, vector, jax.ShapeDtypeStruct((1, LANES), f32)] + [operator] * fetched,
         in_specs=[VMEM] * 4 + [HBM] * fetched,
         out_specs=[VMEM] * (3 + fetched),
         scratch_shapes=[rounded, pltpu.SemaphoreType.DMA((fetched, plan.parts))],
@@ -427,7 +445,7 @@
         name="first",
     )(arrived, place, inside, *masked, *stored)
     tables = (place, inside, *masked, *fetched_masked)
-    sums = exchange(sums, plan.groups)
+    sums = summed(plan, sums)
     current, raw, departing, moment_one = pl.pallas_call(
         functools.partial(later_kernel, plan, True),
         out_shape=[vector, vector, message, moment],

time: 79.6 us -> 85.1 us (1.069)
  blocking collectives: 46.3 us -> 37.7 us
  starting transfers between devices: 7.3 us -> 14.5 us
  waiting for transfers between devices: 7.56 us -> 14.5 us
    all_to_all x3 -> x2, blocking collectives: 46.3 us -> 37.7 us  [exchange(): return lax.all_to_all(shaped, AXES, 0, 0, tiled=True).reshape(values.shape)]
    ppermute x0 -> x7, starting transfers between devices: none -> 7.16 us  [swapped(): lax.ppermute(values, axis, [(source, source ^ mask) for source in range(s...]
    ppermute x0 -> x7, waiting for transfers between devices: none -> 6.93 us  [swapped(): lax.ppermute(values, axis, [(source, source ^ mask) for source in range(s...]
  transfers between devices with their start and end apart: 1 -> 8, of which waited for: 1 -> 6; matrix products, arithmetic and copies ran while one was open for 0% -> 0% of each run, Pallas kernels for 10% -> 10%
where the time goes in v11:
time: 85.1 us; the launch traced here: 84.7 us
  blocking collectives  37.7 us (44%)
  Pallas kernels  17.3 us (20%)
  starting transfers between devices  14.5 us (17%)
  waiting for transfers between devices  14.5 us (17%)
    all_to_all x2, blocking collectives, exchange(): return lax.all_to_all(shaped, AXES, 0, 0, tiled=True).reshape(values.shape)  37.7 us
    all_to_all x1, waiting for transfers between devices, exchange(): return lax.all_to_all(shaped, AXES, 0, 0, tiled=True).reshape(values.shape)  7.56 us
    all_to_all x1, starting transfers between devices, exchange(): return lax.all_to_all(shaped, AXES, 0, 0, tiled=True).reshape(values.shape)  7.3 us
    ppermute x7, starting transfers between devices, swapped(): lax.ppermute(values, axis, [(source, source ^ mask) for source in range(s...  7.16 us
    ppermute x7, waiting for transfers between devices, swapped(): lax.ppermute(values, axis, [(source, source ^ mask) for source in range(s...  6.93 us
    pallas_call x1, Pallas kernels, shards(): pl.pallas_call(functools.partial(store_kernel, plan, kept), out_shape=[op...  5.19 us
    pallas_call x1, Pallas kernels, shards(): pl.pallas_call(functools.partial(first_kernel, plan, kept), out_shape=[ve...  3.05 us
    pallas_call x1, Pallas kernels, shards(): pl.pallas_call(functools.partial(prepare_kernel, plan, kept), out_shape=[...  2.97 us
  transfers between devices with their start and end apart: 8, of which 6 were waited for; matrix products, arithmetic and copies ran while one was open for 0% of the time, Pallas kernels for 10%

profile of v11, /device:TPU:0, one launch (start us, length us, event | category | flops | bytes accessed | tf_op | source)
XLA Modules:
  0.0 84.7 jit_solution(4290639199456202696)
XLA Ops:
  0.6 2.1 %depart.1 = f32[1056,128]{1,0:T(8,128)} custom-call(f32[1024,128]{1,0:T(8,128)} %state_ref.1), custom_call_target="tpu_custom_call" | custom-call | tf_op jit(solution)/shard_map/depart/pallas_call | solution.py:392
  2.7 7.3 %all-to-all-start = ((f32[32,33,1,128]{3,2,1,0:T(1,128)}), f32[32,33,1,128]{3,2,1,0:T(1,128)S(1)}, u32[]{:S(2)}, u32[]{:S(2)}) async-start(f32[32,33,1,128]{3,2,1,0:T(1,128)} %bitcast.12), calls=%async_computation | async-start | bytes 1081344 | tf_op jit(solution)/shard_map/all_to_all | solution.py:358
  10.0 0.0 copy-start
  10.1 0.0 copy-start.1
  10.1 0.0 copy-start.2
  10.1 0.0 copy-start.3
  10.1 0.0 copy-start.4
  10.1 5.2 %store.1 = (bf16[4,1024,256]{2,1,0:T(8,128)(2,1)}, bf16[4,1024,256]{2,1,0:T(8,128)(2,1)}) custom-call(s32[3]{0:T(128)} %bits_ref.3, s32[3,8,8]{2,1,0:T(8,128)} %mask_ref.3, bf16[3,1024,1024]{2,1,0:T(8,128)(2,1)} %operators_ref.3), custom_call_target="tpu_custom_call" | custom-call | flops 1048576 | bytes 8388608 | tf_op jit(solution)/shard_map/store/pallas_call | solution.py:422
  15.3 0.0 copy-done
  15.3 0.0 copy-done.1
  15.3 0.0 copy-done.2
  15.3 0.0 copy-done.3
  15.3 0.0 copy-done.4
  15.3 3.0 %prepare.1 = (f32[6,128,128]{2,1,0:T(8,128)S(1)}, f32[8,1024]{1,0:T(8,128)S(1)}, bf16[4,1024,256]{2,1,0:T(8,128)(2,1)S(1)}) custom-call(s32[3]{0:T(128)S(1)} %copy-done.1, s32[3,8,8]{2,1,0:T(8,128)S(1)} %copy-done, f32[3]{0:T(128)S(1)} %copy-done.2, f32[13]{0:T(128)S(1)} %copy-done.3, f32[64]{0:T(128)S(1)} %copy-done.4, bf16[3,1024,1024]{2,1,0:T(8,128)(2,1)} %operators_ref.3), custom_call_target="tpu_custom_call" | custom-call | flops 1048576 | bytes 4194304 | tf_op jit(solution)/shard_map/prepare/pallas_call | solution.py:405
  18.3 7.6 %all-to-all-done = f32[32,33,1,128]{3,2,1,0:T(1,128)S(1)} async-done(((f32[32,33,1,128]{3,2,1,0:T(1,128)}), f32[32,33,1,128]{3,2,1,0:T(1,128)S(1)}, u32[]{:S(2)}, u32[]{:S(2)}) %all-to-all-start) | async-done | bytes 540704 | tf_op jit(solution)/shard_map/all_to_all | solution.py:358
  25.9 3.1 %first.1 = (f32[128,1024]{1,0:T(8,128)S(1)}, f32[128,1024]{1,0:T(8,128)S(1)}, f32[1,128]{1,0:T(1,128)S(1)}, bf16[4,1024,256]{2,1,0:T(8,128)(2,1)S(1)}, bf16[4,1024,256]{2,1,0:T(8,128)(2,1)S(1)}) custom-call(f32[1056,128]{1,0:T(8,128)S(1)} %bitcast.8, f32[6,128,128]{2,1,0:T(8,128)S(1)} %get-tuple-element.20.place_ref, ...), custom_call_target="tpu_custom_call" | custom-call | flops 805306368 | bytes 524288 | tf_op jit(solution)/shard_map/first/pallas_call | solution.py:437
  28.9 1.0 %collective-permute-start.2 = (f32[1,128]{1,0:T(1,128)S(1)}, f32[1,128]{1,0:T(1,128)S(1)}, u32[]{:S(2)}, u32[]{:S(2)}) collective-permute-start(f32[1,128]{1,0:T(1,128)S(1)} %get-tuple-element.25), channel_id=1, source_target_pairs={{0,3},{1,2},{2,1},{3,0},{4,7},{5,6},{6,5},{7,4},{8,11},{9,10},{10,... | collective-permute-start | bytes 1544 | tf_op jit(solution)/shard_map/ppermute | solution.py:376
  30.0 0.6 collective-permute-start.1
  30.6 0.3 collective-permute-start
  30.9 1.1 %collective-permute-done.2 = f32[1,128]{1,0:T(1,128)S(1)} collective-permute-done((f32[1,128]{1,0:T(1,128)S(1)}, f32[1,128]{1,0:T(1,128)S(1)}, u32[]{:S(2)}, u32[]{:S(2)}) %collective-permute-start.2) | collective-permute-done | bytes 544 | tf_op jit(solution)/shard_map/ppermute | solution.py:376
  32.0 1.5 %collective-permute-done.1 = f32[1,128]{1,0:T(1,128)S(1)} collective-permute-done((f32[1,128]{1,0:T(1,128)S(1)}, f32[1,128]{1,0:T(1,128)S(1)}, u32[]{:S(2)}, u32[]{:S(2)}) %collective-permute-start.1) | collective-permute-done | bytes 544 | tf_op jit(solution)/shard_map/ppermute | solution.py:376
  33.5 0.0 collective-permute-done
  33.5 0.9 %collective-permute-start.5 = (f32[1,128]{1,0:T(1,128)S(1)}, f32[1,128]{1,0:T(1,128)S(1)}, u32[]{:S(2)}, u32[]{:S(2)}) collective-permute-start(f32[1,128]{1,0:T(1,128)S(1)} %add_add_fusion.1), channel_id=1, source_target_pairs={{0,24},{4,28},{8,16},{12,20},{16,8},{20,12},{24,0},{28,4},{1,25},{... | collective-permute-start | bytes 1544 | tf_op jit(solution)/shard_map/ppermute | solution.py:376
  34.5 1.3 %collective-permute-start.4 = (f32[1,128]{1,0:T(1,128)S(1)}, f32[1,128]{1,0:T(1,128)S(1)}, u32[]{:S(2)}, u32[]{:S(2)}) collective-permute-start(f32[1,128]{1,0:T(1,128)S(1)} %add_add_fusion.1), channel_id=1, source_target_pairs={{0,16},{4,20},{8,24},{12,28},{16,0},{20,4},{24,8},{28,12},{1,17},{... | collective-permute-start | bytes 1544 | tf_op jit(solution)/shard_map/ppermute | solution.py:376
  35.8 2.2 %collective-permute-start.3 = (f32[1,128]{1,0:T(1,128)S(1)}, f32[1,128]{1,0:T(1,128)S(1)}, u32[]{:S(2)}, u32[]{:S(2)}) collective-permute-start(f32[1,128]{1,0:T(1,128)S(1)} %add_add_fusion.1), channel_id=1, source_target_pairs={{0,8},{4,12},{8,0},{12,4},{16,24},{20,28},{24,16},{28,20},{1,9},{5... | collective-permute-start | bytes 1544 | tf_op jit(solution)/shard_map/ppermute | solution.py:376
  38.0 0.9 %collective-permute-done.5 = f32[1,128]{1,0:T(1,128)S(1)} collective-permute-done((f32[1,128]{1,0:T(1,128)S(1)}, f32[1,128]{1,0:T(1,128)S(1)}, u32[]{:S(2)}, u32[]{:S(2)}) %collective-permute-start.5) | collective-permute-done | bytes 544 | tf_op jit(solution)/shard_map/ppermute | solution.py:376
  38.9 0.0 collective-permute-done.4
  38.9 0.6 collective-permute-done.3
  39.5 0.8 collective-permute-start.6
  40.3 2.8 %collective-permute-done.6 = f32[1,128]{1,0:T(1,128)S(1)} collective-permute-done((f32[1,128]{1,0:T(1,128)S(1)}, f32[1,128]{1,0:T(1,128)S(1)}, u32[]{:S(2)}, u32[]{:S(2)}) %collective-permute-start.6) | collective-permute-done | bytes 544 | tf_op jit(solution)/shard_map/ppermute | solution.py:376
  43.1 1.3 %second.1 = (f32[128,1024]{1,0:T(8,128)S(1)}, f32[128,1024]{1,0:T(8,128)S(1)}, f32[1056,128]{1,0:T(8,128)S(1)}, f32[8,128]{1,0:T(8,128)S(1)}) custom-call(f32[1,128]{1,0:T(1,128)S(1)} %add.27.arrived_ref, f32[128,1024]{1,0:T(8,128)S(1)} %get-tuple-element.26.raw_ref, f32[128,1024]{1,0:T(8,128)S(1)} %get-tuple-element.27.previous_ref.initial_ref, ...), custom_call_target="tpu_custom_call" | custom-call | flops 805306368 | bytes 524288 | tf_op jit(solution)/shard_map/second/pallas_call | solution.py:449
  44.4 18.9 %all_to_all.15 = f32[32,33,1,128]{3,2,1,0:T(1,128)S(1)} all-to-all(f32[32,33,1,128]{3,2,1,0:T(1,128)S(1)} %bitcast.11), channel_id=1, replica_groups=mesh['site'=8,'phonon'=4] {'site','phonon'}, dimensions={0} | all-to-all | bytes 1081344 | tf_op jit(solution)/shard_map/all_to_all | solution.py:358
  63.3 1.3 %third.1 = f32[1056,128]{1,0:T(8,128)S(1)} custom-call(f32[1056,128]{1,0:T(8,128)S(1)} %bitcast.6, f32[128,1024]{1,0:T(8,128)S(1)} %get-tuple-element.31.raw_ref, f32[128,1024]{1,0:T(8,128)S(1)} %get-tuple-element.32.previous_ref, f32[128,1024]{1,0:T(8,128)S(1)} %get-tuple-element.27.previous_ref.initial_ref, ...), custom_call_target="tpu_custom_call" | custom-call | flops 805306368 | bytes 524288 | tf_op jit(solution)/shard_map/third/pallas_call | solution.py:460
  64.6 18.8 %all_to_all.16 = f32[32,33,1,128]{3,2,1,0:T(1,128)S(1)} all-to-all(f32[32,33,1,128]{3,2,1,0:T(1,128)S(1)} %bitcast.9), channel_id=1, replica_groups=mesh['site'=8,'phonon'=4] {'site','phonon'}, dimensions={0} | all-to-all | bytes 1081344 | tf_op jit(solution)/shard_map/all_to_all | solution.py:358
  83.4 1.3 %arrive.1 = (f32[1024,128]{1,0:T(8,128)}, f32[1024,128]{1,0:T(8,128)}, f32[3]{0:T(128)}) custom-call(f32[1056,128]{1,0:T(8,128)S(1)} %bitcast.7, f32[1056,128]{1,0:T(8,128)S(1)} %bitcast.10, f32[8,128]{1,0:T(8,128)S(1)} %get-tuple-element.33.moment_ref), custom_call_target="tpu_custom_call" | custom-call | tf_op jit(solution)/shard_map/arrive/pallas_call | solution.py:471
  (3 shorter events, 0.0 us)
Async XLA Ops:
  2.7 23.2 %all-to-all-start = ((f32[32,33,1,128]{3,2,1,0:T(1,128)}), f32[32,33,1,128]{3,2,1,0:T(1,128)S(1)}, u32[]{:S(2)}, u32[]{:S(2)}) async-start(f32[32,33,1,128]{3,2,1,0:T(1,128)} %bitcast.12), calls=%async_computation | async-start | bytes 1081344 | tf_op jit(solution)/shard_map/all_to_all | solution.py:358
  10.0 5.3 %copy-start = (s32[3,8,8]{2,1,0:T(8,128)S(1)}, s32[3,8,8]{2,1,0:T(8,128)}, u32[]{:S(2)}) copy-start(s32[3,8,8]{2,1,0:T(8,128)} %mask_ref.3) | copy-start | bytes 2308
  10.1 5.3 %copy-start.1 = (s32[3]{0:T(128)S(1)}, s32[3]{0:T(128)}, u32[]{:S(2)}) copy-start(s32[3]{0:T(128)} %bits_ref.3) | copy-start | bytes 40
  10.1 5.3 %copy-start.2 = (f32[3]{0:T(128)S(1)}, f32[3]{0:T(128)}, u32[]{:S(2)}) copy-start(f32[3]{0:T(128)} %field_ref.1) | copy-start | bytes 40
  10.1 5.3 %copy-start.3 = (f32[13]{0:T(128)S(1)}, f32[13]{0:T(128)}, u32[]{:S(2)}) copy-start(f32[13]{0:T(128)} %coupling_ref.1) | copy-start | bytes 160
  10.1 5.2 %copy-start.4 = (f32[64]{0:T(128)S(1)}, f32[64]{0:T(128)}, u32[]{:S(2)}) copy-start(f32[64]{0:T(128)} %mode_ref.1) | copy-start | bytes 772
  28.9 3.0 %collective-permute-start.2 = (f32[1,128]{1,0:T(1,128)S(1)}, f32[1,128]{1,0:T(1,128)S(1)}, u32[]{:S(2)}, u32[]{:S(2)}) collective-permute-start(f32[1,128]{1,0:T(1,128)S(1)} %get-tuple-element.25), channel_id=1, source_target_pairs={{0,3},{1,2},{2,1},{3,0},{4,7},{5,6},{6,5},{7,4},{8,11},{9,10},{10,... | collective-permute-start | bytes 1544 | tf_op jit(solution)/shard_map/ppermute | solution.py:376
  30.0 3.5 %collective-permute-start.1 = (f32[1,128]{1,0:T(1,128)S(1)}, f32[1,128]{1,0:T(1,128)S(1)}, u32[]{:S(2)}, u32[]{:S(2)}) collective-permute-start(f32[1,128]{1,0:T(1,128)S(1)} %get-tuple-element.25), channel_id=1, source_target_pairs={{0,2},{1,3},{2,0},{3,1},{4,6},{5,7},{6,4},{7,5},{8,10},{9,11},{10,... | collective-permute-start | bytes 1544 | tf_op jit(solution)/shard_map/ppermute | solution.py:376
  30.6 3.0 %collective-permute-start = (f32[1,128]{1,0:T(1,128)S(1)}, f32[1,128]{1,0:T(1,128)S(1)}, u32[]{:S(2)}, u32[]{:S(2)}) collective-permute-start(f32[1,128]{1,0:T(1,128)S(1)} %get-tuple-element.25), channel_id=1, source_target_pairs={{0,1},{1,0},{2,3},{3,2},{4,5},{5,4},{6,7},{7,6},{8,9},{9,8},{10,11... | collective-permute-start | bytes 1544 | tf_op jit(solution)/shard_map/ppermute | solution.py:376
  33.5 5.4 %collective-permute-start.5 = (f32[1,128]{1,0:T(1,128)S(1)}, f32[1,128]{1,0:T(1,128)S(1)}, u32[]{:S(2)}, u32[]{:S(2)}) collective-permute-start(f32[1,128]{1,0:T(1,128)S(1)} %add_add_fusion.1), channel_id=1, source_target_pairs={{0,24},{4,28},{8,16},{12,20},{16,8},{20,12},{24,0},{28,4},{1,25},{... | collective-permute-start | bytes 1544 | tf_op jit(solution)/shard_map/ppermute | solution.py:376
  34.5 4.5 %collective-permute-start.4 = (f32[1,128]{1,0:T(1,128)S(1)}, f32[1,128]{1,0:T(1,128)S(1)}, u32[]{:S(2)}, u32[]{:S(2)}) collective-permute-start(f32[1,128]{1,0:T(1,128)S(1)} %add_add_fusion.1), channel_id=1, source_target_pairs={{0,16},{4,20},{8,24},{12,28},{16,0},{20,4},{24,8},{28,12},{1,17},{... | collective-permute-start | bytes 1544 | tf_op jit(solution)/shard_map/ppermute | solution.py:376
  35.8 3.7 %collective-permute-start.3 = (f32[1,128]{1,0:T(1,128)S(1)}, f32[1,128]{1,0:T(1,128)S(1)}, u32[]{:S(2)}, u32[]{:S(2)}) collective-permute-start(f32[1,128]{1,0:T(1,128)S(1)} %add_add_fusion.1), channel_id=1, source_target_pairs={{0,8},{4,12},{8,0},{12,4},{16,24},{20,28},{24,16},{28,20},{1,9},{5... | collective-permute-start | bytes 1544 | tf_op jit(solution)/shard_map/ppermute | solution.py:376
  39.5 3.5 %collective-permute-start.6 = (f32[1,128]{1,0:T(1,128)S(1)}, f32[1,128]{1,0:T(1,128)S(1)}, u32[]{:S(2)}, u32[]{:S(2)}) collective-permute-start(f32[1,128]{1,0:T(1,128)S(1)} %add_add_fusion), channel_id=1, source_target_pairs={{0,4},{4,0},{8,12},{12,8},{16,20},{20,16},{24,28},{28,24},{1,5},{5... | collective-permute-start | bytes 1544 | tf_op jit(solution)/shard_map/ppermute | solution.py:376

commit v12 on v10

--- a/solution.py
+++ b/solution.py
@@ -12,7 +12,7 @@
 STEPS = 3
 LANES = 128
 SUBLANES = 8
-EXTRA = 1
+SLOTS = 4
 AXES = ("site", "phonon")
 
 epsilon = 1e-06
@@ -39,7 +39,8 @@
         self.pieces = self.levels_here * self.share
         self.lane_blocks = rows // LANES
         self.body = self.pieces * self.lane_blocks
-        self.message = self.body + EXTRA
+        self.inward = self.body + 1
+        self.outward = 2 * self.body + 1
         self.places = self.pieces * self.groups
         self.width = 2 * LANES
         self.parts = rows // self.width
@@ -64,22 +65,25 @@
     return jnp.sum(values, axis=0, keepdims=True)
 
 
-def folded(value):
-    return value + pltpu.roll(value, LANES // 2, 1)
-
-
-def put_sums(out_ref, squares, overlap, start, stride, count):
+def put_sums(out_ref, sums, start, stride, count):
     lane = lax.broadcasted_iota(jnp.int32, (1, LANES), 1)
-    row = jnp.where(lane < LANES // 2, folded(squares), folded(overlap))
+    row = jnp.zeros((1, LANES), jnp.float32)
+    for slot, value in enumerate(sums):
+        width = LANES
+        while width > LANES // SLOTS:
+            width //= 2
+            value = value + pltpu.roll(value, width, 1)
+        row = jnp.where(lane // (LANES // SLOTS) == slot, value, row)
     out_ref[pl.ds(start, count, stride=stride), :] = jnp.broadcast_to(row, (count, LANES))
 
 
 def totals_of(ref, start, stride, count):
     lanes = lane_sums(ref[pl.ds(start, count, stride=stride), :])
     lane = lax.broadcasted_iota(jnp.int32, (1, LANES), 1)
-    squares = jnp.sum(jnp.where(lane < LANES // 2, lanes, 0.0), axis=1, keepdims=True)
-    overlap = jnp.sum(jnp.where(lane < LANES // 2, 0.0, lanes), axis=1, keepdims=True)
-    return squares, overlap
+    return [
+        jnp.sum(jnp.where(lane // (LANES // SLOTS) == slot, lanes, 0.0), axis=1, keepdims=True)
+        for slot in range(SLOTS)
+    ]
 
 
 def scale_of(plan, squares):
@@ -104,10 +108,10 @@
         sums = sums + lane_sums(tile * tile)
         turned = tile.T
         for piece in range(plan.pieces):
-            out_ref[pl.ds(piece * plan.lane_blocks + block, plan.groups, stride=plan.message), :] = turned[
+            out_ref[pl.ds(piece * plan.lane_blocks + block, plan.groups, stride=plan.inward), :] = turned[
                 piece * plan.groups : (piece + 1) * plan.groups
             ]
-    put_sums(out_ref, sums, jnp.zeros_like(sums), plan.body, plan.message, plan.groups)
+    put_sums(out_ref, [sums], plan.body, plan.inward, plan.groups)
 
 
 def mask_operator(plan, chosen, mask_ref, held_ref, out_ref):
@@ -275,23 +279,29 @@
     def ready(part, position):
         fetches[part, position].wait()
 
-    squares, _ = totals_of(arrived_ref, plan.body, plan.message, plan.groups)
+    squares = totals_of(arrived_ref, plan.body, plan.inward, plan.groups)[0]
     inverse = 1.0 / scale_of(plan, squares)
     for piece in range(plan.pieces):
         for block in range(plan.lane_blocks):
-            part = arrived_ref[pl.ds(piece * plan.lane_blocks + block, plan.groups, stride=plan.message), :]
+            part = arrived_ref[pl.ds(piece * plan.lane_blocks + block, plan.groups, stride=plan.inward), :]
             initial_ref[pl.ds(piece * plan.groups, plan.groups), pl.ds(block * LANES, LANES)] = part * inverse
+    tables = ((*masked_refs, *fetched_refs), place_ref, inside_ref, rounded_ref)
     squares = []
     overlap = []
+    ahead = []
 
     def finish(lanes, new):
         new_ref[:, lanes] = new
         squares.append(lane_sums(new * new))
         overlap.append(lane_sums(new * initial_ref[:, lanes]))
 
-    tables = (place_ref, inside_ref)
-    step(plan, initial_ref, (*masked_refs, *fetched_refs), *tables, rounded_ref, finish, kept, ready, new_ref)
-    put_sums(sums_ref, one_row(squares), one_row(overlap), 0, 1, plan.groups)
+    def look_ahead(lanes, total):
+        new = 2.0 * total - initial_ref[:, lanes]
+        ahead.append(lane_sums(new * new))
+
+    step(plan, initial_ref, *tables, finish, kept, ready, new_ref)
+    step(plan, new_ref, *tables, look_ahead, plan.bits)
+    put_sums(sums_ref, [one_row(squares), one_row(overlap), one_row(ahead)], 0, 1, plan.groups)
 
 
 def one_row(rows):
@@ -299,58 +309,63 @@
     return sum(total[:, start : start + LANES] for start in range(0, total.shape[1], LANES))
 
 
-def place(plan, arrived_ref, out_ref):
-    squares, overlap = totals_of(arrived_ref, plan.body, plan.message, plan.groups)
-    inverse = 1.0 / scale_of(plan, squares)
-    for block in range(plan.lane_blocks):
-        parts = [
-            arrived_ref[pl.ds(piece * plan.lane_blocks + block, plan.groups, stride=plan.message), :]
-            for piece in range(plan.pieces)
-        ]
-        out_ref[pl.ds(block * LANES, LANES), :] = (jnp.concatenate(parts, axis=0) * inverse).T
-    return overlap * inverse / plan.entries
-
-
-def later_kernel(plan, keep, arrived_ref, raw_ref, previous_ref, initial_ref, place_ref, inside_ref, *refs):
+def onward_kernel(plan, arrived_ref, raw_ref, initial_ref, place_ref, inside_ref, *refs):
     masked_refs = refs[: plan.bits]
-    if keep:
-        current_ref, new_ref, out_ref, moment_ref, rounded_ref = refs[plan.bits :]
-        squares, overlap = totals_of(arrived_ref, 0, 1, plan.groups)
-    else:
-        out_ref, rounded_ref, current_ref = refs[plan.bits :]
-        squares, overlap = totals_of(arrived_ref, plan.body, plan.message, plan.groups)
-    inverse = 1.0 / scale_of(plan, squares)
-    if keep:
-        moment_ref[...] = jnp.broadcast_to(overlap * inverse / plan.entries, moment_ref.shape)
+    out_ref, known_ref, rounded_ref, second_ref, third_ref = refs[plan.bits :]
+    squares, overlap, ahead, _ = totals_of(arrived_ref, 0, 1, plan.groups)
+    first = 1.0 / scale_of(plan, squares)
+    estimate = scale_of(plan, ahead * first * first)
+    second = 1.0 / estimate
+    known_ref[:1, :] = jnp.broadcast_to(overlap * first / plan.entries, (1, LANES))
+    known_ref[1:, :] = jnp.broadcast_to(estimate, (SUBLANES - 1, LANES))
     for block in range(plan.lane_blocks):
         lanes = pl.ds(block * LANES, LANES)
-        current_ref[:, lanes] = raw_ref[:, lanes] * inverse
-    squares = []
-    overlap = []
-
-    def finish(lanes, total):
-        new = 2.0 * total - previous_ref[:, lanes] * inverse
-        if keep:
-            new_ref[:, lanes] = new
-        squares.append(lane_sums(new * new))
-        overlap.append(lane_sums(new * initial_ref[:, lanes]))
-        for start in range(0, lanes.size, LANES):
+        second_ref[:, lanes] = raw_ref[:, lanes] * first
+    tables = (masked_refs, place_ref, inside_ref, rounded_ref)
+    sums = [[] for _ in range(SLOTS)]
+
+    def send(vector, lanes, new):
+        sums[2 * vector].append(lane_sums(new * new))
+        sums[2 * vector + 1].append(lane_sums(new * initial_ref[:, lanes]))
+        for start in range(0, plan.width, LANES):
             block = (lanes.start + start) // LANES
             for piece in range(plan.pieces):
-                out_ref[pl.ds(piece * plan.lane_blocks + block, plan.groups, stride=plan.message), :] = new[
+                row = vector * plan.body + piece * plan.lane_blocks + block
+                out_ref[pl.ds(row, plan.groups, stride=plan.outward), :] = new[
                     piece * plan.groups : (piece + 1) * plan.groups, start : start + LANES
                 ]
 
-    step(plan, current_ref, masked_refs, place_ref, inside_ref, rounded_ref, finish, plan.bits)
-    put_sums(out_ref, one_row(squares), one_row(overlap), plan.body, plan.message, plan.groups)
-
-
-def arrive_kernel(plan, before_ref, last_ref, moment_ref, before_out_ref, last_out_ref, moments_ref):
-    second = place(plan, before_ref, before_out_ref)
-    third = place(plan, last_ref, last_out_ref)
-    moments_ref[0] = moment_ref[0, 0]
-    moments_ref[1] = second[0, 0]
-    moments_ref[2] = third[0, 0]
+    def finish_second(lanes, total):
+        new = 2.0 * total - initial_ref[:, lanes] * first
+        third_ref[:, lanes] = new * second
+        send(0, lanes, new)
+
+    def finish_third(lanes, total):
+        send(1, lanes, 2.0 * total - second_ref[:, lanes] * second)
+
+    step(plan, second_ref, *tables, finish_second, plan.bits)
+    step(plan, third_ref, *tables, finish_third, plan.bits)
+    put_sums(out_ref, [one_row(rows) for rows in sums], 2 * plan.body, plan.outward, plan.groups)
+
+
+def arrive_kernel(plan, arrived_ref, known_ref, before_ref, last_ref, moments_ref):
+    before_squares, before_overlap, last_squares, last_overlap = totals_of(
+        arrived_ref, 2 * plan.body, plan.outward, plan.groups
+    )
+    before = 1.0 / scale_of(plan, before_squares)
+    back = known_ref[1:2, :1] * before
+    last = back / scale_of(plan, last_squares * back * back)
+    for vector, (out_ref, factor) in enumerate(((before_ref, before), (last_ref, last))):
+        for block in range(plan.lane_blocks):
+            first = vector * plan.body + block
+            parts = [
+                arrived_ref[pl.ds(first + piece * plan.lane_blocks, plan.groups, stride=plan.outward), :]
+                for piece in range(plan.pieces)
+            ]
+            out_ref[pl.ds(block * LANES, LANES), :] = (jnp.concatenate(parts, axis=0) * factor).T
+    moments_ref[0] = known_ref[0, 0]
+    moments_ref[1] = (before_overlap * before / plan.entries)[0, 0]
+    moments_ref[2] = (last_overlap * last / plan.entries)[0, 0]
 
 
 def exchange(values, count):
@@ -360,9 +375,10 @@
 
 def shards(plan, state, operators, op_mask, site_bits, field, site_coupling, mode_coupling):
     f32 = jnp.float32
-    message = jax.ShapeDtypeStruct((plan.groups * plan.message, LANES), f32)
+    inward = jax.ShapeDtypeStruct((plan.groups * plan.inward, LANES), f32)
+    outward = jax.ShapeDtypeStruct((plan.groups * plan.outward, LANES), f32)
     vector = jax.ShapeDtypeStruct((plan.places, plan.rows), f32)
-    moment = jax.ShapeDtypeStruct((SUBLANES, LANES), f32)
+    known = jax.ShapeDtypeStruct((SUBLANES, LANES), f32)
     held = jax.ShapeDtypeStruct((plan.rows, plan.columns), f32)
     rounded = pltpu.VMEM((plan.places, plan.bits * plan.rows), jnp.bfloat16)
     working = pltpu.VMEM((plan.places, plan.rows), f32)
@@ -373,7 +389,7 @@
 
     departing = pl.pallas_call(
         functools.partial(depart_kernel, plan),
-        out_shape=message,
+        out_shape=inward,
         in_specs=[HBM],
         out_specs=VMEM,
         scratch_shapes=[pltpu.VMEM((plan.rows, plan.columns), f32), pltpu.SemaphoreType.DMA((2,))],
@@ -428,36 +444,25 @@
     )(arrived, place, inside, *masked, *stored)
     tables = (place, inside, *masked, *fetched_masked)
     sums = exchange(sums, plan.groups)
-    current, raw, departing, moment_one = pl.pallas_call(
-        functools.partial(later_kernel, plan, True),
-        out_shape=[vector, vector, message, moment],
-        in_specs=[VMEM] * (6 + plan.bits),
-        out_specs=[VMEM] * 4,
-        scratch_shapes=[rounded],
+    departing, told = pl.pallas_call(
+        functools.partial(onward_kernel, plan),
+        out_shape=[outward, known],
+        in_specs=[VMEM] * (5 + plan.bits),
+        out_specs=[VMEM] * 2,
+        scratch_shapes=[rounded, working, working],
         compiler_params=params(32),
-        cost_estimate=cost(work, 4 * plan.places * plan.rows),
-        name="second",
-    )(sums, raw, initial, initial, *tables)
-    before = exchange(departing, plan.groups)
-    departing = pl.pallas_call(
-        functools.partial(later_kernel, plan, False),
-        out_shape=message,
-        in_specs=[VMEM] * (6 + plan.bits),
-        out_specs=VMEM,
-        scratch_shapes=[rounded, working],
-        compiler_params=params(32),
-        cost_estimate=cost(work, 4 * plan.places * plan.rows),
-        name="third",
-    )(before, raw, current, initial, *tables)
-    last = exchange(departing, plan.groups)
+        cost_estimate=cost(2 * work, 8 * plan.places * plan.rows),
+        name="onward",
+    )(sums, raw, initial, *tables)
+    arrived = exchange(departing, plan.groups)
     before, last, moments = pl.pallas_call(
         functools.partial(arrive_kernel, plan),
         out_shape=[held, held, jax.ShapeDtypeStruct((STEPS,), f32)],
-        in_specs=[VMEM] * 3,
+        in_specs=[VMEM] * 2,
         out_specs=[VMEM, VMEM, SMEM],
         compiler_params=params(16),
         name="arrive",
-    )(before, last, moment_one)
+    )(arrived, told)
     return last, before, moments
 
 

time: 79.6 us -> 74.2 us (0.932)
  blocking collectives: 46.3 us -> 40.2 us
    all_to_all x3 -> x2, blocking collectives: 46.3 us -> 40.2 us  [exchange(): return lax.all_to_all(shaped, AXES, 0, 0, tiled=True).reshape(values.shape)]
    pallas_call x1, Pallas kernels: 3.05 us -> 4 us  [shards(): pl.pallas_call(functools.partial(first_kernel, plan, kept), out_shape=[ve...]
    pallas_call x3 -> x2, Pallas kernels: 4.78 us -> 4.51 us  [the longest x1 2.39 us: shards(): pl.pallas_call(functools.partial(onward_kernel, plan), out_shape=[outward...]
  transfers between devices with their start and end apart: 1 -> 1, of which waited for: 1 -> 1; matrix products, arithmetic and copies ran while one was open for 0% -> 0% of each run, Pallas kernels for 10% -> 11%
where the time goes in v12:
time: 74.2 us; the launch traced here: 73.8 us
  blocking collectives  40.2 us (54%)
  Pallas kernels  18 us (24%)
  waiting for transfers between devices  7.56 us (10%)
  starting transfers between devices  7.3 us (10%)
  between operations  0.75 us (1%)
    all_to_all x2, blocking collectives, exchange(): return lax.all_to_all(shaped, AXES, 0, 0, tiled=True).reshape(values.shape)  40.2 us
    all_to_all x1, waiting for transfers between devices, exchange(): return lax.all_to_all(shaped, AXES, 0, 0, tiled=True).reshape(values.shape)  7.56 us
    all_to_all x1, starting transfers between devices, exchange(): return lax.all_to_all(shaped, AXES, 0, 0, tiled=True).reshape(values.shape)  7.3 us
    pallas_call x1, Pallas kernels, shards(): pl.pallas_call(functools.partial(store_kernel, plan, kept), out_shape=[op...  5.18 us
    pallas_call x1, Pallas kernels, shards(): pl.pallas_call(functools.partial(first_kernel, plan, kept), out_shape=[ve...  4 us
    pallas_call x1, Pallas kernels, shards(): pl.pallas_call(functools.partial(prepare_kernel, plan, kept), out_shape=[...  2.97 us
    pallas_call x1, Pallas kernels, shards(): pl.pallas_call(functools.partial(onward_kernel, plan), out_shape=[outward...  2.39 us
    pallas_call x1, Pallas kernels, shards(): pl.pallas_call(functools.partial(depart_kernel, plan), out_shape=inward,...  2.12 us
  transfers between devices with their start and end apart: 1, of which 1 were waited for; matrix products, arithmetic and copies ran while one was open for 0% of the time, Pallas kernels for 11%

profile of v12, /device:TPU:0, one launch (start us, length us, event | category | flops | bytes accessed | tf_op | source)
XLA Modules:
  0.0 73.8 jit_solution(11359850232517776517)
XLA Ops:
  0.6 2.1 %depart.1 = f32[1056,128]{1,0:T(8,128)} custom-call(f32[1024,128]{1,0:T(8,128)} %state_ref.1), custom_call_target="tpu_custom_call" | custom-call | tf_op jit(solution)/shard_map/depart/pallas_call | solution.py:390
  2.8 7.3 %all-to-all-start = ((f32[32,33,1,128]{3,2,1,0:T(1,128)}), f32[32,33,1,128]{3,2,1,0:T(1,128)S(1)}, u32[]{:S(2)}, u32[]{:S(2)}) async-start(f32[32,33,1,128]{3,2,1,0:T(1,128)} %bitcast.13), calls=%async_computation | async-start | bytes 1081344 | tf_op jit(solution)/shard_map/all_to_all | solution.py:373
  10.1 0.0 copy-start
  10.1 0.0 copy-start.1
  10.1 0.0 copy-start.2
  10.1 0.0 copy-start.3
  10.1 0.0 copy-start.4
  10.1 5.2 %store.1 = (bf16[4,1024,256]{2,1,0:T(8,128)(2,1)}, bf16[4,1024,256]{2,1,0:T(8,128)(2,1)}) custom-call(s32[3]{0:T(128)} %bits_ref.3, s32[3,8,8]{2,1,0:T(8,128)} %mask_ref.3, bf16[3,1024,1024]{2,1,0:T(8,128)(2,1)} %operators_ref.3), custom_call_target="tpu_custom_call" | custom-call | flops 1048576 | bytes 8388608 | tf_op jit(solution)/shard_map/store/pallas_call | solution.py:420
  15.3 0.0 copy-done
  15.3 0.0 copy-done.1
  15.3 0.0 copy-done.2
  15.3 0.0 copy-done.3
  15.4 0.0 copy-done.4
  15.4 3.0 %prepare.1 = (f32[6,128,128]{2,1,0:T(8,128)S(1)}, f32[8,1024]{1,0:T(8,128)S(1)}, bf16[4,1024,256]{2,1,0:T(8,128)(2,1)S(1)}) custom-call(s32[3]{0:T(128)S(1)} %copy-done.1, s32[3,8,8]{2,1,0:T(8,128)S(1)} %copy-done, f32[3]{0:T(128)S(1)} %copy-done.2, f32[13]{0:T(128)S(1)} %copy-done.3, f32[64]{0:T(128)S(1)} %copy-done.4, bf16[3,1024,1024]{2,1,0:T(8,128)(2,1)} %operators_ref.3), custom_call_target="tpu_custom_call" | custom-call | flops 1048576 | bytes 4194304 | tf_op jit(solution)/shard_map/prepare/pallas_call | solution.py:403
  18.3 7.6 %all-to-all-done = f32[32,33,1,128]{3,2,1,0:T(1,128)S(1)} async-done(((f32[32,33,1,128]{3,2,1,0:T(1,128)}), f32[32,33,1,128]{3,2,1,0:T(1,128)S(1)}, u32[]{:S(2)}, u32[]{:S(2)}) %all-to-all-start) | async-done | bytes 540704 | tf_op jit(solution)/shard_map/all_to_all | solution.py:373
  25.9 4.0 %first.1 = (f32[128,1024]{1,0:T(8,128)S(1)}, f32[128,1024]{1,0:T(8,128)S(1)}, f32[32,128]{1,0:T(8,128)S(1)}, bf16[4,1024,256]{2,1,0:T(8,128)(2,1)S(1)}, bf16[4,1024,256]{2,1,0:T(8,128)(2,1)S(1)}) custom-call(f32[1056,128]{1,0:T(8,128)S(1)} %bitcast.9, f32[6,128,128]{2,1,0:T(8,128)S(1)} %get-tuple-element.18.place_ref, ...), custom_call_target="tpu_custom_call" | custom-call | flops 805306368 | bytes 524288 | tf_op jit(solution)/shard_map/first/pallas_call | solution.py:435
  29.9 10.1 %all_to_all.15 = f32[32,1,1,128]{3,2,1,0:T(1,128)S(1)} all-to-all(f32[32,1,1,128]{3,2,1,0:T(1,128)S(1)} %bitcast.12), channel_id=1, replica_groups=mesh['site'=8,'phonon'=4] {'site','phonon'}, dimensions={0} | all-to-all | bytes 32768 | tf_op jit(solution)/shard_map/all_to_all | solution.py:373
  40.0 2.4 %onward.1 = (f32[2080,128]{1,0:T(8,128)S(1)}, f32[8,128]{1,0:T(8,128)S(1)}) custom-call(f32[32,128]{1,0:T(8,128)S(1)} %bitcast.11, f32[128,1024]{1,0:T(8,128)S(1)} %get-tuple-element.24.raw_ref, f32[128,1024]{1,0:T(8,128)S(1)} %get-tuple-element.25.initial_ref, f32[6,128,128]{2,1,0:T(8,128)S(1)} %get-tuple-element.18.place_ref, ...), custom_call_target="tpu_custom_call" | custom-call | flops 1610612736 | bytes 1048576 | tf_op jit(solution)/shard_map/onward/pallas_call | solution.py:447
  42.4 30.1 %all_to_all.16 = f32[32,65,1,128]{3,2,1,0:T(1,128)S(1)} all-to-all(f32[32,65,1,128]{3,2,1,0:T(1,128)S(1)} %bitcast.10), channel_id=1, replica_groups=mesh['site'=8,'phonon'=4] {'site','phonon'}, dimensions={0} | all-to-all | bytes 2129920 | tf_op jit(solution)/shard_map/all_to_all | solution.py:373
  72.5 1.3 %arrive.1 = (f32[1024,128]{1,0:T(8,128)}, f32[1024,128]{1,0:T(8,128)}, f32[3]{0:T(128)}) custom-call(f32[2080,128]{1,0:T(8,128)S(1)} %bitcast.8, f32[8,128]{1,0:T(8,128)S(1)} %get-tuple-element.29.known_ref), custom_call_target="tpu_custom_call" | custom-call | tf_op jit(solution)/shard_map/arrive/pallas_call | solution.py:458
Async XLA Ops:
  2.8 23.2 %all-to-all-start = ((f32[32,33,1,128]{3,2,1,0:T(1,128)}), f32[32,33,1,128]{3,2,1,0:T(1,128)S(1)}, u32[]{:S(2)}, u32[]{:S(2)}) async-start(f32[32,33,1,128]{3,2,1,0:T(1,128)} %bitcast.13), calls=%async_computation | async-start | bytes 1081344 | tf_op jit(solution)/shard_map/all_to_all | solution.py:373
  10.1 5.3 %copy-start = (s32[3,8,8]{2,1,0:T(8,128)S(1)}, s32[3,8,8]{2,1,0:T(8,128)}, u32[]{:S(2)}) copy-start(s32[3,8,8]{2,1,0:T(8,128)} %mask_ref.3) | copy-start | bytes 2308
  10.1 5.3 %copy-start.1 = (s32[3]{0:T(128)S(1)}, s32[3]{0:T(128)}, u32[]{:S(2)}) copy-start(s32[3]{0:T(128)} %bits_ref.3) | copy-start | bytes 40
  10.1 5.3 %copy-start.2 = (f32[3]{0:T(128)S(1)}, f32[3]{0:T(128)}, u32[]{:S(2)}) copy-start(f32[3]{0:T(128)} %field_ref.1) | copy-start | bytes 40
  10.1 5.2 %copy-start.3 = (f32[13]{0:T(128)S(1)}, f32[13]{0:T(128)}, u32[]{:S(2)}) copy-start(f32[13]{0:T(128)} %coupling_ref.1) | copy-start | bytes 160
  10.1 5.2 %copy-start.4 = (f32[64]{0:T(128)S(1)}, f32[64]{0:T(128)}, u32[]{:S(2)}) copy-start(f32[64]{0:T(128)} %mode_ref.1) | copy-start | bytes 772

commit v13 on v12

--- a/solution.py
+++ b/solution.py
@@ -44,6 +44,8 @@
         self.places = self.pieces * self.groups
         self.width = 2 * LANES
         self.parts = rows // self.width
+        self.slabs = self.bits * self.parts
+        self.kept = min(self.parts + 1, self.slabs - 1)
         self.entries = float(rows * columns * self.groups)
 
     def fits(self):
@@ -53,6 +55,7 @@
             and self.rows % self.width == 0
             and self.edge % LANES == 0
             and self.width % self.edge == 0
+            and self.bits < SUBLANES
             and self.groups % SUBLANES == 0
         )
 
@@ -114,30 +117,39 @@
     put_sums(out_ref, [sums], plan.body, plan.inward, plan.groups)
 
 
-def mask_operator(plan, chosen, mask_ref, held_ref, out_ref):
-    for across in range(plan.blocks):
-        rows = pl.ds(across * plan.edge, plan.edge)
+def fetch_slabs(plan, slabs, bits_ref, operators_ref, held_ref, semaphores):
+    fetches = []
+    for index, slab in enumerate(slabs):
+        bit, part = divmod(slab, plan.parts)
+        rows = pl.ds(part * plan.width, plan.width)
+        fetch = pltpu.make_async_copy(
+            operators_ref.at[bits_ref[bit], rows, :], held_ref.at[index], semaphores.at[index]
+        )
+        fetch.start()
+        fetches.append(fetch)
+    return fetches
+
+
+def mask_slab(plan, slab, index, bits_ref, mask_ref, held_ref, out_ref):
+    bit, part = divmod(slab, plan.parts)
+    chosen = bits_ref[bit]
+    for start in range(0, plan.width, plan.edge):
+        across = (part * plan.width + start) // plan.edge
+        rows = pl.ds(start, plan.edge)
         for along in range(plan.blocks):
             columns = pl.ds(along * plan.edge, plan.edge)
             keep = (mask_ref[chosen, across, along] > 0).astype(jnp.float32).astype(jnp.bfloat16)
-            part, start = divmod(across * plan.edge, plan.width)
-            out_ref[part, columns, pl.ds(start, plan.edge)] = (held_ref[rows, columns] * keep).T
-
-
-def store_kernel(plan, kept, bits_ref, mask_ref, operators_ref, *refs):
-    count = plan.bits - kept
-    stored_refs, (held_ref, masked_ref, in_semaphores, out_semaphores) = refs[:count], refs[count:]
-    fetches = [
-        pltpu.make_async_copy(operators_ref.at[bits_ref[kept + index]], held_ref.at[index], in_semaphores.at[index])
-        for index in range(count)
-    ]
-    for fetch in fetches:
-        fetch.start()
+            out_ref[index, columns, rows] = (held_ref[index, rows, columns] * keep).T
+
+
+def store_kernel(plan, bits_ref, mask_ref, operators_ref, stored_ref, held_ref, masked_ref, in_semaphores, out_semaphores):
+    slabs = range(plan.kept, plan.slabs)
+    fetches = fetch_slabs(plan, slabs, bits_ref, operators_ref, held_ref, in_semaphores)
     stores = []
-    for index in range(count):
+    for index, slab in enumerate(slabs):
         fetches[index].wait()
-        mask_operator(plan, bits_ref[kept + index], mask_ref, held_ref.at[index], masked_ref.at[index])
-        store = pltpu.make_async_copy(masked_ref.at[index], stored_refs[index], out_semaphores.at[index])
+        mask_slab(plan, slab, index, bits_ref, mask_ref, held_ref, masked_ref)
+        store = pltpu.make_async_copy(masked_ref.at[index], stored_ref.at[index], out_semaphores.at[index])
         store.start()
         stores.append(store)
     for store in stores:
@@ -146,7 +158,6 @@
 
 def prepare_kernel(
     plan,
-    kept,
     bits_ref,
     mask_ref,
     field_ref,
@@ -155,15 +166,12 @@
     operators_ref,
     place_ref,
     inside_ref,
-    *refs,
+    kept_ref,
+    held_ref,
+    semaphores,
 ):
-    masked_refs, (held_ref, semaphores) = refs[:kept], refs[kept:]
-    fetches = [
-        pltpu.make_async_copy(operators_ref.at[bits_ref[index]], held_ref.at[index], semaphores.at[index])
-        for index in range(kept)
-    ]
-    for fetch in fetches:
-        fetch.start()
+    slabs = range(plan.kept)
+    fetches = fetch_slabs(plan, slabs, bits_ref, operators_ref, held_ref, semaphores)
     me = lax.axis_index("site") * plan.phonons + lax.axis_index("phonon")
     place = lax.broadcasted_iota(jnp.int32, (plan.places, LANES), 0)
     phonon = place % plan.phonons
@@ -182,16 +190,17 @@
     place_ref[0] = occupied
     place_ref[1] = strength * jnp.sqrt(height)
     place_ref[2] = jnp.where(level == plan.level_count - 1, 0.0, strength * jnp.sqrt(height + 1.0))
-    for position in range(plan.bits):
-        place_ref[3 + position] = jnp.full((plan.places, LANES), field_ref[bits_ref[position]])
-    inside = lax.broadcasted_iota(jnp.int32, (SUBLANES, plan.rows), 1)
-    weight = jnp.zeros((SUBLANES, plan.rows), jnp.float32)
+    inside = lax.broadcasted_iota(jnp.int32, (1, plan.rows), 1)
+    weight = jnp.zeros((1, plan.rows), jnp.float32)
     for local_bit in range(LBITS):
         weight = weight + coupling_ref[plan.bits + local_bit] * (inside >> local_bit & 1).astype(jnp.float32)
-    inside_ref[...] = weight
-    for index in range(kept):
-        fetches[index].wait()
-        mask_operator(plan, bits_ref[index], mask_ref, held_ref.at[index], masked_refs[index])
+    inside_ref[...] = jnp.zeros_like(inside_ref)
+    inside_ref[:1] = weight
+    for position in range(plan.bits):
+        inside_ref[pl.ds(1 + position, 1)] = jnp.full((1, plan.rows), field_ref[bits_ref[position]])
+    for slab in slabs:
+        fetches[slab].wait()
+        mask_slab(plan, slab, slab, bits_ref, mask_ref, held_ref, kept_ref)
 
 
 def flipped(values, stride):
@@ -214,7 +223,7 @@
     return pltpu.roll(tiles, by % SUBLANES, 1).reshape(places, width)
 
 
-def step(plan, vector_ref, masked_refs, place_ref, inside_ref, rounded_ref, finish, kept, ready=None, begun_ref=None):
+def step(plan, vector_ref, kept_ref, fetched_ref, place_ref, inside_ref, rounded_ref, finish, ready=None, begun_ref=None):
     span = plan.places // plan.levels_here
     for block in range(plan.lane_blocks):
         vector = vector_ref[:, pl.ds(block * LANES, LANES)]
@@ -232,52 +241,62 @@
         weight = place_ref[0] + inside_ref[:1, lanes]
         total = weight * (place_ref[1] * lower + place_ref[2] * upper)
         for position in range(plan.bits):
-            total = total + place_ref[3 + position, :1] * flipped(vector, plan.phonons << position)
+            total = total + inside_ref[pl.ds(1 + position, 1), lanes] * flipped(vector, plan.phonons << position)
         return total
 
-    def product(part, position):
-        return jnp.dot(
-            rounded_ref[:, pl.ds(position * plan.rows, plan.rows)],
-            masked_refs[position][part],
-            preferred_element_type=jnp.float32,
-        )
-
-    def begun(lanes, part):
-        total = jnp.concatenate([local(start) for start in range(lanes.start, lanes.start + plan.width, LANES)], axis=1)
-        for position in range(kept):
-            total = total + product(part, position)
+    def added(total, part, late):
+        for position in range(plan.bits):
+            slab = position * plan.parts + part
+            if late is not None and late != (slab >= plan.kept):
+                continue
+            if late:
+                ready(slab)
+            masked = kept_ref[slab] if slab < plan.kept else fetched_ref[slab - plan.kept]
+            total = total + jnp.dot(
+                rounded_ref[:, pl.ds(position * plan.rows, plan.rows)], masked, preferred_element_type=jnp.float32
+            )
         return total
+
+    def locals_of(lanes):
+        return jnp.concatenate([local(start) for start in range(lanes.start, lanes.start + plan.width, LANES)], axis=1)
 
     parts = [pl.ds(part * plan.width, plan.width) for part in range(plan.parts)]
     if ready is None:
         for part, lanes in enumerate(parts):
-            finish(lanes, begun(lanes, part))
+            finish(lanes, added(locals_of(lanes), part, None))
         return
     for part, lanes in enumerate(parts):
-        begun_ref[:, lanes] = begun(lanes, part)
+        begun_ref[:, lanes] = added(locals_of(lanes), part, False)
     for part, lanes in enumerate(parts):
-        total = begun_ref[:, lanes]
-        for position in range(kept, plan.bits):
-            ready(part, position)
-            total = total + product(part, position)
-        finish(lanes, total)
-
-
-def first_kernel(plan, kept, arrived_ref, place_ref, inside_ref, *refs):
-    masked_refs = refs[:kept]
-    stored_refs = refs[kept : plan.bits]
-    initial_ref, new_ref, sums_ref = refs[plan.bits : plan.bits + 3]
-    fetched_refs = refs[plan.bits + 3 : -2]
-    rounded_ref, semaphores = refs[-2:]
+        finish(lanes, added(begun_ref[:, lanes], part, True))
+
+
+def first_kernel(
+    plan,
+    arrived_ref,
+    place_ref,
+    inside_ref,
+    kept_ref,
+    stored_ref,
+    initial_ref,
+    new_ref,
+    sums_ref,
+    fetched_ref,
+    rounded_ref,
+    semaphores,
+):
     fetches = {}
     for part in range(plan.parts):
-        for index, (stored_ref, fetched_ref) in enumerate(zip(stored_refs, fetched_refs)):
-            fetch = pltpu.make_async_copy(stored_ref.at[part], fetched_ref.at[part], semaphores.at[index, part])
-            fetch.start()
-            fetches[part, kept + index] = fetch
-
-    def ready(part, position):
-        fetches[part, position].wait()
+        for slab in range(part, plan.slabs, plan.parts):
+            if slab >= plan.kept:
+                index = slab - plan.kept
+                fetches[slab] = pltpu.make_async_copy(
+                    stored_ref.at[index], fetched_ref.at[index], semaphores.at[index]
+                )
+                fetches[slab].start()
+
+    def ready(slab):
+        fetches[slab].wait()
 
     squares = totals_of(arrived_ref, plan.body, plan.inward, plan.groups)[0]
     inverse = 1.0 / scale_of(plan, squares)
@@ -285,7 +304,7 @@
         for block in range(plan.lane_blocks):
             part = arrived_ref[pl.ds(piece * plan.lane_blocks + block, plan.groups, stride=plan.inward), :]
             initial_ref[pl.ds(piece * plan.groups, plan.groups), pl.ds(block * LANES, LANES)] = part * inverse
-    tables = ((*masked_refs, *fetched_refs), place_ref, inside_ref, rounded_ref)
+    tables = (kept_ref, fetched_ref, place_ref, inside_ref, rounded_ref)
     squares = []
     overlap = []
     ahead = []
@@ -299,8 +318,8 @@
         new = 2.0 * total - initial_ref[:, lanes]
         ahead.append(lane_sums(new * new))
 
-    step(plan, initial_ref, *tables, finish, kept, ready, new_ref)
-    step(plan, new_ref, *tables, look_ahead, plan.bits)
+    step(plan, initial_ref, *tables, finish, ready, new_ref)
+    step(plan, new_ref, *tables, look_ahead)
     put_sums(sums_ref, [one_row(squares), one_row(overlap), one_row(ahead)], 0, 1, plan.groups)
 
 
@@ -309,9 +328,21 @@
     return sum(total[:, start : start + LANES] for start in range(0, total.shape[1], LANES))
 
 
-def onward_kernel(plan, arrived_ref, raw_ref, initial_ref, place_ref, inside_ref, *refs):
-    masked_refs = refs[: plan.bits]
-    out_ref, known_ref, rounded_ref, second_ref, third_ref = refs[plan.bits :]
+def onward_kernel(
+    plan,
+    arrived_ref,
+    raw_ref,
+    initial_ref,
+    place_ref,
+    inside_ref,
+    kept_ref,
+    fetched_ref,
+    out_ref,
+    known_ref,
+    rounded_ref,
+    second_ref,
+    third_ref,
+):
     squares, overlap, ahead, _ = totals_of(arrived_ref, 0, 1, plan.groups)
     first = 1.0 / scale_of(plan, squares)
     estimate = scale_of(plan, ahead * first * first)
@@ -321,7 +352,7 @@
     for block in range(plan.lane_blocks):
         lanes = pl.ds(block * LANES, LANES)
         second_ref[:, lanes] = raw_ref[:, lanes] * first
-    tables = (masked_refs, place_ref, inside_ref, rounded_ref)
+    tables = (kept_ref, fetched_ref, place_ref, inside_ref, rounded_ref)
     sums = [[] for _ in range(SLOTS)]
 
     def send(vector, lanes, new):
@@ -343,8 +374,8 @@
     def finish_third(lanes, total):
         send(1, lanes, 2.0 * total - second_ref[:, lanes] * second)
 
-    step(plan, second_ref, *tables, finish_second, plan.bits)
-    step(plan, third_ref, *tables, finish_third, plan.bits)
+    step(plan, second_ref, *tables, finish_second)
+    step(plan, third_ref, *tables, finish_third)
     put_sums(out_ref, [one_row(rows) for rows in sums], 2 * plan.body, plan.outward, plan.groups)
 
 
@@ -362,7 +393,7 @@
                 arrived_ref[pl.ds(first + piece * plan.lane_blocks, plan.groups, stride=plan.outward), :]
                 for piece in range(plan.pieces)
             ]
-            out_ref[pl.ds(block * LANES, LANES), :] = (jnp.concatenate(parts, axis=0) * factor).T
+            out_ref[pl.ds(block * LANES, LANES), :] = jnp.concatenate(parts, axis=0).T * factor
     moments_ref[0] = known_ref[0, 0]
     moments_ref[1] = (before_overlap * before / plan.entries)[0, 0]
     moments_ref[2] = (last_overlap * last / plan.entries)[0, 0]
@@ -397,57 +428,63 @@
         name="depart",
     )(state)
     arrived = exchange(departing, plan.groups)
-    operator = jax.ShapeDtypeStruct((plan.parts, plan.rows, plan.width), jnp.bfloat16)
-    kept = 1
-    fetched = plan.bits - kept
-    place, inside, *masked = pl.pallas_call(
-        functools.partial(prepare_kernel, plan, kept),
+    fetched = plan.slabs - plan.kept
+    kept_slabs = (plan.kept, plan.rows, plan.width)
+    fetched_slabs = (fetched, plan.rows, plan.width)
+
+    def held_slabs(count):
+        return pltpu.VMEM((count, plan.width, plan.rows), jnp.bfloat16)
+
+    place, inside, kept = pl.pallas_call(
+        functools.partial(prepare_kernel, plan),
         out_shape=[
-            jax.ShapeDtypeStruct((3 + plan.bits, plan.places, LANES), f32),
+            jax.ShapeDtypeStruct((3, plan.places, LANES), f32),
             jax.ShapeDtypeStruct((SUBLANES, plan.rows), f32),
-        ]
-        + [operator] * kept,
+            jax.ShapeDtypeStruct(kept_slabs, jnp.bfloat16),
+        ],
         in_specs=[SMEM] * 5 + [HBM],
-        out_specs=[VMEM] * (2 + kept),
-        scratch_shapes=[
-            pltpu.VMEM((kept, plan.rows, plan.rows), jnp.bfloat16),
-            pltpu.SemaphoreType.DMA((kept,)),
-        ],
+        out_specs=[VMEM] * 3,
+        scratch_shapes=[held_slabs(plan.kept), pltpu.SemaphoreType.DMA((plan.kept,))],
         compiler_params=params(50),
-        cost_estimate=cost(plan.rows * plan.rows, 4 * kept * plan.rows * plan.rows),
+        cost_estimate=cost(plan.rows * plan.rows, 4 * plan.kept * plan.rows * plan.width),
         name="prepare",
     )(site_bits, op_mask, field, site_coupling, mode_coupling, operators)
     stored = pl.pallas_call(
-        functools.partial(store_kernel, plan, kept),
-        out_shape=[operator] * fetched,
+        functools.partial(store_kernel, plan),
+        out_shape=jax.ShapeDtypeStruct(fetched_slabs, jnp.bfloat16),
         in_specs=[SMEM] * 2 + [HBM],
-        out_specs=[HBM] * fetched,
+        out_specs=HBM,
         scratch_shapes=[
-            pltpu.VMEM((fetched, plan.rows, plan.rows), jnp.bfloat16),
-            pltpu.VMEM((fetched, *operator.shape), jnp.bfloat16),
+            held_slabs(fetched),
+            pltpu.VMEM(fetched_slabs, jnp.bfloat16),
             pltpu.SemaphoreType.DMA((fetched,)),
             pltpu.SemaphoreType.DMA((fetched,)),
         ],
         compiler_params=params(60),
-        cost_estimate=cost(plan.rows * plan.rows, 4 * fetched * plan.rows * plan.rows),
+        cost_estimate=cost(plan.rows * plan.rows, 4 * fetched * plan.rows * plan.width),
         name="store",
     )(site_bits, op_mask, operators)
-    initial, raw, sums, *fetched_masked = pl.pallas_call(
-        functools.partial(first_kernel, plan, kept),
-        out_shape=[vector, vector, jax.ShapeDtypeStruct((plan.groups, LANES), f32)] + [operator] * fetched,
-        in_specs=[VMEM] * 4 + [HBM] * fetched,
-        out_specs=[VMEM] * (3 + fetched),
-        scratch_shapes=[rounded, pltpu.SemaphoreType.DMA((fetched, plan.parts))],
+    initial, raw, sums, late = pl.pallas_call(
+        functools.partial(first_kernel, plan),
+        out_shape=[
+            vector,
+            vector,
+            jax.ShapeDtypeStruct((plan.groups, LANES), f32),
+            jax.ShapeDtypeStruct(fetched_slabs, jnp.bfloat16),
+        ],
+        in_specs=[VMEM] * 4 + [HBM],
+        out_specs=[VMEM] * 4,
+        scratch_shapes=[rounded, pltpu.SemaphoreType.DMA((fetched,))],
         compiler_params=params(46),
-        cost_estimate=cost(work, 4 * plan.places * plan.rows),
+        cost_estimate=cost(2 * work, 4 * plan.places * plan.rows),
         name="first",
-    )(arrived, place, inside, *masked, *stored)
-    tables = (place, inside, *masked, *fetched_masked)
+    )(arrived, place, inside, kept, stored)
+    tables = (place, inside, kept, late)
     sums = exchange(sums, plan.groups)
     departing, told = pl.pallas_call(
         functools.partial(onward_kernel, plan),
         out_shape=[outward, known],
-        in_specs=[VMEM] * (5 + plan.bits),
+        in_specs=[VMEM] * 7,
         out_specs=[VMEM] * 2,
         scratch_shapes=[rounded, working, working],
         compiler_params=params(32),

time: 74.2 us -> 74 us (level)
  Pallas kernels: 18 us -> 16.9 us
  waiting for transfers between devices: 7.56 us -> 8.43 us
    pallas_call x3, Pallas kernels: 12.2 us -> 11.1 us  [the longest x1 4.41 us: shards(): pl.pallas_call(functools.partial(store_kernel, plan), out_shape=jax.Shape...]
    all_to_all x1, waiting for transfers between devices: 7.56 us -> 8.43 us  [exchange(): return lax.all_to_all(shaped, AXES, 0, 0, tiled=True).reshape(values.shape)]
  transfers between devices with their start and end apart: 1 -> 1, of which waited for: 1 -> 1; matrix products, arithmetic and copies ran while one was open for 0% -> 0% of each run, Pallas kernels for 11% -> 10%
where the time goes in v13:
time: 74 us; the launch traced here: 73.6 us
  blocking collectives  40.2 us (54%)
  Pallas kernels  16.9 us (23%)
  waiting for transfers between devices  8.43 us (11%)
  starting transfers between devices  7.3 us (10%)
  between operations  0.75 us (1%)
    all_to_all x2, blocking collectives, exchange(): return lax.all_to_all(shaped, AXES, 0, 0, tiled=True).reshape(values.shape)  40.2 us
    all_to_all x1, waiting for transfers between devices, exchange(): return lax.all_to_all(shaped, AXES, 0, 0, tiled=True).reshape(values.shape)  8.43 us
    all_to_all x1, starting transfers between devices, exchange(): return lax.all_to_all(shaped, AXES, 0, 0, tiled=True).reshape(values.shape)  7.3 us
    pallas_call x1, Pallas kernels, shards(): pl.pallas_call(functools.partial(store_kernel, plan), out_shape=jax.Shape...  4.41 us
    pallas_call x1, Pallas kernels, shards(): pl.pallas_call(functools.partial(first_kernel, plan), out_shape=[vector,...  3.83 us
    pallas_call x1, Pallas kernels, shards(): pl.pallas_call(functools.partial(prepare_kernel, plan), out_shape=[jax.Sh...  2.87 us
    pallas_call x1, Pallas kernels, shards(): pl.pallas_call(functools.partial(onward_kernel, plan), out_shape=[outward...  2.43 us
    pallas_call x1, Pallas kernels, shards(): pl.pallas_call(functools.partial(depart_kernel, plan), out_shape=inward,...  2.12 us
  transfers between devices with their start and end apart: 1, of which 1 were waited for; matrix products, arithmetic and copies ran while one was open for 0% of the time, Pallas kernels for 10%

profile of v13, /device:TPU:0, one launch (start us, length us, event | category | flops | bytes accessed | tf_op | source)
XLA Modules:
  0.0 73.6 jit_solution(8256718116187152985)
XLA Ops:
  0.6 2.1 %depart.1 = f32[1056,128]{1,0:T(8,128)} custom-call(f32[1024,128]{1,0:T(8,128)} %state_ref.1), custom_call_target="tpu_custom_call" | custom-call | tf_op jit(solution)/shard_map/depart/pallas_call | solution.py:421
  2.8 7.3 %all-to-all-start = ((f32[32,33,1,128]{3,2,1,0:T(1,128)}), f32[32,33,1,128]{3,2,1,0:T(1,128)S(1)}, u32[]{:S(2)}, u32[]{:S(2)}) async-start(f32[32,33,1,128]{3,2,1,0:T(1,128)} %bitcast.13), calls=%async_computation | async-start | bytes 1081344 | tf_op jit(solution)/shard_map/all_to_all | solution.py:404
  10.1 0.0 copy-start
  10.1 0.0 copy-start.1
  10.1 0.0 copy-start.2
  10.1 0.0 copy-start.3
  10.1 0.0 copy-start.4
  10.1 4.4 %store.1.stored_ref = bf16[7,1024,256]{2,1,0:T(8,128)(2,1)} custom-call(s32[3]{0:T(128)} %bits_ref.3, s32[3,8,8]{2,1,0:T(8,128)} %mask_ref.3, bf16[3,1024,1024]{2,1,0:T(8,128)(2,1)} %operators_ref.3), custom_call_target="tpu_custom_call" | custom-call | flops 1048576 | bytes 7340032 | tf_op jit(solution)/shard_map/store/pallas_call | solution.py:452
  14.6 0.0 copy-done
  14.6 0.0 copy-done.1
  14.6 0.0 copy-done.2
  14.6 0.0 copy-done.3
  14.6 0.0 copy-done.4
  14.6 2.9 %prepare.1 = (f32[3,128,128]{2,1,0:T(8,128)S(1)}, f32[8,1024]{1,0:T(8,128)S(1)}, bf16[5,1024,256]{2,1,0:T(8,128)(2,1)S(1)}) custom-call(s32[3]{0:T(128)S(1)} %copy-done.1, s32[3,8,8]{2,1,0:T(8,128)S(1)} %copy-done, f32[3]{0:T(128)S(1)} %copy-done.2, f32[13]{0:T(128)S(1)} %copy-done.3, f32[64]{0:T(128)S(1)} %copy-done.4, bf16[3,1024,1024]{2,1,0:T(8,128)(2,1)} %operators_ref.3), custom_call_target="tpu_custom_call" | custom-call | flops 1048576 | bytes 5242880 | tf_op jit(solution)/shard_map/prepare/pallas_call | solution.py:438
  17.5 8.4 %all-to-all-done = f32[32,33,1,128]{3,2,1,0:T(1,128)S(1)} async-done(((f32[32,33,1,128]{3,2,1,0:T(1,128)}), f32[32,33,1,128]{3,2,1,0:T(1,128)S(1)}, u32[]{:S(2)}, u32[]{:S(2)}) %all-to-all-start) | async-done | bytes 540704 | tf_op jit(solution)/shard_map/all_to_all | solution.py:404
  25.9 3.8 %first.1 = (f32[128,1024]{1,0:T(8,128)S(1)}, f32[128,1024]{1,0:T(8,128)S(1)}, f32[32,128]{1,0:T(8,128)S(1)}, bf16[7,1024,256]{2,1,0:T(8,128)(2,1)S(1)}) custom-call(f32[1056,128]{1,0:T(8,128)S(1)} %bitcast.9, f32[3,128,128]{2,1,0:T(8,128)S(1)} %get-tuple-element.15.place_ref, f32[8,1024]{1,0:T(8,128)S(1)} %get-tuple-element.16.inside_ref, ...), custom_call_target="tpu_custom_call" | custom-call | flops 1610612736 | bytes 524288 | tf_op jit(solution)/shard_map/first/pallas_call | solution.py:467
  29.7 10.1 %all_to_all.15 = f32[32,1,1,128]{3,2,1,0:T(1,128)S(1)} all-to-all(f32[32,1,1,128]{3,2,1,0:T(1,128)S(1)} %bitcast.12), channel_id=1, replica_groups=mesh['site'=8,'phonon'=4] {'site','phonon'}, dimensions={0} | all-to-all | bytes 32768 | tf_op jit(solution)/shard_map/all_to_all | solution.py:404
  39.8 2.4 %onward.1 = (f32[2080,128]{1,0:T(8,128)S(1)}, f32[8,128]{1,0:T(8,128)S(1)}) custom-call(f32[32,128]{1,0:T(8,128)S(1)} %bitcast.11, f32[128,1024]{1,0:T(8,128)S(1)} %get-tuple-element.19.raw_ref, f32[128,1024]{1,0:T(8,128)S(1)} %get-tuple-element.20.initial_ref, f32[3,128,128]{2,1,0:T(8,128)S(1)} %get-tuple-element.15.place_ref, ...), custom_call_target="tpu_custom_call" | custom-call | flops 1610612736 | bytes 1048576 | tf_op jit(solution)/shard_map/onward/pallas_call | solution.py:484
  42.3 30.1 %all_to_all.16 = f32[32,65,1,128]{3,2,1,0:T(1,128)S(1)} all-to-all(f32[32,65,1,128]{3,2,1,0:T(1,128)S(1)} %bitcast.10), channel_id=1, replica_groups=mesh['site'=8,'phonon'=4] {'site','phonon'}, dimensions={0} | all-to-all | bytes 2129920 | tf_op jit(solution)/shard_map/all_to_all | solution.py:404
  72.4 1.3 %arrive.1 = (f32[1024,128]{1,0:T(8,128)}, f32[1024,128]{1,0:T(8,128)}, f32[3]{0:T(128)}) custom-call(f32[2080,128]{1,0:T(8,128)S(1)} %bitcast.8, f32[8,128]{1,0:T(8,128)S(1)} %get-tuple-element.23.known_ref), custom_call_target="tpu_custom_call" | custom-call | tf_op jit(solution)/shard_map/arrive/pallas_call | solution.py:495
Async XLA Ops:
  2.8 23.2 %all-to-all-start = ((f32[32,33,1,128]{3,2,1,0:T(1,128)}), f32[32,33,1,128]{3,2,1,0:T(1,128)S(1)}, u32[]{:S(2)}, u32[]{:S(2)}) async-start(f32[32,33,1,128]{3,2,1,0:T(1,128)} %bitcast.13), calls=%async_computation | async-start | bytes 1081344 | tf_op jit(solution)/shard_map/all_to_all | solution.py:404
  10.1 4.5 %copy-start = (s32[3,8,8]{2,1,0:T(8,128)S(1)}, s32[3,8,8]{2,1,0:T(8,128)}, u32[]{:S(2)}) copy-start(s32[3,8,8]{2,1,0:T(8,128)} %mask_ref.3) | copy-start | bytes 2308
  10.1 4.5 %copy-start.1 = (s32[3]{0:T(128)S(1)}, s32[3]{0:T(128)}, u32[]{:S(2)}) copy-start(s32[3]{0:T(128)} %bits_ref.3) | copy-start | bytes 40
  10.1 4.5 %copy-start.2 = (f32[3]{0:T(128)S(1)}, f32[3]{0:T(128)}, u32[]{:S(2)}) copy-start(f32[3]{0:T(128)} %field_ref.1) | copy-start | bytes 40
  10.1 4.5 %copy-start.3 = (f32[13]{0:T(128)S(1)}, f32[13]{0:T(128)}, u32[]{:S(2)}) copy-start(f32[13]{0:T(128)} %coupling_ref.1) | copy-start | bytes 160
  10.1 4.5 %copy-start.4 = (f32[64]{0:T(128)S(1)}, f32[64]{0:T(128)}, u32[]{:S(2)}) copy-start(f32[64]{0:T(128)} %mode_ref.1) | copy-start | bytes 772

commit v14 on v13

--- a/solution.py
+++ b/solution.py
@@ -45,7 +45,7 @@
         self.width = 2 * LANES
         self.parts = rows // self.width
         self.slabs = self.bits * self.parts
-        self.kept = min(self.parts + 1, self.slabs - 1)
+        self.kept = min(5, self.slabs - 1)
         self.entries = float(rows * columns * self.groups)
 
     def fits(self):
@@ -120,7 +120,7 @@
 def fetch_slabs(plan, slabs, bits_ref, operators_ref, held_ref, semaphores):
     fetches = []
     for index, slab in enumerate(slabs):
-        bit, part = divmod(slab, plan.parts)
+        part, bit = divmod(slab, plan.bits)
         rows = pl.ds(part * plan.width, plan.width)
         fetch = pltpu.make_async_copy(
             operators_ref.at[bits_ref[bit], rows, :], held_ref.at[index], semaphores.at[index]
@@ -131,7 +131,7 @@
 
 
 def mask_slab(plan, slab, index, bits_ref, mask_ref, held_ref, out_ref):
-    bit, part = divmod(slab, plan.parts)
+    part, bit = divmod(slab, plan.bits)
     chosen = bits_ref[bit]
     for start in range(0, plan.width, plan.edge):
         across = (part * plan.width + start) // plan.edge
@@ -223,14 +223,15 @@
     return pltpu.roll(tiles, by % SUBLANES, 1).reshape(places, width)
 
 
-def step(plan, vector_ref, kept_ref, fetched_ref, place_ref, inside_ref, rounded_ref, finish, ready=None, begun_ref=None):
+def put_rounded(plan, rounded_ref, vector, start):
+    for position in range(plan.bits):
+        rounded_ref[:, pl.ds(position * plan.rows + start, vector.shape[1])] = flipped(
+            vector, plan.phonons << position
+        ).astype(jnp.bfloat16)
+
+
+def step(plan, vector_ref, rounded_ref, kept_ref, fetched_ref, place_ref, inside_ref, finish, ready=None, begun_ref=None):
     span = plan.places // plan.levels_here
-    for block in range(plan.lane_blocks):
-        vector = vector_ref[:, pl.ds(block * LANES, LANES)]
-        for position in range(plan.bits):
-            rounded_ref[:, pl.ds(position * plan.rows + block * LANES, LANES)] = flipped(
-                vector, plan.phonons << position
-            ).astype(jnp.bfloat16)
 
     def local(start):
         lanes = pl.ds(start, LANES)
@@ -245,16 +246,19 @@
         return total
 
     def added(total, part, late):
-        for position in range(plan.bits):
-            slab = position * plan.parts + part
-            if late is not None and late != (slab >= plan.kept):
+        for ref, low, high in ((kept_ref, 0, plan.kept), (fetched_ref, plan.kept, plan.slabs)):
+            fetched = low > 0
+            begin = max(part * plan.bits, low)
+            count = min((part + 1) * plan.bits, high) - begin
+            if count <= 0 or late not in (None, fetched):
                 continue
             if late:
-                ready(slab)
-            masked = kept_ref[slab] if slab < plan.kept else fetched_ref[slab - plan.kept]
-            total = total + jnp.dot(
-                rounded_ref[:, pl.ds(position * plan.rows, plan.rows)], masked, preferred_element_type=jnp.float32
-            )
+                for slab in range(begin, begin + count):
+                    ready(slab)
+            first = begin - part * plan.bits
+            masked = ref[pl.ds(begin - low, count)].reshape(count * plan.rows, plan.width)
+            operand = rounded_ref[:, pl.ds(first * plan.rows, count * plan.rows)]
+            total = total + jnp.dot(operand, masked, preferred_element_type=jnp.float32)
         return total
 
     def locals_of(lanes):
@@ -283,34 +287,36 @@
     sums_ref,
     fetched_ref,
     rounded_ref,
+    ahead_ref,
     semaphores,
 ):
     fetches = {}
-    for part in range(plan.parts):
-        for slab in range(part, plan.slabs, plan.parts):
-            if slab >= plan.kept:
-                index = slab - plan.kept
-                fetches[slab] = pltpu.make_async_copy(
-                    stored_ref.at[index], fetched_ref.at[index], semaphores.at[index]
-                )
-                fetches[slab].start()
+    for slab in range(plan.kept, plan.slabs):
+        index = slab - plan.kept
+        fetches[slab] = pltpu.make_async_copy(stored_ref.at[index], fetched_ref.at[index], semaphores.at[index])
+        fetches[slab].start()
 
     def ready(slab):
         fetches[slab].wait()
 
     squares = totals_of(arrived_ref, plan.body, plan.inward, plan.groups)[0]
     inverse = 1.0 / scale_of(plan, squares)
-    for piece in range(plan.pieces):
-        for block in range(plan.lane_blocks):
-            part = arrived_ref[pl.ds(piece * plan.lane_blocks + block, plan.groups, stride=plan.inward), :]
-            initial_ref[pl.ds(piece * plan.groups, plan.groups), pl.ds(block * LANES, LANES)] = part * inverse
-    tables = (kept_ref, fetched_ref, place_ref, inside_ref, rounded_ref)
+    for block in range(plan.lane_blocks):
+        parts = [
+            arrived_ref[pl.ds(piece * plan.lane_blocks + block, plan.groups, stride=plan.inward), :]
+            for piece in range(plan.pieces)
+        ]
+        vector = jnp.concatenate(parts, axis=0) * inverse
+        initial_ref[:, pl.ds(block * LANES, LANES)] = vector
+        put_rounded(plan, rounded_ref, vector, block * LANES)
+    tables = (kept_ref, fetched_ref, place_ref, inside_ref)
     squares = []
     overlap = []
     ahead = []
 
     def finish(lanes, new):
         new_ref[:, lanes] = new
+        put_rounded(plan, ahead_ref, new, lanes.start)
         squares.append(lane_sums(new * new))
         overlap.append(lane_sums(new * initial_ref[:, lanes]))
 
@@ -318,8 +324,8 @@
         new = 2.0 * total - initial_ref[:, lanes]
         ahead.append(lane_sums(new * new))
 
-    step(plan, initial_ref, *tables, finish, ready, new_ref)
-    step(plan, new_ref, *tables, look_ahead)
+    step(plan, initial_ref, rounded_ref, *tables, finish, ready, new_ref)
+    step(plan, new_ref, ahead_ref, *tables, look_ahead)
     put_sums(sums_ref, [one_row(squares), one_row(overlap), one_row(ahead)], 0, 1, plan.groups)
 
 
@@ -340,6 +346,7 @@
     out_ref,
     known_ref,
     rounded_ref,
+    ahead_ref,
     second_ref,
     third_ref,
 ):
@@ -351,8 +358,10 @@
     known_ref[1:, :] = jnp.broadcast_to(estimate, (SUBLANES - 1, LANES))
     for block in range(plan.lane_blocks):
         lanes = pl.ds(block * LANES, LANES)
-        second_ref[:, lanes] = raw_ref[:, lanes] * first
-    tables = (kept_ref, fetched_ref, place_ref, inside_ref, rounded_ref)
+        vector = raw_ref[:, lanes] * first
+        second_ref[:, lanes] = vector
+        put_rounded(plan, rounded_ref, vector, block * LANES)
+    tables = (kept_ref, fetched_ref, place_ref, inside_ref)
     sums = [[] for _ in range(SLOTS)]
 
     def send(vector, lanes, new):
@@ -368,14 +377,16 @@
 
     def finish_second(lanes, total):
         new = 2.0 * total - initial_ref[:, lanes] * first
-        third_ref[:, lanes] = new * second
+        vector = new * second
+        third_ref[:, lanes] = vector
+        put_rounded(plan, ahead_ref, vector, lanes.start)
         send(0, lanes, new)
 
     def finish_third(lanes, total):
         send(1, lanes, 2.0 * total - second_ref[:, lanes] * second)
 
-    step(plan, second_ref, *tables, finish_second)
-    step(plan, third_ref, *tables, finish_third)
+    step(plan, second_ref, rounded_ref, *tables, finish_second)
+    step(plan, third_ref, ahead_ref, *tables, finish_third)
     put_sums(out_ref, [one_row(rows) for rows in sums], 2 * plan.body, plan.outward, plan.groups)
 
 
@@ -474,7 +485,7 @@
         ],
         in_specs=[VMEM] * 4 + [HBM],
         out_specs=[VMEM] * 4,
-        scratch_shapes=[rounded, pltpu.SemaphoreType.DMA((fetched,))],
+        scratch_shapes=[rounded, rounded, pltpu.SemaphoreType.DMA((fetched,))],
         compiler_params=params(46),
         cost_estimate=cost(2 * work, 4 * plan.places * plan.rows),
         name="first",
@@ -486,7 +497,7 @@
         out_shape=[outward, known],
         in_specs=[VMEM] * 7,
         out_specs=[VMEM] * 2,
-        scratch_shapes=[rounded, working, working],
+        scratch_shapes=[rounded, rounded, working, working],
         compiler_params=params(32),
         cost_estimate=cost(2 * work, 8 * plan.places * plan.rows),
         name="onward",

time: 74 us -> 73.8 us (level)
  no operation moved by 1% of the time
where the time goes in v14:
time: 73.8 us; the launch traced here: 73.4 us
  blocking collectives  40.2 us (54%)
  Pallas kernels  16.7 us (23%)
  waiting for transfers between devices  8.43 us (11%)
  starting transfers between devices  7.3 us (10%)
  between operations  0.75 us (1%)
    all_to_all x2, blocking collectives, exchange(): return lax.all_to_all(shaped, AXES, 0, 0, tiled=True).reshape(values.shape)  40.2 us
    all_to_all x1, waiting for transfers between devices, exchange(): return lax.all_to_all(shaped, AXES, 0, 0, tiled=True).reshape(values.shape)  8.43 us
    all_to_all x1, starting transfers between devices, exchange(): return lax.all_to_all(shaped, AXES, 0, 0, tiled=True).reshape(values.shape)  7.3 us
    pallas_call x1, Pallas kernels, shards(): pl.pallas_call(functools.partial(store_kernel, plan), out_shape=jax.Shape...  4.41 us
    pallas_call x1, Pallas kernels, shards(): pl.pallas_call(functools.partial(first_kernel, plan), out_shape=[vector,...  3.7 us
    pallas_call x1, Pallas kernels, shards(): pl.pallas_call(functools.partial(prepare_kernel, plan), out_shape=[jax.Sh...  2.87 us
    pallas_call x1, Pallas kernels, shards(): pl.pallas_call(functools.partial(onward_kernel, plan), out_shape=[outward...  2.36 us
    pallas_call x1, Pallas kernels, shards(): pl.pallas_call(functools.partial(depart_kernel, plan), out_shape=inward,...  2.12 us
  transfers between devices with their start and end apart: 1, of which 1 were waited for; matrix products, arithmetic and copies ran while one was open for 0% of the time, Pallas kernels for 10%

profile of v14, /device:TPU:0, one launch (start us, length us, event | category | flops | bytes accessed | tf_op | source)
XLA Modules:
  0.0 73.4 jit_solution(2866592900297058388)
XLA Ops:
  0.6 2.1 %depart.1 = f32[1056,128]{1,0:T(8,128)} custom-call(f32[1024,128]{1,0:T(8,128)} %state_ref.1), custom_call_target="tpu_custom_call" | custom-call | tf_op jit(solution)/shard_map/depart/pallas_call | solution.py:432
  2.8 7.3 %all-to-all-start = ((f32[32,33,1,128]{3,2,1,0:T(1,128)}), f32[32,33,1,128]{3,2,1,0:T(1,128)S(1)}, u32[]{:S(2)}, u32[]{:S(2)}) async-start(f32[32,33,1,128]{3,2,1,0:T(1,128)} %bitcast.13), calls=%async_computation | async-start | bytes 1081344 | tf_op jit(solution)/shard_map/all_to_all | solution.py:415
  10.1 0.0 copy-start
  10.1 0.0 copy-start.1
  10.1 0.0 copy-start.2
  10.1 0.0 copy-start.3
  10.1 0.0 copy-start.4
  10.1 4.4 %store.1.stored_ref = bf16[7,1024,256]{2,1,0:T(8,128)(2,1)} custom-call(s32[3]{0:T(128)} %bits_ref.3, s32[3,8,8]{2,1,0:T(8,128)} %mask_ref.3, bf16[3,1024,1024]{2,1,0:T(8,128)(2,1)} %operators_ref.3), custom_call_target="tpu_custom_call" | custom-call | flops 1048576 | bytes 7340032 | tf_op jit(solution)/shard_map/store/pallas_call | solution.py:463
  14.6 0.0 copy-done
  14.6 0.0 copy-done.1
  14.6 0.0 copy-done.2
  14.6 0.0 copy-done.3
  14.6 0.0 copy-done.4
  14.6 2.9 %prepare.1 = (f32[3,128,128]{2,1,0:T(8,128)S(1)}, f32[8,1024]{1,0:T(8,128)S(1)}, bf16[5,1024,256]{2,1,0:T(8,128)(2,1)S(1)}) custom-call(s32[3]{0:T(128)S(1)} %copy-done.1, s32[3,8,8]{2,1,0:T(8,128)S(1)} %copy-done, f32[3]{0:T(128)S(1)} %copy-done.2, f32[13]{0:T(128)S(1)} %copy-done.3, f32[64]{0:T(128)S(1)} %copy-done.4, bf16[3,1024,1024]{2,1,0:T(8,128)(2,1)} %operators_ref.3), custom_call_target="tpu_custom_call" | custom-call | flops 1048576 | bytes 5242880 | tf_op jit(solution)/shard_map/prepare/pallas_call | solution.py:449
  17.5 8.4 %all-to-all-done = f32[32,33,1,128]{3,2,1,0:T(1,128)S(1)} async-done(((f32[32,33,1,128]{3,2,1,0:T(1,128)}), f32[32,33,1,128]{3,2,1,0:T(1,128)S(1)}, u32[]{:S(2)}, u32[]{:S(2)}) %all-to-all-start) | async-done | bytes 540704 | tf_op jit(solution)/shard_map/all_to_all | solution.py:415
  25.9 3.7 %first.1 = (f32[128,1024]{1,0:T(8,128)S(1)}, f32[128,1024]{1,0:T(8,128)S(1)}, f32[32,128]{1,0:T(8,128)S(1)}, bf16[7,1024,256]{2,1,0:T(8,128)(2,1)S(1)}) custom-call(f32[1056,128]{1,0:T(8,128)S(1)} %bitcast.9, f32[3,128,128]{2,1,0:T(8,128)S(1)} %get-tuple-element.15.place_ref, f32[8,1024]{1,0:T(8,128)S(1)} %get-tuple-element.16.inside_ref, ...), custom_call_target="tpu_custom_call" | custom-call | flops 1610612736 | bytes 524288 | tf_op jit(solution)/shard_map/first/pallas_call | solution.py:478
  29.6 10.1 %all_to_all.15 = f32[32,1,1,128]{3,2,1,0:T(1,128)S(1)} all-to-all(f32[32,1,1,128]{3,2,1,0:T(1,128)S(1)} %bitcast.12), channel_id=1, replica_groups=mesh['site'=8,'phonon'=4] {'site','phonon'}, dimensions={0} | all-to-all | bytes 32768 | tf_op jit(solution)/shard_map/all_to_all | solution.py:415
  39.7 2.4 %onward.1 = (f32[2080,128]{1,0:T(8,128)S(1)}, f32[8,128]{1,0:T(8,128)S(1)}) custom-call(f32[32,128]{1,0:T(8,128)S(1)} %bitcast.11, f32[128,1024]{1,0:T(8,128)S(1)} %get-tuple-element.19.raw_ref, f32[128,1024]{1,0:T(8,128)S(1)} %get-tuple-element.20.initial_ref, f32[3,128,128]{2,1,0:T(8,128)S(1)} %get-tuple-element.15.place_ref, ...), custom_call_target="tpu_custom_call" | custom-call | flops 1610612736 | bytes 1048576 | tf_op jit(solution)/shard_map/onward/pallas_call | solution.py:495
  42.1 30.1 %all_to_all.16 = f32[32,65,1,128]{3,2,1,0:T(1,128)S(1)} all-to-all(f32[32,65,1,128]{3,2,1,0:T(1,128)S(1)} %bitcast.10), channel_id=1, replica_groups=mesh['site'=8,'phonon'=4] {'site','phonon'}, dimensions={0} | all-to-all | bytes 2129920 | tf_op jit(solution)/shard_map/all_to_all | solution.py:415
  72.2 1.3 %arrive.1 = (f32[1024,128]{1,0:T(8,128)}, f32[1024,128]{1,0:T(8,128)}, f32[3]{0:T(128)}) custom-call(f32[2080,128]{1,0:T(8,128)S(1)} %bitcast.8, f32[8,128]{1,0:T(8,128)S(1)} %get-tuple-element.23.known_ref), custom_call_target="tpu_custom_call" | custom-call | tf_op jit(solution)/shard_map/arrive/pallas_call | solution.py:506
Async XLA Ops:
  2.8 23.2 %all-to-all-start = ((f32[32,33,1,128]{3,2,1,0:T(1,128)}), f32[32,33,1,128]{3,2,1,0:T(1,128)S(1)}, u32[]{:S(2)}, u32[]{:S(2)}) async-start(f32[32,33,1,128]{3,2,1,0:T(1,128)} %bitcast.13), calls=%async_computation | async-start | bytes 1081344 | tf_op jit(solution)/shard_map/all_to_all | solution.py:415
  10.1 4.5 %copy-start = (s32[3,8,8]{2,1,0:T(8,128)S(1)}, s32[3,8,8]{2,1,0:T(8,128)}, u32[]{:S(2)}) copy-start(s32[3,8,8]{2,1,0:T(8,128)} %mask_ref.3) | copy-start | bytes 2308
  10.1 4.5 %copy-start.1 = (s32[3]{0:T(128)S(1)}, s32[3]{0:T(128)}, u32[]{:S(2)}) copy-start(s32[3]{0:T(128)} %bits_ref.3) | copy-start | bytes 40
  10.1 4.5 %copy-start.2 = (f32[3]{0:T(128)S(1)}, f32[3]{0:T(128)}, u32[]{:S(2)}) copy-start(f32[3]{0:T(128)} %field_ref.1) | copy-start | bytes 40
  10.1 4.5 %copy-start.3 = (f32[13]{0:T(128)S(1)}, f32[13]{0:T(128)}, u32[]{:S(2)}) copy-start(f32[13]{0:T(128)} %coupling_ref.1) | copy-start | bytes 160
  10.1 4.5 %copy-start.4 = (f32[64]{0:T(128)S(1)}, f32[64]{0:T(128)}, u32[]{:S(2)}) copy-start(f32[64]{0:T(128)} %mode_ref.1) | copy-start | bytes 772

commit v15 on v14

--- a/solution.py
+++ b/solution.py
@@ -94,19 +94,16 @@
 
 
 def depart_kernel(plan, state_ref, out_ref, held_ref, semaphores):
-    half = plan.rows // 2
-    fetches = [
-        pltpu.make_async_copy(
-            state_ref.at[pl.ds(index * half, half), :], held_ref.at[pl.ds(index * half, half), :], semaphores.at[index]
-        )
-        for index in range(2)
-    ]
+    fetches = []
+    for part in range(plan.parts):
+        rows = pl.ds(part * plan.width, plan.width)
+        fetches.append(pltpu.make_async_copy(state_ref.at[rows, :], held_ref.at[rows, :], semaphores.at[part]))
     for fetch in fetches:
         fetch.start()
     sums = jnp.zeros((1, LANES), jnp.float32)
     for block in range(plan.lane_blocks):
-        if block * LANES % half == 0:
-            fetches[block * LANES // half].wait()
+        if block * LANES % plan.width == 0:
+            fetches[block * LANES // plan.width].wait()
         tile = held_ref[pl.ds(block * LANES, LANES), :]
         sums = sums + lane_sums(tile * tile)
         turned = tile.T
@@ -390,14 +387,15 @@
     put_sums(out_ref, [one_row(rows) for rows in sums], 2 * plan.body, plan.outward, plan.groups)
 
 
-def arrive_kernel(plan, arrived_ref, known_ref, before_ref, last_ref, moments_ref):
+def arrive_kernel(plan, arrived_ref, known_ref, before_ref, last_ref, moments_ref, turned_ref, semaphore):
     before_squares, before_overlap, last_squares, last_overlap = totals_of(
         arrived_ref, 2 * plan.body, plan.outward, plan.groups
     )
     before = 1.0 / scale_of(plan, before_squares)
     back = known_ref[1:2, :1] * before
     last = back / scale_of(plan, last_squares * back * back)
-    for vector, (out_ref, factor) in enumerate(((before_ref, before), (last_ref, last))):
+    leave = pltpu.make_async_copy(turned_ref, before_ref, semaphore)
+    for vector, (out_ref, factor) in enumerate(((turned_ref, before), (last_ref, last))):
         for block in range(plan.lane_blocks):
             first = vector * plan.body + block
             parts = [
@@ -405,9 +403,12 @@
                 for piece in range(plan.pieces)
             ]
             out_ref[pl.ds(block * LANES, LANES), :] = jnp.concatenate(parts, axis=0).T * factor
+        if vector == 0:
+            leave.start()
     moments_ref[0] = known_ref[0, 0]
     moments_ref[1] = (before_overlap * before / plan.entries)[0, 0]
     moments_ref[2] = (last_overlap * last / plan.entries)[0, 0]
+    leave.wait()
 
 
 def exchange(values, count):
@@ -434,7 +435,7 @@
         out_shape=inward,
         in_specs=[HBM],
         out_specs=VMEM,
-        scratch_shapes=[pltpu.VMEM((plan.rows, plan.columns), f32), pltpu.SemaphoreType.DMA((2,))],
+        scratch_shapes=[pltpu.VMEM((plan.rows, plan.columns), f32), pltpu.SemaphoreType.DMA((plan.parts,))],
         compiler_params=params(60),
         name="depart",
     )(state)
@@ -507,7 +508,8 @@
         functools.partial(arrive_kernel, plan),
         out_shape=[held, held, jax.ShapeDtypeStruct((STEPS,), f32)],
         in_specs=[VMEM] * 2,
-        out_specs=[VMEM, VMEM, SMEM],
+        out_specs=[HBM, VMEM, SMEM],
+        scratch_shapes=[pltpu.VMEM((plan.rows, plan.columns), f32), pltpu.SemaphoreType.DMA],
         compiler_params=params(16),
         name="arrive",
     )(arrived, told)

time: 73.8 us -> 74.5 us (level)
  Pallas kernels: 16.7 us -> 17.5 us
where the time goes in v15:
time: 74.5 us; the launch traced here: 74.2 us
  blocking collectives  40.2 us (54%)
  Pallas kernels  17.5 us (23%)
  waiting for transfers between devices  8.43 us (11%)
  starting transfers between devices  7.3 us (10%)
  between operations  0.75 us (1%)
    all_to_all x2, blocking collectives, exchange(): return lax.all_to_all(shaped, AXES, 0, 0, tiled=True).reshape(values.shape)  40.2 us
    all_to_all x1, waiting for transfers between devices, exchange(): return lax.all_to_all(shaped, AXES, 0, 0, tiled=True).reshape(values.shape)  8.43 us
    all_to_all x1, starting transfers between devices, exchange(): return lax.all_to_all(shaped, AXES, 0, 0, tiled=True).reshape(values.shape)  7.3 us
    pallas_call x1, Pallas kernels, shards(): pl.pallas_call(functools.partial(store_kernel, plan), out_shape=jax.Shape...  4.41 us
    pallas_call x1, Pallas kernels, shards(): pl.pallas_call(functools.partial(first_kernel, plan), out_shape=[vector,...  3.7 us
    pallas_call x1, Pallas kernels, shards(): pl.pallas_call(functools.partial(prepare_kernel, plan), out_shape=[jax.Sh...  2.87 us
    pallas_call x1, Pallas kernels, shards(): pl.pallas_call(functools.partial(onward_kernel, plan), out_shape=[outward...  2.36 us
    pallas_call x1, Pallas kernels, shards(): pl.pallas_call(functools.partial(depart_kernel, plan), out_shape=inward,...  2.26 us
  transfers between devices with their start and end apart: 1, of which 1 were waited for; matrix products, arithmetic and copies ran while one was open for 0% of the time, Pallas kernels for 10%

profile of v15, /device:TPU:0, one launch (start us, length us, event | category | flops | bytes accessed | tf_op | source)
XLA Modules:
  0.0 74.2 jit_solution(3782083584113771673)
XLA Ops:
  0.6 2.3 %depart.1 = f32[1056,128]{1,0:T(8,128)} custom-call(f32[1024,128]{1,0:T(8,128)} %state_ref.1), custom_call_target="tpu_custom_call" | custom-call | tf_op jit(solution)/shard_map/depart/pallas_call | solution.py:433
  2.9 7.3 %all-to-all-start = ((f32[32,33,1,128]{3,2,1,0:T(1,128)}), f32[32,33,1,128]{3,2,1,0:T(1,128)S(1)}, u32[]{:S(2)}, u32[]{:S(2)}) async-start(f32[32,33,1,128]{3,2,1,0:T(1,128)} %bitcast.13), calls=%async_computation | async-start | bytes 1081344 | tf_op jit(solution)/shard_map/all_to_all | solution.py:416
  10.2 0.0 copy-start
  10.2 0.0 copy-start.1
  10.2 0.0 copy-start.2
  10.2 0.0 copy-start.3
  10.3 0.0 copy-start.4
  10.3 4.4 %store.1.stored_ref = bf16[7,1024,256]{2,1,0:T(8,128)(2,1)} custom-call(s32[3]{0:T(128)} %bits_ref.3, s32[3,8,8]{2,1,0:T(8,128)} %mask_ref.3, bf16[3,1024,1024]{2,1,0:T(8,128)(2,1)} %operators_ref.3), custom_call_target="tpu_custom_call" | custom-call | flops 1048576 | bytes 7340032 | tf_op jit(solution)/shard_map/store/pallas_call | solution.py:464
  14.7 0.0 copy-done
  14.7 0.0 copy-done.1
  14.7 0.0 copy-done.2
  14.7 0.0 copy-done.3
  14.7 0.0 copy-done.4
  14.7 2.9 %prepare.1 = (f32[3,128,128]{2,1,0:T(8,128)S(1)}, f32[8,1024]{1,0:T(8,128)S(1)}, bf16[5,1024,256]{2,1,0:T(8,128)(2,1)S(1)}) custom-call(s32[3]{0:T(128)S(1)} %copy-done.1, s32[3,8,8]{2,1,0:T(8,128)S(1)} %copy-done, f32[3]{0:T(128)S(1)} %copy-done.2, f32[13]{0:T(128)S(1)} %copy-done.3, f32[64]{0:T(128)S(1)} %copy-done.4, bf16[3,1024,1024]{2,1,0:T(8,128)(2,1)} %operators_ref.3), custom_call_target="tpu_custom_call" | custom-call | flops 1048576 | bytes 5242880 | tf_op jit(solution)/shard_map/prepare/pallas_call | solution.py:450
  17.6 8.4 %all-to-all-done = f32[32,33,1,128]{3,2,1,0:T(1,128)S(1)} async-done(((f32[32,33,1,128]{3,2,1,0:T(1,128)}), f32[32,33,1,128]{3,2,1,0:T(1,128)S(1)}, u32[]{:S(2)}, u32[]{:S(2)}) %all-to-all-start) | async-done | bytes 540704 | tf_op jit(solution)/shard_map/all_to_all | solution.py:416
  26.1 3.7 %first.1 = (f32[128,1024]{1,0:T(8,128)S(1)}, f32[128,1024]{1,0:T(8,128)S(1)}, f32[32,128]{1,0:T(8,128)S(1)}, bf16[7,1024,256]{2,1,0:T(8,128)(2,1)S(1)}) custom-call(f32[1056,128]{1,0:T(8,128)S(1)} %bitcast.9, f32[3,128,128]{2,1,0:T(8,128)S(1)} %get-tuple-element.15.place_ref, f32[8,1024]{1,0:T(8,128)S(1)} %get-tuple-element.16.inside_ref, ...), custom_call_target="tpu_custom_call" | custom-call | flops 1610612736 | bytes 524288 | tf_op jit(solution)/shard_map/first/pallas_call | solution.py:479
  29.8 10.1 %all_to_all.15 = f32[32,1,1,128]{3,2,1,0:T(1,128)S(1)} all-to-all(f32[32,1,1,128]{3,2,1,0:T(1,128)S(1)} %bitcast.12), channel_id=1, replica_groups=mesh['site'=8,'phonon'=4] {'site','phonon'}, dimensions={0} | all-to-all | bytes 32768 | tf_op jit(solution)/shard_map/all_to_all | solution.py:416
  39.9 2.4 %onward.1 = (f32[2080,128]{1,0:T(8,128)S(1)}, f32[8,128]{1,0:T(8,128)S(1)}) custom-call(f32[32,128]{1,0:T(8,128)S(1)} %bitcast.11, f32[128,1024]{1,0:T(8,128)S(1)} %get-tuple-element.19.raw_ref, f32[128,1024]{1,0:T(8,128)S(1)} %get-tuple-element.20.initial_ref, f32[3,128,128]{2,1,0:T(8,128)S(1)} %get-tuple-element.15.place_ref, ...), custom_call_target="tpu_custom_call" | custom-call | flops 1610612736 | bytes 1048576 | tf_op jit(solution)/shard_map/onward/pallas_call | solution.py:496
  42.2 30.1 %all_to_all.16 = f32[32,65,1,128]{3,2,1,0:T(1,128)S(1)} all-to-all(f32[32,65,1,128]{3,2,1,0:T(1,128)S(1)} %bitcast.10), channel_id=1, replica_groups=mesh['site'=8,'phonon'=4] {'site','phonon'}, dimensions={0} | all-to-all | bytes 2129920 | tf_op jit(solution)/shard_map/all_to_all | solution.py:416
  72.3 1.9 %arrive.1 = (f32[1024,128]{1,0:T(8,128)}, f32[1024,128]{1,0:T(8,128)}, f32[3]{0:T(128)}) custom-call(f32[2080,128]{1,0:T(8,128)S(1)} %bitcast.8, f32[8,128]{1,0:T(8,128)S(1)} %get-tuple-element.23.known_ref), custom_call_target="tpu_custom_call" | custom-call | tf_op jit(solution)/shard_map/arrive/pallas_call | solution.py:507
Async XLA Ops:
  2.9 23.2 %all-to-all-start = ((f32[32,33,1,128]{3,2,1,0:T(1,128)}), f32[32,33,1,128]{3,2,1,0:T(1,128)S(1)}, u32[]{:S(2)}, u32[]{:S(2)}) async-start(f32[32,33,1,128]{3,2,1,0:T(1,128)} %bitcast.13), calls=%async_computation | async-start | bytes 1081344 | tf_op jit(solution)/shard_map/all_to_all | solution.py:416
  10.2 4.5 %copy-start = (s32[3,8,8]{2,1,0:T(8,128)S(1)}, s32[3,8,8]{2,1,0:T(8,128)}, u32[]{:S(2)}) copy-start(s32[3,8,8]{2,1,0:T(8,128)} %mask_ref.3) | copy-start | bytes 2308
  10.2 4.5 %copy-start.1 = (s32[3]{0:T(128)S(1)}, s32[3]{0:T(128)}, u32[]{:S(2)}) copy-start(s32[3]{0:T(128)} %bits_ref.3) | copy-start | bytes 40
  10.2 4.5 %copy-start.2 = (f32[3]{0:T(128)S(1)}, f32[3]{0:T(128)}, u32[]{:S(2)}) copy-start(f32[3]{0:T(128)} %field_ref.1) | copy-start | bytes 40
  10.2 4.5 %copy-start.3 = (f32[13]{0:T(128)S(1)}, f32[13]{0:T(128)}, u32[]{:S(2)}) copy-start(f32[13]{0:T(128)} %coupling_ref.1) | copy-start | bytes 160
  10.3 4.5 %copy-start.4 = (f32[64]{0:T(128)S(1)}, f32[64]{0:T(128)}, u32[]{:S(2)}) copy-start(f32[64]{0:T(128)} %mode_ref.1) | copy-start | bytes 772

commit v16 on v14

--- a/solution.py
+++ b/solution.py
@@ -93,21 +93,10 @@
     return jnp.sqrt(squares / plan.entries + epsilon)
 
 
-def depart_kernel(plan, state_ref, out_ref, held_ref, semaphores):
-    half = plan.rows // 2
-    fetches = [
-        pltpu.make_async_copy(
-            state_ref.at[pl.ds(index * half, half), :], held_ref.at[pl.ds(index * half, half), :], semaphores.at[index]
-        )
-        for index in range(2)
-    ]
-    for fetch in fetches:
-        fetch.start()
+def depart_kernel(plan, state_ref, out_ref):
     sums = jnp.zeros((1, LANES), jnp.float32)
     for block in range(plan.lane_blocks):
-        if block * LANES % half == 0:
-            fetches[block * LANES // half].wait()
-        tile = held_ref[pl.ds(block * LANES, LANES), :]
+        tile = state_ref[pl.ds(block * LANES, LANES), :]
         sums = sums + lane_sums(tile * tile)
         turned = tile.T
         for piece in range(plan.pieces):
@@ -429,12 +418,13 @@
     def cost(flops, moved):
         return pl.CostEstimate(flops=flops, bytes_accessed=moved, transcendentals=0)
 
+    near = [(source, source ^ 1) for source in range(plan.phonons)]
+    field = lax.ppermute(field, "phonon", near)
     departing = pl.pallas_call(
         functools.partial(depart_kernel, plan),
         out_shape=inward,
-        in_specs=[HBM],
+        in_specs=[VMEM],
         out_specs=VMEM,
-        scratch_shapes=[pltpu.VMEM((plan.rows, plan.columns), f32), pltpu.SemaphoreType.DMA((2,))],
         compiler_params=params(60),
         name="depart",
     )(state)

time: 73.8 us -> 73.8 us (level)
  transfers between devices with their start and end apart: 1 -> 2, of which waited for: 1 -> 1; matrix products, arithmetic and copies ran while one was open for 0% -> 0% of each run, Pallas kernels for 10% -> 10%
where the time goes in v16:
time: 73.8 us; the launch traced here: 73.4 us
  blocking collectives  40.2 us (54%)
  Pallas kernels  16.6 us (22%)
  waiting for transfers between devices  8.26 us (11%)
  starting transfers between devices  7.61 us (10%)
  between operations  0.74 us (1%)
    all_to_all x2, blocking collectives, exchange(): return lax.all_to_all(shaped, AXES, 0, 0, tiled=True).reshape(values.shape)  40.2 us
    all_to_all x1, waiting for transfers between devices, exchange(): return lax.all_to_all(shaped, AXES, 0, 0, tiled=True).reshape(values.shape)  8.26 us
    all_to_all x1, starting transfers between devices, exchange(): return lax.all_to_all(shaped, AXES, 0, 0, tiled=True).reshape(values.shape)  7.3 us
    pallas_call x1, Pallas kernels, shards(): pl.pallas_call(functools.partial(store_kernel, plan), out_shape=jax.Shape...  4.28 us
    pallas_call x1, Pallas kernels, shards(): pl.pallas_call(functools.partial(first_kernel, plan), out_shape=[vector,...  3.7 us
    pallas_call x1, Pallas kernels, shards(): pl.pallas_call(functools.partial(prepare_kernel, plan), out_shape=[jax.Sh...  2.87 us
    pallas_call x1, Pallas kernels, shards(): pl.pallas_call(functools.partial(onward_kernel, plan), out_shape=[outward...  2.36 us
    pallas_call x1, Pallas kernels, shards(): pl.pallas_call(functools.partial(depart_kernel, plan), out_shape=inward,...  2.12 us
  transfers between devices with their start and end apart: 2, of which 1 were waited for; matrix products, arithmetic and copies ran while one was open for 0% of the time, Pallas kernels for 10%

profile of v16, /device:TPU:0, one launch (start us, length us, event | category | flops | bytes accessed | tf_op | source)
XLA Modules:
  0.0 73.4 jit_solution(1813787906764297768)
XLA Ops:
  0.6 2.1 %depart.1 = f32[1056,128]{1,0:T(8,128)} custom-call(f32[1024,128]{1,0:T(8,128)} %state_ref.1), custom_call_target="tpu_custom_call" | custom-call | tf_op jit(solution)/shard_map/depart/pallas_call | solution.py:423
  2.8 7.3 %all-to-all-start = ((f32[32,33,1,128]{3,2,1,0:T(1,128)}), f32[32,33,1,128]{3,2,1,0:T(1,128)S(1)}, u32[]{:S(2)}, u32[]{:S(2)}) async-start(f32[32,33,1,128]{3,2,1,0:T(1,128)} %bitcast.13), calls=%async_computation | async-start | bytes 1081344 | tf_op jit(solution)/shard_map/all_to_all | solution.py:404
  10.1 0.0 copy-start
  10.1 0.0 copy-start.1
  10.1 0.0 copy-start.2
  10.1 0.0 copy-start.3
  10.1 0.3 collective-permute-start
  10.4 4.3 %store.1.stored_ref = bf16[7,1024,256]{2,1,0:T(8,128)(2,1)} custom-call(s32[3]{0:T(128)} %bits_ref.3, s32[3,8,8]{2,1,0:T(8,128)} %mask_ref.3, bf16[3,1024,1024]{2,1,0:T(8,128)(2,1)} %operators_ref.3), custom_call_target="tpu_custom_call" | custom-call | flops 1048576 | bytes 7340032 | tf_op jit(solution)/shard_map/store/pallas_call | solution.py:453
  14.7 0.0 collective-permute-done.field_ref
  14.7 0.0 copy-done
  14.7 0.0 copy-done.1
  14.7 0.0 copy-done.2
  14.7 0.0 copy-done.3
  14.8 2.9 %prepare.1 = (f32[3,128,128]{2,1,0:T(8,128)S(1)}, f32[8,1024]{1,0:T(8,128)S(1)}, bf16[5,1024,256]{2,1,0:T(8,128)(2,1)S(1)}) custom-call(s32[3]{0:T(128)S(1)} %copy-done.1, s32[3,8,8]{2,1,0:T(8,128)S(1)} %copy-done, f32[3]{0:T(128)S(1)} %collective-permute-done.field_ref, f32[13]{0:T(128)S(1)} %copy-done.2, f32[64]{0:T(128)S(1)} %copy-done.3, ...), custom_call_target="tpu_custom_call" | custom-call | flops 1048576 | bytes 5242880 | tf_op jit(solution)/shard_map/prepare/pallas_call | solution.py:439
  17.6 8.3 %all-to-all-done = f32[32,33,1,128]{3,2,1,0:T(1,128)S(1)} async-done(((f32[32,33,1,128]{3,2,1,0:T(1,128)}), f32[32,33,1,128]{3,2,1,0:T(1,128)S(1)}, u32[]{:S(2)}, u32[]{:S(2)}) %all-to-all-start) | async-done | bytes 540704 | tf_op jit(solution)/shard_map/all_to_all | solution.py:404
  25.9 3.7 %first.1 = (f32[128,1024]{1,0:T(8,128)S(1)}, f32[128,1024]{1,0:T(8,128)S(1)}, f32[32,128]{1,0:T(8,128)S(1)}, bf16[7,1024,256]{2,1,0:T(8,128)(2,1)S(1)}) custom-call(f32[1056,128]{1,0:T(8,128)S(1)} %bitcast.9, f32[3,128,128]{2,1,0:T(8,128)S(1)} %get-tuple-element.15.place_ref, f32[8,1024]{1,0:T(8,128)S(1)} %get-tuple-element.16.inside_ref, ...), custom_call_target="tpu_custom_call" | custom-call | flops 1610612736 | bytes 524288 | tf_op jit(solution)/shard_map/first/pallas_call | solution.py:468
  29.6 10.1 %all_to_all.15 = f32[32,1,1,128]{3,2,1,0:T(1,128)S(1)} all-to-all(f32[32,1,1,128]{3,2,1,0:T(1,128)S(1)} %bitcast.12), channel_id=1, replica_groups=mesh['site'=8,'phonon'=4] {'site','phonon'}, dimensions={0} | all-to-all | bytes 32768 | tf_op jit(solution)/shard_map/all_to_all | solution.py:404
  39.7 2.4 %onward.1 = (f32[2080,128]{1,0:T(8,128)S(1)}, f32[8,128]{1,0:T(8,128)S(1)}) custom-call(f32[32,128]{1,0:T(8,128)S(1)} %bitcast.11, f32[128,1024]{1,0:T(8,128)S(1)} %get-tuple-element.19.raw_ref, f32[128,1024]{1,0:T(8,128)S(1)} %get-tuple-element.20.initial_ref, f32[3,128,128]{2,1,0:T(8,128)S(1)} %get-tuple-element.15.place_ref, ...), custom_call_target="tpu_custom_call" | custom-call | flops 1610612736 | bytes 1048576 | tf_op jit(solution)/shard_map/onward/pallas_call | solution.py:485
  42.1 30.1 %all_to_all.16 = f32[32,65,1,128]{3,2,1,0:T(1,128)S(1)} all-to-all(f32[32,65,1,128]{3,2,1,0:T(1,128)S(1)} %bitcast.10), channel_id=1, replica_groups=mesh['site'=8,'phonon'=4] {'site','phonon'}, dimensions={0} | all-to-all | bytes 2129920 | tf_op jit(solution)/shard_map/all_to_all | solution.py:404
  72.2 1.3 %arrive.1 = (f32[1024,128]{1,0:T(8,128)}, f32[1024,128]{1,0:T(8,128)}, f32[3]{0:T(128)}) custom-call(f32[2080,128]{1,0:T(8,128)S(1)} %bitcast.8, f32[8,128]{1,0:T(8,128)S(1)} %get-tuple-element.23.known_ref), custom_call_target="tpu_custom_call" | custom-call | tf_op jit(solution)/shard_map/arrive/pallas_call | solution.py:496
Async XLA Ops:
  2.8 23.1 %all-to-all-start = ((f32[32,33,1,128]{3,2,1,0:T(1,128)}), f32[32,33,1,128]{3,2,1,0:T(1,128)S(1)}, u32[]{:S(2)}, u32[]{:S(2)}) async-start(f32[32,33,1,128]{3,2,1,0:T(1,128)} %bitcast.13), calls=%async_computation | async-start | bytes 1081344 | tf_op jit(solution)/shard_map/all_to_all | solution.py:404
  10.1 4.7 %copy-start = (s32[3,8,8]{2,1,0:T(8,128)S(1)}, s32[3,8,8]{2,1,0:T(8,128)}, u32[]{:S(2)}) copy-start(s32[3,8,8]{2,1,0:T(8,128)} %mask_ref.3) | copy-start | bytes 2308
  10.1 4.7 %copy-start.1 = (s32[3]{0:T(128)S(1)}, s32[3]{0:T(128)}, u32[]{:S(2)}) copy-start(s32[3]{0:T(128)} %bits_ref.3) | copy-start | bytes 40
  10.1 4.7 %copy-start.2 = (f32[13]{0:T(128)S(1)}, f32[13]{0:T(128)}, u32[]{:S(2)}) copy-start(f32[13]{0:T(128)} %coupling_ref.1) | copy-start | bytes 160
  10.1 4.7 %copy-start.3 = (f32[64]{0:T(128)S(1)}, f32[64]{0:T(128)}, u32[]{:S(2)}) copy-start(f32[64]{0:T(128)} %mode_ref.1) | copy-start | bytes 772
  10.1 4.6 %collective-permute-start = (f32[3]{0:T(128)}, f32[3]{0:T(128)S(1)}, u32[]{:S(2)}, u32[]{:S(2)}) collective-permute-start(f32[3]{0:T(128)} %param.11), channel_id=1, source_target_pairs={{0,1},{1,0},{2,3},{3,2},{4,5},{5,4},{6,7},{7,6},{8,9},{9,8},{10,11... | collective-permute-start | bytes 44 | tf_op jit(solution)/shard_map/ppermute | solution.py:422

commit v17 on v14

--- a/solution.py
+++ b/solution.py
@@ -293,11 +293,18 @@
     fetches = {}
     for slab in range(plan.kept, plan.slabs):
         index = slab - plan.kept
-        fetches[slab] = pltpu.make_async_copy(stored_ref.at[index], fetched_ref.at[index], semaphores.at[index])
-        fetches[slab].start()
+        fetches[slab] = []
+        for half in range(2):
+            rows = pl.ds(half * (plan.rows // 2), plan.rows // 2)
+            fetch = pltpu.make_async_copy(
+                stored_ref.at[index, rows, :], fetched_ref.at[index, rows, :], semaphores.at[index, half]
+            )
+            fetch.start()
+            fetches[slab].append(fetch)
 
     def ready(slab):
-        fetches[slab].wait()
+        for fetch in fetches[slab]:
+            fetch.wait()
 
     squares = totals_of(arrived_ref, plan.body, plan.inward, plan.groups)[0]
     inverse = 1.0 / scale_of(plan, squares)
@@ -485,7 +492,7 @@
         ],
         in_specs=[VMEM] * 4 + [HBM],
         out_specs=[VMEM] * 4,
-        scratch_shapes=[rounded, rounded, pltpu.SemaphoreType.DMA((fetched,))],
+        scratch_shapes=[rounded, rounded, pltpu.SemaphoreType.DMA((fetched, 2))],
         compiler_params=params(46),
         cost_estimate=cost(2 * work, 4 * plan.places * plan.rows),
         name="first",

time: 73.8 us -> 73.9 us (level)
  no operation moved by 1% of the time
where the time goes in v17:
time: 73.9 us; the launch traced here: 73.5 us
  blocking collectives  40.2 us (54%)
  Pallas kernels  16.8 us (23%)
  waiting for transfers between devices  8.43 us (11%)
  starting transfers between devices  7.3 us (10%)
  between operations  0.75 us (1%)
    all_to_all x2, blocking collectives, exchange(): return lax.all_to_all(shaped, AXES, 0, 0, tiled=True).reshape(values.shape)  40.2 us
    all_to_all x1, waiting for transfers between devices, exchange(): return lax.all_to_all(shaped, AXES, 0, 0, tiled=True).reshape(values.shape)  8.43 us
    all_to_all x1, starting transfers between devices, exchange(): return lax.all_to_all(shaped, AXES, 0, 0, tiled=True).reshape(values.shape)  7.3 us
    pallas_call x1, Pallas kernels, shards(): pl.pallas_call(functools.partial(store_kernel, plan), out_shape=jax.Shape...  4.41 us
    pallas_call x1, Pallas kernels, shards(): pl.pallas_call(functools.partial(first_kernel, plan), out_shape=[vector,...  3.76 us
    pallas_call x1, Pallas kernels, shards(): pl.pallas_call(functools.partial(prepare_kernel, plan), out_shape=[jax.Sh...  2.87 us
    pallas_call x1, Pallas kernels, shards(): pl.pallas_call(functools.partial(onward_kernel, plan), out_shape=[outward...  2.36 us
    pallas_call x1, Pallas kernels, shards(): pl.pallas_call(functools.partial(depart_kernel, plan), out_shape=inward,...  2.12 us
  transfers between devices with their start and end apart: 1, of which 1 were waited for; matrix products, arithmetic and copies ran while one was open for 0% of the time, Pallas kernels for 10%

profile of v17, /device:TPU:0, one launch (start us, length us, event | category | flops | bytes accessed | tf_op | source)
XLA Modules:
  0.0 73.5 jit_solution(17536866772468232968)
XLA Ops:
  0.6 2.1 %depart.1 = f32[1056,128]{1,0:T(8,128)} custom-call(f32[1024,128]{1,0:T(8,128)} %state_ref.1), custom_call_target="tpu_custom_call" | custom-call | tf_op jit(solution)/shard_map/depart/pallas_call | solution.py:439
  2.8 7.3 %all-to-all-start = ((f32[32,33,1,128]{3,2,1,0:T(1,128)}), f32[32,33,1,128]{3,2,1,0:T(1,128)S(1)}, u32[]{:S(2)}, u32[]{:S(2)}) async-start(f32[32,33,1,128]{3,2,1,0:T(1,128)} %bitcast.13), calls=%async_computation | async-start | bytes 1081344 | tf_op jit(solution)/shard_map/all_to_all | solution.py:422
  10.1 0.0 copy-start
  10.1 0.0 copy-start.1
  10.1 0.0 copy-start.2
  10.1 0.0 copy-start.3
  10.1 0.0 copy-start.4
  10.1 4.4 %store.1.stored_ref = bf16[7,1024,256]{2,1,0:T(8,128)(2,1)} custom-call(s32[3]{0:T(128)} %bits_ref.3, s32[3,8,8]{2,1,0:T(8,128)} %mask_ref.3, bf16[3,1024,1024]{2,1,0:T(8,128)(2,1)} %operators_ref.3), custom_call_target="tpu_custom_call" | custom-call | flops 1048576 | bytes 7340032 | tf_op jit(solution)/shard_map/store/pallas_call | solution.py:470
  14.6 0.0 copy-done
  14.6 0.0 copy-done.1
  14.6 0.0 copy-done.2
  14.6 0.0 copy-done.3
  14.6 0.0 copy-done.4
  14.6 2.9 %prepare.1 = (f32[3,128,128]{2,1,0:T(8,128)S(1)}, f32[8,1024]{1,0:T(8,128)S(1)}, bf16[5,1024,256]{2,1,0:T(8,128)(2,1)S(1)}) custom-call(s32[3]{0:T(128)S(1)} %copy-done.1, s32[3,8,8]{2,1,0:T(8,128)S(1)} %copy-done, f32[3]{0:T(128)S(1)} %copy-done.2, f32[13]{0:T(128)S(1)} %copy-done.3, f32[64]{0:T(128)S(1)} %copy-done.4, bf16[3,1024,1024]{2,1,0:T(8,128)(2,1)} %operators_ref.3), custom_call_target="tpu_custom_call" | custom-call | flops 1048576 | bytes 5242880 | tf_op jit(solution)/shard_map/prepare/pallas_call | solution.py:456
  17.5 8.4 %all-to-all-done = f32[32,33,1,128]{3,2,1,0:T(1,128)S(1)} async-done(((f32[32,33,1,128]{3,2,1,0:T(1,128)}), f32[32,33,1,128]{3,2,1,0:T(1,128)S(1)}, u32[]{:S(2)}, u32[]{:S(2)}) %all-to-all-start) | async-done | bytes 540704 | tf_op jit(solution)/shard_map/all_to_all | solution.py:422
  25.9 3.8 %first.1 = (f32[128,1024]{1,0:T(8,128)S(1)}, f32[128,1024]{1,0:T(8,128)S(1)}, f32[32,128]{1,0:T(8,128)S(1)}, bf16[7,1024,256]{2,1,0:T(8,128)(2,1)S(1)}) custom-call(f32[1056,128]{1,0:T(8,128)S(1)} %bitcast.9, f32[3,128,128]{2,1,0:T(8,128)S(1)} %get-tuple-element.15.place_ref, f32[8,1024]{1,0:T(8,128)S(1)} %get-tuple-element.16.inside_ref, ...), custom_call_target="tpu_custom_call" | custom-call | flops 1610612736 | bytes 524288 | tf_op jit(solution)/shard_map/first/pallas_call | solution.py:485
  29.7 10.1 %all_to_all.15 = f32[32,1,1,128]{3,2,1,0:T(1,128)S(1)} all-to-all(f32[32,1,1,128]{3,2,1,0:T(1,128)S(1)} %bitcast.12), channel_id=1, replica_groups=mesh['site'=8,'phonon'=4] {'site','phonon'}, dimensions={0} | all-to-all | bytes 32768 | tf_op jit(solution)/shard_map/all_to_all | solution.py:422
  39.8 2.4 %onward.1 = (f32[2080,128]{1,0:T(8,128)S(1)}, f32[8,128]{1,0:T(8,128)S(1)}) custom-call(f32[32,128]{1,0:T(8,128)S(1)} %bitcast.11, f32[128,1024]{1,0:T(8,128)S(1)} %get-tuple-element.19.raw_ref, f32[128,1024]{1,0:T(8,128)S(1)} %get-tuple-element.20.initial_ref, f32[3,128,128]{2,1,0:T(8,128)S(1)} %get-tuple-element.15.place_ref, ...), custom_call_target="tpu_custom_call" | custom-call | flops 1610612736 | bytes 1048576 | tf_op jit(solution)/shard_map/onward/pallas_call | solution.py:502
  42.1 30.1 %all_to_all.16 = f32[32,65,1,128]{3,2,1,0:T(1,128)S(1)} all-to-all(f32[32,65,1,128]{3,2,1,0:T(1,128)S(1)} %bitcast.10), channel_id=1, replica_groups=mesh['site'=8,'phonon'=4] {'site','phonon'}, dimensions={0} | all-to-all | bytes 2129920 | tf_op jit(solution)/shard_map/all_to_all | solution.py:422
  72.2 1.3 %arrive.1 = (f32[1024,128]{1,0:T(8,128)}, f32[1024,128]{1,0:T(8,128)}, f32[3]{0:T(128)}) custom-call(f32[2080,128]{1,0:T(8,128)S(1)} %bitcast.8, f32[8,128]{1,0:T(8,128)S(1)} %get-tuple-element.23.known_ref), custom_call_target="tpu_custom_call" | custom-call | tf_op jit(solution)/shard_map/arrive/pallas_call | solution.py:513
Async XLA Ops:
  2.8 23.2 %all-to-all-start = ((f32[32,33,1,128]{3,2,1,0:T(1,128)}), f32[32,33,1,128]{3,2,1,0:T(1,128)S(1)}, u32[]{:S(2)}, u32[]{:S(2)}) async-start(f32[32,33,1,128]{3,2,1,0:T(1,128)} %bitcast.13), calls=%async_computation | async-start | bytes 1081344 | tf_op jit(solution)/shard_map/all_to_all | solution.py:422
  10.1 4.5 %copy-start = (s32[3,8,8]{2,1,0:T(8,128)S(1)}, s32[3,8,8]{2,1,0:T(8,128)}, u32[]{:S(2)}) copy-start(s32[3,8,8]{2,1,0:T(8,128)} %mask_ref.3) | copy-start | bytes 2308
  10.1 4.5 %copy-start.1 = (s32[3]{0:T(128)S(1)}, s32[3]{0:T(128)}, u32[]{:S(2)}) copy-start(s32[3]{0:T(128)} %bits_ref.3) | copy-start | bytes 40
  10.1 4.5 %copy-start.2 = (f32[3]{0:T(128)S(1)}, f32[3]{0:T(128)}, u32[]{:S(2)}) copy-start(f32[3]{0:T(128)} %field_ref.1) | copy-start | bytes 40
  10.1 4.5 %copy-start.3 = (f32[13]{0:T(128)S(1)}, f32[13]{0:T(128)}, u32[]{:S(2)}) copy-start(f32[13]{0:T(128)} %coupling_ref.1) | copy-start | bytes 160
  10.1 4.5 %copy-start.4 = (f32[64]{0:T(128)S(1)}, f32[64]{0:T(128)}, u32[]{:S(2)}) copy-start(f32[64]{0:T(128)} %mode_ref.1) | copy-start | bytes 772

commit v18 on v16

--- a/solution.py
+++ b/solution.py
@@ -93,17 +93,26 @@
     return jnp.sqrt(squares / plan.entries + epsilon)
 
 
-def depart_kernel(plan, state_ref, out_ref):
-    sums = jnp.zeros((1, LANES), jnp.float32)
-    for block in range(plan.lane_blocks):
-        tile = state_ref[pl.ds(block * LANES, LANES), :]
-        sums = sums + lane_sums(tile * tile)
+def depart_kernel(plan, state_ref, out_ref, sums_ref):
+    part = pl.program_id(0)
+
+    @pl.when(part == 0)
+    def _():
+        sums_ref[...] = jnp.zeros_like(sums_ref)
+
+    for start in range(0, plan.width, LANES):
+        tile = state_ref[pl.ds(start, LANES), :]
+        sums_ref[...] += lane_sums(tile * tile)
         turned = tile.T
+        block = part * (plan.width // LANES) + start // LANES
         for piece in range(plan.pieces):
             out_ref[pl.ds(piece * plan.lane_blocks + block, plan.groups, stride=plan.inward), :] = turned[
                 piece * plan.groups : (piece + 1) * plan.groups
             ]
-    put_sums(out_ref, [sums], plan.body, plan.inward, plan.groups)
+
+    @pl.when(part == plan.parts - 1)
+    def _():
+        put_sums(out_ref, [sums_ref[...]], plan.body, plan.inward, plan.groups)
 
 
 def fetch_slabs(plan, slabs, bits_ref, operators_ref, held_ref, semaphores):
@@ -219,7 +228,7 @@
         ).astype(jnp.bfloat16)
 
 
-def step(plan, vector_ref, rounded_ref, kept_ref, fetched_ref, place_ref, inside_ref, finish, ready=None, begun_ref=None):
+def step(plan, vector_ref, rounded_ref, kept_ref, fetched_ref, place_ref, inside_ref, finish, ready=None, begun_ref=None, factor=None):
     span = plan.places // plan.levels_here
 
     def local(start):
@@ -232,7 +241,7 @@
         total = weight * (place_ref[1] * lower + place_ref[2] * upper)
         for position in range(plan.bits):
             total = total + inside_ref[pl.ds(1 + position, 1), lanes] * flipped(vector, plan.phonons << position)
-        return total
+        return total if factor is None else total * factor
 
     def added(total, part, late):
         for ref, low, high in ((kept_ref, 0, plan.kept), (fetched_ref, plan.kept, plan.slabs)):
@@ -336,20 +345,18 @@
     known_ref,
     rounded_ref,
     ahead_ref,
-    second_ref,
     third_ref,
 ):
     squares, overlap, ahead, _ = totals_of(arrived_ref, 0, 1, plan.groups)
     first = 1.0 / scale_of(plan, squares)
     estimate = scale_of(plan, ahead * first * first)
     second = 1.0 / estimate
+    both = first * second
     known_ref[:1, :] = jnp.broadcast_to(overlap * first / plan.entries, (1, LANES))
     known_ref[1:, :] = jnp.broadcast_to(estimate, (SUBLANES - 1, LANES))
     for block in range(plan.lane_blocks):
         lanes = pl.ds(block * LANES, LANES)
-        vector = raw_ref[:, lanes] * first
-        second_ref[:, lanes] = vector
-        put_rounded(plan, rounded_ref, vector, block * LANES)
+        put_rounded(plan, rounded_ref, raw_ref[:, lanes] * first, block * LANES)
     tables = (kept_ref, fetched_ref, place_ref, inside_ref)
     sums = [[] for _ in range(SLOTS)]
 
@@ -372,31 +379,38 @@
         send(0, lanes, new)
 
     def finish_third(lanes, total):
-        send(1, lanes, 2.0 * total - second_ref[:, lanes] * second)
-
-    step(plan, second_ref, rounded_ref, *tables, finish_second)
+        send(1, lanes, 2.0 * total - raw_ref[:, lanes] * both)
+
+    step(plan, raw_ref, rounded_ref, *tables, finish_second, factor=first)
     step(plan, third_ref, ahead_ref, *tables, finish_third)
     put_sums(out_ref, [one_row(rows) for rows in sums], 2 * plan.body, plan.outward, plan.groups)
 
 
-def arrive_kernel(plan, arrived_ref, known_ref, before_ref, last_ref, moments_ref):
-    before_squares, before_overlap, last_squares, last_overlap = totals_of(
-        arrived_ref, 2 * plan.body, plan.outward, plan.groups
-    )
-    before = 1.0 / scale_of(plan, before_squares)
-    back = known_ref[1:2, :1] * before
-    last = back / scale_of(plan, last_squares * back * back)
-    for vector, (out_ref, factor) in enumerate(((before_ref, before), (last_ref, last))):
-        for block in range(plan.lane_blocks):
-            first = vector * plan.body + block
+def arrive_kernel(plan, arrived_ref, known_ref, before_ref, last_ref, moments_ref, factors_ref):
+    part = pl.program_id(0)
+
+    @pl.when(part == 0)
+    def _():
+        before_squares, before_overlap, last_squares, last_overlap = totals_of(
+            arrived_ref, 2 * plan.body, plan.outward, plan.groups
+        )
+        before = 1.0 / scale_of(plan, before_squares)
+        back = known_ref[1:2, :1] * before
+        last = back / scale_of(plan, last_squares * back * back)
+        factors_ref[0:1, :] = jnp.broadcast_to(before, (1, LANES))
+        factors_ref[1:2, :] = jnp.broadcast_to(last, (1, LANES))
+        moments_ref[0] = known_ref[0, 0]
+        moments_ref[1] = (before_overlap * before / plan.entries)[0, 0]
+        moments_ref[2] = (last_overlap * last / plan.entries)[0, 0]
+
+    for vector, out_ref in enumerate((before_ref, last_ref)):
+        for start in range(0, plan.width, LANES):
+            first = vector * plan.body + part * (plan.width // LANES) + start // LANES
             parts = [
                 arrived_ref[pl.ds(first + piece * plan.lane_blocks, plan.groups, stride=plan.outward), :]
                 for piece in range(plan.pieces)
             ]
-            out_ref[pl.ds(block * LANES, LANES), :] = jnp.concatenate(parts, axis=0).T * factor
-    moments_ref[0] = known_ref[0, 0]
-    moments_ref[1] = (before_overlap * before / plan.entries)[0, 0]
-    moments_ref[2] = (last_overlap * last / plan.entries)[0, 0]
+            out_ref[pl.ds(start, LANES), :] = jnp.concatenate(parts, axis=0).T * factors_ref[vector : vector + 1, :]
 
 
 def exchange(values, count):
@@ -418,13 +432,13 @@
     def cost(flops, moved):
         return pl.CostEstimate(flops=flops, bytes_accessed=moved, transcendentals=0)
 
-    near = [(source, source ^ 1) for source in range(plan.phonons)]
-    field = lax.ppermute(field, "phonon", near)
     departing = pl.pallas_call(
         functools.partial(depart_kernel, plan),
         out_shape=inward,
-        in_specs=[VMEM],
-        out_specs=VMEM,
+        grid=(plan.parts,),
+        in_specs=[pl.BlockSpec((plan.width, plan.columns), lambda part: (part, 0))],
+        out_specs=pl.BlockSpec(inward.shape, lambda part: (0, 0)),
+        scratch_shapes=[pltpu.VMEM((1, LANES), f32)],
         compiler_params=params(60),
         name="depart",
     )(state)
@@ -487,7 +501,7 @@
         out_shape=[outward, known],
         in_specs=[VMEM] * 7,
         out_specs=[VMEM] * 2,
-        scratch_shapes=[rounded, rounded, working, working],
+        scratch_shapes=[rounded, rounded, working],
         compiler_params=params(32),
         cost_estimate=cost(2 * work, 8 * plan.places * plan.rows),
         name="onward",
@@ -496,8 +510,10 @@
     before, last, moments = pl.pallas_call(
         functools.partial(arrive_kernel, plan),
         out_shape=[held, held, jax.ShapeDtypeStruct((STEPS,), f32)],
+        grid=(plan.parts,),
         in_specs=[VMEM] * 2,
-        out_specs=[VMEM, VMEM, SMEM],
+        out_specs=[pl.BlockSpec((plan.width, plan.columns), lambda part: (part, 0))] * 2 + [SMEM],
+        scratch_shapes=[pltpu.VMEM((SUBLANES, LANES), f32)],
         compiler_params=params(16),
         name="arrive",
     )(arrived, told)

time: 73.8 us -> 75.4 us (1.022)
  Pallas kernels: 16.6 us -> 18.3 us
    pallas_call x1, Pallas kernels: 2.12 us -> 3.06 us  [shards(): pl.pallas_call(functools.partial(depart_kernel, plan), out_shape=inward,...]
  transfers between devices with their start and end apart: 2 -> 1, of which waited for: 1 -> 1; matrix products, arithmetic and copies ran while one was open for 0% -> 0% of each run, Pallas kernels for 10% -> 10%
where the time goes in v18:
time: 75.4 us; the launch traced here: 75 us
  blocking collectives  40.2 us (53%)
  Pallas kernels  18.3 us (24%)
  waiting for transfers between devices  8.43 us (11%)
  starting transfers between devices  7.3 us (10%)
    all_to_all x2, blocking collectives, exchange(): return lax.all_to_all(shaped, AXES, 0, 0, tiled=True).reshape(values.shape)  40.2 us
    all_to_all x1, waiting for transfers between devices, exchange(): return lax.all_to_all(shaped, AXES, 0, 0, tiled=True).reshape(values.shape)  8.43 us
    all_to_all x1, starting transfers between devices, exchange(): return lax.all_to_all(shaped, AXES, 0, 0, tiled=True).reshape(values.shape)  7.3 us
    pallas_call x1, Pallas kernels, shards(): pl.pallas_call(functools.partial(store_kernel, plan), out_shape=jax.Shape...  4.41 us
    pallas_call x1, Pallas kernels, shards(): pl.pallas_call(functools.partial(first_kernel, plan), out_shape=[vector,...  3.7 us
    pallas_call x1, Pallas kernels, shards(): pl.pallas_call(functools.partial(depart_kernel, plan), out_shape=inward,...  3.06 us
    pallas_call x1, Pallas kernels, shards(): pl.pallas_call(functools.partial(prepare_kernel, plan), out_shape=[jax.Sh...  2.87 us
    pallas_call x1, Pallas kernels, shards(): pl.pallas_call(functools.partial(onward_kernel, plan), out_shape=[outward...  2.32 us
  transfers between devices with their start and end apart: 1, of which 1 were waited for; matrix products, arithmetic and copies ran while one was open for 0% of the time, Pallas kernels for 10%

profile of v18, /device:TPU:0, one launch (start us, length us, event | category | flops | bytes accessed | tf_op | source)
XLA Modules:
  0.0 75.0 jit_solution(1038249969965783367)
XLA Ops:
  0.6 3.1 %depart.1 = f32[1056,128]{1,0:T(8,128)} custom-call(f32[1024,128]{1,0:T(8,128)} %state_ref.1), custom_call_target="tpu_custom_call" | custom-call | tf_op jit(solution)/shard_map/depart/pallas_call | solution.py:435
  3.7 7.3 %all-to-all-start = ((f32[32,33,1,128]{3,2,1,0:T(1,128)}), f32[32,33,1,128]{3,2,1,0:T(1,128)S(1)}, u32[]{:S(2)}, u32[]{:S(2)}) async-start(f32[32,33,1,128]{3,2,1,0:T(1,128)} %bitcast.13), calls=%async_computation | async-start | bytes 1081344 | tf_op jit(solution)/shard_map/all_to_all | solution.py:418
  11.0 0.0 copy-start
  11.0 0.0 copy-start.1
  11.0 0.0 copy-start.2
  11.0 0.0 copy-start.3
  11.0 0.0 copy-start.4
  11.1 4.4 %store.1.stored_ref = bf16[7,1024,256]{2,1,0:T(8,128)(2,1)} custom-call(s32[3]{0:T(128)} %bits_ref.3, s32[3,8,8]{2,1,0:T(8,128)} %mask_ref.3, bf16[3,1024,1024]{2,1,0:T(8,128)(2,1)} %operators_ref.3), custom_call_target="tpu_custom_call" | custom-call | flops 1048576 | bytes 7340032 | tf_op jit(solution)/shard_map/store/pallas_call | solution.py:467
  15.5 0.0 copy-done
  15.5 0.0 copy-done.1
  15.5 0.0 copy-done.2
  15.5 0.0 copy-done.3
  15.5 0.0 copy-done.4
  15.5 2.9 %prepare.1 = (f32[3,128,128]{2,1,0:T(8,128)S(1)}, f32[8,1024]{1,0:T(8,128)S(1)}, bf16[5,1024,256]{2,1,0:T(8,128)(2,1)S(1)}) custom-call(s32[3]{0:T(128)S(1)} %copy-done.1, s32[3,8,8]{2,1,0:T(8,128)S(1)} %copy-done, f32[3]{0:T(128)S(1)} %copy-done.2, f32[13]{0:T(128)S(1)} %copy-done.3, f32[64]{0:T(128)S(1)} %copy-done.4, bf16[3,1024,1024]{2,1,0:T(8,128)(2,1)} %operators_ref.3), custom_call_target="tpu_custom_call" | custom-call | flops 1048576 | bytes 5242880 | tf_op jit(solution)/shard_map/prepare/pallas_call | solution.py:453
  18.4 8.4 %all-to-all-done = f32[32,33,1,128]{3,2,1,0:T(1,128)S(1)} async-done(((f32[32,33,1,128]{3,2,1,0:T(1,128)}), f32[32,33,1,128]{3,2,1,0:T(1,128)S(1)}, u32[]{:S(2)}, u32[]{:S(2)}) %all-to-all-start) | async-done | bytes 540704 | tf_op jit(solution)/shard_map/all_to_all | solution.py:418
  26.8 3.7 %first.1 = (f32[128,1024]{1,0:T(8,128)S(1)}, f32[128,1024]{1,0:T(8,128)S(1)}, f32[32,128]{1,0:T(8,128)S(1)}, bf16[7,1024,256]{2,1,0:T(8,128)(2,1)S(1)}) custom-call(f32[1056,128]{1,0:T(8,128)S(1)} %bitcast.9, f32[3,128,128]{2,1,0:T(8,128)S(1)} %get-tuple-element.15.place_ref, f32[8,1024]{1,0:T(8,128)S(1)} %get-tuple-element.16.inside_ref, ...), custom_call_target="tpu_custom_call" | custom-call | flops 1610612736 | bytes 524288 | tf_op jit(solution)/shard_map/first/pallas_call | solution.py:482
  30.5 10.1 %all_to_all.15 = f32[32,1,1,128]{3,2,1,0:T(1,128)S(1)} all-to-all(f32[32,1,1,128]{3,2,1,0:T(1,128)S(1)} %bitcast.12), channel_id=1, replica_groups=mesh['site'=8,'phonon'=4] {'site','phonon'}, dimensions={0} | all-to-all | bytes 32768 | tf_op jit(solution)/shard_map/all_to_all | solution.py:418
  40.6 2.3 %onward.1 = (f32[2080,128]{1,0:T(8,128)S(1)}, f32[8,128]{1,0:T(8,128)S(1)}) custom-call(f32[32,128]{1,0:T(8,128)S(1)} %bitcast.11, f32[128,1024]{1,0:T(8,128)S(1)} %get-tuple-element.19.raw_ref, f32[128,1024]{1,0:T(8,128)S(1)} %get-tuple-element.20.initial_ref, f32[3,128,128]{2,1,0:T(8,128)S(1)} %get-tuple-element.15.place_ref, ...), custom_call_target="tpu_custom_call" | custom-call | flops 1610612736 | bytes 1048576 | tf_op jit(solution)/shard_map/onward/pallas_call | solution.py:499
  43.0 30.1 %all_to_all.16 = f32[32,65,1,128]{3,2,1,0:T(1,128)S(1)} all-to-all(f32[32,65,1,128]{3,2,1,0:T(1,128)S(1)} %bitcast.10), channel_id=1, replica_groups=mesh['site'=8,'phonon'=4] {'site','phonon'}, dimensions={0} | all-to-all | bytes 2129920 | tf_op jit(solution)/shard_map/all_to_all | solution.py:418
  73.1 2.0 %arrive.1 = (f32[1024,128]{1,0:T(8,128)}, f32[1024,128]{1,0:T(8,128)}, f32[3]{0:T(128)}) custom-call(f32[2080,128]{1,0:T(8,128)S(1)} %bitcast.8, f32[8,128]{1,0:T(8,128)S(1)} %get-tuple-element.23.known_ref), custom_call_target="tpu_custom_call" | custom-call | tf_op jit(solution)/shard_map/arrive/pallas_call | solution.py:510
Async XLA Ops:
  3.7 23.1 %all-to-all-start = ((f32[32,33,1,128]{3,2,1,0:T(1,128)}), f32[32,33,1,128]{3,2,1,0:T(1,128)S(1)}, u32[]{:S(2)}, u32[]{:S(2)}) async-start(f32[32,33,1,128]{3,2,1,0:T(1,128)} %bitcast.13), calls=%async_computation | async-start | bytes 1081344 | tf_op jit(solution)/shard_map/all_to_all | solution.py:418
  11.0 4.5 %copy-start = (s32[3,8,8]{2,1,0:T(8,128)S(1)}, s32[3,8,8]{2,1,0:T(8,128)}, u32[]{:S(2)}) copy-start(s32[3,8,8]{2,1,0:T(8,128)} %mask_ref.3) | copy-start | bytes 2308
  11.0 4.5 %copy-start.1 = (s32[3]{0:T(128)S(1)}, s32[3]{0:T(128)}, u32[]{:S(2)}) copy-start(s32[3]{0:T(128)} %bits_ref.3) | copy-start | bytes 40
  11.0 4.5 %copy-start.2 = (f32[3]{0:T(128)S(1)}, f32[3]{0:T(128)}, u32[]{:S(2)}) copy-start(f32[3]{0:T(128)} %field_ref.1) | copy-start | bytes 40
  11.0 4.5 %copy-start.3 = (f32[13]{0:T(128)S(1)}, f32[13]{0:T(128)}, u32[]{:S(2)}) copy-start(f32[13]{0:T(128)} %coupling_ref.1) | copy-start | bytes 160
  11.0 4.5 %copy-start.4 = (f32[64]{0:T(128)S(1)}, f32[64]{0:T(128)}, u32[]{:S(2)}) copy-start(f32[64]{0:T(128)} %mode_ref.1) | copy-start | bytes 772

commit v19 on v14

--- a/solution.py
+++ b/solution.py
@@ -44,6 +44,7 @@
         self.places = self.pieces * self.groups
         self.width = 2 * LANES
         self.parts = rows // self.width
+        self.half = self.groups // 2
         self.slabs = self.bits * self.parts
         self.kept = min(5, self.slabs - 1)
         self.entries = float(rows * columns * self.groups)
@@ -56,7 +57,7 @@
             and self.edge % LANES == 0
             and self.width % self.edge == 0
             and self.bits < SUBLANES
-            and self.groups % SUBLANES == 0
+            and self.half % SUBLANES == 0
         )
 
 
@@ -165,6 +166,7 @@
     mode_ref,
     operators_ref,
     place_ref,
+    partner_ref,
     inside_ref,
     kept_ref,
     held_ref,
@@ -182,14 +184,17 @@
     for position in range(plan.bits):
         held = (site >> position & 1).astype(jnp.float32)
         occupied = occupied + coupling_ref[bits_ref[position]] * held
-    strength = jnp.zeros((plan.places, LANES), jnp.float32)
-    for index in range(plan.share):
-        strength = jnp.where(mode == index, mode_ref[index * plan.groups + me], strength)
-    strength = strength / jnp.sqrt(jnp.full((1, LANES), plan.level_count, jnp.float32))
     height = level.astype(jnp.float32)
+    lower = jnp.sqrt(height)
+    upper = jnp.where(level == plan.level_count - 1, 0.0, jnp.sqrt(height + 1.0))
     place_ref[0] = occupied
-    place_ref[1] = strength * jnp.sqrt(height)
-    place_ref[2] = jnp.where(level == plan.level_count - 1, 0.0, strength * jnp.sqrt(height + 1.0))
+    for ref, start, owner in ((place_ref, 1, me), (partner_ref, 0, me ^ plan.half)):
+        strength = jnp.zeros((plan.places, LANES), jnp.float32)
+        for index in range(plan.share):
+            strength = jnp.where(mode == index, mode_ref[index * plan.groups + owner], strength)
+        strength = strength / jnp.sqrt(jnp.full((1, LANES), plan.level_count, jnp.float32))
+        ref[start] = strength * lower
+        ref[start + 1] = strength * upper
     inside = lax.broadcasted_iota(jnp.int32, (1, plan.rows), 1)
     weight = jnp.zeros((1, plan.rows), jnp.float32)
     for local_bit in range(LBITS):
@@ -230,7 +235,7 @@
         ).astype(jnp.bfloat16)
 
 
-def step(plan, vector_ref, rounded_ref, kept_ref, fetched_ref, place_ref, inside_ref, finish, ready=None, begun_ref=None):
+def step(plan, vector_ref, rounded_ref, kept_ref, fetched_ref, place, inside_ref, finish, ready=None, begun_ref=None):
     span = plan.places // plan.levels_here
 
     def local(start):
@@ -239,8 +244,9 @@
         levels = [vector[index * span : (index + 1) * span] for index in range(plan.levels_here)]
         lower = jnp.concatenate([shifted(levels[-1], 1)] + levels[:-1], axis=0)
         upper = jnp.concatenate(levels[1:] + [shifted(levels[0], -1)], axis=0)
-        weight = place_ref[0] + inside_ref[:1, lanes]
-        total = weight * (place_ref[1] * lower + place_ref[2] * upper)
+        occupied, (ladder_ref, first) = place
+        weight = occupied[0] + inside_ref[:1, lanes]
+        total = weight * (ladder_ref[first] * lower + ladder_ref[first + 1] * upper)
         for position in range(plan.bits):
             total = total + inside_ref[pl.ds(1 + position, 1), lanes] * flipped(vector, plan.phonons << position)
         return total
@@ -309,7 +315,7 @@
         vector = jnp.concatenate(parts, axis=0) * inverse
         initial_ref[:, pl.ds(block * LANES, LANES)] = vector
         put_rounded(plan, rounded_ref, vector, block * LANES)
-    tables = (kept_ref, fetched_ref, place_ref, inside_ref)
+    tables = (kept_ref, fetched_ref, (place_ref, (place_ref, 1)), inside_ref)
     squares = []
     overlap = []
     ahead = []
@@ -354,26 +360,43 @@
     first = 1.0 / scale_of(plan, squares)
     estimate = scale_of(plan, ahead * first * first)
     second = 1.0 / estimate
-    known_ref[:1, :] = jnp.broadcast_to(overlap * first / plan.entries, (1, LANES))
-    known_ref[1:, :] = jnp.broadcast_to(estimate, (SUBLANES - 1, LANES))
+    known_ref[...] = jnp.broadcast_to(first, (SUBLANES, LANES))
+    known_ref[0:1, :] = jnp.broadcast_to(overlap * first / plan.entries, (1, LANES))
+    known_ref[1:2, :] = jnp.broadcast_to(estimate, (1, LANES))
     for block in range(plan.lane_blocks):
         lanes = pl.ds(block * LANES, LANES)
         vector = raw_ref[:, lanes] * first
         second_ref[:, lanes] = vector
         put_rounded(plan, rounded_ref, vector, block * LANES)
-    tables = (kept_ref, fetched_ref, place_ref, inside_ref)
+    tables = (kept_ref, fetched_ref, (place_ref, (place_ref, 1)), inside_ref)
     sums = [[] for _ in range(SLOTS)]
 
-    def send(vector, lanes, new):
+    def note(vector, lanes, new):
         sums[2 * vector].append(lane_sums(new * new))
         sums[2 * vector + 1].append(lane_sums(new * initial_ref[:, lanes]))
+
+    last_steps(
+        plan, tables, first, second, initial_ref, second_ref, third_ref, rounded_ref, ahead_ref, out_ref, plan.outward, note
+    )
+    put_sums(out_ref, [one_row(rows) for rows in sums], 2 * plan.body, plan.outward, plan.half)
+
+
+def last_steps(
+    plan, tables, first, second, initial_ref, second_ref, third_ref, rounded_ref, ahead_ref, out_ref, stride, note
+):
+    upper = lax.axis_index("site") >= plan.sites // 2
+
+    def send(vector, lanes, new):
+        if note:
+            note(vector, lanes, new)
         for start in range(0, plan.width, LANES):
             block = (lanes.start + start) // LANES
             for piece in range(plan.pieces):
                 row = vector * plan.body + piece * plan.lane_blocks + block
-                out_ref[pl.ds(row, plan.groups, stride=plan.outward), :] = new[
-                    piece * plan.groups : (piece + 1) * plan.groups, start : start + LANES
-                ]
+                rows = new[piece * plan.groups : (piece + 1) * plan.groups, start : start + LANES]
+                out_ref[pl.ds(row, plan.half, stride=stride), :] = jnp.where(
+                    upper, rows[plan.half :], rows[: plan.half]
+                )
 
     def finish_second(lanes, total):
         new = 2.0 * total - initial_ref[:, lanes] * first
@@ -387,29 +410,88 @@
 
     step(plan, second_ref, rounded_ref, *tables, finish_second)
     step(plan, third_ref, ahead_ref, *tables, finish_third)
-    put_sums(out_ref, [one_row(rows) for rows in sums], 2 * plan.body, plan.outward, plan.groups)
-
-
-def arrive_kernel(plan, arrived_ref, known_ref, before_ref, last_ref, moments_ref):
-    before_squares, before_overlap, last_squares, last_overlap = totals_of(
-        arrived_ref, 2 * plan.body, plan.outward, plan.groups
+
+
+def partner_kernel(
+    plan,
+    state_ref,
+    known_ref,
+    own_ref,
+    place_ref,
+    partner_ref,
+    inside_ref,
+    kept_ref,
+    fetched_ref,
+    out_ref,
+    sums_ref,
+    first_ref,
+    second_ref,
+    third_ref,
+    initial_ref,
+    vector_ref,
+    later_ref,
+):
+    sums_ref[...] = jnp.broadcast_to(
+        lane_sums(own_ref[pl.ds(2 * plan.body, plan.half, stride=plan.outward), :]), (SUBLANES, LANES)
     )
+    squares = totals_of(state_ref, plan.body, plan.inward, plan.groups)[0]
+    inverse = 1.0 / scale_of(plan, squares)
+    first = known_ref[2:3, :1]
+    second = 1.0 / known_ref[1:2, :1]
+    for block in range(plan.lane_blocks):
+        parts = [
+            state_ref[pl.ds(piece * plan.lane_blocks + block, plan.groups, stride=plan.inward), :]
+            for piece in range(plan.pieces)
+        ]
+        vector = jnp.concatenate(parts, axis=0) * inverse
+        initial_ref[:, pl.ds(block * LANES, LANES)] = vector
+        put_rounded(plan, first_ref, vector, block * LANES)
+    tables = (kept_ref, fetched_ref, (place_ref, (partner_ref, 0)), inside_ref)
+
+    def finish(lanes, new):
+        vector = new * first
+        vector_ref[:, lanes] = vector
+        put_rounded(plan, second_ref, vector, lanes.start)
+
+    step(plan, initial_ref, first_ref, *tables, finish)
+    last_steps(
+        plan, tables, first, second, initial_ref, vector_ref, later_ref, second_ref, third_ref, out_ref, 2 * plan.body, None
+    )
+
+
+def arrive_kernel(
+    plan, own_ref, other_ref, known_ref, sums_ref, other_sums_ref, before_ref, last_ref, moments_ref, total_ref
+):
+    upper = lax.axis_index("site") >= plan.sites // 2
+    total_ref[...] = sums_ref[...] + other_sums_ref[...]
+    before_squares, before_overlap, last_squares, last_overlap = totals_of(total_ref, 0, 1, 1)
     before = 1.0 / scale_of(plan, before_squares)
     back = known_ref[1:2, :1] * before
     last = back / scale_of(plan, last_squares * back * back)
     for vector, (out_ref, factor) in enumerate(((before_ref, before), (last_ref, last))):
         for block in range(plan.lane_blocks):
-            first = vector * plan.body + block
-            parts = [
-                arrived_ref[pl.ds(first + piece * plan.lane_blocks, plan.groups, stride=plan.outward), :]
-                for piece in range(plan.pieces)
-            ]
+            parts = []
+            for piece in range(plan.pieces):
+                row = vector * plan.body + piece * plan.lane_blocks + block
+                own = own_ref[pl.ds(row, plan.half, stride=plan.outward), :]
+                other = other_ref[pl.ds(row, plan.half, stride=2 * plan.body), :]
+                parts += [jnp.where(upper, other, own), jnp.where(upper, own, other)]
             out_ref[pl.ds(block * LANES, LANES), :] = jnp.concatenate(parts, axis=0).T * factor
     moments_ref[0] = known_ref[0, 0]
     moments_ref[1] = (before_overlap * before / plan.entries)[0, 0]
     moments_ref[2] = (last_overlap * last / plan.entries)[0, 0]
 
 
+def exchange_half(plan, values):
+    shaped = values.reshape(plan.half, values.shape[0] // plan.half, 1, LANES)
+    halves = [list(range(start, start + plan.half)) for start in (0, plan.half)]
+    return lax.all_to_all(shaped, AXES, 0, 0, axis_index_groups=halves, tiled=True).reshape(values.shape)
+
+
+def crossed(plan, values):
+    return lax.ppermute(values, "site", [(site, site ^ plan.sites // 2) for site in range(plan.sites)])
+
+
 def exchange(values, count):
     shaped = values.reshape(count, values.shape[0] // count, 1, LANES)
     return lax.all_to_all(shaped, AXES, 0, 0, tiled=True).reshape(values.shape)
@@ -418,7 +500,8 @@
 def shards(plan, state, operators, op_mask, site_bits, field, site_coupling, mode_coupling):
     f32 = jnp.float32
     inward = jax.ShapeDtypeStruct((plan.groups * plan.inward, LANES), f32)
-    outward = jax.ShapeDtypeStruct((plan.groups * plan.outward, LANES), f32)
+    outward = jax.ShapeDtypeStruct((plan.half * plan.outward, LANES), f32)
+    unsummed = jax.ShapeDtypeStruct((plan.half * 2 * plan.body, LANES), f32)
     vector = jax.ShapeDtypeStruct((plan.places, plan.rows), f32)
     known = jax.ShapeDtypeStruct((SUBLANES, LANES), f32)
     held = jax.ShapeDtypeStruct((plan.rows, plan.columns), f32)
@@ -439,6 +522,7 @@
         name="depart",
     )(state)
     arrived = exchange(departing, plan.groups)
+    partner_state = crossed(plan, arrived)
     fetched = plan.slabs - plan.kept
     kept_slabs = (plan.kept, plan.rows, plan.width)
     fetched_slabs = (fetched, plan.rows, plan.width)
@@ -446,15 +530,16 @@
     def held_slabs(count):
         return pltpu.VMEM((count, plan.width, plan.rows), jnp.bfloat16)
 
-    place, inside, kept = pl.pallas_call(
+    place, partner, inside, kept = pl.pallas_call(
         functools.partial(prepare_kernel, plan),
         out_shape=[
             jax.ShapeDtypeStruct((3, plan.places, LANES), f32),
+            jax.ShapeDtypeStruct((2, plan.places, LANES), f32),
             jax.ShapeDtypeStruct((SUBLANES, plan.rows), f32),
             jax.ShapeDtypeStruct(kept_slabs, jnp.bfloat16),
         ],
         in_specs=[SMEM] * 5 + [HBM],
-        out_specs=[VMEM] * 3,
+        out_specs=[VMEM] * 4,
         scratch_shapes=[held_slabs(plan.kept), pltpu.SemaphoreType.DMA((plan.kept,))],
         compiler_params=params(50),
         cost_estimate=cost(plan.rows * plan.rows, 4 * plan.kept * plan.rows * plan.width),
@@ -502,15 +587,28 @@
         cost_estimate=cost(2 * work, 8 * plan.places * plan.rows),
         name="onward",
     )(sums, raw, initial, *tables)
-    arrived = exchange(departing, plan.groups)
+    own = exchange_half(plan, departing)
+    departing, share = pl.pallas_call(
+        functools.partial(partner_kernel, plan),
+        out_shape=[unsummed, known],
+        in_specs=[VMEM] * 8,
+        out_specs=[VMEM] * 2,
+        scratch_shapes=[rounded, rounded, rounded, working, working, working],
+        compiler_params=params(32),
+        cost_estimate=cost(3 * work, 8 * plan.places * plan.rows),
+        name="partner",
+    )(partner_state, told, own, place, partner, inside, kept, late)
+    other_share = crossed(plan, share)
+    other = exchange_half(plan, departing)
     before, last, moments = pl.pallas_call(
         functools.partial(arrive_kernel, plan),
         out_shape=[held, held, jax.ShapeDtypeStruct((STEPS,), f32)],
-        in_specs=[VMEM] * 2,
+        in_specs=[VMEM] * 5,
         out_specs=[VMEM, VMEM, SMEM],
+        scratch_shapes=[pltpu.VMEM((SUBLANES, LANES), f32)],
         compiler_params=params(16),
         name="arrive",
-    )(arrived, told)
+    )(own, other, told, share, other_share)
     return last, before, moments
 
 

time: 73.8 us -> 101 us (1.37)
  waiting for transfers between devices: 8.43 us -> 43.7 us
  blocking collectives: 40.2 us -> 10.1 us
  starting transfers between devices: 7.3 us -> 18 us
  Pallas kernels: 16.7 us -> 23.1 us
  local copies, waits for them, and re-layouts: 0.03 us -> 4.75 us
    ppermute x0 -> x2, waiting for transfers between devices: none -> 31.4 us  [crossed(): lax.ppermute(values, 'site', [(site, site ^ plan.sites // 2) for site in...]
    all_to_all x2 -> x1, blocking collectives: 40.2 us -> 10.1 us  [exchange(): return lax.all_to_all(shaped, AXES, 0, 0, tiled=True).reshape(values.shape)]
    all_to_all x0 -> x2, starting transfers between devices: none -> 8.4 us  [exchange_half(): lax.all_to_all(shaped, AXES, 0, 0, axis_index_groups=halves, tiled=True)]
    pallas_call x0 -> x1, Pallas kernels: none -> 5.28 us  [shards(): pl.pallas_call(functools.partial(partner_kernel, plan), out_shape=[unsumm...]
    unnamed x10 -> x20, local copies, waits for them, and re-layouts: 0.03 us -> 4.75 us
    all_to_all x0 -> x2, waiting for transfers between devices: none -> 3.78 us  [exchange_half(): lax.all_to_all(shaped, AXES, 0, 0, axis_index_groups=halves, tiled=True)]
    ppermute x0 -> x2, starting transfers between devices: none -> 2.26 us  [crossed(): lax.ppermute(values, 'site', [(site, site ^ plan.sites // 2) for site in...]
    pallas_call x1, Pallas kernels: 1.27 us -> 2.39 us  [shards(): pl.pallas_call(functools.partial(arrive_kernel, plan), out_shape=[held, h...]
  transfers between devices with their start and end apart: 1 -> 5, of which waited for: 1 -> 4; matrix products, arithmetic and copies ran while one was open for 0% -> 0% of each run, Pallas kernels for 10% -> 7%
where the time goes in v19:
time: 101 us
  waiting for transfers between devices  43.7 us (43%)
  Pallas kernels  23.1 us (23%)
  starting transfers between devices  18 us (18%)
  blocking collectives  10.1 us (10%)
  local copies, waits for them, and re-layouts  4.75 us (5%)
    ppermute x2, waiting for transfers between devices, crossed(): lax.ppermute(values, 'site', [(site, site ^ plan.sites // 2) for site in...  31.4 us
    all_to_all x1, blocking collectives, exchange(): return lax.all_to_all(shaped, AXES, 0, 0, tiled=True).reshape(values.shape)  10.1 us
    all_to_all x1, waiting for transfers between devices, exchange(): return lax.all_to_all(shaped, AXES, 0, 0, tiled=True).reshape(values.shape)  8.45 us
    all_to_all x2, starting transfers between devices, exchange_half(): lax.all_to_all(shaped, AXES, 0, 0, axis_index_groups=halves, tiled=True)  8.4 us
    all_to_all x1, starting transfers between devices, exchange(): return lax.all_to_all(shaped, AXES, 0, 0, tiled=True).reshape(values.shape)  7.3 us
    pallas_call x1, Pallas kernels, shards(): pl.pallas_call(functools.partial(partner_kernel, plan), out_shape=[unsumm...  5.28 us
    unnamed x20, local copies, waits for them, and re-layouts  4.75 us
    pallas_call x1, Pallas kernels, shards(): pl.pallas_call(functools.partial(store_kernel, plan), out_shape=jax.Shape...  4.4 us
  transfers between devices with their start and end apart: 5, of which 4 were waited for; matrix products, arithmetic and copies ran while one was open for 0% of the time, Pallas kernels for 7%

profile of v19, /device:TPU:0, one launch (start us, length us, event | category | flops | bytes accessed | tf_op | source)
XLA Modules:
  0.0 100.5 jit_solution(10735892977534540532)
XLA Ops:
  0.6 2.1 %depart.1 = f32[1056,128]{1,0:T(8,128)} custom-call(f32[1024,128]{1,0:T(8,128)} %state_ref.1), custom_call_target="tpu_custom_call" | custom-call | tf_op jit(solution)/shard_map/depart/pallas_call | solution.py:515
  2.8 7.3 %all-to-all-start = ((f32[32,33,1,128]{3,2,1,0:T(1,128)}), f32[32,33,1,128]{3,2,1,0:T(1,128)S(1)}, u32[]{:S(2)}, u32[]{:S(2)}) async-start(f32[32,33,1,128]{3,2,1,0:T(1,128)} %bitcast.18), calls=%async_computation | async-start | bytes 1081344 | tf_op jit(solution)/shard_map/all_to_all | solution.py:497
  10.1 0.0 copy-start.3
  10.1 0.0 copy-start.4
  10.1 0.0 copy-start.5
  10.1 0.0 copy-start.6
  10.1 0.0 copy-start.7
  10.1 4.4 %store.1.stored_ref = bf16[7,1024,256]{2,1,0:T(8,128)(2,1)} custom-call(s32[3]{0:T(128)} %bits_ref.3, s32[3,8,8]{2,1,0:T(8,128)} %mask_ref.3, bf16[3,1024,1024]{2,1,0:T(8,128)(2,1)} %operators_ref.3), custom_call_target="tpu_custom_call" | custom-call | flops 1048576 | bytes 7340032 | tf_op jit(solution)/shard_map/store/pallas_call | solution.py:548
  14.5 0.0 copy-done.3
  14.5 0.0 copy-done.4
  14.6 0.0 copy-done.5
  14.6 0.0 copy-done.6
  14.6 0.0 copy-done.7
  14.6 2.9 %prepare.1 = (f32[3,128,128]{2,1,0:T(8,128)S(1)}, f32[2,128,128]{2,1,0:T(8,128)S(1)}, f32[8,1024]{1,0:T(8,128)S(1)}, bf16[5,1024,256]{2,1,0:T(8,128)(2,1)S(1)}) custom-call(s32[3]{0:T(128)S(1)} %copy-done.4, s32[3,8,8]{2,1,0:T(8,128)S(1)} %copy-done.3, f32[3]{0:T(128)S(1)} %copy-done.5, f32[13]{0:T(128)S(1)} %copy-done.6, f32[64]{0:T(128)S(1)} %copy-done.7, ...), custom_call_target="tpu_custom_call" | custom-call | flops 1048576 | bytes 5242880 | tf_op jit(solution)/shard_map/prepare/pallas_call | solution.py:533
  17.5 8.4 %all-to-all-done = f32[32,33,1,128]{3,2,1,0:T(1,128)S(1)} async-done(((f32[32,33,1,128]{3,2,1,0:T(1,128)}), f32[32,33,1,128]{3,2,1,0:T(1,128)S(1)}, u32[]{:S(2)}, u32[]{:S(2)}) %all-to-all-start) | async-done | bytes 540704 | tf_op jit(solution)/shard_map/all_to_all | solution.py:497
  25.9 3.7 %first.1 = (f32[128,1024]{1,0:T(8,128)S(1)}, f32[128,1024]{1,0:T(8,128)S(1)}, f32[32,128]{1,0:T(8,128)S(1)}, bf16[7,1024,256]{2,1,0:T(8,128)(2,1)S(1)}) custom-call(f32[1056,128]{1,0:T(8,128)S(1)} %bitcast.12, f32[3,128,128]{2,1,0:T(8,128)S(1)} %get-tuple-element.18.place_ref, f32[8,1024]{1,0:T(8,128)S(1)} %get-tuple-element.19.inside_ref, ...), custom_call_target="tpu_custom_call" | custom-call | flops 1610612736 | bytes 524288 | tf_op jit(solution)/shard_map/first/pallas_call | solution.py:563
  29.6 0.0 copy-start
  29.6 10.1 %all_to_all.20 = f32[32,1,1,128]{3,2,1,0:T(1,128)S(1)} all-to-all(f32[32,1,1,128]{3,2,1,0:T(1,128)S(1)} %bitcast.17), channel_id=1, replica_groups=mesh['site'=8,'phonon'=4] {'site','phonon'}, dimensions={0} | all-to-all | bytes 32768 | tf_op jit(solution)/shard_map/all_to_all | solution.py:497
  39.7 2.4 %onward.1 = (f32[1040,128]{1,0:T(8,128)S(1)}, f32[8,128]{1,0:T(8,128)S(1)}) custom-call(f32[32,128]{1,0:T(8,128)S(1)} %bitcast.16, f32[128,1024]{1,0:T(8,128)S(1)} %get-tuple-element.22.raw_ref, f32[128,1024]{1,0:T(8,128)S(1)} %get-tuple-element.23.initial_ref, f32[3,128,128]{2,1,0:T(8,128)S(1)} %get-tuple-element.18.place_ref, ...), custom_call_target="tpu_custom_call" | custom-call | flops 1610612736 | bytes 1048576 | tf_op jit(solution)/shard_map/onward/pallas_call | solution.py:580
  42.1 0.0 copy-done
  42.1 0.0 copy-start.2
  42.1 0.8 copy-done.2
  42.9 4.4 %all-to-all-start.2 = ((f32[16,65,1,128]{3,2,1,0:T(1,128)}), f32[16,65,1,128]{3,2,1,0:T(1,128)}, u32[]{:S(2)}, u32[]{:S(2)}) async-start(f32[16,65,1,128]{3,2,1,0:T(1,128)} %bitcast.15), calls=%async_computation.2 | async-start | bytes 1064960 | tf_op jit(solution)/shard_map/all_to_all | solution.py:488
  47.3 0.7 collective-permute-start
  48.0 26.2 %collective-permute-done.state_ref = f32[1056,128]{1,0:T(8,128)S(1)} collective-permute-done((f32[1056,128]{1,0:T(8,128)S(1)}, f32[1056,128]{1,0:T(8,128)S(1)}, u32[]{:S(2)}, u32[]{:S(2)}) %collective-permute-start) | collective-permute-done | bytes 540704 | tf_op jit(solution)/shard_map/ppermute | solution.py:492
  74.2 0.0 copy-start.8
  74.2 0.8 copy-done.8
  75.0 0.0 all-to-all-done.2
  75.0 0.0 copy-start.1
  75.0 2.0 %copy-done.1 = bf16[7,1024,256]{2,1,0:T(8,128)(2,1)S(1)} copy-done((bf16[7,1024,256]{2,1,0:T(8,128)(2,1)S(1)}, bf16[7,1024,256]{2,1,0:T(8,128)(2,1)}, u32[]{:S(2)}) %copy-start.1) | copy-done | bytes 3670040
  77.0 0.0 copy-start.9
  77.0 1.0 %copy-done.9 = f32[1056,128]{1,0:T(8,128)S(1)} copy-done((f32[1056,128]{1,0:T(8,128)S(1)}, f32[1056,128]{1,0:T(8,128)}, u32[]{:S(2)}) %copy-start.9) | copy-done | bytes 540696
  78.1 5.3 %partner.1 = (f32[1024,128]{1,0:T(8,128)}, f32[8,128]{1,0:T(8,128)S(1)}) custom-call(f32[1056,128]{1,0:T(8,128)S(1)} %copy-done.9, f32[8,128]{1,0:T(8,128)S(1)} %get-tuple-element.26.known_ref, f32[1040,128]{1,0:T(8,128)} %bitcast.6.own_ref, f32[3,128,128]{2,1,0:T(8,128)S(1)} %get-tuple-element.18.place_ref, ...), custom_call_target="tpu_custom_call" | custom-call | flops 2415919104 | bytes 1048576 | tf_op jit(solution)/shard_map/partner/pallas_call | solution.py:591
  83.3 4.0 %all-to-all-start.3 = ((f32[16,64,1,128]{3,1,2,0:T(8,128)}), f32[16,64,1,128]{3,1,2,0:T(8,128)S(1)}, u32[]{:S(2)}, u32[]{:S(2)}) async-start(f32[16,64,1,128]{3,1,2,0:T(8,128)} %bitcast.8), calls=%async_computation.3 | async-start | bytes 1048576 | tf_op jit(solution)/shard_map/all_to_all | solution.py:488
  87.3 1.6 %collective-permute-start.1 = (f32[8,128]{1,0:T(8,128)S(1)}, f32[8,128]{1,0:T(8,128)S(1)}, u32[]{:S(2)}, u32[]{:S(2)}) collective-permute-start(f32[8,128]{1,0:T(8,128)S(1)} %get-tuple-element.29.sums_ref), channel_id=1, source_target_pairs={{0,16},{4,20},{8,24},{12,28},{16,0},{20,4},{24,8},{28,12},{1,17},{... | collective-permute-start | bytes 12296 | tf_op jit(solution)/shard_map/ppermute | solution.py:492
  88.9 5.3 %collective-permute-done.1.other_sums_ref = f32[8,128]{1,0:T(8,128)S(1)} collective-permute-done((f32[8,128]{1,0:T(8,128)S(1)}, f32[8,128]{1,0:T(8,128)S(1)}, u32[]{:S(2)}, u32[]{:S(2)}) %collective-permute-start.1) | collective-permute-done | bytes 4128 | tf_op jit(solution)/shard_map/ppermute | solution.py:492
  94.2 3.8 %all-to-all-done.3 = f32[16,64,1,128]{3,1,2,0:T(8,128)S(1)} async-done(((f32[16,64,1,128]{3,1,2,0:T(8,128)}), f32[16,64,1,128]{3,1,2,0:T(8,128)S(1)}, u32[]{:S(2)}, u32[]{:S(2)}) %all-to-all-start.3) | async-done | bytes 524320 | tf_op jit(solution)/shard_map/all_to_all | solution.py:488
  98.0 2.4 %arrive.1 = (f32[1024,128]{1,0:T(8,128)}, f32[1024,128]{1,0:T(8,128)}, f32[3]{0:T(128)}) custom-call(f32[1040,128]{1,0:T(8,128)} %bitcast.6.own_ref, f32[1024,128]{1,0:T(8,128)S(1)} %bitcast.14, f32[8,128]{1,0:T(8,128)S(1)} %get-tuple-element.26.known_ref, f32[8,128]{1,0:T(8,128)S(1)} %get-tuple-element.29.sums_ref, ...), custom_call_target="tpu_custom_call" | custom-call | tf_op jit(solution)/shard_map/arrive/pallas_call | solution.py:603
Async XLA Ops:
  2.8 23.2 %all-to-all-start = ((f32[32,33,1,128]{3,2,1,0:T(1,128)}), f32[32,33,1,128]{3,2,1,0:T(1,128)S(1)}, u32[]{:S(2)}, u32[]{:S(2)}) async-start(f32[32,33,1,128]{3,2,1,0:T(1,128)} %bitcast.18), calls=%async_computation | async-start | bytes 1081344 | tf_op jit(solution)/shard_map/all_to_all | solution.py:497
  10.1 4.5 %copy-start.3 = (s32[3,8,8]{2,1,0:T(8,128)S(1)}, s32[3,8,8]{2,1,0:T(8,128)}, u32[]{:S(2)}) copy-start(s32[3,8,8]{2,1,0:T(8,128)} %mask_ref.3) | copy-start | bytes 2308
  10.1 4.5 %copy-start.4 = (s32[3]{0:T(128)S(1)}, s32[3]{0:T(128)}, u32[]{:S(2)}) copy-start(s32[3]{0:T(128)} %bits_ref.3) | copy-start | bytes 40
  10.1 4.5 %copy-start.5 = (f32[3]{0:T(128)S(1)}, f32[3]{0:T(128)}, u32[]{:S(2)}) copy-start(f32[3]{0:T(128)} %field_ref.1) | copy-start | bytes 40
  10.1 4.5 %copy-start.6 = (f32[13]{0:T(128)S(1)}, f32[13]{0:T(128)}, u32[]{:S(2)}) copy-start(f32[13]{0:T(128)} %coupling_ref.1) | copy-start | bytes 160
  10.1 4.5 %copy-start.7 = (f32[64]{0:T(128)S(1)}, f32[64]{0:T(128)}, u32[]{:S(2)}) copy-start(f32[64]{0:T(128)} %mode_ref.1) | copy-start | bytes 772
  29.6 12.5 %copy-start = (bf16[7,1024,256]{2,1,0:T(8,128)(2,1)}, bf16[7,1024,256]{2,1,0:T(8,128)(2,1)S(1)}, u32[]{:S(2)}) copy-start(bf16[7,1024,256]{2,1,0:T(8,128)(2,1)S(1)} %get-tuple-element.24.fetched_ref) | copy-start | bytes 11010052
  42.1 0.8 copy-start.2
  42.9 32.0 %all-to-all-start.2 = ((f32[16,65,1,128]{3,2,1,0:T(1,128)}), f32[16,65,1,128]{3,2,1,0:T(1,128)}, u32[]{:S(2)}, u32[]{:S(2)}) async-start(f32[16,65,1,128]{3,2,1,0:T(1,128)} %bitcast.15), calls=%async_computation.2 | async-start | bytes 1064960 | tf_op jit(solution)/shard_map/all_to_all | solution.py:488
  47.3 26.8 %collective-permute-start = (f32[1056,128]{1,0:T(8,128)S(1)}, f32[1056,128]{1,0:T(8,128)S(1)}, u32[]{:S(2)}, u32[]{:S(2)}) collective-permute-start(f32[1056,128]{1,0:T(8,128)S(1)} %bitcast.13), channel_id=1, source_target_pairs={{0,16},{4,20},{8,24},{12,28},{16,0},{20,4},{24,8},{28,12},{1,17},{... | collective-permute-start | bytes 1622024 | tf_op jit(solution)/shard_map/ppermute | solution.py:492
  74.2 0.8 copy-start.8
  75.0 2.0 %copy-start.1 = (bf16[7,1024,256]{2,1,0:T(8,128)(2,1)S(1)}, bf16[7,1024,256]{2,1,0:T(8,128)(2,1)}, u32[]{:S(2)}) copy-start(bf16[7,1024,256]{2,1,0:T(8,128)(2,1)} %copy-done) | copy-start | bytes 11010052
  77.0 1.0 %copy-start.9 = (f32[1056,128]{1,0:T(8,128)S(1)}, f32[1056,128]{1,0:T(8,128)}, u32[]{:S(2)}) copy-start(f32[1056,128]{1,0:T(8,128)} %copy-done.8) | copy-start | bytes 1622020
  83.3 14.6 %all-to-all-start.3 = ((f32[16,64,1,128]{3,1,2,0:T(8,128)}), f32[16,64,1,128]{3,1,2,0:T(8,128)S(1)}, u32[]{:S(2)}, u32[]{:S(2)}) async-start(f32[16,64,1,128]{3,1,2,0:T(8,128)} %bitcast.8), calls=%async_computation.3 | async-start | bytes 1048576 | tf_op jit(solution)/shard_map/all_to_all | solution.py:488
  87.3 6.9 %collective-permute-start.1 = (f32[8,128]{1,0:T(8,128)S(1)}, f32[8,128]{1,0:T(8,128)S(1)}, u32[]{:S(2)}, u32[]{:S(2)}) collective-permute-start(f32[8,128]{1,0:T(8,128)S(1)} %get-tuple-element.29.sums_ref), channel_id=1, source_target_pairs={{0,16},{4,20},{8,24},{12,28},{16,0},{20,4},{24,8},{28,12},{1,17},{... | collective-permute-start | bytes 12296 | tf_op jit(solution)/shard_map/ppermute | solution.py:492

commit v20 on v14

--- a/solution.py
+++ b/solution.py
@@ -48,6 +48,13 @@
         self.kept = min(5, self.slabs - 1)
         self.entries = float(rows * columns * self.groups)
 
+    def stride(self, position):
+        return self.phonons << (self.bits - 1 - position)
+
+    def order(self):
+        sites = [sum((site >> bit & 1) << (self.bits - 1 - bit) for bit in range(self.bits)) for site in range(self.sites)]
+        return [site * self.phonons + phonon for site in sites for phonon in range(self.phonons)]
+
     def fits(self):
         return (
             MODES % self.groups == 0
@@ -172,15 +179,16 @@
 ):
     slabs = range(plan.kept)
     fetches = fetch_slabs(plan, slabs, bits_ref, operators_ref, held_ref, semaphores)
-    me = lax.axis_index("site") * plan.phonons + lax.axis_index("phonon")
+    me = lax.axis_index("phonon")
+    for position in range(plan.bits):
+        me = me + (lax.axis_index("site") >> position & 1) * plan.stride(position)
     place = lax.broadcasted_iota(jnp.int32, (plan.places, LANES), 0)
     phonon = place % plan.phonons
-    site = place // plan.phonons % plan.sites
     mode = place // plan.groups % plan.share
     level = phonon * plan.levels_here + place // (plan.groups * plan.share)
     occupied = jnp.zeros((plan.places, LANES), jnp.float32)
     for position in range(plan.bits):
-        held = (site >> position & 1).astype(jnp.float32)
+        held = (place // plan.stride(position) % 2).astype(jnp.float32)
         occupied = occupied + coupling_ref[bits_ref[position]] * held
     strength = jnp.zeros((plan.places, LANES), jnp.float32)
     for index in range(plan.share):
@@ -226,7 +234,7 @@
 def put_rounded(plan, rounded_ref, vector, start):
     for position in range(plan.bits):
         rounded_ref[:, pl.ds(position * plan.rows + start, vector.shape[1])] = flipped(
-            vector, plan.phonons << position
+            vector, plan.stride(position)
         ).astype(jnp.bfloat16)
 
 
@@ -242,7 +250,7 @@
         weight = place_ref[0] + inside_ref[:1, lanes]
         total = weight * (place_ref[1] * lower + place_ref[2] * upper)
         for position in range(plan.bits):
-            total = total + inside_ref[pl.ds(1 + position, 1), lanes] * flipped(vector, plan.phonons << position)
+            total = total + inside_ref[pl.ds(1 + position, 1), lanes] * flipped(vector, plan.stride(position))
         return total
 
     def added(total, part, late):
@@ -410,9 +418,9 @@
     moments_ref[2] = (last_overlap * last / plan.entries)[0, 0]
 
 
-def exchange(values, count):
-    shaped = values.reshape(count, values.shape[0] // count, 1, LANES)
-    return lax.all_to_all(shaped, AXES, 0, 0, tiled=True).reshape(values.shape)
+def exchange(plan, values):
+    shaped = values.reshape(plan.groups, values.shape[0] // plan.groups, 1, LANES)
+    return lax.all_to_all(shaped, AXES, 0, 0, axis_index_groups=[plan.order()], tiled=True).reshape(values.shape)
 
 
 def shards(plan, state, operators, op_mask, site_bits, field, site_coupling, mode_coupling):
@@ -438,7 +446,7 @@
         compiler_params=params(60),
         name="depart",
     )(state)
-    arrived = exchange(departing, plan.groups)
+    arrived = exchange(plan, departing)
     fetched = plan.slabs - plan.kept
     kept_slabs = (plan.kept, plan.rows, plan.width)
     fetched_slabs = (fetched, plan.rows, plan.width)
@@ -491,7 +499,7 @@
         name="first",
     )(arrived, place, inside, kept, stored)
     tables = (place, inside, kept, late)
-    sums = exchange(sums, plan.groups)
+    sums = exchange(plan, sums)
     departing, told = pl.pallas_call(
         functools.partial(onward_kernel, plan),
         out_shape=[outward, known],
@@ -502,7 +510,7 @@
         cost_estimate=cost(2 * work, 8 * plan.places * plan.rows),
         name="onward",
     )(sums, raw, initial, *tables)
-    arrived = exchange(departing, plan.groups)
+    arrived = exchange(plan, departing)
     before, last, moments = pl.pallas_call(
         functools.partial(arrive_kernel, plan),
         out_shape=[held, held, jax.ShapeDtypeStruct((STEPS,), f32)],

time: 73.8 us -> 73.8 us (level)
  no operation moved by 1% of the time
where the time goes in v20:
time: 73.8 us; the launch traced here: 73.4 us
  blocking collectives  39.8 us (54%)
  Pallas kernels  17 us (23%)
  waiting for transfers between devices  8.5 us (12%)
  starting transfers between devices  7.3 us (10%)
  between operations  0.75 us (1%)
    all_to_all x2, blocking collectives, exchange(): lax.all_to_all(shaped, AXES, 0, 0, axis_index_groups=[plan.order()], tile...  39.8 us
    all_to_all x1, waiting for transfers between devices, exchange(): lax.all_to_all(shaped, AXES, 0, 0, axis_index_groups=[plan.order()], tile...  8.5 us
    all_to_all x1, starting transfers between devices, exchange(): lax.all_to_all(shaped, AXES, 0, 0, axis_index_groups=[plan.order()], tile...  7.3 us
    pallas_call x1, Pallas kernels, shards(): pl.pallas_call(functools.partial(store_kernel, plan), out_shape=jax.Shape...  4.41 us
    pallas_call x1, Pallas kernels, shards(): pl.pallas_call(functools.partial(first_kernel, plan), out_shape=[vector,...  3.97 us
    pallas_call x1, Pallas kernels, shards(): pl.pallas_call(functools.partial(prepare_kernel, plan), out_shape=[jax.Sh...  2.87 us
    pallas_call x1, Pallas kernels, shards(): pl.pallas_call(functools.partial(onward_kernel, plan), out_shape=[outward...  2.37 us
    pallas_call x1, Pallas kernels, shards(): pl.pallas_call(functools.partial(depart_kernel, plan), out_shape=inward,...  2.12 us
  transfers between devices with their start and end apart: 1, of which 1 were waited for; matrix products, arithmetic and copies ran while one was open for 0% of the time, Pallas kernels for 10%

profile of v20, /device:TPU:0, one launch (start us, length us, event | category | flops | bytes accessed | tf_op | source)
XLA Modules:
  0.0 73.4 jit_solution(3604111460941933804)
XLA Ops:
  0.6 2.1 %depart.1 = f32[1056,128]{1,0:T(8,128)} custom-call(f32[1024,128]{1,0:T(8,128)} %state_ref.1), custom_call_target="tpu_custom_call" | custom-call | tf_op jit(solution)/shard_map/depart/pallas_call | solution.py:440
  2.8 7.3 %all-to-all-start = ((f32[32,33,1,128]{3,2,1,0:T(1,128)}), f32[32,33,1,128]{3,2,1,0:T(1,128)S(1)}, u32[]{:S(2)}, u32[]{:S(2)}) async-start(f32[32,33,1,128]{3,2,1,0:T(1,128)} %bitcast.13), calls=%async_computation | async-start | bytes 1081344 | tf_op jit(solution)/shard_map/all_to_all | solution.py:423
  10.1 0.0 copy-start
  10.1 0.0 copy-start.1
  10.1 0.0 copy-start.2
  10.1 0.0 copy-start.3
  10.1 0.0 copy-start.4
  10.1 4.4 %store.1.stored_ref = bf16[7,1024,256]{2,1,0:T(8,128)(2,1)} custom-call(s32[3]{0:T(128)} %bits_ref.3, s32[3,8,8]{2,1,0:T(8,128)} %mask_ref.3, bf16[3,1024,1024]{2,1,0:T(8,128)(2,1)} %operators_ref.3), custom_call_target="tpu_custom_call" | custom-call | flops 1048576 | bytes 7340032 | tf_op jit(solution)/shard_map/store/pallas_call | solution.py:471
  14.6 0.0 copy-done
  14.6 0.0 copy-done.1
  14.6 0.0 copy-done.2
  14.6 0.0 copy-done.3
  14.6 0.0 copy-done.4
  14.6 2.9 %prepare.1 = (f32[3,128,128]{2,1,0:T(8,128)S(1)}, f32[8,1024]{1,0:T(8,128)S(1)}, bf16[5,1024,256]{2,1,0:T(8,128)(2,1)S(1)}) custom-call(s32[3]{0:T(128)S(1)} %copy-done.1, s32[3,8,8]{2,1,0:T(8,128)S(1)} %copy-done, f32[3]{0:T(128)S(1)} %copy-done.2, f32[13]{0:T(128)S(1)} %copy-done.3, f32[64]{0:T(128)S(1)} %copy-done.4, bf16[3,1024,1024]{2,1,0:T(8,128)(2,1)} %operators_ref.3), custom_call_target="tpu_custom_call" | custom-call | flops 1048576 | bytes 5242880 | tf_op jit(solution)/shard_map/prepare/pallas_call | solution.py:457
  17.5 8.5 %all-to-all-done = f32[32,33,1,128]{3,2,1,0:T(1,128)S(1)} async-done(((f32[32,33,1,128]{3,2,1,0:T(1,128)}), f32[32,33,1,128]{3,2,1,0:T(1,128)S(1)}, u32[]{:S(2)}, u32[]{:S(2)}) %all-to-all-start) | async-done | bytes 540704 | tf_op jit(solution)/shard_map/all_to_all | solution.py:423
  26.0 4.0 %first.1 = (f32[128,1024]{1,0:T(8,128)S(1)}, f32[128,1024]{1,0:T(8,128)S(1)}, f32[32,128]{1,0:T(8,128)S(1)}, bf16[7,1024,256]{2,1,0:T(8,128)(2,1)S(1)}) custom-call(f32[1056,128]{1,0:T(8,128)S(1)} %bitcast.9, f32[3,128,128]{2,1,0:T(8,128)S(1)} %get-tuple-element.15.place_ref, f32[8,1024]{1,0:T(8,128)S(1)} %get-tuple-element.16.inside_ref, ...), custom_call_target="tpu_custom_call" | custom-call | flops 1610612736 | bytes 524288 | tf_op jit(solution)/shard_map/first/pallas_call | solution.py:486
  30.0 9.7 %all_to_all.15 = f32[32,1,1,128]{3,2,1,0:T(1,128)S(1)} all-to-all(f32[32,1,1,128]{3,2,1,0:T(1,128)S(1)} %bitcast.12), channel_id=1, replica_groups={{0,1,2,3,16,17,18,19,8,9,10,11,24,25,26,27,4,5,6,7,20,21,22,23,12,13,14..., dimensions={0} | all-to-all | bytes 32768 | tf_op jit(solution)/shard_map/all_to_all | solution.py:423
  39.7 2.4 %onward.1 = (f32[2080,128]{1,0:T(8,128)S(1)}, f32[8,128]{1,0:T(8,128)S(1)}) custom-call(f32[32,128]{1,0:T(8,128)S(1)} %bitcast.11, f32[128,1024]{1,0:T(8,128)S(1)} %get-tuple-element.19.raw_ref, f32[128,1024]{1,0:T(8,128)S(1)} %get-tuple-element.20.initial_ref, f32[3,128,128]{2,1,0:T(8,128)S(1)} %get-tuple-element.15.place_ref, ...), custom_call_target="tpu_custom_call" | custom-call | flops 1610612736 | bytes 1048576 | tf_op jit(solution)/shard_map/onward/pallas_call | solution.py:503
  42.0 30.1 %all_to_all.16 = f32[32,65,1,128]{3,2,1,0:T(1,128)S(1)} all-to-all(f32[32,65,1,128]{3,2,1,0:T(1,128)S(1)} %bitcast.10), channel_id=1, replica_groups={{0,1,2,3,16,17,18,19,8,9,10,11,24,25,26,27,4,5,6,7,20,21,22,23,12,13,14..., dimensions={0} | all-to-all | bytes 2129920 | tf_op jit(solution)/shard_map/all_to_all | solution.py:423
  72.2 1.3 %arrive.1 = (f32[1024,128]{1,0:T(8,128)}, f32[1024,128]{1,0:T(8,128)}, f32[3]{0:T(128)}) custom-call(f32[2080,128]{1,0:T(8,128)S(1)} %bitcast.8, f32[8,128]{1,0:T(8,128)S(1)} %get-tuple-element.23.known_ref), custom_call_target="tpu_custom_call" | custom-call | tf_op jit(solution)/shard_map/arrive/pallas_call | solution.py:514
Async XLA Ops:
  2.8 23.2 %all-to-all-start = ((f32[32,33,1,128]{3,2,1,0:T(1,128)}), f32[32,33,1,128]{3,2,1,0:T(1,128)S(1)}, u32[]{:S(2)}, u32[]{:S(2)}) async-start(f32[32,33,1,128]{3,2,1,0:T(1,128)} %bitcast.13), calls=%async_computation | async-start | bytes 1081344 | tf_op jit(solution)/shard_map/all_to_all | solution.py:423
  10.1 4.5 %copy-start = (s32[3,8,8]{2,1,0:T(8,128)S(1)}, s32[3,8,8]{2,1,0:T(8,128)}, u32[]{:S(2)}) copy-start(s32[3,8,8]{2,1,0:T(8,128)} %mask_ref.3) | copy-start | bytes 2308
  10.1 4.5 %copy-start.1 = (s32[3]{0:T(128)S(1)}, s32[3]{0:T(128)}, u32[]{:S(2)}) copy-start(s32[3]{0:T(128)} %bits_ref.3) | copy-start | bytes 40
  10.1 4.5 %copy-start.2 = (f32[3]{0:T(128)S(1)}, f32[3]{0:T(128)}, u32[]{:S(2)}) copy-start(f32[3]{0:T(128)} %field_ref.1) | copy-start | bytes 40
  10.1 4.5 %copy-start.3 = (f32[13]{0:T(128)S(1)}, f32[13]{0:T(128)}, u32[]{:S(2)}) copy-start(f32[13]{0:T(128)} %coupling_ref.1) | copy-start | bytes 160
  10.1 4.5 %copy-start.4 = (f32[64]{0:T(128)S(1)}, f32[64]{0:T(128)}, u32[]{:S(2)}) copy-start(f32[64]{0:T(128)} %mode_ref.1) | copy-start | bytes 772

commit v21 on v14

--- a/solution.py
+++ b/solution.py
@@ -101,8 +101,8 @@
         )
         for index in range(2)
     ]
-    for fetch in fetches:
-        fetch.start()
+    for index, fetch in enumerate(fetches):
+        fetch.start(priority=index)
     sums = jnp.zeros((1, LANES), jnp.float32)
     for block in range(plan.lane_blocks):
         if block * LANES % half == 0:
@@ -294,7 +294,7 @@
     for slab in range(plan.kept, plan.slabs):
         index = slab - plan.kept
         fetches[slab] = pltpu.make_async_copy(stored_ref.at[index], fetched_ref.at[index], semaphores.at[index])
-        fetches[slab].start()
+        fetches[slab].start(priority=index % 2)
 
     def ready(slab):
         fetches[slab].wait()

time: 73.8 us -> 74.1 us (level)
  no operation moved by 1% of the time
where the time goes in v21:
time: 74.1 us; the launch traced here: 73.8 us
  blocking collectives  40.2 us (54%)
  Pallas kernels  17.1 us (23%)
  waiting for transfers between devices  8.43 us (11%)
  starting transfers between devices  7.3 us (10%)
  between operations  0.75 us (1%)
    all_to_all x2, blocking collectives, exchange(): return lax.all_to_all(shaped, AXES, 0, 0, tiled=True).reshape(values.shape)  40.2 us
    all_to_all x1, waiting for transfers between devices, exchange(): return lax.all_to_all(shaped, AXES, 0, 0, tiled=True).reshape(values.shape)  8.43 us
    all_to_all x1, starting transfers between devices, exchange(): return lax.all_to_all(shaped, AXES, 0, 0, tiled=True).reshape(values.shape)  7.3 us
    pallas_call x1, Pallas kernels, shards(): pl.pallas_call(functools.partial(store_kernel, plan), out_shape=jax.Shape...  4.41 us
    pallas_call x1, Pallas kernels, shards(): pl.pallas_call(functools.partial(first_kernel, plan), out_shape=[vector,...  4.02 us
    pallas_call x1, Pallas kernels, shards(): pl.pallas_call(functools.partial(prepare_kernel, plan), out_shape=[jax.Sh...  2.87 us
    pallas_call x1, Pallas kernels, shards(): pl.pallas_call(functools.partial(onward_kernel, plan), out_shape=[outward...  2.36 us
    pallas_call x1, Pallas kernels, shards(): pl.pallas_call(functools.partial(depart_kernel, plan), out_shape=inward,...  2.12 us
  transfers between devices with their start and end apart: 1, of which 1 were waited for; matrix products, arithmetic and copies ran while one was open for 0% of the time, Pallas kernels for 10%

profile of v21, /device:TPU:0, one launch (start us, length us, event | category | flops | bytes accessed | tf_op | source)
XLA Modules:
  0.0 73.8 jit_solution(6663143990922727931)
XLA Ops:
  0.6 2.1 %depart.1 = f32[1056,128]{1,0:T(8,128)} custom-call(f32[1024,128]{1,0:T(8,128)} %state_ref.1), custom_call_target="tpu_custom_call" | custom-call | tf_op jit(solution)/shard_map/depart/pallas_call | solution.py:432
  2.8 7.3 %all-to-all-start = ((f32[32,33,1,128]{3,2,1,0:T(1,128)}), f32[32,33,1,128]{3,2,1,0:T(1,128)S(1)}, u32[]{:S(2)}, u32[]{:S(2)}) async-start(f32[32,33,1,128]{3,2,1,0:T(1,128)} %bitcast.13), calls=%async_computation | async-start | bytes 1081344 | tf_op jit(solution)/shard_map/all_to_all | solution.py:415
  10.1 0.0 copy-start
  10.1 0.0 copy-start.1
  10.1 0.0 copy-start.2
  10.1 0.0 copy-start.3
  10.1 0.0 copy-start.4
  10.1 4.4 %store.1.stored_ref = bf16[7,1024,256]{2,1,0:T(8,128)(2,1)} custom-call(s32[3]{0:T(128)} %bits_ref.3, s32[3,8,8]{2,1,0:T(8,128)} %mask_ref.3, bf16[3,1024,1024]{2,1,0:T(8,128)(2,1)} %operators_ref.3), custom_call_target="tpu_custom_call" | custom-call | flops 1048576 | bytes 7340032 | tf_op jit(solution)/shard_map/store/pallas_call | solution.py:463
  14.6 0.0 copy-done
  14.6 0.0 copy-done.1
  14.6 0.0 copy-done.2
  14.6 0.0 copy-done.3
  14.6 0.0 copy-done.4
  14.6 2.9 %prepare.1 = (f32[3,128,128]{2,1,0:T(8,128)S(1)}, f32[8,1024]{1,0:T(8,128)S(1)}, bf16[5,1024,256]{2,1,0:T(8,128)(2,1)S(1)}) custom-call(s32[3]{0:T(128)S(1)} %copy-done.1, s32[3,8,8]{2,1,0:T(8,128)S(1)} %copy-done, f32[3]{0:T(128)S(1)} %copy-done.2, f32[13]{0:T(128)S(1)} %copy-done.3, f32[64]{0:T(128)S(1)} %copy-done.4, bf16[3,1024,1024]{2,1,0:T(8,128)(2,1)} %operators_ref.3), custom_call_target="tpu_custom_call" | custom-call | flops 1048576 | bytes 5242880 | tf_op jit(solution)/shard_map/prepare/pallas_call | solution.py:449
  17.5 8.4 %all-to-all-done = f32[32,33,1,128]{3,2,1,0:T(1,128)S(1)} async-done(((f32[32,33,1,128]{3,2,1,0:T(1,128)}), f32[32,33,1,128]{3,2,1,0:T(1,128)S(1)}, u32[]{:S(2)}, u32[]{:S(2)}) %all-to-all-start) | async-done | bytes 540704 | tf_op jit(solution)/shard_map/all_to_all | solution.py:415
  25.9 4.0 %first.1 = (f32[128,1024]{1,0:T(8,128)S(1)}, f32[128,1024]{1,0:T(8,128)S(1)}, f32[32,128]{1,0:T(8,128)S(1)}, bf16[7,1024,256]{2,1,0:T(8,128)(2,1)S(1)}) custom-call(f32[1056,128]{1,0:T(8,128)S(1)} %bitcast.9, f32[3,128,128]{2,1,0:T(8,128)S(1)} %get-tuple-element.15.place_ref, f32[8,1024]{1,0:T(8,128)S(1)} %get-tuple-element.16.inside_ref, ...), custom_call_target="tpu_custom_call" | custom-call | flops 1610612736 | bytes 524288 | tf_op jit(solution)/shard_map/first/pallas_call | solution.py:478
  29.9 10.1 %all_to_all.15 = f32[32,1,1,128]{3,2,1,0:T(1,128)S(1)} all-to-all(f32[32,1,1,128]{3,2,1,0:T(1,128)S(1)} %bitcast.12), channel_id=1, replica_groups=mesh['site'=8,'phonon'=4] {'site','phonon'}, dimensions={0} | all-to-all | bytes 32768 | tf_op jit(solution)/shard_map/all_to_all | solution.py:415
  40.0 2.4 %onward.1 = (f32[2080,128]{1,0:T(8,128)S(1)}, f32[8,128]{1,0:T(8,128)S(1)}) custom-call(f32[32,128]{1,0:T(8,128)S(1)} %bitcast.11, f32[128,1024]{1,0:T(8,128)S(1)} %get-tuple-element.19.raw_ref, f32[128,1024]{1,0:T(8,128)S(1)} %get-tuple-element.20.initial_ref, f32[3,128,128]{2,1,0:T(8,128)S(1)} %get-tuple-element.15.place_ref, ...), custom_call_target="tpu_custom_call" | custom-call | flops 1610612736 | bytes 1048576 | tf_op jit(solution)/shard_map/onward/pallas_call | solution.py:495
  42.4 30.1 %all_to_all.16 = f32[32,65,1,128]{3,2,1,0:T(1,128)S(1)} all-to-all(f32[32,65,1,128]{3,2,1,0:T(1,128)S(1)} %bitcast.10), channel_id=1, replica_groups=mesh['site'=8,'phonon'=4] {'site','phonon'}, dimensions={0} | all-to-all | bytes 2129920 | tf_op jit(solution)/shard_map/all_to_all | solution.py:415
  72.5 1.3 %arrive.1 = (f32[1024,128]{1,0:T(8,128)}, f32[1024,128]{1,0:T(8,128)}, f32[3]{0:T(128)}) custom-call(f32[2080,128]{1,0:T(8,128)S(1)} %bitcast.8, f32[8,128]{1,0:T(8,128)S(1)} %get-tuple-element.23.known_ref), custom_call_target="tpu_custom_call" | custom-call | tf_op jit(solution)/shard_map/arrive/pallas_call | solution.py:506
Async XLA Ops:
  2.8 23.2 %all-to-all-start = ((f32[32,33,1,128]{3,2,1,0:T(1,128)}), f32[32,33,1,128]{3,2,1,0:T(1,128)S(1)}, u32[]{:S(2)}, u32[]{:S(2)}) async-start(f32[32,33,1,128]{3,2,1,0:T(1,128)} %bitcast.13), calls=%async_computation | async-start | bytes 1081344 | tf_op jit(solution)/shard_map/all_to_all | solution.py:415
  10.1 4.5 %copy-start = (s32[3,8,8]{2,1,0:T(8,128)S(1)}, s32[3,8,8]{2,1,0:T(8,128)}, u32[]{:S(2)}) copy-start(s32[3,8,8]{2,1,0:T(8,128)} %mask_ref.3) | copy-start | bytes 2308
  10.1 4.5 %copy-start.1 = (s32[3]{0:T(128)S(1)}, s32[3]{0:T(128)}, u32[]{:S(2)}) copy-start(s32[3]{0:T(128)} %bits_ref.3) | copy-start | bytes 40
  10.1 4.5 %copy-start.2 = (f32[3]{0:T(128)S(1)}, f32[3]{0:T(128)}, u32[]{:S(2)}) copy-start(f32[3]{0:T(128)} %field_ref.1) | copy-start | bytes 40
  10.1 4.5 %copy-start.3 = (f32[13]{0:T(128)S(1)}, f32[13]{0:T(128)}, u32[]{:S(2)}) copy-start(f32[13]{0:T(128)} %coupling_ref.1) | copy-start | bytes 160
  10.1 4.5 %copy-start.4 = (f32[64]{0:T(128)S(1)}, f32[64]{0:T(128)}, u32[]{:S(2)}) copy-start(f32[64]{0:T(128)} %mode_ref.1) | copy-start | bytes 772

commit v22 on v14

--- a/solution.py
+++ b/solution.py
@@ -12,7 +12,7 @@
 STEPS = 3
 LANES = 128
 SUBLANES = 8
-SLOTS = 4
+SLOTS = 8
 AXES = ("site", "phonon")
 
 epsilon = 1e-06
@@ -40,7 +40,7 @@
         self.lane_blocks = rows // LANES
         self.body = self.pieces * self.lane_blocks
         self.inward = self.body + 1
-        self.outward = 2 * self.body + 1
+        self.outward = 2 * self.body
         self.places = self.pieces * self.groups
         self.width = 2 * LANES
         self.parts = rows // self.width
@@ -288,6 +288,7 @@
     fetched_ref,
     rounded_ref,
     ahead_ref,
+    vector_ref,
     semaphores,
 ):
     fetches = {}
@@ -310,23 +311,30 @@
         initial_ref[:, pl.ds(block * LANES, LANES)] = vector
         put_rounded(plan, rounded_ref, vector, block * LANES)
     tables = (kept_ref, fetched_ref, place_ref, inside_ref)
-    squares = []
-    overlap = []
-    ahead = []
+    sums = [[] for _ in range(2 * STEPS)]
+
+    def note(vector, lanes, new):
+        sums[2 * vector].append(lane_sums(new * new))
+        sums[2 * vector + 1].append(lane_sums(new * initial_ref[:, lanes]))
 
     def finish(lanes, new):
         new_ref[:, lanes] = new
         put_rounded(plan, ahead_ref, new, lanes.start)
-        squares.append(lane_sums(new * new))
-        overlap.append(lane_sums(new * initial_ref[:, lanes]))
+        note(0, lanes, new)
 
     def look_ahead(lanes, total):
         new = 2.0 * total - initial_ref[:, lanes]
-        ahead.append(lane_sums(new * new))
+        vector_ref[:, lanes] = new
+        put_rounded(plan, rounded_ref, new, lanes.start)
+        note(1, lanes, new)
+
+    def look_further(lanes, total):
+        note(2, lanes, 2.0 * total - new_ref[:, lanes])
 
     step(plan, initial_ref, rounded_ref, *tables, finish, ready, new_ref)
     step(plan, new_ref, ahead_ref, *tables, look_ahead)
-    put_sums(sums_ref, [one_row(squares), one_row(overlap), one_row(ahead)], 0, 1, plan.groups)
+    step(plan, vector_ref, rounded_ref, *tables, look_further)
+    put_sums(sums_ref, [one_row(rows) for rows in sums], 0, 1, plan.groups)
 
 
 def one_row(rows):
@@ -350,23 +358,22 @@
     second_ref,
     third_ref,
 ):
-    squares, overlap, ahead, _ = totals_of(arrived_ref, 0, 1, plan.groups)
-    first = 1.0 / scale_of(plan, squares)
-    estimate = scale_of(plan, ahead * first * first)
-    second = 1.0 / estimate
-    known_ref[:1, :] = jnp.broadcast_to(overlap * first / plan.entries, (1, LANES))
-    known_ref[1:, :] = jnp.broadcast_to(estimate, (SUBLANES - 1, LANES))
+    totals = totals_of(arrived_ref, 0, 1, plan.groups)
+    first = 1.0 / scale_of(plan, totals[0])
+    second = 1.0 / scale_of(plan, totals[2] * first * first)
+    both = first * second
+    third = 1.0 / scale_of(plan, totals[4] * both * both)
+    for row, moment in enumerate((totals[1] * first, totals[3] * both, totals[5] * both * third)):
+        known_ref[pl.ds(row, 1), :] = jnp.broadcast_to(moment / plan.entries, (1, LANES))
+    known_ref[STEPS:, :] = jnp.zeros((SUBLANES - STEPS, LANES), jnp.float32)
     for block in range(plan.lane_blocks):
         lanes = pl.ds(block * LANES, LANES)
         vector = raw_ref[:, lanes] * first
         second_ref[:, lanes] = vector
         put_rounded(plan, rounded_ref, vector, block * LANES)
     tables = (kept_ref, fetched_ref, place_ref, inside_ref)
-    sums = [[] for _ in range(SLOTS)]
 
     def send(vector, lanes, new):
-        sums[2 * vector].append(lane_sums(new * new))
-        sums[2 * vector + 1].append(lane_sums(new * initial_ref[:, lanes]))
         for start in range(0, plan.width, LANES):
             block = (lanes.start + start) // LANES
             for piece in range(plan.pieces):
@@ -380,34 +387,26 @@
         vector = new * second
         third_ref[:, lanes] = vector
         put_rounded(plan, ahead_ref, vector, lanes.start)
-        send(0, lanes, new)
+        send(0, lanes, vector)
 
     def finish_third(lanes, total):
-        send(1, lanes, 2.0 * total - second_ref[:, lanes] * second)
+        send(1, lanes, (2.0 * total - second_ref[:, lanes] * second) * third)
 
     step(plan, second_ref, rounded_ref, *tables, finish_second)
     step(plan, third_ref, ahead_ref, *tables, finish_third)
-    put_sums(out_ref, [one_row(rows) for rows in sums], 2 * plan.body, plan.outward, plan.groups)
 
 
 def arrive_kernel(plan, arrived_ref, known_ref, before_ref, last_ref, moments_ref):
-    before_squares, before_overlap, last_squares, last_overlap = totals_of(
-        arrived_ref, 2 * plan.body, plan.outward, plan.groups
-    )
-    before = 1.0 / scale_of(plan, before_squares)
-    back = known_ref[1:2, :1] * before
-    last = back / scale_of(plan, last_squares * back * back)
-    for vector, (out_ref, factor) in enumerate(((before_ref, before), (last_ref, last))):
+    for vector, out_ref in enumerate((before_ref, last_ref)):
         for block in range(plan.lane_blocks):
             first = vector * plan.body + block
             parts = [
                 arrived_ref[pl.ds(first + piece * plan.lane_blocks, plan.groups, stride=plan.outward), :]
                 for piece in range(plan.pieces)
             ]
-            out_ref[pl.ds(block * LANES, LANES), :] = jnp.concatenate(parts, axis=0).T * factor
-    moments_ref[0] = known_ref[0, 0]
-    moments_ref[1] = (before_overlap * before / plan.entries)[0, 0]
-    moments_ref[2] = (last_overlap * last / plan.entries)[0, 0]
+            out_ref[pl.ds(block * LANES, LANES), :] = jnp.concatenate(parts, axis=0).T
+    for step_index in range(STEPS):
+        moments_ref[step_index] = known_ref[step_index, 0]
 
 
 def exchange(values, count):
@@ -485,7 +484,7 @@
         ],
         in_specs=[VMEM] * 4 + [HBM],
         out_specs=[VMEM] * 4,
-        scratch_shapes=[rounded, rounded, pltpu.SemaphoreType.DMA((fetched,))],
+        scratch_shapes=[rounded, rounded, working, pltpu.SemaphoreType.DMA((fetched,))],
         compiler_params=params(46),
         cost_estimate=cost(2 * work, 4 * plan.places * plan.rows),
         name="first",

time: 73.8 us -> 73.5 us (level)
  blocking collectives: 40.2 us -> 38 us
  Pallas kernels: 16.7 us -> 18.6 us
    all_to_all x2, blocking collectives: 40.2 us -> 38 us  [exchange(): return lax.all_to_all(shaped, AXES, 0, 0, tiled=True).reshape(values.shape)]
    pallas_call x1, Pallas kernels: 3.7 us -> 4.73 us  [shards(): pl.pallas_call(functools.partial(first_kernel, plan), out_shape=[vector,...]
where the time goes in v22:
time: 73.5 us; the launch traced here: 73.2 us
  blocking collectives  38 us (52%)
  Pallas kernels  18.6 us (25%)
  waiting for transfers between devices  8.43 us (11%)
  starting transfers between devices  7.3 us (10%)
  between operations  0.76 us (1%)
    all_to_all x2, blocking collectives, exchange(): return lax.all_to_all(shaped, AXES, 0, 0, tiled=True).reshape(values.shape)  38 us
    all_to_all x1, waiting for transfers between devices, exchange(): return lax.all_to_all(shaped, AXES, 0, 0, tiled=True).reshape(values.shape)  8.43 us
    all_to_all x1, starting transfers between devices, exchange(): return lax.all_to_all(shaped, AXES, 0, 0, tiled=True).reshape(values.shape)  7.3 us
    pallas_call x1, Pallas kernels, shards(): pl.pallas_call(functools.partial(first_kernel, plan), out_shape=[vector,...  4.73 us
    pallas_call x1, Pallas kernels, shards(): pl.pallas_call(functools.partial(store_kernel, plan), out_shape=jax.Shape...  4.41 us
    pallas_call x1, Pallas kernels, shards(): pl.pallas_call(functools.partial(prepare_kernel, plan), out_shape=[jax.Sh...  2.87 us
    pallas_call x1, Pallas kernels, shards(): pl.pallas_call(functools.partial(onward_kernel, plan), out_shape=[outward...  2.84 us
    pallas_call x1, Pallas kernels, shards(): pl.pallas_call(functools.partial(depart_kernel, plan), out_shape=inward,...  2.19 us
  transfers between devices with their start and end apart: 1, of which 1 were waited for; matrix products, arithmetic and copies ran while one was open for 0% of the time, Pallas kernels for 10%

profile of v22, /device:TPU:0, one launch (start us, length us, event | category | flops | bytes accessed | tf_op | source)
XLA Modules:
  0.0 73.2 jit_solution(8540754531669983545)
XLA Ops:
  0.6 2.2 %depart.1 = f32[1056,128]{1,0:T(8,128)} custom-call(f32[1024,128]{1,0:T(8,128)} %state_ref.1), custom_call_target="tpu_custom_call" | custom-call | tf_op jit(solution)/shard_map/depart/pallas_call | solution.py:431
  2.8 7.3 %all-to-all-start = ((f32[32,33,1,128]{3,2,1,0:T(1,128)}), f32[32,33,1,128]{3,2,1,0:T(1,128)S(1)}, u32[]{:S(2)}, u32[]{:S(2)}) async-start(f32[32,33,1,128]{3,2,1,0:T(1,128)} %bitcast.15), calls=%async_computation | async-start | bytes 1081344 | tf_op jit(solution)/shard_map/all_to_all | solution.py:414
  10.1 0.0 copy-start
  10.2 0.0 copy-start.1
  10.2 0.0 copy-start.2
  10.2 0.0 copy-start.3
  10.2 0.0 copy-start.4
  10.2 4.4 %store.1.stored_ref = bf16[7,1024,256]{2,1,0:T(8,128)(2,1)} custom-call(s32[3]{0:T(128)} %bits_ref.3, s32[3,8,8]{2,1,0:T(8,128)} %mask_ref.3, bf16[3,1024,1024]{2,1,0:T(8,128)(2,1)} %operators_ref.3), custom_call_target="tpu_custom_call" | custom-call | flops 1048576 | bytes 7340032 | tf_op jit(solution)/shard_map/store/pallas_call | solution.py:462
  14.6 0.0 copy-done
  14.6 0.0 copy-done.1
  14.6 0.0 copy-done.2
  14.6 0.0 copy-done.3
  14.7 0.0 copy-done.4
  14.7 2.9 %prepare.1 = (f32[3,128,128]{2,1,0:T(8,128)S(1)}, f32[8,1024]{1,0:T(8,128)S(1)}, bf16[5,1024,256]{2,1,0:T(8,128)(2,1)S(1)}) custom-call(s32[3]{0:T(128)S(1)} %copy-done.1, s32[3,8,8]{2,1,0:T(8,128)S(1)} %copy-done, f32[3]{0:T(128)S(1)} %copy-done.2, f32[13]{0:T(128)S(1)} %copy-done.3, f32[64]{0:T(128)S(1)} %copy-done.4, bf16[3,1024,1024]{2,1,0:T(8,128)(2,1)} %operators_ref.3), custom_call_target="tpu_custom_call" | custom-call | flops 1048576 | bytes 5242880 | tf_op jit(solution)/shard_map/prepare/pallas_call | solution.py:448
  17.5 8.4 %all-to-all-done = f32[32,33,1,128]{3,2,1,0:T(1,128)S(1)} async-done(((f32[32,33,1,128]{3,2,1,0:T(1,128)}), f32[32,33,1,128]{3,2,1,0:T(1,128)S(1)}, u32[]{:S(2)}, u32[]{:S(2)}) %all-to-all-start) | async-done | bytes 540704 | tf_op jit(solution)/shard_map/all_to_all | solution.py:414
  26.0 4.7 %first.1 = (f32[128,1024]{1,0:T(8,128)S(1)}, f32[128,1024]{1,0:T(8,128)S(1)}, f32[32,128]{1,0:T(8,128)S(1)}, bf16[7,1024,256]{2,1,0:T(8,128)(2,1)S(1)}) custom-call(f32[1056,128]{1,0:T(8,128)S(1)} %bitcast.11, f32[3,128,128]{2,1,0:T(8,128)S(1)} %get-tuple-element.15.place_ref, f32[8,1024]{1,0:T(8,128)S(1)} %get-tuple-element.16.inside_ref, ...), custom_call_target="tpu_custom_call" | custom-call | flops 1610612736 | bytes 524288 | tf_op jit(solution)/shard_map/first/pallas_call | solution.py:477
  30.7 10.1 %all_to_all.15 = f32[32,1,1,128]{3,2,1,0:T(1,128)S(1)} all-to-all(f32[32,1,1,128]{3,2,1,0:T(1,128)S(1)} %bitcast.14), channel_id=1, replica_groups=mesh['site'=8,'phonon'=4] {'site','phonon'}, dimensions={0} | all-to-all | bytes 32768 | tf_op jit(solution)/shard_map/all_to_all | solution.py:414
  40.8 2.8 %onward.1 = (f32[2048,128]{1,0:T(8,128)S(1)}, f32[8,128]{1,0:T(8,128)S(1)}) custom-call(f32[32,128]{1,0:T(8,128)S(1)} %bitcast.13, f32[128,1024]{1,0:T(8,128)S(1)} %get-tuple-element.19.raw_ref, f32[128,1024]{1,0:T(8,128)S(1)} %get-tuple-element.20.initial_ref, f32[3,128,128]{2,1,0:T(8,128)S(1)} %get-tuple-element.15.place_ref, ...), custom_call_target="tpu_custom_call" | custom-call | flops 1610612736 | bytes 1048576 | tf_op jit(solution)/shard_map/onward/pallas_call | solution.py:494
  43.7 28.0 %all_to_all.16 = f32[32,64,1,128]{3,1,2,0:T(8,128)S(1)} all-to-all(f32[32,64,1,128]{3,1,2,0:T(8,128)S(1)} %bitcast.12), channel_id=1, replica_groups=mesh['site'=8,'phonon'=4] {'site','phonon'}, dimensions={0} | all-to-all | bytes 2097152 | tf_op jit(solution)/shard_map/all_to_all | solution.py:414
  71.6 1.5 %arrive.1 = (f32[1024,128]{1,0:T(8,128)}, f32[1024,128]{1,0:T(8,128)}, f32[3]{0:T(128)}) custom-call(f32[2048,128]{1,0:T(8,128)S(1)} %bitcast.10, f32[8,128]{1,0:T(8,128)S(1)} %get-tuple-element.23.known_ref), custom_call_target="tpu_custom_call" | custom-call | tf_op jit(solution)/shard_map/arrive/pallas_call | solution.py:505
Async XLA Ops:
  2.8 23.2 %all-to-all-start = ((f32[32,33,1,128]{3,2,1,0:T(1,128)}), f32[32,33,1,128]{3,2,1,0:T(1,128)S(1)}, u32[]{:S(2)}, u32[]{:S(2)}) async-start(f32[32,33,1,128]{3,2,1,0:T(1,128)} %bitcast.15), calls=%async_computation | async-start | bytes 1081344 | tf_op jit(solution)/shard_map/all_to_all | solution.py:414
  10.1 4.5 %copy-start = (s32[3,8,8]{2,1,0:T(8,128)S(1)}, s32[3,8,8]{2,1,0:T(8,128)}, u32[]{:S(2)}) copy-start(s32[3,8,8]{2,1,0:T(8,128)} %mask_ref.3) | copy-start | bytes 2308
  10.2 4.5 %copy-start.1 = (s32[3]{0:T(128)S(1)}, s32[3]{0:T(128)}, u32[]{:S(2)}) copy-start(s32[3]{0:T(128)} %bits_ref.3) | copy-start | bytes 40
  10.2 4.5 %copy-start.2 = (f32[3]{0:T(128)S(1)}, f32[3]{0:T(128)}, u32[]{:S(2)}) copy-start(f32[3]{0:T(128)} %field_ref.1) | copy-start | bytes 40
  10.2 4.5 %copy-start.3 = (f32[13]{0:T(128)S(1)}, f32[13]{0:T(128)}, u32[]{:S(2)}) copy-start(f32[13]{0:T(128)} %coupling_ref.1) | copy-start | bytes 160
  10.2 4.5 %copy-start.4 = (f32[64]{0:T(128)S(1)}, f32[64]{0:T(128)}, u32[]{:S(2)}) copy-start(f32[64]{0:T(128)} %mode_ref.1) | copy-start | bytes 772

commit v23 on v22

--- a/solution.py
+++ b/solution.py
@@ -82,11 +82,12 @@
 
 def totals_of(ref, start, stride, count):
     lanes = lane_sums(ref[pl.ds(start, count, stride=stride), :])
-    lane = lax.broadcasted_iota(jnp.int32, (1, LANES), 1)
-    return [
-        jnp.sum(jnp.where(lane // (LANES // SLOTS) == slot, lanes, 0.0), axis=1, keepdims=True)
-        for slot in range(SLOTS)
-    ]
+    width = LANES // SLOTS
+    reach = width
+    while reach > 1:
+        reach //= 2
+        lanes = lanes + pltpu.roll(lanes, LANES - reach, 1)
+    return [lanes[:, slot * width : slot * width + 1] for slot in range(SLOTS)]
 
 
 def scale_of(plan, squares):
@@ -230,7 +231,7 @@
         ).astype(jnp.bfloat16)
 
 
-def step(plan, vector_ref, rounded_ref, kept_ref, fetched_ref, place_ref, inside_ref, finish, ready=None, begun_ref=None):
+def step(plan, vector_ref, rounded_ref, kept_ref, fetched_ref, place_ref, inside_ref, finish, ready=None, begun_ref=None, factor=None):
     span = plan.places // plan.levels_here
 
     def local(start):
@@ -243,7 +244,7 @@
         total = weight * (place_ref[1] * lower + place_ref[2] * upper)
         for position in range(plan.bits):
             total = total + inside_ref[pl.ds(1 + position, 1), lanes] * flipped(vector, plan.phonons << position)
-        return total
+        return total if factor is None else total * factor
 
     def added(total, part, late):
         for ref, low, high in ((kept_ref, 0, plan.kept), (fetched_ref, plan.kept, plan.slabs)):
@@ -355,7 +356,6 @@
     known_ref,
     rounded_ref,
     ahead_ref,
-    second_ref,
     third_ref,
 ):
     totals = totals_of(arrived_ref, 0, 1, plan.groups)
@@ -368,9 +368,7 @@
     known_ref[STEPS:, :] = jnp.zeros((SUBLANES - STEPS, LANES), jnp.float32)
     for block in range(plan.lane_blocks):
         lanes = pl.ds(block * LANES, LANES)
-        vector = raw_ref[:, lanes] * first
-        second_ref[:, lanes] = vector
-        put_rounded(plan, rounded_ref, vector, block * LANES)
+        put_rounded(plan, rounded_ref, raw_ref[:, lanes] * first, block * LANES)
     tables = (kept_ref, fetched_ref, place_ref, inside_ref)
 
     def send(vector, lanes, new):
@@ -390,9 +388,9 @@
         send(0, lanes, vector)
 
     def finish_third(lanes, total):
-        send(1, lanes, (2.0 * total - second_ref[:, lanes] * second) * third)
-
-    step(plan, second_ref, rounded_ref, *tables, finish_second)
+        send(1, lanes, 2.0 * third * total - raw_ref[:, lanes] * (both * third))
+
+    step(plan, raw_ref, rounded_ref, *tables, finish_second, factor=first)
     step(plan, third_ref, ahead_ref, *tables, finish_third)
 
 
@@ -496,7 +494,7 @@
         out_shape=[outward, known],
         in_specs=[VMEM] * 7,
         out_specs=[VMEM] * 2,
-        scratch_shapes=[rounded, rounded, working, working],
+        scratch_shapes=[rounded, rounded, working],
         compiler_params=params(32),
         cost_estimate=cost(2 * work, 8 * plan.places * plan.rows),
         name="onward",

time: 73.5 us -> 73.7 us (level)
  no operation moved by 1% of the time
where the time goes in v23:
time: 73.7 us; the launch traced here: 73.3 us
  blocking collectives  38 us (52%)
  Pallas kernels  18.7 us (25%)
  waiting for transfers between devices  8.43 us (11%)
  starting transfers between devices  7.3 us (10%)
  between operations  0.76 us (1%)
    all_to_all x2, blocking collectives, exchange(): return lax.all_to_all(shaped, AXES, 0, 0, tiled=True).reshape(values.shape)  38 us
    all_to_all x1, waiting for transfers between devices, exchange(): return lax.all_to_all(shaped, AXES, 0, 0, tiled=True).reshape(values.shape)  8.43 us
    all_to_all x1, starting transfers between devices, exchange(): return lax.all_to_all(shaped, AXES, 0, 0, tiled=True).reshape(values.shape)  7.3 us
    pallas_call x1, Pallas kernels, shards(): pl.pallas_call(functools.partial(first_kernel, plan), out_shape=[vector,...  4.77 us
    pallas_call x1, Pallas kernels, shards(): pl.pallas_call(functools.partial(store_kernel, plan), out_shape=jax.Shape...  4.41 us
    pallas_call x1, Pallas kernels, shards(): pl.pallas_call(functools.partial(onward_kernel, plan), out_shape=[outward...  2.94 us
    pallas_call x1, Pallas kernels, shards(): pl.pallas_call(functools.partial(prepare_kernel, plan), out_shape=[jax.Sh...  2.87 us
    pallas_call x1, Pallas kernels, shards(): pl.pallas_call(functools.partial(depart_kernel, plan), out_shape=inward,...  2.19 us
  transfers between devices with their start and end apart: 1, of which 1 were waited for; matrix products, arithmetic and copies ran while one was open for 0% of the time, Pallas kernels for 10%

profile of v23, /device:TPU:0, one launch (start us, length us, event | category | flops | bytes accessed | tf_op | source)
XLA Modules:
  0.0 73.3 jit_solution(7804920227651385905)
XLA Ops:
  0.6 2.2 %depart.1 = f32[1056,128]{1,0:T(8,128)} custom-call(f32[1024,128]{1,0:T(8,128)} %state_ref.1), custom_call_target="tpu_custom_call" | custom-call | tf_op jit(solution)/shard_map/depart/pallas_call | solution.py:429
  2.8 7.3 %all-to-all-start = ((f32[32,33,1,128]{3,2,1,0:T(1,128)}), f32[32,33,1,128]{3,2,1,0:T(1,128)S(1)}, u32[]{:S(2)}, u32[]{:S(2)}) async-start(f32[32,33,1,128]{3,2,1,0:T(1,128)} %bitcast.15), calls=%async_computation | async-start | bytes 1081344 | tf_op jit(solution)/shard_map/all_to_all | solution.py:412
  10.1 0.0 copy-start
  10.2 0.0 copy-start.1
  10.2 0.0 copy-start.2
  10.2 0.0 copy-start.3
  10.2 0.0 copy-start.4
  10.2 4.4 %store.1.stored_ref = bf16[7,1024,256]{2,1,0:T(8,128)(2,1)} custom-call(s32[3]{0:T(128)} %bits_ref.3, s32[3,8,8]{2,1,0:T(8,128)} %mask_ref.3, bf16[3,1024,1024]{2,1,0:T(8,128)(2,1)} %operators_ref.3), custom_call_target="tpu_custom_call" | custom-call | flops 1048576 | bytes 7340032 | tf_op jit(solution)/shard_map/store/pallas_call | solution.py:460
  14.6 0.0 copy-done
  14.6 0.0 copy-done.1
  14.6 0.0 copy-done.2
  14.6 0.0 copy-done.3
  14.7 0.0 copy-done.4
  14.7 2.9 %prepare.1 = (f32[3,128,128]{2,1,0:T(8,128)S(1)}, f32[8,1024]{1,0:T(8,128)S(1)}, bf16[5,1024,256]{2,1,0:T(8,128)(2,1)S(1)}) custom-call(s32[3]{0:T(128)S(1)} %copy-done.1, s32[3,8,8]{2,1,0:T(8,128)S(1)} %copy-done, f32[3]{0:T(128)S(1)} %copy-done.2, f32[13]{0:T(128)S(1)} %copy-done.3, f32[64]{0:T(128)S(1)} %copy-done.4, bf16[3,1024,1024]{2,1,0:T(8,128)(2,1)} %operators_ref.3), custom_call_target="tpu_custom_call" | custom-call | flops 1048576 | bytes 5242880 | tf_op jit(solution)/shard_map/prepare/pallas_call | solution.py:446
  17.5 8.4 %all-to-all-done = f32[32,33,1,128]{3,2,1,0:T(1,128)S(1)} async-done(((f32[32,33,1,128]{3,2,1,0:T(1,128)}), f32[32,33,1,128]{3,2,1,0:T(1,128)S(1)}, u32[]{:S(2)}, u32[]{:S(2)}) %all-to-all-start) | async-done | bytes 540704 | tf_op jit(solution)/shard_map/all_to_all | solution.py:412
  26.0 4.8 %first.1 = (f32[128,1024]{1,0:T(8,128)S(1)}, f32[128,1024]{1,0:T(8,128)S(1)}, f32[32,128]{1,0:T(8,128)S(1)}, bf16[7,1024,256]{2,1,0:T(8,128)(2,1)S(1)}) custom-call(f32[1056,128]{1,0:T(8,128)S(1)} %bitcast.11, f32[3,128,128]{2,1,0:T(8,128)S(1)} %get-tuple-element.15.place_ref, f32[8,1024]{1,0:T(8,128)S(1)} %get-tuple-element.16.inside_ref, ...), custom_call_target="tpu_custom_call" | custom-call | flops 1610612736 | bytes 524288 | tf_op jit(solution)/shard_map/first/pallas_call | solution.py:475
  30.8 10.1 %all_to_all.15 = f32[32,1,1,128]{3,2,1,0:T(1,128)S(1)} all-to-all(f32[32,1,1,128]{3,2,1,0:T(1,128)S(1)} %bitcast.14), channel_id=1, replica_groups=mesh['site'=8,'phonon'=4] {'site','phonon'}, dimensions={0} | all-to-all | bytes 32768 | tf_op jit(solution)/shard_map/all_to_all | solution.py:412
  40.8 2.9 %onward.1 = (f32[2048,128]{1,0:T(8,128)S(1)}, f32[8,128]{1,0:T(8,128)S(1)}) custom-call(f32[32,128]{1,0:T(8,128)S(1)} %bitcast.13, f32[128,1024]{1,0:T(8,128)S(1)} %get-tuple-element.19.raw_ref, f32[128,1024]{1,0:T(8,128)S(1)} %get-tuple-element.20.initial_ref, f32[3,128,128]{2,1,0:T(8,128)S(1)} %get-tuple-element.15.place_ref, ...), custom_call_target="tpu_custom_call" | custom-call | flops 1610612736 | bytes 1048576 | tf_op jit(solution)/shard_map/onward/pallas_call | solution.py:492
  43.8 28.0 %all_to_all.16 = f32[32,64,1,128]{3,1,2,0:T(8,128)S(1)} all-to-all(f32[32,64,1,128]{3,1,2,0:T(8,128)S(1)} %bitcast.12), channel_id=1, replica_groups=mesh['site'=8,'phonon'=4] {'site','phonon'}, dimensions={0} | all-to-all | bytes 2097152 | tf_op jit(solution)/shard_map/all_to_all | solution.py:412
  71.8 1.5 %arrive.1 = (f32[1024,128]{1,0:T(8,128)}, f32[1024,128]{1,0:T(8,128)}, f32[3]{0:T(128)}) custom-call(f32[2048,128]{1,0:T(8,128)S(1)} %bitcast.10, f32[8,128]{1,0:T(8,128)S(1)} %get-tuple-element.23.known_ref), custom_call_target="tpu_custom_call" | custom-call | tf_op jit(solution)/shard_map/arrive/pallas_call | solution.py:503
Async XLA Ops:
  2.8 23.2 %all-to-all-start = ((f32[32,33,1,128]{3,2,1,0:T(1,128)}), f32[32,33,1,128]{3,2,1,0:T(1,128)S(1)}, u32[]{:S(2)}, u32[]{:S(2)}) async-start(f32[32,33,1,128]{3,2,1,0:T(1,128)} %bitcast.15), calls=%async_computation | async-start | bytes 1081344 | tf_op jit(solution)/shard_map/all_to_all | solution.py:412
  10.1 4.5 %copy-start = (s32[3,8,8]{2,1,0:T(8,128)S(1)}, s32[3,8,8]{2,1,0:T(8,128)}, u32[]{:S(2)}) copy-start(s32[3,8,8]{2,1,0:T(8,128)} %mask_ref.3) | copy-start | bytes 2308
  10.2 4.5 %copy-start.1 = (s32[3]{0:T(128)S(1)}, s32[3]{0:T(128)}, u32[]{:S(2)}) copy-start(s32[3]{0:T(128)} %bits_ref.3) | copy-start | bytes 40
  10.2 4.5 %copy-start.2 = (f32[3]{0:T(128)S(1)}, f32[3]{0:T(128)}, u32[]{:S(2)}) copy-start(f32[3]{0:T(128)} %field_ref.1) | copy-start | bytes 40
  10.2 4.5 %copy-start.3 = (f32[13]{0:T(128)S(1)}, f32[13]{0:T(128)}, u32[]{:S(2)}) copy-start(f32[13]{0:T(128)} %coupling_ref.1) | copy-start | bytes 160
  10.2 4.5 %copy-start.4 = (f32[64]{0:T(128)S(1)}, f32[64]{0:T(128)}, u32[]{:S(2)}) copy-start(f32[64]{0:T(128)} %mode_ref.1) | copy-start | bytes 772

commit v24 on v14

--- a/solution.py
+++ b/solution.py
@@ -82,11 +82,12 @@
 
 def totals_of(ref, start, stride, count):
     lanes = lane_sums(ref[pl.ds(start, count, stride=stride), :])
-    lane = lax.broadcasted_iota(jnp.int32, (1, LANES), 1)
-    return [
-        jnp.sum(jnp.where(lane // (LANES // SLOTS) == slot, lanes, 0.0), axis=1, keepdims=True)
-        for slot in range(SLOTS)
-    ]
+    width = LANES // SLOTS
+    reach = width
+    while reach > 1:
+        reach //= 2
+        lanes = lanes + pltpu.roll(lanes, LANES - reach, 1)
+    return [lanes[:, slot * width : slot * width + 1] for slot in range(SLOTS)]
 
 
 def scale_of(plan, squares):
@@ -354,8 +355,6 @@
     first = 1.0 / scale_of(plan, squares)
     estimate = scale_of(plan, ahead * first * first)
     second = 1.0 / estimate
-    known_ref[:1, :] = jnp.broadcast_to(overlap * first / plan.entries, (1, LANES))
-    known_ref[1:, :] = jnp.broadcast_to(estimate, (SUBLANES - 1, LANES))
     for block in range(plan.lane_blocks):
         lanes = pl.ds(block * LANES, LANES)
         vector = raw_ref[:, lanes] * first
@@ -388,6 +387,8 @@
     step(plan, second_ref, rounded_ref, *tables, finish_second)
     step(plan, third_ref, ahead_ref, *tables, finish_third)
     put_sums(out_ref, [one_row(rows) for rows in sums], 2 * plan.body, plan.outward, plan.groups)
+    known_ref[:1, :] = jnp.broadcast_to(overlap * first / plan.entries, (1, LANES))
+    known_ref[1:, :] = jnp.broadcast_to(estimate, (SUBLANES - 1, LANES))
 
 
 def arrive_kernel(plan, arrived_ref, known_ref, before_ref, last_ref, moments_ref):

time: 73.8 us -> 74.5 us (level)
  Pallas kernels: 16.7 us -> 17.5 us
where the time goes in v24:
time: 74.5 us; the launch traced here: 74.2 us
  blocking collectives  40.2 us (54%)
  Pallas kernels  17.5 us (23%)
  waiting for transfers between devices  8.43 us (11%)
  starting transfers between devices  7.3 us (10%)
  between operations  0.75 us (1%)
    all_to_all x2, blocking collectives, exchange(): return lax.all_to_all(shaped, AXES, 0, 0, tiled=True).reshape(values.shape)  40.2 us
    all_to_all x1, waiting for transfers between devices, exchange(): return lax.all_to_all(shaped, AXES, 0, 0, tiled=True).reshape(values.shape)  8.43 us
    all_to_all x1, starting transfers between devices, exchange(): return lax.all_to_all(shaped, AXES, 0, 0, tiled=True).reshape(values.shape)  7.3 us
    pallas_call x1, Pallas kernels, shards(): pl.pallas_call(functools.partial(store_kernel, plan), out_shape=jax.Shape...  4.41 us
    pallas_call x1, Pallas kernels, shards(): pl.pallas_call(functools.partial(first_kernel, plan), out_shape=[vector,...  3.76 us
    pallas_call x1, Pallas kernels, shards(): pl.pallas_call(functools.partial(prepare_kernel, plan), out_shape=[jax.Sh...  2.87 us
    pallas_call x1, Pallas kernels, shards(): pl.pallas_call(functools.partial(onward_kernel, plan), out_shape=[outward...  2.71 us
    pallas_call x1, Pallas kernels, shards(): pl.pallas_call(functools.partial(depart_kernel, plan), out_shape=inward,...  2.12 us
  transfers between devices with their start and end apart: 1, of which 1 were waited for; matrix products, arithmetic and copies ran while one was open for 0% of the time, Pallas kernels for 10%

profile of v24, /device:TPU:0, one launch (start us, length us, event | category | flops | bytes accessed | tf_op | source)
XLA Modules:
  0.0 74.2 jit_solution(15247045662426035840)
XLA Ops:
  0.6 2.1 %depart.1 = f32[1056,128]{1,0:T(8,128)} custom-call(f32[1024,128]{1,0:T(8,128)} %state_ref.1), custom_call_target="tpu_custom_call" | custom-call | tf_op jit(solution)/shard_map/depart/pallas_call | solution.py:433
  2.8 7.3 %all-to-all-start = ((f32[32,33,1,128]{3,2,1,0:T(1,128)}), f32[32,33,1,128]{3,2,1,0:T(1,128)S(1)}, u32[]{:S(2)}, u32[]{:S(2)}) async-start(f32[32,33,1,128]{3,2,1,0:T(1,128)} %bitcast.13), calls=%async_computation | async-start | bytes 1081344 | tf_op jit(solution)/shard_map/all_to_all | solution.py:416
  10.1 0.0 copy-start
  10.1 0.0 copy-start.1
  10.1 0.0 copy-start.2
  10.1 0.0 copy-start.3
  10.1 0.0 copy-start.4
  10.1 4.4 %store.1.stored_ref = bf16[7,1024,256]{2,1,0:T(8,128)(2,1)} custom-call(s32[3]{0:T(128)} %bits_ref.3, s32[3,8,8]{2,1,0:T(8,128)} %mask_ref.3, bf16[3,1024,1024]{2,1,0:T(8,128)(2,1)} %operators_ref.3), custom_call_target="tpu_custom_call" | custom-call | flops 1048576 | bytes 7340032 | tf_op jit(solution)/shard_map/store/pallas_call | solution.py:464
  14.6 0.0 copy-done
  14.6 0.0 copy-done.1
  14.6 0.0 copy-done.2
  14.6 0.0 copy-done.3
  14.6 0.0 copy-done.4
  14.6 2.9 %prepare.1 = (f32[3,128,128]{2,1,0:T(8,128)S(1)}, f32[8,1024]{1,0:T(8,128)S(1)}, bf16[5,1024,256]{2,1,0:T(8,128)(2,1)S(1)}) custom-call(s32[3]{0:T(128)S(1)} %copy-done.1, s32[3,8,8]{2,1,0:T(8,128)S(1)} %copy-done, f32[3]{0:T(128)S(1)} %copy-done.2, f32[13]{0:T(128)S(1)} %copy-done.3, f32[64]{0:T(128)S(1)} %copy-done.4, bf16[3,1024,1024]{2,1,0:T(8,128)(2,1)} %operators_ref.3), custom_call_target="tpu_custom_call" | custom-call | flops 1048576 | bytes 5242880 | tf_op jit(solution)/shard_map/prepare/pallas_call | solution.py:450
  17.5 8.4 %all-to-all-done = f32[32,33,1,128]{3,2,1,0:T(1,128)S(1)} async-done(((f32[32,33,1,128]{3,2,1,0:T(1,128)}), f32[32,33,1,128]{3,2,1,0:T(1,128)S(1)}, u32[]{:S(2)}, u32[]{:S(2)}) %all-to-all-start) | async-done | bytes 540704 | tf_op jit(solution)/shard_map/all_to_all | solution.py:416
  25.9 3.8 %first.1 = (f32[128,1024]{1,0:T(8,128)S(1)}, f32[128,1024]{1,0:T(8,128)S(1)}, f32[32,128]{1,0:T(8,128)S(1)}, bf16[7,1024,256]{2,1,0:T(8,128)(2,1)S(1)}) custom-call(f32[1056,128]{1,0:T(8,128)S(1)} %bitcast.9, f32[3,128,128]{2,1,0:T(8,128)S(1)} %get-tuple-element.15.place_ref, f32[8,1024]{1,0:T(8,128)S(1)} %get-tuple-element.16.inside_ref, ...), custom_call_target="tpu_custom_call" | custom-call | flops 1610612736 | bytes 524288 | tf_op jit(solution)/shard_map/first/pallas_call | solution.py:479
  29.7 10.1 %all_to_all.15 = f32[32,1,1,128]{3,2,1,0:T(1,128)S(1)} all-to-all(f32[32,1,1,128]{3,2,1,0:T(1,128)S(1)} %bitcast.12), channel_id=1, replica_groups=mesh['site'=8,'phonon'=4] {'site','phonon'}, dimensions={0} | all-to-all | bytes 32768 | tf_op jit(solution)/shard_map/all_to_all | solution.py:416
  39.8 2.7 %onward.1 = (f32[2080,128]{1,0:T(8,128)S(1)}, f32[8,128]{1,0:T(8,128)S(1)}) custom-call(f32[32,128]{1,0:T(8,128)S(1)} %bitcast.11, f32[128,1024]{1,0:T(8,128)S(1)} %get-tuple-element.19.raw_ref, f32[128,1024]{1,0:T(8,128)S(1)} %get-tuple-element.20.initial_ref, f32[3,128,128]{2,1,0:T(8,128)S(1)} %get-tuple-element.15.place_ref, ...), custom_call_target="tpu_custom_call" | custom-call | flops 1610612736 | bytes 1048576 | tf_op jit(solution)/shard_map/onward/pallas_call | solution.py:496
  42.5 30.1 %all_to_all.16 = f32[32,65,1,128]{3,2,1,0:T(1,128)S(1)} all-to-all(f32[32,65,1,128]{3,2,1,0:T(1,128)S(1)} %bitcast.10), channel_id=1, replica_groups=mesh['site'=8,'phonon'=4] {'site','phonon'}, dimensions={0} | all-to-all | bytes 2129920 | tf_op jit(solution)/shard_map/all_to_all | solution.py:416
  72.6 1.6 %arrive.1 = (f32[1024,128]{1,0:T(8,128)}, f32[1024,128]{1,0:T(8,128)}, f32[3]{0:T(128)}) custom-call(f32[2080,128]{1,0:T(8,128)S(1)} %bitcast.8, f32[8,128]{1,0:T(8,128)S(1)} %get-tuple-element.23.known_ref), custom_call_target="tpu_custom_call" | custom-call | tf_op jit(solution)/shard_map/arrive/pallas_call | solution.py:507
Async XLA Ops:
  2.8 23.2 %all-to-all-start = ((f32[32,33,1,128]{3,2,1,0:T(1,128)}), f32[32,33,1,128]{3,2,1,0:T(1,128)S(1)}, u32[]{:S(2)}, u32[]{:S(2)}) async-start(f32[32,33,1,128]{3,2,1,0:T(1,128)} %bitcast.13), calls=%async_computation | async-start | bytes 1081344 | tf_op jit(solution)/shard_map/all_to_all | solution.py:416
  10.1 4.5 %copy-start = (s32[3,8,8]{2,1,0:T(8,128)S(1)}, s32[3,8,8]{2,1,0:T(8,128)}, u32[]{:S(2)}) copy-start(s32[3,8,8]{2,1,0:T(8,128)} %mask_ref.3) | copy-start | bytes 2308
  10.1 4.5 %copy-start.1 = (s32[3]{0:T(128)S(1)}, s32[3]{0:T(128)}, u32[]{:S(2)}) copy-start(s32[3]{0:T(128)} %bits_ref.3) | copy-start | bytes 40
  10.1 4.5 %copy-start.2 = (f32[3]{0:T(128)S(1)}, f32[3]{0:T(128)}, u32[]{:S(2)}) copy-start(f32[3]{0:T(128)} %field_ref.1) | copy-start | bytes 40
  10.1 4.5 %copy-start.3 = (f32[13]{0:T(128)S(1)}, f32[13]{0:T(128)}, u32[]{:S(2)}) copy-start(f32[13]{0:T(128)} %coupling_ref.1) | copy-start | bytes 160
  10.1 4.5 %copy-start.4 = (f32[64]{0:T(128)S(1)}, f32[64]{0:T(128)}, u32[]{:S(2)}) copy-start(f32[64]{0:T(128)} %mode_ref.1) | copy-start | bytes 772

commit v25 on v14

--- a/solution.py
+++ b/solution.py
@@ -13,6 +13,7 @@
 LANES = 128
 SUBLANES = 8
 SLOTS = 4
+SMALL = 3
 AXES = ("site", "phonon")
 
 epsilon = 1e-06
@@ -80,6 +81,15 @@
     out_ref[pl.ds(start, count, stride=stride), :] = jnp.broadcast_to(row, (count, LANES))
 
 
+def put_rows(out_ref, sums, start, stride, count):
+    for index, value in enumerate(sums):
+        out_ref[pl.ds(start + index, count, stride=stride), :] = jnp.broadcast_to(value, (count, LANES))
+
+
+def total_of(ref, start, stride, count):
+    return jnp.sum(lane_sums(ref[pl.ds(start, count, stride=stride), :]), axis=1, keepdims=True)
+
+
 def totals_of(ref, start, stride, count):
     lanes = lane_sums(ref[pl.ds(start, count, stride=stride), :])
     lane = lax.broadcasted_iota(jnp.int32, (1, LANES), 1)
@@ -114,7 +124,7 @@
             out_ref[pl.ds(piece * plan.lane_blocks + block, plan.groups, stride=plan.inward), :] = turned[
                 piece * plan.groups : (piece + 1) * plan.groups
             ]
-    put_sums(out_ref, [sums], plan.body, plan.inward, plan.groups)
+    put_rows(out_ref, [sums], plan.body, plan.inward, plan.groups)
 
 
 def fetch_slabs(plan, slabs, bits_ref, operators_ref, held_ref, semaphores):
@@ -299,7 +309,7 @@
     def ready(slab):
         fetches[slab].wait()
 
-    squares = totals_of(arrived_ref, plan.body, plan.inward, plan.groups)[0]
+    squares = total_of(arrived_ref, plan.body, plan.inward, plan.groups)
     inverse = 1.0 / scale_of(plan, squares)
     for block in range(plan.lane_blocks):
         parts = [
@@ -326,7 +336,7 @@
 
     step(plan, initial_ref, rounded_ref, *tables, finish, ready, new_ref)
     step(plan, new_ref, ahead_ref, *tables, look_ahead)
-    put_sums(sums_ref, [one_row(squares), one_row(overlap), one_row(ahead)], 0, 1, plan.groups)
+    put_rows(sums_ref, [one_row(squares), one_row(overlap), one_row(ahead)], 0, SMALL, plan.groups)
 
 
 def one_row(rows):
@@ -350,7 +360,7 @@
     second_ref,
     third_ref,
 ):
-    squares, overlap, ahead, _ = totals_of(arrived_ref, 0, 1, plan.groups)
+    squares, overlap, ahead = [total_of(arrived_ref, row, SMALL, plan.groups) for row in range(SMALL)]
     first = 1.0 / scale_of(plan, squares)
     estimate = scale_of(plan, ahead * first * first)
     second = 1.0 / estimate
@@ -480,7 +490,7 @@
         out_shape=[
             vector,
             vector,
-            jax.ShapeDtypeStruct((plan.groups, LANES), f32),
+            jax.ShapeDtypeStruct((plan.groups * SMALL, LANES), f32),
             jax.ShapeDtypeStruct(fetched_slabs, jnp.bfloat16),
         ],
         in_specs=[VMEM] * 4 + [HBM],

time: 73.8 us -> 73.8 us (level)
  no operation moved by 1% of the time
where the time goes in v25:
time: 73.8 us; the launch traced here: 73.4 us
  blocking collectives  40.4 us (55%)
  Pallas kernels  16.5 us (22%)
  waiting for transfers between devices  8.43 us (11%)
  starting transfers between devices  7.3 us (10%)
  between operations  0.75 us (1%)
    all_to_all x2, blocking collectives, exchange(): return lax.all_to_all(shaped, AXES, 0, 0, tiled=True).reshape(values.shape)  40.4 us
    all_to_all x1, waiting for transfers between devices, exchange(): return lax.all_to_all(shaped, AXES, 0, 0, tiled=True).reshape(values.shape)  8.43 us
    all_to_all x1, starting transfers between devices, exchange(): return lax.all_to_all(shaped, AXES, 0, 0, tiled=True).reshape(values.shape)  7.3 us
    pallas_call x1, Pallas kernels, shards(): pl.pallas_call(functools.partial(store_kernel, plan), out_shape=jax.Shape...  4.41 us
    pallas_call x1, Pallas kernels, shards(): pl.pallas_call(functools.partial(first_kernel, plan), out_shape=[vector,...  3.56 us
    pallas_call x1, Pallas kernels, shards(): pl.pallas_call(functools.partial(prepare_kernel, plan), out_shape=[jax.Sh...  2.87 us
    pallas_call x1, Pallas kernels, shards(): pl.pallas_call(functools.partial(onward_kernel, plan), out_shape=[outward...  2.4 us
    pallas_call x1, Pallas kernels, shards(): pl.pallas_call(functools.partial(depart_kernel, plan), out_shape=inward,...  2.04 us
  transfers between devices with their start and end apart: 1, of which 1 were waited for; matrix products, arithmetic and copies ran while one was open for 0% of the time, Pallas kernels for 10%

profile of v25, /device:TPU:0, one launch (start us, length us, event | category | flops | bytes accessed | tf_op | source)
XLA Modules:
  0.0 73.4 jit_solution(4032637931647442326)
XLA Ops:
  0.6 2.0 %depart.1 = f32[1056,128]{1,0:T(8,128)} custom-call(f32[1024,128]{1,0:T(8,128)} %state_ref.1), custom_call_target="tpu_custom_call" | custom-call | tf_op jit(solution)/shard_map/depart/pallas_call | solution.py:442
  2.7 7.3 %all-to-all-start = ((f32[32,33,1,128]{3,2,1,0:T(1,128)}), f32[32,33,1,128]{3,2,1,0:T(1,128)S(1)}, u32[]{:S(2)}, u32[]{:S(2)}) async-start(f32[32,33,1,128]{3,2,1,0:T(1,128)} %bitcast.11), calls=%async_computation | async-start | bytes 1081344 | tf_op jit(solution)/shard_map/all_to_all | solution.py:425
  10.0 0.0 copy-start
  10.0 0.0 copy-start.1
  10.0 0.0 copy-start.2
  10.0 0.0 copy-start.3
  10.0 0.0 copy-start.4
  10.0 4.4 %store.1.stored_ref = bf16[7,1024,256]{2,1,0:T(8,128)(2,1)} custom-call(s32[3]{0:T(128)} %bits_ref.3, s32[3,8,8]{2,1,0:T(8,128)} %mask_ref.3, bf16[3,1024,1024]{2,1,0:T(8,128)(2,1)} %operators_ref.3), custom_call_target="tpu_custom_call" | custom-call | flops 1048576 | bytes 7340032 | tf_op jit(solution)/shard_map/store/pallas_call | solution.py:473
  14.5 0.0 copy-done
  14.5 0.0 copy-done.1
  14.5 0.0 copy-done.2
  14.5 0.0 copy-done.3
  14.5 0.0 copy-done.4
  14.5 2.9 %prepare.1 = (f32[3,128,128]{2,1,0:T(8,128)S(1)}, f32[8,1024]{1,0:T(8,128)S(1)}, bf16[5,1024,256]{2,1,0:T(8,128)(2,1)S(1)}) custom-call(s32[3]{0:T(128)S(1)} %copy-done.1, s32[3,8,8]{2,1,0:T(8,128)S(1)} %copy-done, f32[3]{0:T(128)S(1)} %copy-done.2, f32[13]{0:T(128)S(1)} %copy-done.3, f32[64]{0:T(128)S(1)} %copy-done.4, bf16[3,1024,1024]{2,1,0:T(8,128)(2,1)} %operators_ref.3), custom_call_target="tpu_custom_call" | custom-call | flops 1048576 | bytes 5242880 | tf_op jit(solution)/shard_map/prepare/pallas_call | solution.py:459
  17.4 8.4 %all-to-all-done = f32[32,33,1,128]{3,2,1,0:T(1,128)S(1)} async-done(((f32[32,33,1,128]{3,2,1,0:T(1,128)}), f32[32,33,1,128]{3,2,1,0:T(1,128)S(1)}, u32[]{:S(2)}, u32[]{:S(2)}) %all-to-all-start) | async-done | bytes 540704 | tf_op jit(solution)/shard_map/all_to_all | solution.py:425
  25.8 3.6 %first.1 = (f32[128,1024]{1,0:T(8,128)S(1)}, f32[128,1024]{1,0:T(8,128)S(1)}, f32[96,128]{1,0:T(8,128)S(1)}, bf16[7,1024,256]{2,1,0:T(8,128)(2,1)S(1)}) custom-call(f32[1056,128]{1,0:T(8,128)S(1)} %bitcast.7, f32[3,128,128]{2,1,0:T(8,128)S(1)} %get-tuple-element.15.place_ref, f32[8,1024]{1,0:T(8,128)S(1)} %get-tuple-element.16.inside_ref, ...), custom_call_target="tpu_custom_call" | custom-call | flops 1610612736 | bytes 524288 | tf_op jit(solution)/shard_map/first/pallas_call | solution.py:488
  29.4 10.3 %all_to_all.15 = f32[32,3,1,128]{3,2,1,0:T(1,128)S(1)} all-to-all(f32[32,3,1,128]{3,2,1,0:T(1,128)S(1)} %bitcast.10), channel_id=1, replica_groups=mesh['site'=8,'phonon'=4] {'site','phonon'}, dimensions={0} | all-to-all | bytes 98304 | tf_op jit(solution)/shard_map/all_to_all | solution.py:425
  39.7 2.4 %onward.1 = (f32[2080,128]{1,0:T(8,128)S(1)}, f32[8,128]{1,0:T(8,128)S(1)}) custom-call(f32[96,128]{1,0:T(8,128)S(1)} %bitcast.9, f32[128,1024]{1,0:T(8,128)S(1)} %get-tuple-element.19.raw_ref, f32[128,1024]{1,0:T(8,128)S(1)} %get-tuple-element.20.initial_ref, f32[3,128,128]{2,1,0:T(8,128)S(1)} %get-tuple-element.15.place_ref, ...), custom_call_target="tpu_custom_call" | custom-call | flops 1610612736 | bytes 1048576 | tf_op jit(solution)/shard_map/onward/pallas_call | solution.py:505
  42.1 30.1 %all_to_all.16 = f32[32,65,1,128]{3,2,1,0:T(1,128)S(1)} all-to-all(f32[32,65,1,128]{3,2,1,0:T(1,128)S(1)} %bitcast.8), channel_id=1, replica_groups=mesh['site'=8,'phonon'=4] {'site','phonon'}, dimensions={0} | all-to-all | bytes 2129920 | tf_op jit(solution)/shard_map/all_to_all | solution.py:425
  72.2 1.3 %arrive.1 = (f32[1024,128]{1,0:T(8,128)}, f32[1024,128]{1,0:T(8,128)}, f32[3]{0:T(128)}) custom-call(f32[2080,128]{1,0:T(8,128)S(1)} %bitcast.6, f32[8,128]{1,0:T(8,128)S(1)} %get-tuple-element.23.known_ref), custom_call_target="tpu_custom_call" | custom-call | tf_op jit(solution)/shard_map/arrive/pallas_call | solution.py:516
Async XLA Ops:
  2.7 23.2 %all-to-all-start = ((f32[32,33,1,128]{3,2,1,0:T(1,128)}), f32[32,33,1,128]{3,2,1,0:T(1,128)S(1)}, u32[]{:S(2)}, u32[]{:S(2)}) async-start(f32[32,33,1,128]{3,2,1,0:T(1,128)} %bitcast.11), calls=%async_computation | async-start | bytes 1081344 | tf_op jit(solution)/shard_map/all_to_all | solution.py:425
  10.0 4.5 %copy-start = (s32[3,8,8]{2,1,0:T(8,128)S(1)}, s32[3,8,8]{2,1,0:T(8,128)}, u32[]{:S(2)}) copy-start(s32[3,8,8]{2,1,0:T(8,128)} %mask_ref.3) | copy-start | bytes 2308
  10.0 4.5 %copy-start.1 = (s32[3]{0:T(128)S(1)}, s32[3]{0:T(128)}, u32[]{:S(2)}) copy-start(s32[3]{0:T(128)} %bits_ref.3) | copy-start | bytes 40
  10.0 4.5 %copy-start.2 = (f32[3]{0:T(128)S(1)}, f32[3]{0:T(128)}, u32[]{:S(2)}) copy-start(f32[3]{0:T(128)} %field_ref.1) | copy-start | bytes 40
  10.0 4.5 %copy-start.3 = (f32[13]{0:T(128)S(1)}, f32[13]{0:T(128)}, u32[]{:S(2)}) copy-start(f32[13]{0:T(128)} %coupling_ref.1) | copy-start | bytes 160
  10.0 4.5 %copy-start.4 = (f32[64]{0:T(128)S(1)}, f32[64]{0:T(128)}, u32[]{:S(2)}) copy-start(f32[64]{0:T(128)} %mode_ref.1) | copy-start | bytes 772

commit v26 on v14

--- a/solution.py
+++ b/solution.py
@@ -12,7 +12,8 @@
 STEPS = 3
 LANES = 128
 SUBLANES = 8
-SLOTS = 4
+HOME = (32, 32, 32, 32)
+SMALL = (32, 32, 64)
 AXES = ("site", "phonon")
 
 epsilon = 1e-06
@@ -68,25 +69,30 @@
     return jnp.sum(values, axis=0, keepdims=True)
 
 
-def put_sums(out_ref, sums, start, stride, count):
+def slots_of(widths):
     lane = lax.broadcasted_iota(jnp.int32, (1, LANES), 1)
+    starts = [sum(widths[:index]) for index in range(len(widths))]
+    return [(width, (lane >= start) & (lane < start + width)) for width, start in zip(widths, starts)]
+
+
+def put_sums(out_ref, sums, widths, start, stride, count):
     row = jnp.zeros((1, LANES), jnp.float32)
-    for slot, value in enumerate(sums):
-        width = LANES
-        while width > LANES // SLOTS:
-            width //= 2
-            value = value + pltpu.roll(value, width, 1)
-        row = jnp.where(lane // (LANES // SLOTS) == slot, value, row)
+    for value, (width, inside) in zip(sums, slots_of(widths)):
+        reach = LANES
+        while reach > width:
+            reach //= 2
+            value = value + pltpu.roll(value, reach, 1)
+        row = jnp.where(inside, value, row)
     out_ref[pl.ds(start, count, stride=stride), :] = jnp.broadcast_to(row, (count, LANES))
 
 
-def totals_of(ref, start, stride, count):
+def total_of(ref, start, stride, count):
+    return jnp.sum(lane_sums(ref[pl.ds(start, count, stride=stride), :]), axis=1, keepdims=True)
+
+
+def totals_of(ref, widths, start, stride, count):
     lanes = lane_sums(ref[pl.ds(start, count, stride=stride), :])
-    lane = lax.broadcasted_iota(jnp.int32, (1, LANES), 1)
-    return [
-        jnp.sum(jnp.where(lane // (LANES // SLOTS) == slot, lanes, 0.0), axis=1, keepdims=True)
-        for slot in range(SLOTS)
-    ]
+    return [jnp.sum(jnp.where(inside, lanes, 0.0), axis=1, keepdims=True) for _, inside in slots_of(widths)]
 
 
 def scale_of(plan, squares):
@@ -114,7 +120,7 @@
             out_ref[pl.ds(piece * plan.lane_blocks + block, plan.groups, stride=plan.inward), :] = turned[
                 piece * plan.groups : (piece + 1) * plan.groups
             ]
-    put_sums(out_ref, [sums], plan.body, plan.inward, plan.groups)
+    put_sums(out_ref, [sums], (LANES,), plan.body, plan.inward, plan.groups)
 
 
 def fetch_slabs(plan, slabs, bits_ref, operators_ref, held_ref, semaphores):
@@ -299,7 +305,7 @@
     def ready(slab):
         fetches[slab].wait()
 
-    squares = totals_of(arrived_ref, plan.body, plan.inward, plan.groups)[0]
+    squares = total_of(arrived_ref, plan.body, plan.inward, plan.groups)
     inverse = 1.0 / scale_of(plan, squares)
     for block in range(plan.lane_blocks):
         parts = [
@@ -326,7 +332,7 @@
 
     step(plan, initial_ref, rounded_ref, *tables, finish, ready, new_ref)
     step(plan, new_ref, ahead_ref, *tables, look_ahead)
-    put_sums(sums_ref, [one_row(squares), one_row(overlap), one_row(ahead)], 0, 1, plan.groups)
+    put_sums(sums_ref, [one_row(squares), one_row(overlap), one_row(ahead)], SMALL, 0, 1, plan.groups)
 
 
 def one_row(rows):
@@ -350,7 +356,7 @@
     second_ref,
     third_ref,
 ):
-    squares, overlap, ahead, _ = totals_of(arrived_ref, 0, 1, plan.groups)
+    squares, overlap, ahead = totals_of(arrived_ref, SMALL, 0, 1, plan.groups)
     first = 1.0 / scale_of(plan, squares)
     estimate = scale_of(plan, ahead * first * first)
     second = 1.0 / estimate
@@ -362,7 +368,7 @@
         second_ref[:, lanes] = vector
         put_rounded(plan, rounded_ref, vector, block * LANES)
     tables = (kept_ref, fetched_ref, place_ref, inside_ref)
-    sums = [[] for _ in range(SLOTS)]
+    sums = [[] for _ in HOME]
 
     def send(vector, lanes, new):
         sums[2 * vector].append(lane_sums(new * new))
@@ -387,12 +393,12 @@
 
     step(plan, second_ref, rounded_ref, *tables, finish_second)
     step(plan, third_ref, ahead_ref, *tables, finish_third)
-    put_sums(out_ref, [one_row(rows) for rows in sums], 2 * plan.body, plan.outward, plan.groups)
+    put_sums(out_ref, [one_row(rows) for rows in sums], HOME, 2 * plan.body, plan.outward, plan.groups)
 
 
 def arrive_kernel(plan, arrived_ref, known_ref, before_ref, last_ref, moments_ref):
     before_squares, before_overlap, last_squares, last_overlap = totals_of(
-        arrived_ref, 2 * plan.body, plan.outward, plan.groups
+        arrived_ref, HOME, 2 * plan.body, plan.outward, plan.groups
     )
     before = 1.0 / scale_of(plan, before_squares)
     back = known_ref[1:2, :1] * before

time: 73.8 us -> 73.6 us (level)
  no operation moved by 1% of the time
where the time goes in v26:
time: 73.6 us; the launch traced here: 73.3 us
  blocking collectives  40.2 us (55%)
  Pallas kernels  16.6 us (23%)
  waiting for transfers between devices  8.43 us (11%)
  starting transfers between devices  7.3 us (10%)
  between operations  0.75 us (1%)
    all_to_all x2, blocking collectives, exchange(): return lax.all_to_all(shaped, AXES, 0, 0, tiled=True).reshape(values.shape)  40.2 us
    all_to_all x1, waiting for transfers between devices, exchange(): return lax.all_to_all(shaped, AXES, 0, 0, tiled=True).reshape(values.shape)  8.43 us
    all_to_all x1, starting transfers between devices, exchange(): return lax.all_to_all(shaped, AXES, 0, 0, tiled=True).reshape(values.shape)  7.3 us
    pallas_call x1, Pallas kernels, shards(): pl.pallas_call(functools.partial(store_kernel, plan), out_shape=jax.Shape...  4.41 us
    pallas_call x1, Pallas kernels, shards(): pl.pallas_call(functools.partial(first_kernel, plan), out_shape=[vector,...  3.63 us
    pallas_call x1, Pallas kernels, shards(): pl.pallas_call(functools.partial(prepare_kernel, plan), out_shape=[jax.Sh...  2.87 us
    pallas_call x1, Pallas kernels, shards(): pl.pallas_call(functools.partial(onward_kernel, plan), out_shape=[outward...  2.36 us
    pallas_call x1, Pallas kernels, shards(): pl.pallas_call(functools.partial(depart_kernel, plan), out_shape=inward,...  2.04 us
  transfers between devices with their start and end apart: 1, of which 1 were waited for; matrix products, arithmetic and copies ran while one was open for 0% of the time, Pallas kernels for 10%

profile of v26, /device:TPU:0, one launch (start us, length us, event | category | flops | bytes accessed | tf_op | source)
XLA Modules:
  0.0 73.3 jit_solution(16716876760377098940)
XLA Ops:
  0.6 2.0 %depart.1 = f32[1056,128]{1,0:T(8,128)} custom-call(f32[1024,128]{1,0:T(8,128)} %state_ref.1), custom_call_target="tpu_custom_call" | custom-call | tf_op jit(solution)/shard_map/depart/pallas_call | solution.py:438
  2.7 7.3 %all-to-all-start = ((f32[32,33,1,128]{3,2,1,0:T(1,128)}), f32[32,33,1,128]{3,2,1,0:T(1,128)S(1)}, u32[]{:S(2)}, u32[]{:S(2)}) async-start(f32[32,33,1,128]{3,2,1,0:T(1,128)} %bitcast.13), calls=%async_computation | async-start | bytes 1081344 | tf_op jit(solution)/shard_map/all_to_all | solution.py:421
  10.0 0.0 copy-start
  10.0 0.0 copy-start.1
  10.0 0.0 copy-start.2
  10.0 0.0 copy-start.3
  10.0 0.0 copy-start.4
  10.0 4.4 %store.1.stored_ref = bf16[7,1024,256]{2,1,0:T(8,128)(2,1)} custom-call(s32[3]{0:T(128)} %bits_ref.3, s32[3,8,8]{2,1,0:T(8,128)} %mask_ref.3, bf16[3,1024,1024]{2,1,0:T(8,128)(2,1)} %operators_ref.3), custom_call_target="tpu_custom_call" | custom-call | flops 1048576 | bytes 7340032 | tf_op jit(solution)/shard_map/store/pallas_call | solution.py:469
  14.5 0.0 copy-done
  14.5 0.0 copy-done.1
  14.5 0.0 copy-done.2
  14.5 0.0 copy-done.3
  14.5 0.0 copy-done.4
  14.5 2.9 %prepare.1 = (f32[3,128,128]{2,1,0:T(8,128)S(1)}, f32[8,1024]{1,0:T(8,128)S(1)}, bf16[5,1024,256]{2,1,0:T(8,128)(2,1)S(1)}) custom-call(s32[3]{0:T(128)S(1)} %copy-done.1, s32[3,8,8]{2,1,0:T(8,128)S(1)} %copy-done, f32[3]{0:T(128)S(1)} %copy-done.2, f32[13]{0:T(128)S(1)} %copy-done.3, f32[64]{0:T(128)S(1)} %copy-done.4, bf16[3,1024,1024]{2,1,0:T(8,128)(2,1)} %operators_ref.3), custom_call_target="tpu_custom_call" | custom-call | flops 1048576 | bytes 5242880 | tf_op jit(solution)/shard_map/prepare/pallas_call | solution.py:455
  17.4 8.4 %all-to-all-done = f32[32,33,1,128]{3,2,1,0:T(1,128)S(1)} async-done(((f32[32,33,1,128]{3,2,1,0:T(1,128)}), f32[32,33,1,128]{3,2,1,0:T(1,128)S(1)}, u32[]{:S(2)}, u32[]{:S(2)}) %all-to-all-start) | async-done | bytes 540704 | tf_op jit(solution)/shard_map/all_to_all | solution.py:421
  25.8 3.6 %first.1 = (f32[128,1024]{1,0:T(8,128)S(1)}, f32[128,1024]{1,0:T(8,128)S(1)}, f32[32,128]{1,0:T(8,128)S(1)}, bf16[7,1024,256]{2,1,0:T(8,128)(2,1)S(1)}) custom-call(f32[1056,128]{1,0:T(8,128)S(1)} %bitcast.9, f32[3,128,128]{2,1,0:T(8,128)S(1)} %get-tuple-element.15.place_ref, f32[8,1024]{1,0:T(8,128)S(1)} %get-tuple-element.16.inside_ref, ...), custom_call_target="tpu_custom_call" | custom-call | flops 1610612736 | bytes 524288 | tf_op jit(solution)/shard_map/first/pallas_call | solution.py:484
  29.5 10.1 %all_to_all.15 = f32[32,1,1,128]{3,2,1,0:T(1,128)S(1)} all-to-all(f32[32,1,1,128]{3,2,1,0:T(1,128)S(1)} %bitcast.12), channel_id=1, replica_groups=mesh['site'=8,'phonon'=4] {'site','phonon'}, dimensions={0} | all-to-all | bytes 32768 | tf_op jit(solution)/shard_map/all_to_all | solution.py:421
  39.6 2.4 %onward.1 = (f32[2080,128]{1,0:T(8,128)S(1)}, f32[8,128]{1,0:T(8,128)S(1)}) custom-call(f32[32,128]{1,0:T(8,128)S(1)} %bitcast.11, f32[128,1024]{1,0:T(8,128)S(1)} %get-tuple-element.19.raw_ref, f32[128,1024]{1,0:T(8,128)S(1)} %get-tuple-element.20.initial_ref, f32[3,128,128]{2,1,0:T(8,128)S(1)} %get-tuple-element.15.place_ref, ...), custom_call_target="tpu_custom_call" | custom-call | flops 1610612736 | bytes 1048576 | tf_op jit(solution)/shard_map/onward/pallas_call | solution.py:501
  41.9 30.1 %all_to_all.16 = f32[32,65,1,128]{3,2,1,0:T(1,128)S(1)} all-to-all(f32[32,65,1,128]{3,2,1,0:T(1,128)S(1)} %bitcast.10), channel_id=1, replica_groups=mesh['site'=8,'phonon'=4] {'site','phonon'}, dimensions={0} | all-to-all | bytes 2129920 | tf_op jit(solution)/shard_map/all_to_all | solution.py:421
  72.0 1.3 %arrive.1 = (f32[1024,128]{1,0:T(8,128)}, f32[1024,128]{1,0:T(8,128)}, f32[3]{0:T(128)}) custom-call(f32[2080,128]{1,0:T(8,128)S(1)} %bitcast.8, f32[8,128]{1,0:T(8,128)S(1)} %get-tuple-element.23.known_ref), custom_call_target="tpu_custom_call" | custom-call | tf_op jit(solution)/shard_map/arrive/pallas_call | solution.py:512
Async XLA Ops:
  2.7 23.2 %all-to-all-start = ((f32[32,33,1,128]{3,2,1,0:T(1,128)}), f32[32,33,1,128]{3,2,1,0:T(1,128)S(1)}, u32[]{:S(2)}, u32[]{:S(2)}) async-start(f32[32,33,1,128]{3,2,1,0:T(1,128)} %bitcast.13), calls=%async_computation | async-start | bytes 1081344 | tf_op jit(solution)/shard_map/all_to_all | solution.py:421
  10.0 4.5 %copy-start = (s32[3,8,8]{2,1,0:T(8,128)S(1)}, s32[3,8,8]{2,1,0:T(8,128)}, u32[]{:S(2)}) copy-start(s32[3,8,8]{2,1,0:T(8,128)} %mask_ref.3) | copy-start | bytes 2308
  10.0 4.5 %copy-start.1 = (s32[3]{0:T(128)S(1)}, s32[3]{0:T(128)}, u32[]{:S(2)}) copy-start(s32[3]{0:T(128)} %bits_ref.3) | copy-start | bytes 40
  10.0 4.5 %copy-start.2 = (f32[3]{0:T(128)S(1)}, f32[3]{0:T(128)}, u32[]{:S(2)}) copy-start(f32[3]{0:T(128)} %field_ref.1) | copy-start | bytes 40
  10.0 4.5 %copy-start.3 = (f32[13]{0:T(128)S(1)}, f32[13]{0:T(128)}, u32[]{:S(2)}) copy-start(f32[13]{0:T(128)} %coupling_ref.1) | copy-start | bytes 160
  10.0 4.5 %copy-start.4 = (f32[64]{0:T(128)S(1)}, f32[64]{0:T(128)}, u32[]{:S(2)}) copy-start(f32[64]{0:T(128)} %mode_ref.1) | copy-start | bytes 772

commit v27 on v26

--- a/solution.py
+++ b/solution.py
@@ -236,7 +236,7 @@
         ).astype(jnp.bfloat16)
 
 
-def step(plan, vector_ref, rounded_ref, kept_ref, fetched_ref, place_ref, inside_ref, finish, ready=None, begun_ref=None):
+def step(plan, vector_ref, rounded_ref, kept_ref, fetched_ref, place_ref, inside_ref, finish, ready=None, begun_ref=None, factor=None):
     span = plan.places // plan.levels_here
 
     def local(start):
@@ -249,7 +249,7 @@
         total = weight * (place_ref[1] * lower + place_ref[2] * upper)
         for position in range(plan.bits):
             total = total + inside_ref[pl.ds(1 + position, 1), lanes] * flipped(vector, plan.phonons << position)
-        return total
+        return total if factor is None else total * factor
 
     def added(total, part, late):
         for ref, low, high in ((kept_ref, 0, plan.kept), (fetched_ref, plan.kept, plan.slabs)):
@@ -353,20 +353,18 @@
     known_ref,
     rounded_ref,
     ahead_ref,
-    second_ref,
     third_ref,
 ):
     squares, overlap, ahead = totals_of(arrived_ref, SMALL, 0, 1, plan.groups)
     first = 1.0 / scale_of(plan, squares)
     estimate = scale_of(plan, ahead * first * first)
     second = 1.0 / estimate
+    both = first * second
     known_ref[:1, :] = jnp.broadcast_to(overlap * first / plan.entries, (1, LANES))
     known_ref[1:, :] = jnp.broadcast_to(estimate, (SUBLANES - 1, LANES))
     for block in range(plan.lane_blocks):
         lanes = pl.ds(block * LANES, LANES)
-        vector = raw_ref[:, lanes] * first
-        second_ref[:, lanes] = vector
-        put_rounded(plan, rounded_ref, vector, block * LANES)
+        put_rounded(plan, rounded_ref, raw_ref[:, lanes] * first, block * LANES)
     tables = (kept_ref, fetched_ref, place_ref, inside_ref)
     sums = [[] for _ in HOME]
 
@@ -389,9 +387,9 @@
         send(0, lanes, new)
 
     def finish_third(lanes, total):
-        send(1, lanes, 2.0 * total - second_ref[:, lanes] * second)
-
-    step(plan, second_ref, rounded_ref, *tables, finish_second)
+        send(1, lanes, 2.0 * total - raw_ref[:, lanes] * both)
+
+    step(plan, raw_ref, rounded_ref, *tables, finish_second, factor=first)
     step(plan, third_ref, ahead_ref, *tables, finish_third)
     put_sums(out_ref, [one_row(rows) for rows in sums], HOME, 2 * plan.body, plan.outward, plan.groups)
 
@@ -503,7 +501,7 @@
         out_shape=[outward, known],
         in_specs=[VMEM] * 7,
         out_specs=[VMEM] * 2,
-        scratch_shapes=[rounded, rounded, working, working],
+        scratch_shapes=[rounded, rounded, working],
         compiler_params=params(32),
         cost_estimate=cost(2 * work, 8 * plan.places * plan.rows),
         name="onward",

time: 73.6 us -> 73.6 us (level)
  no operation moved by 1% of the time
where the time goes in v27:
time: 73.6 us; the launch traced here: 73.2 us
  blocking collectives  40.2 us (55%)
  Pallas kernels  16.5 us (22%)
  waiting for transfers between devices  8.43 us (11%)
  starting transfers between devices  7.3 us (10%)
  between operations  0.75 us (1%)
    all_to_all x2, blocking collectives, exchange(): return lax.all_to_all(shaped, AXES, 0, 0, tiled=True).reshape(values.shape)  40.2 us
    all_to_all x1, waiting for transfers between devices, exchange(): return lax.all_to_all(shaped, AXES, 0, 0, tiled=True).reshape(values.shape)  8.43 us
    all_to_all x1, starting transfers between devices, exchange(): return lax.all_to_all(shaped, AXES, 0, 0, tiled=True).reshape(values.shape)  7.3 us
    pallas_call x1, Pallas kernels, shards(): pl.pallas_call(functools.partial(store_kernel, plan), out_shape=jax.Shape...  4.41 us
    pallas_call x1, Pallas kernels, shards(): pl.pallas_call(functools.partial(first_kernel, plan), out_shape=[vector,...  3.63 us
    pallas_call x1, Pallas kernels, shards(): pl.pallas_call(functools.partial(prepare_kernel, plan), out_shape=[jax.Sh...  2.87 us
    pallas_call x1, Pallas kernels, shards(): pl.pallas_call(functools.partial(onward_kernel, plan), out_shape=[outward...  2.31 us
    pallas_call x1, Pallas kernels, shards(): pl.pallas_call(functools.partial(depart_kernel, plan), out_shape=inward,...  2.04 us
  transfers between devices with their start and end apart: 1, of which 1 were waited for; matrix products, arithmetic and copies ran while one was open for 0% of the time, Pallas kernels for 10%

profile of v27, /device:TPU:0, one launch (start us, length us, event | category | flops | bytes accessed | tf_op | source)
XLA Modules:
  0.0 73.2 jit_solution(7683384327336920070)
XLA Ops:
  0.6 2.0 %depart.1 = f32[1056,128]{1,0:T(8,128)} custom-call(f32[1024,128]{1,0:T(8,128)} %state_ref.1), custom_call_target="tpu_custom_call" | custom-call | tf_op jit(solution)/shard_map/depart/pallas_call | solution.py:436
  2.7 7.3 %all-to-all-start = ((f32[32,33,1,128]{3,2,1,0:T(1,128)}), f32[32,33,1,128]{3,2,1,0:T(1,128)S(1)}, u32[]{:S(2)}, u32[]{:S(2)}) async-start(f32[32,33,1,128]{3,2,1,0:T(1,128)} %bitcast.13), calls=%async_computation | async-start | bytes 1081344 | tf_op jit(solution)/shard_map/all_to_all | solution.py:419
  10.0 0.0 copy-start
  10.0 0.0 copy-start.1
  10.0 0.0 copy-start.2
  10.0 0.0 copy-start.3
  10.0 0.0 copy-start.4
  10.0 4.4 %store.1.stored_ref = bf16[7,1024,256]{2,1,0:T(8,128)(2,1)} custom-call(s32[3]{0:T(128)} %bits_ref.3, s32[3,8,8]{2,1,0:T(8,128)} %mask_ref.3, bf16[3,1024,1024]{2,1,0:T(8,128)(2,1)} %operators_ref.3), custom_call_target="tpu_custom_call" | custom-call | flops 1048576 | bytes 7340032 | tf_op jit(solution)/shard_map/store/pallas_call | solution.py:467
  14.5 0.0 copy-done
  14.5 0.0 copy-done.1
  14.5 0.0 copy-done.2
  14.5 0.0 copy-done.3
  14.5 0.0 copy-done.4
  14.5 2.9 %prepare.1 = (f32[3,128,128]{2,1,0:T(8,128)S(1)}, f32[8,1024]{1,0:T(8,128)S(1)}, bf16[5,1024,256]{2,1,0:T(8,128)(2,1)S(1)}) custom-call(s32[3]{0:T(128)S(1)} %copy-done.1, s32[3,8,8]{2,1,0:T(8,128)S(1)} %copy-done, f32[3]{0:T(128)S(1)} %copy-done.2, f32[13]{0:T(128)S(1)} %copy-done.3, f32[64]{0:T(128)S(1)} %copy-done.4, bf16[3,1024,1024]{2,1,0:T(8,128)(2,1)} %operators_ref.3), custom_call_target="tpu_custom_call" | custom-call | flops 1048576 | bytes 5242880 | tf_op jit(solution)/shard_map/prepare/pallas_call | solution.py:453
  17.4 8.4 %all-to-all-done = f32[32,33,1,128]{3,2,1,0:T(1,128)S(1)} async-done(((f32[32,33,1,128]{3,2,1,0:T(1,128)}), f32[32,33,1,128]{3,2,1,0:T(1,128)S(1)}, u32[]{:S(2)}, u32[]{:S(2)}) %all-to-all-start) | async-done | bytes 540704 | tf_op jit(solution)/shard_map/all_to_all | solution.py:419
  25.8 3.6 %first.1 = (f32[128,1024]{1,0:T(8,128)S(1)}, f32[128,1024]{1,0:T(8,128)S(1)}, f32[32,128]{1,0:T(8,128)S(1)}, bf16[7,1024,256]{2,1,0:T(8,128)(2,1)S(1)}) custom-call(f32[1056,128]{1,0:T(8,128)S(1)} %bitcast.9, f32[3,128,128]{2,1,0:T(8,128)S(1)} %get-tuple-element.15.place_ref, f32[8,1024]{1,0:T(8,128)S(1)} %get-tuple-element.16.inside_ref, ...), custom_call_target="tpu_custom_call" | custom-call | flops 1610612736 | bytes 524288 | tf_op jit(solution)/shard_map/first/pallas_call | solution.py:482
  29.5 10.1 %all_to_all.15 = f32[32,1,1,128]{3,2,1,0:T(1,128)S(1)} all-to-all(f32[32,1,1,128]{3,2,1,0:T(1,128)S(1)} %bitcast.12), channel_id=1, replica_groups=mesh['site'=8,'phonon'=4] {'site','phonon'}, dimensions={0} | all-to-all | bytes 32768 | tf_op jit(solution)/shard_map/all_to_all | solution.py:419
  39.6 2.3 %onward.1 = (f32[2080,128]{1,0:T(8,128)S(1)}, f32[8,128]{1,0:T(8,128)S(1)}) custom-call(f32[32,128]{1,0:T(8,128)S(1)} %bitcast.11, f32[128,1024]{1,0:T(8,128)S(1)} %get-tuple-element.19.raw_ref, f32[128,1024]{1,0:T(8,128)S(1)} %get-tuple-element.20.initial_ref, f32[3,128,128]{2,1,0:T(8,128)S(1)} %get-tuple-element.15.place_ref, ...), custom_call_target="tpu_custom_call" | custom-call | flops 1610612736 | bytes 1048576 | tf_op jit(solution)/shard_map/onward/pallas_call | solution.py:499
  41.9 30.1 %all_to_all.16 = f32[32,65,1,128]{3,2,1,0:T(1,128)S(1)} all-to-all(f32[32,65,1,128]{3,2,1,0:T(1,128)S(1)} %bitcast.10), channel_id=1, replica_groups=mesh['site'=8,'phonon'=4] {'site','phonon'}, dimensions={0} | all-to-all | bytes 2129920 | tf_op jit(solution)/shard_map/all_to_all | solution.py:419
  72.0 1.3 %arrive.1 = (f32[1024,128]{1,0:T(8,128)}, f32[1024,128]{1,0:T(8,128)}, f32[3]{0:T(128)}) custom-call(f32[2080,128]{1,0:T(8,128)S(1)} %bitcast.8, f32[8,128]{1,0:T(8,128)S(1)} %get-tuple-element.23.known_ref), custom_call_target="tpu_custom_call" | custom-call | tf_op jit(solution)/shard_map/arrive/pallas_call | solution.py:510
Async XLA Ops:
  2.7 23.2 %all-to-all-start = ((f32[32,33,1,128]{3,2,1,0:T(1,128)}), f32[32,33,1,128]{3,2,1,0:T(1,128)S(1)}, u32[]{:S(2)}, u32[]{:S(2)}) async-start(f32[32,33,1,128]{3,2,1,0:T(1,128)} %bitcast.13), calls=%async_computation | async-start | bytes 1081344 | tf_op jit(solution)/shard_map/all_to_all | solution.py:419
  10.0 4.5 %copy-start = (s32[3,8,8]{2,1,0:T(8,128)S(1)}, s32[3,8,8]{2,1,0:T(8,128)}, u32[]{:S(2)}) copy-start(s32[3,8,8]{2,1,0:T(8,128)} %mask_ref.3) | copy-start | bytes 2308
  10.0 4.5 %copy-start.1 = (s32[3]{0:T(128)S(1)}, s32[3]{0:T(128)}, u32[]{:S(2)}) copy-start(s32[3]{0:T(128)} %bits_ref.3) | copy-start | bytes 40
  10.0 4.5 %copy-start.2 = (f32[3]{0:T(128)S(1)}, f32[3]{0:T(128)}, u32[]{:S(2)}) copy-start(f32[3]{0:T(128)} %field_ref.1) | copy-start | bytes 40
  10.0 4.5 %copy-start.3 = (f32[13]{0:T(128)S(1)}, f32[13]{0:T(128)}, u32[]{:S(2)}) copy-start(f32[13]{0:T(128)} %coupling_ref.1) | copy-start | bytes 160
  10.0 4.5 %copy-start.4 = (f32[64]{0:T(128)S(1)}, f32[64]{0:T(128)}, u32[]{:S(2)}) copy-start(f32[64]{0:T(128)} %mode_ref.1) | copy-start | bytes 772

commit v28 on v25

--- a/solution.py
+++ b/solution.py
@@ -240,7 +240,7 @@
         ).astype(jnp.bfloat16)
 
 
-def step(plan, vector_ref, rounded_ref, kept_ref, fetched_ref, place_ref, inside_ref, finish, ready=None, begun_ref=None):
+def step(plan, vector_ref, rounded_ref, kept_ref, fetched_ref, place_ref, inside_ref, finish, ready=None, begun_ref=None, factor=None):
     span = plan.places // plan.levels_here
 
     def local(start):
@@ -253,7 +253,7 @@
         total = weight * (place_ref[1] * lower + place_ref[2] * upper)
         for position in range(plan.bits):
             total = total + inside_ref[pl.ds(1 + position, 1), lanes] * flipped(vector, plan.phonons << position)
-        return total
+        return total if factor is None else total * factor
 
     def added(total, part, late):
         for ref, low, high in ((kept_ref, 0, plan.kept), (fetched_ref, plan.kept, plan.slabs)):
@@ -357,20 +357,18 @@
     known_ref,
     rounded_ref,
     ahead_ref,
-    second_ref,
     third_ref,
 ):
     squares, overlap, ahead = [total_of(arrived_ref, row, SMALL, plan.groups) for row in range(SMALL)]
     first = 1.0 / scale_of(plan, squares)
     estimate = scale_of(plan, ahead * first * first)
     second = 1.0 / estimate
+    both = first * second
     known_ref[:1, :] = jnp.broadcast_to(overlap * first / plan.entries, (1, LANES))
     known_ref[1:, :] = jnp.broadcast_to(estimate, (SUBLANES - 1, LANES))
     for block in range(plan.lane_blocks):
         lanes = pl.ds(block * LANES, LANES)
-        vector = raw_ref[:, lanes] * first
-        second_ref[:, lanes] = vector
-        put_rounded(plan, rounded_ref, vector, block * LANES)
+        put_rounded(plan, rounded_ref, raw_ref[:, lanes] * first, block * LANES)
     tables = (kept_ref, fetched_ref, place_ref, inside_ref)
     sums = [[] for _ in range(SLOTS)]
 
@@ -393,9 +391,9 @@
         send(0, lanes, new)
 
     def finish_third(lanes, total):
-        send(1, lanes, 2.0 * total - second_ref[:, lanes] * second)
-
-    step(plan, second_ref, rounded_ref, *tables, finish_second)
+        send(1, lanes, 2.0 * total - raw_ref[:, lanes] * both)
+
+    step(plan, raw_ref, rounded_ref, *tables, finish_second, factor=first)
     step(plan, third_ref, ahead_ref, *tables, finish_third)
     put_sums(out_ref, [one_row(rows) for rows in sums], 2 * plan.body, plan.outward, plan.groups)
 
@@ -507,7 +505,7 @@
         out_shape=[outward, known],
         in_specs=[VMEM] * 7,
         out_specs=[VMEM] * 2,
-        scratch_shapes=[rounded, rounded, working, working],
+        scratch_shapes=[rounded, rounded, working],
         compiler_params=params(32),
         cost_estimate=cost(2 * work, 8 * plan.places * plan.rows),
         name="onward",

time: 73.8 us -> 73.7 us (level)
  no operation moved by 1% of the time
where the time goes in v28:
time: 73.7 us; the launch traced here: 73.4 us
  blocking collectives  40.4 us (55%)
  Pallas kernels  16.5 us (22%)
  waiting for transfers between devices  8.43 us (11%)
  starting transfers between devices  7.3 us (10%)
  between operations  0.75 us (1%)
    all_to_all x2, blocking collectives, exchange(): return lax.all_to_all(shaped, AXES, 0, 0, tiled=True).reshape(values.shape)  40.4 us
    all_to_all x1, waiting for transfers between devices, exchange(): return lax.all_to_all(shaped, AXES, 0, 0, tiled=True).reshape(values.shape)  8.43 us
    all_to_all x1, starting transfers between devices, exchange(): return lax.all_to_all(shaped, AXES, 0, 0, tiled=True).reshape(values.shape)  7.3 us
    pallas_call x1, Pallas kernels, shards(): pl.pallas_call(functools.partial(store_kernel, plan), out_shape=jax.Shape...  4.41 us
    pallas_call x1, Pallas kernels, shards(): pl.pallas_call(functools.partial(first_kernel, plan), out_shape=[vector,...  3.56 us
    pallas_call x1, Pallas kernels, shards(): pl.pallas_call(functools.partial(prepare_kernel, plan), out_shape=[jax.Sh...  2.87 us
    pallas_call x1, Pallas kernels, shards(): pl.pallas_call(functools.partial(onward_kernel, plan), out_shape=[outward...  2.32 us
    pallas_call x1, Pallas kernels, shards(): pl.pallas_call(functools.partial(depart_kernel, plan), out_shape=inward,...  2.04 us
  transfers between devices with their start and end apart: 1, of which 1 were waited for; matrix products, arithmetic and copies ran while one was open for 0% of the time, Pallas kernels for 10%

profile of v28, /device:TPU:0, one launch (start us, length us, event | category | flops | bytes accessed | tf_op | source)
XLA Modules:
  0.0 73.4 jit_solution(8024931532148316421)
XLA Ops:
  0.6 2.0 %depart.1 = f32[1056,128]{1,0:T(8,128)} custom-call(f32[1024,128]{1,0:T(8,128)} %state_ref.1), custom_call_target="tpu_custom_call" | custom-call | tf_op jit(solution)/shard_map/depart/pallas_call | solution.py:440
  2.7 7.3 %all-to-all-start = ((f32[32,33,1,128]{3,2,1,0:T(1,128)}), f32[32,33,1,128]{3,2,1,0:T(1,128)S(1)}, u32[]{:S(2)}, u32[]{:S(2)}) async-start(f32[32,33,1,128]{3,2,1,0:T(1,128)} %bitcast.11), calls=%async_computation | async-start | bytes 1081344 | tf_op jit(solution)/shard_map/all_to_all | solution.py:423
  10.0 0.0 copy-start
  10.0 0.0 copy-start.1
  10.0 0.0 copy-start.2
  10.0 0.0 copy-start.3
  10.0 0.0 copy-start.4
  10.0 4.4 %store.1.stored_ref = bf16[7,1024,256]{2,1,0:T(8,128)(2,1)} custom-call(s32[3]{0:T(128)} %bits_ref.3, s32[3,8,8]{2,1,0:T(8,128)} %mask_ref.3, bf16[3,1024,1024]{2,1,0:T(8,128)(2,1)} %operators_ref.3), custom_call_target="tpu_custom_call" | custom-call | flops 1048576 | bytes 7340032 | tf_op jit(solution)/shard_map/store/pallas_call | solution.py:471
  14.5 0.0 copy-done
  14.5 0.0 copy-done.1
  14.5 0.0 copy-done.2
  14.5 0.0 copy-done.3
  14.5 0.0 copy-done.4
  14.5 2.9 %prepare.1 = (f32[3,128,128]{2,1,0:T(8,128)S(1)}, f32[8,1024]{1,0:T(8,128)S(1)}, bf16[5,1024,256]{2,1,0:T(8,128)(2,1)S(1)}) custom-call(s32[3]{0:T(128)S(1)} %copy-done.1, s32[3,8,8]{2,1,0:T(8,128)S(1)} %copy-done, f32[3]{0:T(128)S(1)} %copy-done.2, f32[13]{0:T(128)S(1)} %copy-done.3, f32[64]{0:T(128)S(1)} %copy-done.4, bf16[3,1024,1024]{2,1,0:T(8,128)(2,1)} %operators_ref.3), custom_call_target="tpu_custom_call" | custom-call | flops 1048576 | bytes 5242880 | tf_op jit(solution)/shard_map/prepare/pallas_call | solution.py:457
  17.4 8.4 %all-to-all-done = f32[32,33,1,128]{3,2,1,0:T(1,128)S(1)} async-done(((f32[32,33,1,128]{3,2,1,0:T(1,128)}), f32[32,33,1,128]{3,2,1,0:T(1,128)S(1)}, u32[]{:S(2)}, u32[]{:S(2)}) %all-to-all-start) | async-done | bytes 540704 | tf_op jit(solution)/shard_map/all_to_all | solution.py:423
  25.8 3.6 %first.1 = (f32[128,1024]{1,0:T(8,128)S(1)}, f32[128,1024]{1,0:T(8,128)S(1)}, f32[96,128]{1,0:T(8,128)S(1)}, bf16[7,1024,256]{2,1,0:T(8,128)(2,1)S(1)}) custom-call(f32[1056,128]{1,0:T(8,128)S(1)} %bitcast.7, f32[3,128,128]{2,1,0:T(8,128)S(1)} %get-tuple-element.15.place_ref, f32[8,1024]{1,0:T(8,128)S(1)} %get-tuple-element.16.inside_ref, ...), custom_call_target="tpu_custom_call" | custom-call | flops 1610612736 | bytes 524288 | tf_op jit(solution)/shard_map/first/pallas_call | solution.py:486
  29.4 10.3 %all_to_all.15 = f32[32,3,1,128]{3,2,1,0:T(1,128)S(1)} all-to-all(f32[32,3,1,128]{3,2,1,0:T(1,128)S(1)} %bitcast.10), channel_id=1, replica_groups=mesh['site'=8,'phonon'=4] {'site','phonon'}, dimensions={0} | all-to-all | bytes 98304 | tf_op jit(solution)/shard_map/all_to_all | solution.py:423
  39.7 2.3 %onward.1 = (f32[2080,128]{1,0:T(8,128)S(1)}, f32[8,128]{1,0:T(8,128)S(1)}) custom-call(f32[96,128]{1,0:T(8,128)S(1)} %bitcast.9, f32[128,1024]{1,0:T(8,128)S(1)} %get-tuple-element.19.raw_ref, f32[128,1024]{1,0:T(8,128)S(1)} %get-tuple-element.20.initial_ref, f32[3,128,128]{2,1,0:T(8,128)S(1)} %get-tuple-element.15.place_ref, ...), custom_call_target="tpu_custom_call" | custom-call | flops 1610612736 | bytes 1048576 | tf_op jit(solution)/shard_map/onward/pallas_call | solution.py:503
  42.0 30.1 %all_to_all.16 = f32[32,65,1,128]{3,2,1,0:T(1,128)S(1)} all-to-all(f32[32,65,1,128]{3,2,1,0:T(1,128)S(1)} %bitcast.8), channel_id=1, replica_groups=mesh['site'=8,'phonon'=4] {'site','phonon'}, dimensions={0} | all-to-all | bytes 2129920 | tf_op jit(solution)/shard_map/all_to_all | solution.py:423
  72.1 1.3 %arrive.1 = (f32[1024,128]{1,0:T(8,128)}, f32[1024,128]{1,0:T(8,128)}, f32[3]{0:T(128)}) custom-call(f32[2080,128]{1,0:T(8,128)S(1)} %bitcast.6, f32[8,128]{1,0:T(8,128)S(1)} %get-tuple-element.23.known_ref), custom_call_target="tpu_custom_call" | custom-call | tf_op jit(solution)/shard_map/arrive/pallas_call | solution.py:514
Async XLA Ops:
  2.7 23.2 %all-to-all-start = ((f32[32,33,1,128]{3,2,1,0:T(1,128)}), f32[32,33,1,128]{3,2,1,0:T(1,128)S(1)}, u32[]{:S(2)}, u32[]{:S(2)}) async-start(f32[32,33,1,128]{3,2,1,0:T(1,128)} %bitcast.11), calls=%async_computation | async-start | bytes 1081344 | tf_op jit(solution)/shard_map/all_to_all | solution.py:423
  10.0 4.5 %copy-start = (s32[3,8,8]{2,1,0:T(8,128)S(1)}, s32[3,8,8]{2,1,0:T(8,128)}, u32[]{:S(2)}) copy-start(s32[3,8,8]{2,1,0:T(8,128)} %mask_ref.3) | copy-start | bytes 2308
  10.0 4.5 %copy-start.1 = (s32[3]{0:T(128)S(1)}, s32[3]{0:T(128)}, u32[]{:S(2)}) copy-start(s32[3]{0:T(128)} %bits_ref.3) | copy-start | bytes 40
  10.0 4.5 %copy-start.2 = (f32[3]{0:T(128)S(1)}, f32[3]{0:T(128)}, u32[]{:S(2)}) copy-start(f32[3]{0:T(128)} %field_ref.1) | copy-start | bytes 40
  10.0 4.5 %copy-start.3 = (f32[13]{0:T(128)S(1)}, f32[13]{0:T(128)}, u32[]{:S(2)}) copy-start(f32[13]{0:T(128)} %coupling_ref.1) | copy-start | bytes 160
  10.0 4.5 %copy-start.4 = (f32[64]{0:T(128)S(1)}, f32[64]{0:T(128)}, u32[]{:S(2)}) copy-start(f32[64]{0:T(128)} %mode_ref.1) | copy-start | bytes 772
